TPU v7x, 32 devices: a whole 2x2x4 slice. The times are simulated.
32 devices in a mesh: dp: 4 (over z), row: 4 (over y, x), col: 2 (over core).
Axes of the slice: x: 2, y: 2, z: 4, core: 2. Of those that a mesh axis runs over, the one named last changes fastest.
Arguments:
- tokens: bfloat16 [4096, 2048], P(('dp', 'row'), 'col'), may hold values from -6 to 6
- cotangent: bfloat16 [4096, 2048], P(('dp', 'row'), 'col'), may hold values from -6 to 6
- seq_lengths: int32 [4, 3], P('dp'), may hold values from 0 to 896, as said below
- gains: float32 [4, 2048], replicated, may hold values from 0.4 to 6.5
- gain_mean: float32 [4, 2048], replicated, may hold values from -40 to 40
- gain_square: float32 [4, 2048], replicated, may hold values from 204.8 to 1638.4
- entry_weight: float32 [3, 2048, 2048], P(None, ('col', 'dp'), 'row'), may hold values from -0.125 to 0.125
- entry_mean: float32 [3, 2048, 2048], P(None, ('col', 'dp'), 'row'), may hold values from -40 to 40
- entry_square: float32 [3, 2048, 2048], P(None, ('col', 'dp'), 'row'), may hold values from 204.8 to 1638.4
- mixer_weight: float32 [2048, 2048], P(('row', 'dp'), 'col'), may hold values from -0.125 to 0.125
- mixer_mean: float32 [2048, 2048], P(('row', 'dp'), 'col'), may hold values from -80 to 80
- mixer_square: float32 [2048, 2048], P(('row', 'dp'), 'col'), may hold values from 819.2 to 6553.6
- expand_weight: float32 [2, 2048, 8192], P(None, ('col', 'dp'), 'row'), may hold values from -0.125 to 0.125
- expand_mean: float32 [2, 2048, 8192], P(None, ('col', 'dp'), 'row'), may hold values from -20 to 20
- expand_square: float32 [2, 2048, 8192], P(None, ('col', 'dp'), 'row'), may hold values from 51.2 to 409.6
- reduce_weight: float32 [8192, 2048], P(('row', 'dp'), 'col'), may hold values from -0.0625 to 0.0625
- reduce_mean: float32 [8192, 2048], P(('row', 'dp'), 'col'), may hold values from -80 to 80
- reduce_square: float32 [8192, 2048], P(('row', 'dp'), 'col'), may hold values from 819.2 to 6553.6
Outputs:
- layer_output: float32 [4096, 2048], P(('dp', 'row'), 'col')
- input_grad: float32 [4096, 2048], P(('dp', 'row'), 'col')
- gain_grad: float32 [4, 2048], replicated
- gain_momentum: float32 [4, 2048], replicated
- gain_variance: float32 [4, 2048], replicated
- gain_updated: float32 [4, 2048], replicated
- entry_grad: float32 [3, 2048, 2048], P(None, ('col', 'dp'), 'row')
- entry_momentum: float32 [3, 2048, 2048], P(None, ('col', 'dp'), 'row')
- entry_variance: float32 [3, 2048, 2048], P(None, ('col', 'dp'), 'row')
- entry_updated: float32 [3, 2048, 2048], P(None, ('col', 'dp'), 'row')
- mixer_grad: float32 [2048, 2048], P(('row', 'dp'), 'col')
- mixer_momentum: float32 [2048, 2048], P(('row', 'dp'), 'col')
- mixer_variance: float32 [2048, 2048], P(('row', 'dp'), 'col')
- mixer_updated: float32 [2048, 2048], P(('row', 'dp'), 'col')
- expand_grad: float32 [2, 2048, 8192], P(None, ('col', 'dp'), 'row')
- expand_momentum: float32 [2, 2048, 8192], P(None, ('col', 'dp'), 'row')
- expand_variance: float32 [2, 2048, 8192], P(None, ('col', 'dp'), 'row')
- expand_updated: float32 [2, 2048, 8192], P(None, ('col', 'dp'), 'row')
- reduce_grad: float32 [8192, 2048], P(('row', 'dp'), 'col')
- reduce_momentum: float32 [8192, 2048], P(('row', 'dp'), 'col')
- reduce_variance: float32 [8192, 2048], P(('row', 'dp'), 'col')
- reduce_updated: float32 [8192, 2048], P(('row', 'dp'), 'col')
Inputs may be any that keep to these rules, and one draw needn't show every extreme that they name: `seq_lengths`: each group's 3 lengths sum to at most 1024; one of them, in a slot drawn from the seed, lies between 769 and 896, and equals 896 in some group; the others may be zero.
All inputs are finite; a program needn't handle non-finite values.
Results may differ from a plain program's by a relative error of at most 0.03.
Values may be sent and summed in bfloat16 or wider, within the bound.
No kernel may reach another device: no remote copies, remote signals or barrier semaphores. Data moves between devices by JAX's collectives and lax.ppermute only.
A program may use at most 192 MiB of HBM per device.

v0:
```python
import jax
import jax.numpy as jnp
from jax import lax
from jax.sharding import PartitionSpec as P

D = 2048
HD = 128
FF = 8192
STEP = 10


NORM_EPSILON = 1e-06
ROPE_BASE = 500000.0
BETA_FIRST = 0.9
BETA_SECOND = 0.95
ADAM_EPSILON = 1e-08
WEIGHT_DECAY = 0.1


def layout_info(lengths, extent):
    indices = jnp.arange(extent, dtype=jnp.int32)
    closing = jnp.cumsum(lengths)
    starts = closing - lengths
    segment = jnp.sum((indices[:, None] >= closing[None, :]).astype(jnp.int32), 1)
    member = segment[:, None] == jnp.arange(lengths.shape[0], dtype=jnp.int32)[None, :]
    anchor = jnp.sum(jnp.where(member, starts[None, :], 0), 1)
    anchor = jnp.where(segment >= lengths.shape[0], closing[-1], anchor)
    return (segment, indices - anchor)


def rotary_tables(positions, width):
    half_width = width // 2
    freqs = ROPE_BASE ** (-jnp.arange(half_width, dtype=jnp.float32) * 2.0 / width)
    angles = positions.astype(jnp.float32)[:, None] * freqs[None, :]
    return (jnp.cos(angles), jnp.sin(angles))


def rotate(values, cosine, sine_table):
    half_width = values.shape[-1] // 2
    first = values[..., :half_width]
    second = values[..., half_width:]
    cos_wide = cosine[:, None, :]
    sin_wide = sine_table[:, None, :]
    return jnp.concatenate(
        [first * cos_wide - second * sin_wide, second * cos_wide + first * sin_wide], -1
    )


def rotate_back(values, cosine, sine_table):
    half_width = values.shape[-1] // 2
    first = values[..., :half_width]
    second = values[..., half_width:]
    cos_wide = cosine[:, None, :]
    sin_wide = sine_table[:, None, :]
    return jnp.concatenate(
        [first * cos_wide + second * sin_wide, second * cos_wide - first * sin_wide], -1
    )


def adam_step(weight, gradient, moment, square, step_rate, decay_rate):
    moment_new = BETA_FIRST * moment + (1.0 - BETA_FIRST) * gradient
    square_new = BETA_SECOND * square + (1.0 - BETA_SECOND) * gradient * gradient
    ratio = (
        moment_new
        / (1.0 - BETA_FIRST**STEP)
        / (jnp.sqrt(square_new / (1.0 - BETA_SECOND**STEP)) + ADAM_EPSILON)
    )
    return (moment_new, square_new, weight - step_rate * (ratio + decay_rate * weight))


def collect_features(values):
    return lax.all_gather(values, "col", axis=1, tiled=True)


def feature_total(values):
    return lax.psum(values, "col")


def grid_total(values):
    return lax.psum((values[0], values[1]), ("row", "col"))


def widen_rows(row_block, blocks):
    gathered = lax.all_gather(row_block, "row", axis=0, tiled=True)
    partial_value = jnp.einsum("td,kdf->ktf", gathered, blocks, preferred_element_type=jnp.float32)
    result = lax.psum_scatter(partial_value, "col", scatter_dimension=2, tiled=True)
    return (gathered, result)


def narrow_rows(features, block_matrix):
    gathered = collect_features(features)
    result = lax.psum_scatter(
        jnp.dot(gathered, block_matrix, preferred_element_type=jnp.float32),
        "row",
        scatter_dimension=0,
        tiled=True,
    )
    return (gathered, result)


def narrow_back(grad_local, gathered_in, block_matrix):
    incoming = lax.all_gather(grad_local, "row", axis=0, tiled=True)
    weight_sum = jnp.einsum("tf,td->fd", gathered_in, incoming, preferred_element_type=jnp.float32)
    update = jnp.einsum("td,fd->tf", incoming, block_matrix, preferred_element_type=jnp.float32)
    partial_value = update
    partial_value, weight_sum = (partial_value, weight_sum)
    feature_grad = lax.psum_scatter(
        partial_value.astype(jnp.bfloat16), "col", scatter_dimension=1, tiled=True
    ).astype(jnp.float32)
    return (feature_grad, weight_sum)


def widen_back(grad_local, gathered_rows, blocks):
    incoming = lax.all_gather(grad_local, "col", axis=2, tiled=True)
    partial_value = jnp.einsum("ktw,kdw->td", incoming, blocks, preferred_element_type=jnp.float32)
    update = jnp.einsum("td,ktw->kdw", gathered_rows, incoming, preferred_element_type=jnp.float32)
    weight_sum = update
    partial_value, weight_sum = (partial_value, weight_sum)
    row_grad = lax.psum_scatter(
        partial_value.astype(jnp.bfloat16), "row", scatter_dimension=0, tiled=True
    ).astype(jnp.float32)
    return (row_grad, weight_sum)


def on_device(
    tokens,
    cotangent,
    seq_lengths,
    gains,
    gain_mean,
    gain_square,
    entry_weight,
    entry_mean,
    entry_square,
    mixer_weight,
    mixer_mean,
    mixer_square,
    expand_weight,
    expand_mean,
    expand_square,
    reduce_weight,
    reduce_mean,
    reduce_square,
):
    entry_block, mixer_block, expand_block, reduce_block = (
        lax.all_gather(entry_weight.astype(jnp.bfloat16), "dp", axis=1, tiled=True),
        lax.all_gather(mixer_weight.astype(jnp.bfloat16), "dp", axis=0, tiled=True),
        lax.all_gather(expand_weight.astype(jnp.bfloat16), "dp", axis=1, tiled=True),
        lax.all_gather(reduce_weight.astype(jnp.bfloat16), "dp", axis=0, tiled=True),
    )
    row_size = lax.axis_size("row")
    col_size = lax.axis_size("col")
    local_rows = tokens.shape[0]
    feature_local = tokens.shape[1]
    extent = local_rows * row_size
    segment, positions = layout_info(seq_lengths[0], extent)
    row_start = lax.axis_index("row") * local_rows
    local_valid = (
        lax.dynamic_slice_in_dim(segment, row_start, local_rows, 0) < seq_lengths.shape[1]
    ).astype(jnp.float32)
    head_width = entry_block.shape[2] // col_size
    head_start = (lax.axis_index("row") * col_size + lax.axis_index("col")) * head_width
    col_start = lax.axis_index("col") * feature_local
    post_gain = lax.dynamic_slice_in_dim(gains[0:2], col_start, feature_local, 1)
    head_gain = lax.dynamic_slice_in_dim(gains[2:4], head_start, head_width, 1)
    head_count = head_width // HD
    shrink = HD ** (-0.5)
    inputs = tokens.astype(jnp.float32)
    token_rows, projected = widen_rows(tokens, entry_block)
    squares = grid_total(
        (jnp.sum(projected[0] * projected[0], -1), jnp.sum(projected[1] * projected[1], -1))
    )
    query_scale = lax.rsqrt(squares[0] / D + NORM_EPSILON)[:, None]
    key_scale = lax.rsqrt(squares[1] / D + NORM_EPSILON)[:, None]
    query_hat = projected[0] * query_scale
    key_hat = projected[1] * key_scale
    cosine, sine_table = rotary_tables(positions, HD)
    query_rot = rotate(
        (query_hat * head_gain[0]).reshape(extent, head_count, HD), cosine, sine_table
    ).astype(jnp.bfloat16)
    key_rot = rotate(
        (key_hat * head_gain[1]).reshape(extent, head_count, HD), cosine, sine_table
    ).astype(jnp.bfloat16)
    value_rows = projected[2].astype(jnp.bfloat16).reshape(extent, head_count, HD)
    block_rows = min(512, extent)
    indices = jnp.arange(extent, dtype=jnp.int32)

    def block_scores(offset):
        query_block = query_rot[offset : offset + block_rows]
        scores = (
            jnp.einsum("qhd,khd->hqk", query_block, key_rot, preferred_element_type=jnp.float32)
            * shrink
        )
        rows_here = indices[offset : offset + block_rows]
        allowed = (segment[offset : offset + block_rows][:, None] == segment[None, :]) & (
            indices[None, :] <= rows_here[:, None]
        )
        return (query_block, jnp.where(allowed[None], scores, -1e30))

    outputs = []
    logsums = []
    for offset in range(0, extent, block_rows):
        query_block, masked = block_scores(offset)
        peak = jnp.max(masked, -1, keepdims=True)
        expo = jnp.exp(masked - peak)
        totals = jnp.sum(expo, -1, keepdims=True)
        shares = (expo / totals).astype(jnp.bfloat16)
        outputs.append(
            jnp.einsum("hqk,khd->qhd", shares, value_rows, preferred_element_type=jnp.float32)
        )
        logsums.append(peak + jnp.log(totals))
    attended = jnp.concatenate(outputs, 0).astype(jnp.bfloat16).reshape(extent, head_width)
    attended_cols, branch = narrow_rows(attended, mixer_block)
    branch_scale = lax.rsqrt(feature_total(jnp.sum(branch * branch, -1)) / D + NORM_EPSILON)[
        :, None
    ]
    branch_hat = branch * branch_scale
    hidden = inputs + branch_hat * post_gain[0]
    hidden_rows, gated = widen_rows(hidden.astype(jnp.bfloat16), expand_block)
    product = (jax.nn.silu(gated[0]) * gated[1]).astype(jnp.bfloat16)
    product_cols, second = narrow_rows(product, reduce_block)
    second_scale = lax.rsqrt(feature_total(jnp.sum(second * second, -1)) / D + NORM_EPSILON)[
        :, None
    ]
    second_hat = second * second_scale
    layer_output = hidden + second_hat * post_gain[1]
    upstream = cotangent.astype(jnp.float32) * local_valid[:, None]
    gain_second_post = jnp.sum(upstream * second_hat, 0)
    scaled = upstream * post_gain[1]
    inner_sum = feature_total(jnp.sum(scaled * second_hat, -1))
    second_grad = (second_scale * (scaled - second_hat * inner_sum[:, None] / D)).astype(
        jnp.bfloat16
    )
    product_grad, reduce_sum = narrow_back(second_grad, product_cols, reduce_block)
    sigmoid = jax.nn.sigmoid(gated[0])
    gate_grad = product_grad * gated[1] * sigmoid * (1.0 + gated[0] * (1.0 - sigmoid))
    up_grad = product_grad * jax.nn.silu(gated[0])
    hidden_back, expand_sum = widen_back(
        jnp.stack([gate_grad, up_grad]).astype(jnp.bfloat16), hidden_rows, expand_block
    )
    hidden_grad = upstream + hidden_back
    gain_first_post = jnp.sum(hidden_grad * branch_hat, 0)
    scaled = hidden_grad * post_gain[0]
    inner_sum = feature_total(jnp.sum(scaled * branch_hat, -1))
    branch_grad = (branch_scale * (scaled - branch_hat * inner_sum[:, None] / D)).astype(
        jnp.bfloat16
    )
    attended_grad, mixer_sum = narrow_back(branch_grad, attended_cols, mixer_block)
    attended_low = attended_grad.astype(jnp.bfloat16).reshape(extent, head_count, HD)
    query_parts = []
    key_accum = jnp.zeros((extent, head_count, HD), jnp.float32)
    value_accum = jnp.zeros((extent, head_count, HD), jnp.float32)
    for number, offset in enumerate(range(0, extent, block_rows)):
        query_block, masked = block_scores(offset)
        shares = jnp.exp(masked - logsums[number])
        grad_block = attended_low[offset : offset + block_rows]
        flow_grad = jnp.einsum(
            "qhd,khd->hqk", grad_block, value_rows, preferred_element_type=jnp.float32
        )
        row_delta = jnp.sum(shares * flow_grad, -1, keepdims=True)
        score_grad = (shares * (flow_grad - row_delta)).astype(jnp.bfloat16)
        query_parts.append(
            jnp.einsum("hqk,khd->qhd", score_grad, key_rot, preferred_element_type=jnp.float32)
            * shrink
        )
        key_accum = (
            key_accum
            + jnp.einsum(
                "hqk,qhd->khd", score_grad, query_block, preferred_element_type=jnp.float32
            )
            * shrink
        )
        value_accum = value_accum + jnp.einsum(
            "hqk,qhd->khd",
            shares.astype(jnp.bfloat16),
            grad_block,
            preferred_element_type=jnp.float32,
        )
    query_grad = rotate_back(jnp.concatenate(query_parts, 0), cosine, sine_table).reshape(
        extent, head_width
    )
    key_grad = rotate_back(key_accum, cosine, sine_table).reshape(extent, head_width)
    gain_query = jnp.sum(query_grad * query_hat, 0)
    gain_key = jnp.sum(key_grad * key_hat, 0)
    query_scaled = query_grad * head_gain[0]
    key_scaled = key_grad * head_gain[1]
    head_dots = grid_total(
        (jnp.sum(query_scaled * query_hat, -1), jnp.sum(key_scaled * key_hat, -1))
    )
    query_raw = query_scale * (query_scaled - query_hat * head_dots[0][:, None] / D)
    key_raw = key_scale * (key_scaled - key_hat * head_dots[1][:, None] / D)
    value_grad = value_accum.reshape(extent, head_width)
    entry_back, entry_sum = widen_back(
        jnp.stack([query_raw, key_raw, value_grad]).astype(jnp.bfloat16), token_rows, entry_block
    )
    input_grad = hidden_grad + entry_back
    entry_grad, mixer_grad, expand_grad, reduce_grad = (
        lax.psum_scatter(
            entry_sum.astype(jnp.bfloat16), "dp", scatter_dimension=1, tiled=True
        ).astype(jnp.float32),
        lax.psum_scatter(
            mixer_sum.astype(jnp.bfloat16), "dp", scatter_dimension=0, tiled=True
        ).astype(jnp.float32),
        lax.psum_scatter(
            expand_sum.astype(jnp.bfloat16), "dp", scatter_dimension=1, tiled=True
        ).astype(jnp.float32),
        lax.psum_scatter(
            reduce_sum.astype(jnp.bfloat16), "dp", scatter_dimension=0, tiled=True
        ).astype(jnp.float32),
    )
    gain_local = jnp.zeros((4, D), jnp.float32)
    gain_local = lax.dynamic_update_slice(
        gain_local, jnp.stack([gain_first_post, gain_second_post]), (0, col_start)
    )
    gain_local = lax.dynamic_update_slice(
        gain_local, jnp.stack([gain_query, gain_key]), (2, head_start)
    )
    gain_grad = lax.psum(gain_local, ("dp", "row", "col"))
    gain_momentum, gain_variance, gain_updated = adam_step(
        gains, gain_grad, gain_mean, gain_square, 1.0, 0.0
    )
    entry_momentum, entry_variance, entry_updated = adam_step(
        entry_weight, entry_grad, entry_mean, entry_square, 2.0 * D ** (-0.5), WEIGHT_DECAY
    )
    mixer_momentum, mixer_variance, mixer_updated = adam_step(
        mixer_weight, mixer_grad, mixer_mean, mixer_square, 2.0 * D ** (-0.5), WEIGHT_DECAY
    )
    expand_momentum, expand_variance, expand_updated = adam_step(
        expand_weight, expand_grad, expand_mean, expand_square, 2.0 * D ** (-0.5), WEIGHT_DECAY
    )
    reduce_momentum, reduce_variance, reduce_updated = adam_step(
        reduce_weight, reduce_grad, reduce_mean, reduce_square, 2.0 * FF ** (-0.5), WEIGHT_DECAY
    )
    return (
        layer_output,
        input_grad,
        gain_grad,
        gain_momentum,
        gain_variance,
        gain_updated,
        entry_grad,
        entry_momentum,
        entry_variance,
        entry_updated,
        mixer_grad,
        mixer_momentum,
        mixer_variance,
        mixer_updated,
        expand_grad,
        expand_momentum,
        expand_variance,
        expand_updated,
        reduce_grad,
        reduce_momentum,
        reduce_variance,
        reduce_updated,
    )


def solution(mesh):
    placed = (
        P(("dp", "row"), "col"),
        P(("dp", "row"), "col"),
        P("dp", None),
        P(),
        P(),
        P(),
        P(None, ("col", "dp"), "row"),
        P(None, ("col", "dp"), "row"),
        P(None, ("col", "dp"), "row"),
        P(("row", "dp"), "col"),
        P(("row", "dp"), "col"),
        P(("row", "dp"), "col"),
        P(None, ("col", "dp"), "row"),
        P(None, ("col", "dp"), "row"),
        P(None, ("col", "dp"), "row"),
        P(("row", "dp"), "col"),
        P(("row", "dp"), "col"),
        P(("row", "dp"), "col"),
    )
    return jax.shard_map(
        on_device,
        mesh=mesh,
        in_specs=placed,
        out_specs=(
            P(("dp", "row"), "col"),
            P(("dp", "row"), "col"),
            P(),
            P(),
            P(),
            P(),
            P(None, ("col", "dp"), "row"),
            P(None, ("col", "dp"), "row"),
            P(None, ("col", "dp"), "row"),
            P(None, ("col", "dp"), "row"),
            P(("row", "dp"), "col"),
            P(("row", "dp"), "col"),
            P(("row", "dp"), "col"),
            P(("row", "dp"), "col"),
            P(None, ("col", "dp"), "row"),
            P(None, ("col", "dp"), "row"),
            P(None, ("col", "dp"), "row"),
            P(None, ("col", "dp"), "row"),
            P(("row", "dp"), "col"),
            P(("row", "dp"), "col"),
            P(("row", "dp"), "col"),
            P(("row", "dp"), "col"),
        ),
        check_vma=False,
    )
```

profile of v0, /device:TPU:0, one launch (start us, length us, event | category | flops | bytes accessed | tf_op | source)
XLA Modules:
  0.0 1273.9 jit_solution(5691639292150265874)
XLA Ops:
  11.0 36.9 %all-gather.15.cloned.1.call-done = bf16[1024,1024]{1,0:T(8,128)(2,1)} async-done(((bf16[256,1024]{1,0:T(8,128)(2,1)}), bf16[1024,1024]{1,0:T(8,128)(2,1)}) %all-gather.15.cloned.1.call-update) | async-done | bytes 2097168 | tf_op jit(solution)/shard_map/all_gather | solution.py:84
  47.9 65.6 %all-gather.13.cloned.1.call-done = bf16[3,1024,512]{1,2,0:T(8,128)(2,1)} async-done(((bf16[3,256,512]{1,2,0:T(8,128)(2,1)}), bf16[3,1024,512]{1,2,0:T(8,128)(2,1)}) %all-gather.13.cloned.1.call-update) | async-done | bytes 3145744 | tf_op jit(solution)/shard_map/all_gather | solution.py:146
  113.5 8.7 convolution_bitcast_fusion.1
  129.7 5.4 reduce-scatter.13.cloned.1.call-done
  135.0 2.9 multiply_reduce_fusion.10
  139.8 15.2 %all-reduce.1 = (f32[1024]{0:T(1024)S(1)}, f32[1024]{0:T(1024)S(1)}) all-reduce(f32[1024]{0:T(1024)S(1)} %get-tuple-element.73, f32[1024]{0:T(1024)S(1)} %get-tuple-element.72), channel_id=1, replica_groups=mesh['dp'=4,'row'=4,'col'=2] {'row','col'}, use_global_device_ids=true, to_apply=%region_4.5 | all-reduce | flops 2048 | bytes 16384 | tf_op jit(solution)/shard_map/psum | solution.py:80
  166.3 10.6 all-gather.17.cloned.1.call-done
  176.9 4.8 fusion.63
  181.8 3.9 convert_element_type.134
  185.8 49.9 %reduce-scatter.15.cloned.1.call-done = f32[256,1024]{1,0:T(8,128)} async-done(((f32[1024,1024]{1,0:T(8,128)}), f32[256,1024]{1,0:T(8,128)}) %reduce-scatter.15.cloned.1.call-update) | async-done | bytes 1048592 | tf_op jit(solution)/shard_map/reduce_scatter | solution.py:92
  237.1 2.5 psum.65
  242.1 145.4 %all-gather.23.cloned.1.call-done = bf16[2,1024,2048]{2,1,0:T(8,128)(2,1)} async-done(((bf16[2,256,2048]{2,1,0:T(8,128)(2,1)}), bf16[2,1024,2048]{2,1,0:T(8,128)(2,1)}) %all-gather.23.cloned.1.call-update) | async-done | bytes 8388624 | tf_op jit(solution)/shard_map/all_gather | solution.py:148
  387.6 36.0 %all-gather.21.cloned.1.call-done = bf16[1024,1024]{1,0:T(8,128)(2,1)} async-done(((bf16[256,1024]{1,0:T(8,128)(2,1)}), bf16[1024,1024]{1,0:T(8,128)(2,1)}) %all-gather.21.cloned.1.call-update) | async-done | bytes 2097168 | tf_op jit(solution)/shard_map/all_gather | solution.py:84
  423.5 16.0 %convolution_bitcast_fusion = f32[2,1024,2048]{2,1,0:T(8,128)} fusion(bf16[2,1024,2048]{2,1,0:T(8,128)(2,1)} %all-gather.23.cloned.1.call-done, bf16[1024,1024]{1,0:T(8,128)(2,1)} %all-gather.21.cloned.1.call-done), kind=kOutput, calls=%fused_computation.1 | convolution fusion | flops 8589934592 | bytes 27262976 | tf_op jit(solution)/shard_map/td,kdf->ktf/dot_general | solution.py:85
  442.3 23.6 %reduce-scatter.17.cloned.1.call-done = f32[2,1024,1024]{2,1,0:T(8,128)} async-done(((f32[2,1024,2048]{2,1,0:T(8,128)}), f32[2,1024,1024]{2,1,0:T(8,128)}) %reduce-scatter.17.cloned.1.call-update) | async-done | bytes 8388624 | tf_op jit(solution)/shard_map/reduce_scatter | solution.py:86
  465.9 6.1 multiply_convert_fusion.2
  472.1 77.9 %all-gather.27.cloned.1.call-done = bf16[2048,1024]{1,0:T(8,128)(2,1)} async-done(((bf16[512,1024]{1,0:T(8,128)(2,1)}), bf16[2048,1024]{1,0:T(8,128)(2,1)}) %all-gather.27.cloned.1.call-update) | async-done | bytes 4194320 | tf_op jit(solution)/shard_map/all_gather | solution.py:149
  550.0 14.4 %all-gather.25.cloned.1.call-done = bf16[1024,2048]{1,0:T(8,128)(2,1)} async-done(((bf16[1024,1024]{1,0:T(8,128)(2,1)}), bf16[1024,2048]{1,0:T(8,128)(2,1)}) %all-gather.25.cloned.1.call-update) | async-done | bytes 4194320 | tf_op jit(solution)/shard_map/all_gather | solution.py:72
  564.5 10.0 fusion.64
  574.6 53.9 %reduce-scatter.19.cloned.1.call-done = f32[256,1024]{1,0:T(8,128)} async-done(((f32[1024,1024]{1,0:T(8,128)}), f32[256,1024]{1,0:T(8,128)}) %reduce-scatter.19.cloned.1.call-update) | async-done | bytes 1048592 | tf_op jit(solution)/shard_map/reduce_scatter | solution.py:92
  629.9 2.5 psum.66
  634.0 2.5 psum.67
  639.4 35.0 %all-gather.29.cloned.1.call-done = bf16[1024,1024]{1,0:T(8,128)(2,1)} async-done(((bf16[256,1024]{1,0:T(8,128)(2,1)}), bf16[1024,1024]{1,0:T(8,128)(2,1)}) %all-gather.29.cloned.1.call-update) | async-done | bytes 2097168 | tf_op jit(solution)/shard_map/all_gather | solution.py:102
  674.4 9.4 convolution_convert_fusion.1
  683.8 12.1 reduce-scatter.21.cloned.1.call-done
  696.0 5.2 fusion.26
  703.6 21.2 %all-gather.31.cloned.1.call-done = bf16[2,1024,2048]{2,1,0:T(8,128)(2,1)} async-done(((bf16[2,1024,1024]{2,1,0:T(8,128)(2,1)}), bf16[2,1024,2048]{2,1,0:T(8,128)(2,1)}) %all-gather.31.cloned.1.call-update) | async-done | bytes 8388624 | tf_op jit(solution)/shard_map/all_gather | solution.py:114
  724.9 14.7 %bitcast_convert_fusion.1 = bf16[1024,1024]{1,0:T(8,128)(2,1)} fusion(bf16[2,1024,2048]{2,1,0:T(8,128)(2,1)} %all-gather.31.cloned.1.call-done, bf16[2,1024,2048]{2,1,0:T(8,128)(2,1)} %all-gather.23.cloned.1.call-done), kind=kOutput, calls=%fused_computation.14 | convolution fusion | flops 8590983168 | bytes 18874368 | tf_op jit(solution)/shard_map/ktw,kdw->td/dot_general | solution.py:115
  739.6 36.5 %reduce-scatter.23.cloned.1.call-done = bf16[256,1024]{1,0:T(8,128)(2,1)} async-done(((bf16[1024,1024]{1,0:T(8,128)(2,1)}), bf16[256,1024]{1,0:T(8,128)(2,1)}) %reduce-scatter.23.cloned.1.call-update) | async-done | bytes 524304 | tf_op jit(solution)/shard_map/reduce_scatter | solution.py:119
  777.7 2.5 psum.68
  780.1 3.0 multiply_convert_fusion.5
  783.2 35.4 %all-gather.33.cloned.1.call-done = bf16[1024,1024]{1,0:T(8,128)(2,1)} async-done(((bf16[256,1024]{1,0:T(8,128)(2,1)}), bf16[1024,1024]{1,0:T(8,128)(2,1)}) %all-gather.33.cloned.1.call-update) | async-done | bytes 2097168 | tf_op jit(solution)/shard_map/all_gather | solution.py:102
  818.6 4.1 convolution_convert_fusion.3
  823.0 8.4 reduce-scatter.25.cloned.1.call-done
  832.6 3.2 fusion.11
  836.1 3.1 multiply_reduce_fusion
  839.4 3.5 multiply_reduce_fusion.1
  854.2 2.7 copy.89
  856.9 2.9 pad_maximum_fusion.4
  859.7 2.5 copy.94
  864.4 14.6 %all-reduce = (f32[1024]{0:T(1024)S(1)}, f32[1024]{0:T(1024)S(1)}) all-reduce(f32[1024]{0:T(1024)S(1)} %get-tuple-element.70, f32[1024]{0:T(1024)S(1)} %get-tuple-element.67), channel_id=1, replica_groups=mesh['dp'=4,'row'=4,'col'=2] {'row','col'}, use_global_device_ids=true, to_apply=%region_31.32 | all-reduce | flops 2048 | bytes 16384 | tf_op jit(solution)/shard_map/psum | solution.py:80
  883.3 8.3 convolution_convert_fusion
  892.8 3.8 convolution_convert_fusion.2
  896.7 14.6 %convert_bitcast_fusion = bf16[2,1024,2048]{1,2,0:T(8,128)(2,1)} fusion(bf16[2,1024,2048]{2,1,0:T(8,128)(2,1)} %all-gather.31.cloned.1.call-done, bf16[1024,1024]{1,0:T(8,128)(2,1)S(1)} %copy-done.45), kind=kOutput, calls=%fused_computation | convolution fusion | flops 8594128896 | bytes 18874368 | tf_op jit(solution)/shard_map/td,ktw->kdw/dot_general | solution.py:116
  913.2 6.6 bitcast_convert_fusion
  920.2 7.6 convert_bitcast_fusion.1
  927.9 5.5 copy.107
  936.6 5.4 copy.105
  942.0 5.5 copy.104
  947.5 27.1 %reduce-scatter.35.cloned.1.call-done = bf16[512,1024]{1,0:T(8,128)(2,1)} async-done(((bf16[2048,1024]{1,0:T(8,128)(2,1)}), bf16[512,1024]{1,0:T(8,128)(2,1)}) %reduce-scatter.35.cloned.1.call-update) | async-done | bytes 1048592 | tf_op jit(solution)/shard_map/reduce_scatter | solution.py:307
  974.6 6.6 multiply_subtract_fusion.1
  981.2 42.0 %psum.71 = f32[4,2048]{1,0:T(4,128)S(1)} all-reduce(f32[4,2048]{1,0:T(4,128)S(1)} %maximum_dynamic-update-slice_fusion.1), channel_id=1, replica_groups=mesh['dp'=4,'row'=4,'col'=2] {'dp','row','col'}, use_global_device_ids=true, to_apply=%region_37.38 | all-reduce | flops 8192 | bytes 65536 | tf_op jit(solution)/shard_map/psum | solution.py:318
  1023.4 2.6 multiply_subtract_fusion.5
  1026.6 124.6 %reduce-scatter.33.cloned.1.call-done = bf16[2,256,2048]{1,2,0:T(8,128)(2,1)} async-done(((bf16[2,1024,2048]{1,2,0:T(8,128)(2,1)}), bf16[2,256,2048]{1,2,0:T(8,128)(2,1)}) %reduce-scatter.33.cloned.1.call-update) | async-done | bytes 2097168 | tf_op jit(solution)/shard_map/reduce_scatter | solution.py:304
  1151.3 10.0 multiply_subtract_fusion
  1161.2 5.5 copy.113
  1166.7 5.4 copy.114
  1172.2 5.4 copy.115
  1177.5 4.3 copy.112
  1181.8 8.7 reduce-scatter.27.cloned.1.call-done
  1192.8 60.2 %reduce-scatter.29.cloned.1.call-done = bf16[3,256,512]{1,2,0:T(8,128)(2,1)} async-done(((bf16[3,1024,512]{1,2,0:T(8,128)(2,1)}), bf16[3,256,512]{1,2,0:T(8,128)(2,1)}) %reduce-scatter.29.cloned.1.call-update) | async-done | bytes 786448 | tf_op jit(solution)/shard_map/reduce_scatter | solution.py:298
  1252.9 5.0 multiply_subtract_fusion.2
  1257.9 3.1 copy.109
  1264.3 2.6 copy.108
  (220 shorter events, 73.6 us)
Async XLA Ops:
  7.2 40.7 %all-gather.15.cloned.1.call-start = ((), (), s32[]{:S(2)}) async-start(), calls=%async_computation.13 | async-start | bytes 2621440 | tf_op jit(solution)/shard_map/all_gather | solution.py:84
  7.9 105.6 %all-gather.13.cloned.1.call-start = ((), (), s32[]{:S(2)}) async-start(), calls=%async_computation.12 | async-start | bytes 3932160 | tf_op jit(solution)/shard_map/all_gather | solution.py:146
  9.9 112.3 %copy-start.9 = (f32[3,256,512]{1,2,0:T(8,128)}, f32[3,256,512]{1,2,0:T(8,128)S(1)}, u32[]{:S(2)}) copy-start(f32[3,256,512]{1,2,0:T(8,128)S(1)} %copy.78) | copy-start | bytes 4718596
  10.9 124.1 %reduce-scatter.13.cloned.1.call-start = ((), (), s32[]{:S(2)}) async-start(), calls=%async_computation.14 | async-start | bytes 9437184 | tf_op jit(solution)/shard_map/reduce_scatter | solution.py:86
  122.2 1.9 copy-start.47
  122.2 2.6 copy-start.39
  122.2 44.0 %all-gather.19.cloned.1.call-start = ((), (), s32[]{:S(2)}) async-start(), calls=%async_computation.16 | async-start | bytes 1310720 | tf_op jit(solution)/shard_map/all_gather | solution.py:147
  124.0 52.9 %all-gather.17.cloned.1.call-start = ((), (), s32[]{:S(2)}) async-start(), calls=%async_computation.15 | async-start | bytes 1572864 | tf_op jit(solution)/shard_map/all_gather | solution.py:72
  127.6 27.8 %copy-start.18 = (f32[1024,64]{1,0:T(8,128)}, f32[1024,64]{1,0:T(8,128)S(1)}, u32[]{:S(2)}) copy-start(f32[1024,64]{1,0:T(8,128)S(1)} %get-tuple-element.127) | copy-start | bytes 786436
  127.6 27.8 %copy-start.20 = (f32[1024,64]{1,0:T(8,128)}, f32[1024,64]{1,0:T(8,128)S(1)}, u32[]{:S(2)}) copy-start(f32[1024,64]{1,0:T(8,128)S(1)} %get-tuple-element.128) | copy-start | bytes 786436
  156.7 2.3 copy-start.24
  157.9 5.8 copy-start.3
  159.0 3.6 copy-start
  165.8 70.0 %reduce-scatter.15.cloned.1.call-start = ((), (), s32[]{:S(2)}) async-start(), calls=%async_computation.17 | async-start | bytes 5242880 | tf_op jit(solution)/shard_map/reduce_scatter | solution.py:92
  181.7 57.9 %copy-start.23 = (bf16[256,1024]{1,0:T(8,128)(2,1)S(1)}, bf16[256,1024]{1,0:T(8,128)(2,1)}, u32[]{:S(2)}) copy-start(bf16[256,1024]{1,0:T(8,128)(2,1)} %param.18) | copy-start | bytes 1572868
  181.7 205.8 %all-gather.23.cloned.1.call-start = ((), (), s32[]{:S(2)}) async-start(), calls=%async_computation.19 | async-start | bytes 10485760 | tf_op jit(solution)/shard_map/all_gather | solution.py:148
  185.7 237.8 %all-gather.21.cloned.1.call-start = ((), (), s32[]{:S(2)}) async-start(), calls=%async_computation.18 | async-start | bytes 2621440 | tf_op jit(solution)/shard_map/all_gather | solution.py:84
  241.9 224.0 %reduce-scatter.17.cloned.1.call-start = ((), (), s32[]{:S(2)}) async-start(), calls=%async_computation.20 | async-start | bytes 25165824 | tf_op jit(solution)/shard_map/reduce_scatter | solution.py:86
  439.5 110.5 %all-gather.27.cloned.1.call-start = ((), (), s32[]{:S(2)}) async-start(), calls=%async_computation.22 | async-start | bytes 5242880 | tf_op jit(solution)/shard_map/all_gather | solution.py:149
  442.2 122.3 %all-gather.25.cloned.1.call-start = ((), (), s32[]{:S(2)}) async-start(), calls=%async_computation.21 | async-start | bytes 6291456 | tf_op jit(solution)/shard_map/all_gather | solution.py:72
  472.1 156.4 %reduce-scatter.19.cloned.1.call-start = ((), (), s32[]{:S(2)}) async-start(), calls=%async_computation.23 | async-start | bytes 5242880 | tf_op jit(solution)/shard_map/reduce_scatter | solution.py:92
  574.4 57.9 %copy-start.11 = (bf16[256,1024]{1,0:T(8,128)(2,1)S(1)}, bf16[256,1024]{1,0:T(8,128)(2,1)}, u32[]{:S(2)}) copy-start(bf16[256,1024]{1,0:T(8,128)(2,1)} %param.19) | copy-start | bytes 1572868
  574.5 99.9 %all-gather.29.cloned.1.call-start = ((), (), s32[]{:S(2)}) async-start(), calls=%async_computation.24 | async-start | bytes 2621440 | tf_op jit(solution)/shard_map/all_gather | solution.py:102
  638.9 57.1 %reduce-scatter.21.cloned.1.call-start = ((), (), s32[]{:S(2)}) async-start(), calls=%async_computation.25 | async-start | bytes 6291456 | tf_op jit(solution)/shard_map/reduce_scatter | solution.py:107
  683.8 41.1 %all-gather.31.cloned.1.call-start = ((), (), s32[]{:S(2)}) async-start(), calls=%async_computation.26 | async-start | bytes 12582912 | tf_op jit(solution)/shard_map/all_gather | solution.py:114
  703.6 72.5 %copy-start.6 = (f32[256,1024]{1,0:T(8,128)S(1)}, f32[256,1024]{1,0:T(8,128)}, u32[]{:S(2)}) copy-start(f32[256,1024]{1,0:T(8,128)} %reduce-scatter.15.cloned.1.call-done) | copy-start | bytes 3145732
  703.6 72.5 %reduce-scatter.23.cloned.1.call-start = ((), (), s32[]{:S(2)}) async-start(), calls=%async_computation.27 | async-start | bytes 2621440 | tf_op jit(solution)/shard_map/reduce_scatter | solution.py:119
  739.6 40.6 %copy-start.7 = (f32[256,1024]{1,0:T(8,128)S(1)}, f32[256,1024]{1,0:T(8,128)}, u32[]{:S(2)}) copy-start(f32[256,1024]{1,0:T(8,128)} %reduce-scatter.19.cloned.1.call-done) | copy-start | bytes 3145732
  739.6 79.0 %all-gather.33.cloned.1.call-start = ((), (), s32[]{:S(2)}) async-start(), calls=%async_computation.28 | async-start | bytes 2621440 | tf_op jit(solution)/shard_map/all_gather | solution.py:102
  783.1 48.3 %reduce-scatter.25.cloned.1.call-start = ((), (), s32[]{:S(2)}) async-start(), calls=%async_computation.29 | async-start | bytes 1572864 | tf_op jit(solution)/shard_map/reduce_scatter | solution.py:107
  822.7 13.2 %copy-start.27 = (bf16[1,1024,256]{1,2,0:T(8,128)(2,1)S(1)}, bf16[1,1024,256]{1,2,0:T(8,128)(2,1)}, u32[]{:S(2)}) copy-start(bf16[1,1024,256]{1,2,0:T(8,128)(2,1)} %copy-done.26) | copy-start | bytes 1572868
  822.7 88.6 %all-gather.35.cloned.1.call-start = ((), (), s32[]{:S(2)}) async-start(), calls=%async_computation.30 | async-start | bytes 4718592 | tf_op jit(solution)/shard_map/all_gather | solution.py:114
  832.6 3.5 copy-start.1
  839.3 3.6 copy-start.28
  839.3 3.6 copy-start.4
  842.9 1.8 copy-start.16
  844.0 1.8 copy-start.29
  844.7 2.8 copy-start.2
  844.7 3.7 copy-start.5
  849.2 1.7 copy-start.19
  849.2 1.7 copy-start.21
  854.2 8.1 copy-start.8
  879.0 2.1 copy-start.33
  881.1 2.2 copy-start.46
  882.5 92.2 %reduce-scatter.35.cloned.1.call-start = ((), (), s32[]{:S(2)}) async-start(), calls=%async_computation.35 | async-start | bytes 5242880 | tf_op jit(solution)/shard_map/reduce_scatter | solution.py:307
  891.6 5.1 copy-start.45
  891.6 131.7 %reduce-scatter.31.cloned.1.call-start = ((), (), s32[]{:S(2)}) async-start(), calls=%async_computation.33 | async-start | bytes 1310720 | tf_op jit(solution)/shard_map/reduce_scatter | solution.py:301
  896.6 254.6 %reduce-scatter.33.cloned.1.call-start = ((), (), s32[]{:S(2)}) async-start(), calls=%async_computation.34 | async-start | bytes 10485760 | tf_op jit(solution)/shard_map/reduce_scatter | solution.py:304
  911.3 1.9 copy-start.44
  911.3 279.2 %reduce-scatter.27.cloned.1.call-start = ((), (), s32[]{:S(2)}) async-start(), calls=%async_computation.31 | async-start | bytes 2621440 | tf_op jit(solution)/shard_map/reduce_scatter | solution.py:119
  919.8 333.1 %reduce-scatter.29.cloned.1.call-start = ((), (), s32[]{:S(2)}) async-start(), calls=%async_computation.32 | async-start | bytes 3932160 | tf_op jit(solution)/shard_map/reduce_scatter | solution.py:298
  927.9 5.5 copy-start.36
  927.9 7.1 copy-start.37
  942.0 32.6 %copy-start.14 = (f32[512,1024]{1,0:T(8,128)S(1)}, f32[512,1024]{1,0:T(8,128)}, u32[]{:S(2)}) copy-start(f32[512,1024]{1,0:T(8,128)} %param.33) | copy-start | bytes 6291460
  947.5 75.8 %copy-start.31 = (f32[128,1024]{1,0:T(8,128)S(1)}, f32[128,1024]{1,0:T(8,128)}, u32[]{:S(2)}) copy-start(f32[128,1024]{1,0:T(8,128)} %param.27) | copy-start | bytes 1572868
  947.5 75.8 %copy-start.38 = (f32[128,1024]{1,0:T(8,128)S(1)}, f32[128,1024]{1,0:T(8,128)}, u32[]{:S(2)}) copy-start(f32[128,1024]{1,0:T(8,128)} %param.29) | copy-start | bytes 1572868
  947.5 78.4 %copy-start.40 = (f32[4,2048]{1,0:T(4,128)S(1)}, f32[4,2048]{1,0:T(4,128)}, u32[]{:S(2)}) copy-start(f32[4,2048]{1,0:T(4,128)} %param.21) | copy-start | bytes 98308
  947.5 78.4 %copy-start.42 = (f32[4,2048]{1,0:T(4,128)S(1)}, f32[4,2048]{1,0:T(4,128)}, u32[]{:S(2)}) copy-start(f32[4,2048]{1,0:T(4,128)} %param.23) | copy-start | bytes 98308
  947.5 78.4 %copy-start.43 = (f32[4,2048]{1,0:T(4,128)S(1)}, f32[4,2048]{1,0:T(4,128)}, u32[]{:S(2)}) copy-start(f32[4,2048]{1,0:T(4,128)} %param.22) | copy-start | bytes 98308
  1023.3 137.9 %copy-start.41 = (f32[4,2048]{1,0:T(4,128)}, f32[4,2048]{1,0:T(4,128)S(1)}, u32[]{:S(2)}) copy-start(f32[4,2048]{1,0:T(4,128)S(1)} %psum.71) | copy-start | bytes 98308
  1177.5 12.9 %copy-start.12 = (bf16[256,1024]{1,0:T(8,128)(2,1)S(1)}, bf16[256,1024]{1,0:T(8,128)(2,1)}, u32[]{:S(2)}) copy-start(bf16[256,1024]{1,0:T(8,128)(2,1)} %param.19) | copy-start | bytes 1572868
  1177.5 12.9 %copy-start.22 = (bf16[256,1024]{1,0:T(8,128)(2,1)S(1)}, bf16[256,1024]{1,0:T(8,128)(2,1)}, u32[]{:S(2)}) copy-start(bf16[256,1024]{1,0:T(8,128)(2,1)} %reduce-scatter.23.cloned.1.call-done) | copy-start | bytes 1572868
  1177.5 75.4 %copy-start.10 = (f32[3,256,512]{1,2,0:T(8,128)S(1)}, f32[3,256,512]{1,2,0:T(8,128)}, u32[]{:S(2)}) copy-start(f32[3,256,512]{1,2,0:T(8,128)} %copy-done.9) | copy-start | bytes 4718596
  1257.9 3.1 copy-start.17
  (8 other events, 10.6 us)
Sparse Core Ops, SparseCore 0:
  9.9 38.0 all-gather.14
  50.0 63.4 all-gather.12
  122.3 12.6 reduce-scatter.12
  137.1 29.0 all-gather.18
  168.3 8.5 all-gather.16
  181.8 53.8 reduce-scatter.14
  237.9 149.6 all-gather.22
  390.0 33.4 all-gather.20
  439.6 26.2 reduce-scatter.16
  468.0 82.0 all-gather.26
  552.2 12.1 all-gather.24
  574.6 53.8 reduce-scatter.18
  639.0 35.2 all-gather.28
  683.9 12.0 reduce-scatter.20
  703.7 21.1 all-gather.30
  739.7 36.3 reduce-scatter.22
  783.2 35.2 all-gather.32
  822.8 8.5 reduce-scatter.24
  882.6 11.2 all-gather.34
  896.7 77.9 reduce-scatter.34
  977.5 28.0 reduce-scatter.30
  1008.1 143.1 reduce-scatter.32
  1154.5 35.9 reduce-scatter.26
  1192.6 60.2 reduce-scatter.28
where the time goes:
time: 1280 us; the launch traced here: 1270 us
  waiting for transfers between devices  890 us (70%)
  matrix products  128 us (10%)
  other arithmetic  87 us (7%)
  blocking collectives  81.7 us (6%)
  local copies, waits for them, and re-layouts  68.8 us (5%)
  between operations  15.4 us (1%)
    all_gather x1, waiting for transfers between devices, on_device(): lax.all_gather(expand_weight.astype(jnp.bfloat16), 'dp', axis=1, tiled=True)  145 us
    reduce_scatter x1, waiting for transfers between devices, on_device(): lax.psum_scatter(expand_sum.astype(jnp.bfloat16), 'dp', scatter_dimension...  125 us
    reduce_scatter x2, waiting for transfers between devices, narrow_rows(): lax.psum_scatter(jnp.dot(gathered, block_matrix, preferred_element_type=j...  104 us
    all_gather x1, waiting for transfers between devices, on_device(): lax.all_gather(reduce_weight.astype(jnp.bfloat16), 'dp', axis=0, tiled=True)  77.9 us
    all_gather x2, waiting for transfers between devices, widen_rows(): gathered = lax.all_gather(row_block, 'row', axis=0, tiled=True)  72.9 us
    all_gather x2, waiting for transfers between devices, narrow_back(): incoming = lax.all_gather(grad_local, 'row', axis=0, tiled=True)  70.4 us
    all_gather x1, waiting for transfers between devices, on_device(): lax.all_gather(entry_weight.astype(jnp.bfloat16), 'dp', axis=1, tiled=True)  65.6 us
    reduce_scatter x1, waiting for transfers between devices, on_device(): lax.psum_scatter(entry_sum.astype(jnp.bfloat16), 'dp', scatter_dimension=...  60.2 us
  transfers between devices with their start and end apart: 24, of which 22 were waited for; matrix products, arithmetic and copies ran while one was open for 11% of the time, Pallas kernels for 0%

commit v1 on v0

--- a/solution.py
+++ b/solution.py
@@ -17,8 +17,7 @@
 WEIGHT_DECAY = 0.1
 
 
-def layout_info(lengths, extent):
-    indices = jnp.arange(extent, dtype=jnp.int32)
+def layout_info(lengths, indices):
     closing = jnp.cumsum(lengths)
     starts = closing - lengths
     segment = jnp.sum((indices[:, None] >= closing[None, :]).astype(jnp.int32), 1)
@@ -68,58 +67,72 @@
     return (moment_new, square_new, weight - step_rate * (ratio + decay_rate * weight))
 
 
-def collect_features(values):
-    return lax.all_gather(values, "col", axis=1, tiled=True)
+def swap(values, axis, distance):
+    return lax.ppermute(values, axis, [(i, i ^ distance) for i in range(lax.axis_size(axis))])
+
+
+def swap_col(values):
+    return swap(values, "col", 1)
 
 
 def feature_total(values):
-    return lax.psum(values, "col")
+    return values + swap_col(values)
 
 
 def grid_total(values):
-    return lax.psum((values[0], values[1]), ("row", "col"))
-
-
-def widen_rows(row_block, blocks):
-    gathered = lax.all_gather(row_block, "row", axis=0, tiled=True)
-    partial_value = jnp.einsum("td,kdf->ktf", gathered, blocks, preferred_element_type=jnp.float32)
-    result = lax.psum_scatter(partial_value, "col", scatter_dimension=2, tiled=True)
-    return (gathered, result)
-
-
-def narrow_rows(features, block_matrix):
-    gathered = collect_features(features)
-    result = lax.psum_scatter(
-        jnp.dot(gathered, block_matrix, preferred_element_type=jnp.float32),
-        "row",
-        scatter_dimension=0,
-        tiled=True,
-    )
-    return (gathered, result)
-
-
-def narrow_back(grad_local, gathered_in, block_matrix):
-    incoming = lax.all_gather(grad_local, "row", axis=0, tiled=True)
-    weight_sum = jnp.einsum("tf,td->fd", gathered_in, incoming, preferred_element_type=jnp.float32)
-    update = jnp.einsum("td,fd->tf", incoming, block_matrix, preferred_element_type=jnp.float32)
-    partial_value = update
-    partial_value, weight_sum = (partial_value, weight_sum)
-    feature_grad = lax.psum_scatter(
-        partial_value.astype(jnp.bfloat16), "col", scatter_dimension=1, tiled=True
-    ).astype(jnp.float32)
-    return (feature_grad, weight_sum)
-
-
-def widen_back(grad_local, gathered_rows, blocks):
-    incoming = lax.all_gather(grad_local, "col", axis=2, tiled=True)
-    partial_value = jnp.einsum("ktw,kdw->td", incoming, blocks, preferred_element_type=jnp.float32)
-    update = jnp.einsum("td,ktw->kdw", gathered_rows, incoming, preferred_element_type=jnp.float32)
-    weight_sum = update
-    partial_value, weight_sum = (partial_value, weight_sum)
-    row_grad = lax.psum_scatter(
-        partial_value.astype(jnp.bfloat16), "row", scatter_dimension=0, tiled=True
-    ).astype(jnp.float32)
-    return (row_grad, weight_sum)
+    values = feature_total(values)
+    count = lax.axis_size("row")
+    blocks = values.reshape(values.shape[0], count, -1)
+    total = blocks
+    for k in range(1, count):
+        part = swap(blocks, "row", k)
+        total = total + jnp.stack([part[:, j ^ k] for j in range(count)], 1)
+    return total.reshape(values.shape)
+
+
+def mesh_total(values):
+    for axis in ("col", "row", "dp"):
+        distance = 1
+        while distance < lax.axis_size(axis):
+            values = values + swap(values, axis, distance)
+            distance *= 2
+    return values
+
+
+def gather_rows(block):
+    return jnp.concatenate(
+        [block] + [swap(block, "row", k) for k in range(1, lax.axis_size("row"))], 0
+    )
+
+
+def scatter_rows(partial_value):
+    count = lax.axis_size("row")
+    parts = partial_value.reshape(count, partial_value.shape[0] // count, -1)
+    low = parts.astype(jnp.bfloat16)
+    total = parts[0]
+    for k in range(1, count):
+        total = total + swap(low[k], "row", k).astype(jnp.float32)
+    return total
+
+
+def join_halves(own, axis):
+    half = own.shape[axis]
+    place = lax.axis_index("col") * half
+    shape = list(own.shape)
+    shape[axis] = 2 * half
+    whole = lax.dynamic_update_slice_in_dim(jnp.zeros(shape, own.dtype), own, place, axis)
+    return lax.dynamic_update_slice_in_dim(whole, swap_col(own), half - place, axis)
+
+
+def split_halves(block, axis):
+    half = block.shape[axis] // 2
+    place = lax.axis_index("col") * half
+    own = lax.dynamic_slice_in_dim(block, place, half, axis)
+    return (own, swap_col(lax.dynamic_slice_in_dim(block, half - place, half, axis)))
+
+
+def dot(equation, left, right):
+    return jnp.einsum(equation, left, right, preferred_element_type=jnp.float32)
 
 
 def on_device(
@@ -153,23 +166,28 @@
     local_rows = tokens.shape[0]
     feature_local = tokens.shape[1]
     extent = local_rows * row_size
-    segment, positions = layout_info(seq_lengths[0], extent)
-    row_start = lax.axis_index("row") * local_rows
-    local_valid = (
-        lax.dynamic_slice_in_dim(segment, row_start, local_rows, 0) < seq_lengths.shape[1]
-    ).astype(jnp.float32)
+    row_index = lax.axis_index("row")
+    blocks = row_index ^ jnp.arange(row_size, dtype=jnp.int32)
+    indices = (
+        blocks[:, None] * local_rows + jnp.arange(local_rows, dtype=jnp.int32)[None, :]
+    ).reshape(extent)
+    segment, positions = layout_info(seq_lengths[0], indices)
+    local_valid = (segment[:local_rows] < seq_lengths.shape[1]).astype(jnp.float32)
     head_width = entry_block.shape[2] // col_size
-    head_start = (lax.axis_index("row") * col_size + lax.axis_index("col")) * head_width
+    head_start = (row_index * col_size + lax.axis_index("col")) * head_width
     col_start = lax.axis_index("col") * feature_local
     post_gain = lax.dynamic_slice_in_dim(gains[0:2], col_start, feature_local, 1)
     head_gain = lax.dynamic_slice_in_dim(gains[2:4], head_start, head_width, 1)
     head_count = head_width // HD
     shrink = HD ** (-0.5)
     inputs = tokens.astype(jnp.float32)
-    token_rows, projected = widen_rows(tokens, entry_block)
-    squares = grid_total(
-        (jnp.sum(projected[0] * projected[0], -1), jnp.sum(projected[1] * projected[1], -1))
-    )
+    token_rows = gather_rows(tokens)
+    token_other = swap_col(token_rows)
+    entry_own, entry_far = split_halves(entry_block, 2)
+    projected = dot("td,kdf->ktf", token_rows, entry_own) + dot(
+        "td,kdf->ktf", token_other, entry_far
+    )
+    squares = grid_total(jnp.sum(projected[0:2] * projected[0:2], -1))
     query_scale = lax.rsqrt(squares[0] / D + NORM_EPSILON)[:, None]
     key_scale = lax.rsqrt(squares[1] / D + NORM_EPSILON)[:, None]
     query_hat = projected[0] * query_scale
@@ -183,7 +201,6 @@
     ).astype(jnp.bfloat16)
     value_rows = projected[2].astype(jnp.bfloat16).reshape(extent, head_count, HD)
     block_rows = min(512, extent)
-    indices = jnp.arange(extent, dtype=jnp.int32)
 
     def block_scores(offset):
         query_block = query_rot[offset : offset + block_rows]
@@ -210,15 +227,22 @@
         )
         logsums.append(peak + jnp.log(totals))
     attended = jnp.concatenate(outputs, 0).astype(jnp.bfloat16).reshape(extent, head_width)
-    attended_cols, branch = narrow_rows(attended, mixer_block)
+    attended_cols = join_halves(attended, 1)
+    branch = scatter_rows(dot("tf,fd->td", attended_cols, mixer_block))
     branch_scale = lax.rsqrt(feature_total(jnp.sum(branch * branch, -1)) / D + NORM_EPSILON)[
         :, None
     ]
     branch_hat = branch * branch_scale
     hidden = inputs + branch_hat * post_gain[0]
-    hidden_rows, gated = widen_rows(hidden.astype(jnp.bfloat16), expand_block)
+    hidden_rows = gather_rows(hidden.astype(jnp.bfloat16))
+    hidden_other = swap_col(hidden_rows)
+    expand_own, expand_far = split_halves(expand_block, 2)
+    gated = dot("td,kdf->ktf", hidden_rows, expand_own) + dot(
+        "td,kdf->ktf", hidden_other, expand_far
+    )
     product = (jax.nn.silu(gated[0]) * gated[1]).astype(jnp.bfloat16)
-    product_cols, second = narrow_rows(product, reduce_block)
+    product_cols = join_halves(product, 1)
+    second = scatter_rows(dot("tf,fd->td", product_cols, reduce_block))
     second_scale = lax.rsqrt(feature_total(jnp.sum(second * second, -1)) / D + NORM_EPSILON)[
         :, None
     ]
@@ -231,13 +255,19 @@
     second_grad = (second_scale * (scaled - second_hat * inner_sum[:, None] / D)).astype(
         jnp.bfloat16
     )
-    product_grad, reduce_sum = narrow_back(second_grad, product_cols, reduce_block)
+    second_rows = gather_rows(second_grad)
+    second_other = swap_col(second_rows)
+    reduce_sum = dot("tf,td->fd", product_cols, second_rows)
+    reduce_own, reduce_far = split_halves(reduce_block, 0)
+    product_grad = dot("td,fd->tf", second_rows, reduce_own) + dot(
+        "td,fd->tf", second_other, reduce_far
+    )
     sigmoid = jax.nn.sigmoid(gated[0])
     gate_grad = product_grad * gated[1] * sigmoid * (1.0 + gated[0] * (1.0 - sigmoid))
     up_grad = product_grad * jax.nn.silu(gated[0])
-    hidden_back, expand_sum = widen_back(
-        jnp.stack([gate_grad, up_grad]).astype(jnp.bfloat16), hidden_rows, expand_block
-    )
+    gated_grad = join_halves(jnp.stack([gate_grad, up_grad]).astype(jnp.bfloat16), 2)
+    hidden_back = scatter_rows(dot("ktw,kdw->td", gated_grad, expand_block))
+    expand_sum = dot("td,ktw->kdw", hidden_rows, gated_grad)
     hidden_grad = upstream + hidden_back
     gain_first_post = jnp.sum(hidden_grad * branch_hat, 0)
     scaled = hidden_grad * post_gain[0]
@@ -245,7 +275,13 @@
     branch_grad = (branch_scale * (scaled - branch_hat * inner_sum[:, None] / D)).astype(
         jnp.bfloat16
     )
-    attended_grad, mixer_sum = narrow_back(branch_grad, attended_cols, mixer_block)
+    branch_rows = gather_rows(branch_grad)
+    branch_other = swap_col(branch_rows)
+    mixer_sum = dot("tf,td->fd", attended_cols, branch_rows)
+    mixer_own, mixer_far = split_halves(mixer_block, 0)
+    attended_grad = dot("td,fd->tf", branch_rows, mixer_own) + dot(
+        "td,fd->tf", branch_other, mixer_far
+    )
     attended_low = attended_grad.astype(jnp.bfloat16).reshape(extent, head_count, HD)
     query_parts = []
     key_accum = jnp.zeros((extent, head_count, HD), jnp.float32)
@@ -285,14 +321,18 @@
     query_scaled = query_grad * head_gain[0]
     key_scaled = key_grad * head_gain[1]
     head_dots = grid_total(
-        (jnp.sum(query_scaled * query_hat, -1), jnp.sum(key_scaled * key_hat, -1))
+        jnp.stack(
+            [jnp.sum(query_scaled * query_hat, -1), jnp.sum(key_scaled * key_hat, -1)]
+        )
     )
     query_raw = query_scale * (query_scaled - query_hat * head_dots[0][:, None] / D)
     key_raw = key_scale * (key_scaled - key_hat * head_dots[1][:, None] / D)
     value_grad = value_accum.reshape(extent, head_width)
-    entry_back, entry_sum = widen_back(
-        jnp.stack([query_raw, key_raw, value_grad]).astype(jnp.bfloat16), token_rows, entry_block
-    )
+    projected_grad = join_halves(
+        jnp.stack([query_raw, key_raw, value_grad]).astype(jnp.bfloat16), 2
+    )
+    entry_back = scatter_rows(dot("ktw,kdw->td", projected_grad, entry_block))
+    entry_sum = dot("td,ktw->kdw", token_rows, projected_grad)
     input_grad = hidden_grad + entry_back
     entry_grad, mixer_grad, expand_grad, reduce_grad = (
         lax.psum_scatter(
@@ -315,7 +355,7 @@
     gain_local = lax.dynamic_update_slice(
         gain_local, jnp.stack([gain_query, gain_key]), (2, head_start)
     )
-    gain_grad = lax.psum(gain_local, ("dp", "row", "col"))
+    gain_grad = mesh_total(gain_local)
     gain_momentum, gain_variance, gain_updated = adam_step(
         gains, gain_grad, gain_mean, gain_square, 1.0, 0.0
     )

time: 1280 us -> 901 us (0.70)
  waiting for transfers between devices: 890 us -> 557 us
  blocking collectives: 81.7 us -> 0 us
  starting transfers between devices: 2.4 us -> 44 us
  local copies, waits for them, and re-layouts: 68.8 us -> 92.5 us
  matrix products: 128 us -> 113 us
  other arithmetic: 87 us -> 73.6 us
    reduce_scatter x8 -> x0, waiting for transfers between devices: 199 us -> none  [the longest x2 104 us: narrow_rows(): lax.psum_scatter(jnp.dot(gathered, block_matrix, preferred_element_type=j...]
    ppermute x0 -> x53, waiting for transfers between devices: none -> 191 us  [swap(): lax.ppermute(values, axis, [(i, i ^ distance) for i in range(lax.axis_siz...]
    all_gather x8 -> x0, waiting for transfers between devices: 190 us -> none  [the longest x2 72.9 us: widen_rows(): gathered = lax.all_gather(row_block, 'row', axis=0, tiled=True)]
    psum x7 -> x0, blocking collectives: 81.7 us -> none  [the longest x1 42 us: on_device(): gain_grad = lax.psum(gain_local, ('dp', 'row', 'col'))]
    ppermute x0 -> x53, starting transfers between devices: none -> 43.7 us  [swap(): lax.ppermute(values, axis, [(i, i ^ distance) for i in range(lax.axis_siz...]
    all_gather x1, waiting for transfers between devices: 65.6 us -> 26.1 us  [on_device(): lax.all_gather(entry_weight.astype(jnp.bfloat16), 'dp', axis=1, tiled=True)]
    reduce_scatter x1, waiting for transfers between devices: 60.2 us -> 29.7 us  [on_device(): lax.psum_scatter(entry_sum.astype(jnp.bfloat16), 'dp', scatter_dimension=...]
    all_gather x1, waiting for transfers between devices: 77.9 us -> 50.4 us  [on_device(): lax.all_gather(reduce_weight.astype(jnp.bfloat16), 'dp', axis=0, tiled=True)]
  transfers between devices with their start and end apart: 24 -> 61, of which waited for: 22 -> 38; matrix products, arithmetic and copies ran while one was open for 11% -> 22% of each run, Pallas kernels for 0% -> 0%
where the time goes in v1:
time: 901 us; the launch traced here: 896 us
  waiting for transfers between devices  557 us (62%)
  matrix products  113 us (13%)
  local copies, waits for them, and re-layouts  92.5 us (10%)
  other arithmetic  73.6 us (8%)
  starting transfers between devices  44 us (5%)
  between operations  16.3 us (2%)
    ppermute x53, waiting for transfers between devices, swap(): lax.ppermute(values, axis, [(i, i ^ distance) for i in range(lax.axis_siz...  191 us
    reduce_scatter x1, waiting for transfers between devices, on_device(): lax.psum_scatter(expand_sum.astype(jnp.bfloat16), 'dp', scatter_dimension...  133 us
    all_gather x1, waiting for transfers between devices, on_device(): lax.all_gather(expand_weight.astype(jnp.bfloat16), 'dp', axis=1, tiled=True)  127 us
    dot_general x16, matrix products, dot(): return jnp.einsum(equation, left, right, preferred_element_type=jnp.float32)  95.5 us
    unnamed x194, local copies, waits for them, and re-layouts  60.1 us
    all_gather x1, waiting for transfers between devices, on_device(): lax.all_gather(reduce_weight.astype(jnp.bfloat16), 'dp', axis=0, tiled=True)  50.4 us
    ppermute x53, starting transfers between devices, swap(): lax.ppermute(values, axis, [(i, i ^ distance) for i in range(lax.axis_siz...  43.7 us
    reduce_scatter x1, waiting for transfers between devices, on_device(): lax.psum_scatter(entry_sum.astype(jnp.bfloat16), 'dp', scatter_dimension=...  29.7 us
  transfers between devices with their start and end apart: 61, of which 38 were waited for; matrix products, arithmetic and copies ran while one was open for 22% of the time, Pallas kernels for 0%

profile of v1, /device:TPU:0, one launch (start us, length us, event | category | flops | bytes accessed | tf_op | source)
XLA Modules:
  0.0 896.4 jit_solution(5390876226721501161)
XLA Ops:
  11.2 5.4 copy.83
  16.5 3.8 convert_element_type.169
  20.4 3.1 collective-permute-start
  26.1 10.1 %collective-permute-done = bf16[256,1024]{1,0:T(8,128)(2,1)S(1)} collective-permute-done((bf16[256,1024]{1,0:T(8,128)(2,1)S(1)}, bf16[256,1024]{1,0:T(8,128)(2,1)S(1)}, u32[]{:S(2)}, u32[]{:S(2)}) %collective-permute-start) | collective-permute-done | bytes 524320 | tf_op jit(solution)/shard_map/ppermute | solution.py:71
  37.1 10.9 %collective-permute-done.1 = bf16[256,1024]{1,0:T(8,128)(2,1)S(1)} collective-permute-done((bf16[256,1024]{1,0:T(8,128)(2,1)S(1)}, bf16[256,1024]{1,0:T(8,128)(2,1)S(1)}, u32[]{:S(2)}, u32[]{:S(2)}) %collective-permute-start.1) | collective-permute-done | bytes 524320 | tf_op jit(solution)/shard_map/ppermute | solution.py:71
  50.4 26.1 %all-gather.5.cloned.1.call-done = bf16[3,1024,512]{1,2,0:T(8,128)(2,1)} async-done(((bf16[3,256,512]{1,2,0:T(8,128)(2,1)}), bf16[3,1024,512]{1,2,0:T(8,128)(2,1)}) %all-gather.5.cloned.1.call-update) | async-done | bytes 3145744 | tf_op jit(solution)/shard_map/all_gather | solution.py:159
  78.8 3.1 multiply_cosine_fusion
  93.8 2.5 copy.82
  118.7 4.9 fusion.117
  128.3 127.3 %all-gather.9.cloned.1.call-done = bf16[2,1024,2048]{1,2,0:T(8,128)(2,1)} async-done(((bf16[2,256,2048]{1,2,0:T(8,128)(2,1)}), bf16[2,1024,2048]{1,2,0:T(8,128)(2,1)}) %all-gather.9.cloned.1.call-update) | async-done | bytes 8388624 | tf_op jit(solution)/shard_map/all_gather | solution.py:161
  255.7 4.6 constant_dynamic-slice_fusion.2
  264.1 3.3 collective-permute-done.13
  272.3 12.2 %collective-permute-done.16 = bf16[256,1024]{1,0:T(8,128)(2,1)S(1)} collective-permute-done((bf16[256,1024]{1,0:T(8,128)(2,1)S(1)}, bf16[256,1024]{1,0:T(8,128)(2,1)S(1)}, u32[]{:S(2)}, u32[]{:S(2)}) %collective-permute-start.16) | collective-permute-done | bytes 524320 | tf_op jit(solution)/shard_map/ppermute | solution.py:71
  284.5 10.4 %collective-permute-done.15 = bf16[256,1024]{1,0:T(8,128)(2,1)S(1)} collective-permute-done((bf16[256,1024]{1,0:T(8,128)(2,1)S(1)}, bf16[256,1024]{1,0:T(8,128)(2,1)S(1)}, u32[]{:S(2)}, u32[]{:S(2)}) %collective-permute-start.15) | collective-permute-done | bytes 524320 | tf_op jit(solution)/shard_map/ppermute | solution.py:71
  297.9 3.2 collective-permute-done.18
  301.1 7.4 fusion.17
  308.5 6.5 add_bitcast_fusion
  315.1 2.9 broadcast_in_dim.60
  317.9 2.5 constant_dynamic-update-slice_fusion.9
  320.5 4.1 collective-permute-done.19
  326.1 50.4 %all-gather.11.cloned.1.call-done = bf16[2048,1024]{1,0:T(8,128)(2,1)} async-done(((bf16[512,1024]{1,0:T(8,128)(2,1)}), bf16[2048,1024]{1,0:T(8,128)(2,1)}) %all-gather.11.cloned.1.call-update) | async-done | bytes 4194320 | tf_op jit(solution)/shard_map/all_gather | solution.py:162
  376.4 7.6 fusion.118
  384.2 2.5 collective-permute-start.22
  387.7 12.3 %collective-permute-done.22 = bf16[256,1024]{1,0:T(8,128)(2,1)S(1)} collective-permute-done((bf16[256,1024]{1,0:T(8,128)(2,1)S(1)}, bf16[256,1024]{1,0:T(8,128)(2,1)S(1)}, u32[]{:S(2)}, u32[]{:S(2)}) %collective-permute-start.22) | collective-permute-done | bytes 524320 | tf_op jit(solution)/shard_map/ppermute | solution.py:71
  400.0 10.1 %collective-permute-done.21 = bf16[256,1024]{1,0:T(8,128)(2,1)S(1)} collective-permute-done((bf16[256,1024]{1,0:T(8,128)(2,1)S(1)}, bf16[256,1024]{1,0:T(8,128)(2,1)S(1)}, u32[]{:S(2)}, u32[]{:S(2)}) %collective-permute-start.21) | collective-permute-done | bytes 524320 | tf_op jit(solution)/shard_map/ppermute | solution.py:71
  417.5 12.0 %collective-permute-done.27 = bf16[256,1024]{1,0:T(8,128)(2,1)S(1)} collective-permute-done((bf16[256,1024]{1,0:T(8,128)(2,1)S(1)}, bf16[256,1024]{1,0:T(8,128)(2,1)S(1)}, u32[]{:S(2)}, u32[]{:S(2)}) %collective-permute-start.27) | collective-permute-done | bytes 524320 | tf_op jit(solution)/shard_map/ppermute | solution.py:71
  429.5 10.4 %collective-permute-done.26 = bf16[256,1024]{1,0:T(8,128)(2,1)S(1)} collective-permute-done((bf16[256,1024]{1,0:T(8,128)(2,1)S(1)}, bf16[256,1024]{1,0:T(8,128)(2,1)S(1)}, u32[]{:S(2)}, u32[]{:S(2)}) %collective-permute-start.26) | collective-permute-done | bytes 524320 | tf_op jit(solution)/shard_map/ppermute | solution.py:71
  440.2 4.1 collective-permute-done.28
  446.8 7.8 fusion.32
  456.7 7.0 collective-permute-done.30
  464.3 14.4 %fusion.119 = (bf16[1024,1024]{1,0:T(8,128)(2,1)S(1)}, f32[1024,1024]{1,0:T(8,128)S(1)}) fusion(bf16[2,1024,2048]{1,2,0:T(8,128)(2,1)S(1)} %constant_dynamic-update-slice_fusion.6, bf16[2,1024,2048]{1,2,0:T(8,128)(2,1)} %all-gather.9.cloned.1.call-done), kind=kOutput, calls=%fused_computation.237 | convolution fusion | flops 8590983168 | bytes 23068672 | tf_op jit(solution)/shard_map/ktw,kdw->td/dot_general | solution.py:135
  482.4 12.2 %collective-permute-done.33 = bf16[256,1024]{1,0:T(8,128)(2,1)S(1)} collective-permute-done((bf16[256,1024]{1,0:T(8,128)(2,1)S(1)}, bf16[256,1024]{1,0:T(8,128)(2,1)S(1)}, u32[]{:S(2)}, u32[]{:S(2)}) %collective-permute-start.33) | collective-permute-done | bytes 524320 | tf_op jit(solution)/shard_map/ppermute | solution.py:71
  494.6 10.4 %collective-permute-done.32 = bf16[256,1024]{1,0:T(8,128)(2,1)S(1)} collective-permute-done((bf16[256,1024]{1,0:T(8,128)(2,1)S(1)}, bf16[256,1024]{1,0:T(8,128)(2,1)S(1)}, u32[]{:S(2)}, u32[]{:S(2)}) %collective-permute-start.32) | collective-permute-done | bytes 524320 | tf_op jit(solution)/shard_map/ppermute | solution.py:71
  512.0 12.2 %collective-permute-done.37 = bf16[256,1024]{1,0:T(8,128)(2,1)S(1)} collective-permute-done((bf16[256,1024]{1,0:T(8,128)(2,1)S(1)}, bf16[256,1024]{1,0:T(8,128)(2,1)S(1)}, u32[]{:S(2)}, u32[]{:S(2)}) %collective-permute-start.37) | collective-permute-done | bytes 524320 | tf_op jit(solution)/shard_map/ppermute | solution.py:71
  524.2 10.4 %collective-permute-done.36 = bf16[256,1024]{1,0:T(8,128)(2,1)S(1)} collective-permute-done((bf16[256,1024]{1,0:T(8,128)(2,1)S(1)}, bf16[256,1024]{1,0:T(8,128)(2,1)S(1)}, u32[]{:S(2)}, u32[]{:S(2)}) %collective-permute-start.36) | collective-permute-done | bytes 524320 | tf_op jit(solution)/shard_map/ppermute | solution.py:71
  537.7 8.6 convolution_convert_fusion
  546.4 2.6 fusion.124
  564.3 2.7 copy.96
  567.0 2.9 pad_maximum_fusion.7
  569.9 2.6 copy.101
  575.3 2.8 fusion.11
  579.7 3.4 fusion.45
  596.2 6.4 convert_bitcast_fusion.1
  602.7 15.2 %convert_bitcast_fusion = bf16[2,1024,2048]{1,2,0:T(8,128)(2,1)} fusion(bf16[2,1024,2048]{1,2,0:T(8,128)(2,1)} %copy-done.15, bf16[256,1024]{1,0:T(8,128)(2,1)} %copy-done.47, bf16[256,1024]{1,0:T(8,128)(2,1)} %copy-done.49, bf16[256,1024]{1,0:T(8,128)(2,1)} %copy-done.51, bf16[256,1024]{1,0:T(8,128)(2,1)} %copy-done.39), kind=kOutput, calls=%fused_computation | convolution fusion | flops 8602517504 | bytes 18874368 | tf_op jit(solution)/shard_map/td,ktw->kdw/dot_general | solution.py:135
  624.8 3.0 copy.105
  627.8 3.0 copy.104
  630.8 5.3 copy.109
  636.2 5.4 copy.108
  641.7 7.3 multiply_subtract_fusion.1
  650.1 5.2 fusion.120
  660.0 2.9 multiply_subtract_fusion.5
  663.6 8.9 collective-permute-done.47
  672.5 8.5 collective-permute-done.46
  680.9 2.9 fusion.55
  683.8 29.7 %reduce-scatter.5.cloned.1.call-done = bf16[3,256,512]{1,2,0:T(8,128)(2,1)} async-done(((bf16[3,1024,512]{1,2,0:T(8,128)(2,1)}), bf16[3,256,512]{1,2,0:T(8,128)(2,1)}) %reduce-scatter.5.cloned.1.call-update) | async-done | bytes 786448 | tf_op jit(solution)/shard_map/reduce_scatter | solution.py:338
  713.5 5.0 multiply_subtract_fusion.2
  718.5 3.1 copy.113
  724.9 2.6 copy.112
  727.4 133.0 %reduce-scatter.9.cloned.1.call-done = bf16[2,256,2048]{1,2,0:T(8,128)(2,1)} async-done(((bf16[2,1024,2048]{1,2,0:T(8,128)(2,1)}), bf16[2,256,2048]{1,2,0:T(8,128)(2,1)}) %reduce-scatter.9.cloned.1.call-update) | async-done | bytes 2097168 | tf_op jit(solution)/shard_map/reduce_scatter | solution.py:344
  860.4 10.0 %multiply_subtract_fusion = (f32[2,256,2048]{1,2,0:T(8,128)}, f32[2,256,2048]{1,2,0:T(8,128)}, f32[2,256,2048]{1,2,0:T(8,128)}) fusion(f32[2,256,2048]{1,2,0:T(8,128)} %copy.83, bf16[2,256,2048]{1,2,0:T(8,128)(2,1)} %reduce-scatter.9.cloned.1.call-done, f32[2,256,2048]{1,2,0:T(8,128)} %copy.109, f32[2,256,2048]{1,2,0:T(8,128)} %copy.108), kind=kLoop, calls=%fused_computation.7 | loop fusion | flops 16777216 | bytes 27262976 | tf_op jit(solution)/shard_map/sub | solution.py:67
  870.3 5.3 copy.117
  875.7 5.3 copy.118
  881.0 5.5 copy.119
  886.5 2.8 copy.116
  (394 shorter events, 140.4 us)
Async XLA Ops:
  7.2 69.4 %all-gather.5.cloned.1.call-start = ((), (), s32[]{:S(2)}) async-start(), calls=%async_computation.4 | async-start | bytes 3932160 | tf_op jit(solution)/shard_map/all_gather | solution.py:159
  10.3 108.5 %all-gather.7.cloned.1.call-start = ((), (), s32[]{:S(2)}) async-start(), calls=%async_computation.5 | async-start | bytes 1310720 | tf_op jit(solution)/shard_map/all_gather | solution.py:160
  11.1 244.5 %all-gather.9.cloned.1.call-start = ((), (), s32[]{:S(2)}) async-start(), calls=%async_computation.6 | async-start | bytes 10485760 | tf_op jit(solution)/shard_map/all_gather | solution.py:161
  20.3 356.1 %all-gather.11.cloned.1.call-start = ((), (), s32[]{:S(2)}) async-start(), calls=%async_computation.7 | async-start | bytes 5242880 | tf_op jit(solution)/shard_map/all_gather | solution.py:162
  20.4 15.9 %collective-permute-start = (bf16[256,1024]{1,0:T(8,128)(2,1)S(1)}, bf16[256,1024]{1,0:T(8,128)(2,1)S(1)}, u32[]{:S(2)}, u32[]{:S(2)}) collective-permute-start(bf16[256,1024]{1,0:T(8,128)(2,1)S(1)} %copy-done.27), channel_id=1, source_target_pairs={{0,2},{2,0},{4,6},{6,4},{1,3},{3,1},{5,7},{7,5},{8,10},{10,8},{12,... | collective-permute-start | bytes 1572872 | tf_op jit(solution)/shard_map/ppermute | solution.py:71
  23.5 24.5 %collective-permute-start.1 = (bf16[256,1024]{1,0:T(8,128)(2,1)S(1)}, bf16[256,1024]{1,0:T(8,128)(2,1)S(1)}, u32[]{:S(2)}, u32[]{:S(2)}) collective-permute-start(bf16[256,1024]{1,0:T(8,128)(2,1)S(1)} %copy-done.27), channel_id=1, source_target_pairs={{0,4},{2,6},{4,0},{6,2},{1,5},{3,7},{5,1},{7,3},{8,12},{10,14},{12... | collective-permute-start | bytes 1572872 | tf_op jit(solution)/shard_map/ppermute | solution.py:71
  25.0 23.8 %collective-permute-start.2 = (bf16[256,1024]{1,0:T(8,128)(2,1)S(1)}, bf16[256,1024]{1,0:T(8,128)(2,1)S(1)}, u32[]{:S(2)}, u32[]{:S(2)}) collective-permute-start(bf16[256,1024]{1,0:T(8,128)(2,1)S(1)} %copy-done.27), channel_id=1, source_target_pairs={{0,6},{2,4},{4,2},{6,0},{1,7},{3,5},{5,3},{7,1},{8,14},{10,12},{12... | collective-permute-start | bytes 1572872 | tf_op jit(solution)/shard_map/ppermute | solution.py:71
  26.1 57.7 %copy-start.68 = (f32[4,2048]{1,0:T(4,128)S(1)}, f32[4,2048]{1,0:T(4,128)}, u32[]{:S(2)}) copy-start(f32[4,2048]{1,0:T(4,128)} %param.21) | copy-start | bytes 98308
  49.7 34.2 %collective-permute-start.4 = (bf16[1024,1024]{1,0:T(8,128)(2,1)}, bf16[1024,1024]{1,0:T(8,128)(2,1)S(1)}, u32[]{:S(2)}, u32[]{:S(2)}) collective-permute-start(bf16[1024,1024]{1,0:T(8,128)(2,1)} %constant_dynamic-update-slice_fusion), channel_id=1, source_target_pairs={{0,1},{1,0},{2,3},{3,2},{4,5},{5,4},{6,7},{7,6},{8,9},{9,8},{10,11... | collective-permute-start | bytes 6291464 | tf_op jit(solution)/shard_map/ppermute | solution.py:71
  78.1 5.8 collective-permute-start.3
  88.6 1.4 collective-permute-start.5
  90.0 10.1 %collective-permute-start.6 = (f32[2,4,256]{2,1,0:T(4,128)S(1)}, f32[2,4,256]{2,1,0:T(4,128)S(1)}, u32[]{:S(2)}, u32[]{:S(2)}) collective-permute-start(f32[2,4,256]{2,1,0:T(4,128)S(1)} %reshape.585), channel_id=1, source_target_pairs={{0,2},{2,0},{4,6},{6,4},{1,3},{3,1},{5,7},{7,5},{8,10},{10,8},{12,... | collective-permute-start | bytes 24584 | tf_op jit(solution)/shard_map/ppermute | solution.py:71
  98.0 3.7 collective-permute-start.7
  99.6 4.5 collective-permute-start.8
  115.0 2.3 collective-permute-start.9
  124.8 135.5 %collective-permute-start.12 = (bf16[256,1024]{1,0:T(8,128)(2,1)}, bf16[256,1024]{1,0:T(8,128)(2,1)S(1)}, u32[]{:S(2)}, u32[]{:S(2)}) collective-permute-start(bf16[256,1024]{1,0:T(8,128)(2,1)} %get-tuple-element.123), channel_id=1, source_target_pairs={{0,6},{2,4},{4,2},{6,0},{1,7},{3,5},{5,3},{7,1},{8,14},{10,12},{12... | collective-permute-start | bytes 1572872 | tf_op jit(solution)/shard_map/ppermute | solution.py:71
  125.4 134.9 %collective-permute-start.11 = (bf16[256,1024]{1,0:T(8,128)(2,1)}, bf16[256,1024]{1,0:T(8,128)(2,1)S(1)}, u32[]{:S(2)}, u32[]{:S(2)}) collective-permute-start(bf16[256,1024]{1,0:T(8,128)(2,1)} %get-tuple-element.124), channel_id=1, source_target_pairs={{0,4},{2,6},{4,0},{6,2},{1,5},{3,7},{5,1},{7,3},{8,12},{10,14},{12... | collective-permute-start | bytes 1572872 | tf_op jit(solution)/shard_map/ppermute | solution.py:71
  126.9 133.4 %collective-permute-start.10 = (bf16[256,1024]{1,0:T(8,128)(2,1)}, bf16[256,1024]{1,0:T(8,128)(2,1)}, u32[]{:S(2)}, u32[]{:S(2)}) collective-permute-start(bf16[256,1024]{1,0:T(8,128)(2,1)} %get-tuple-element.122), channel_id=1, source_target_pairs={{0,2},{2,0},{4,6},{6,4},{1,3},{3,1},{5,7},{7,5},{8,10},{10,8},{12,... | collective-permute-start | bytes 1572872 | tf_op jit(solution)/shard_map/ppermute | solution.py:71
  260.3 40.8 %collective-permute-start.17 = (bf16[2,1024,1024]{1,2,0:T(8,128)(2,1)}, bf16[2,1024,1024]{1,2,0:T(8,128)(2,1)}, u32[]{:S(2)}, u32[]{:S(2)}) collective-permute-start(bf16[2,1024,1024]{1,2,0:T(8,128)(2,1)} %constant_dynamic-slice_fusion.2), channel_id=1, source_target_pairs={{0,1},{1,0},{2,3},{3,2},{4,5},{5,4},{6,7},{7,6},{8,9},{9,8},{10,11... | collective-permute-start | bytes 12582920 | tf_op jit(solution)/shard_map/ppermute | solution.py:71
  261.3 35.3 %copy-start.13 = (f32[512,1024]{1,0:T(8,128)S(1)}, f32[512,1024]{1,0:T(8,128)}, u32[]{:S(2)}) copy-start(f32[512,1024]{1,0:T(8,128)} %param.33) | copy-start | bytes 6291460
  263.5 4.0 collective-permute-start.13
  268.7 15.8 %collective-permute-start.16 = (bf16[256,1024]{1,0:T(8,128)(2,1)S(1)}, bf16[256,1024]{1,0:T(8,128)(2,1)S(1)}, u32[]{:S(2)}, u32[]{:S(2)}) collective-permute-start(bf16[256,1024]{1,0:T(8,128)(2,1)S(1)} %fusion.66), channel_id=1, source_target_pairs={{0,6},{2,4},{4,2},{6,0},{1,7},{3,5},{5,3},{7,1},{8,14},{10,12},{12... | collective-permute-start | bytes 1572872 | tf_op jit(solution)/shard_map/ppermute | solution.py:71
  271.2 23.7 %collective-permute-start.15 = (bf16[256,1024]{1,0:T(8,128)(2,1)S(1)}, bf16[256,1024]{1,0:T(8,128)(2,1)S(1)}, u32[]{:S(2)}, u32[]{:S(2)}) collective-permute-start(bf16[256,1024]{1,0:T(8,128)(2,1)S(1)} %fusion.66), channel_id=1, source_target_pairs={{0,4},{2,6},{4,0},{6,2},{1,5},{3,7},{5,1},{7,3},{8,12},{10,14},{12... | collective-permute-start | bytes 1572872 | tf_op jit(solution)/shard_map/ppermute | solution.py:71
  271.7 23.2 %collective-permute-start.14 = (bf16[256,1024]{1,0:T(8,128)(2,1)S(1)}, bf16[256,1024]{1,0:T(8,128)(2,1)S(1)}, u32[]{:S(2)}, u32[]{:S(2)}) collective-permute-start(bf16[256,1024]{1,0:T(8,128)(2,1)S(1)} %fusion.66), channel_id=1, source_target_pairs={{0,2},{2,0},{4,6},{6,4},{1,3},{3,1},{5,7},{7,5},{8,10},{10,8},{12,... | collective-permute-start | bytes 1572872 | tf_op jit(solution)/shard_map/ppermute | solution.py:71
  296.6 4.5 collective-permute-start.18
  297.8 343.9 %reduce-scatter.11.cloned.1.call-start = ((), (), s32[]{:S(2)}) async-start(), calls=%async_computation.11 | async-start | bytes 5242880 | tf_op jit(solution)/shard_map/reduce_scatter | solution.py:347
  320.4 4.2 collective-permute-start.19
  384.2 15.8 %collective-permute-start.22 = (bf16[256,1024]{1,0:T(8,128)(2,1)S(1)}, bf16[256,1024]{1,0:T(8,128)(2,1)S(1)}, u32[]{:S(2)}, u32[]{:S(2)}) collective-permute-start(bf16[256,1024]{1,0:T(8,128)(2,1)S(1)} %get-tuple-element.120), channel_id=1, source_target_pairs={{0,6},{2,4},{4,2},{6,0},{1,7},{3,5},{5,3},{7,1},{8,14},{10,12},{12... | collective-permute-start | bytes 1572872 | tf_op jit(solution)/shard_map/ppermute | solution.py:71
  386.6 23.4 %collective-permute-start.21 = (bf16[256,1024]{1,0:T(8,128)(2,1)S(1)}, bf16[256,1024]{1,0:T(8,128)(2,1)S(1)}, u32[]{:S(2)}, u32[]{:S(2)}) collective-permute-start(bf16[256,1024]{1,0:T(8,128)(2,1)S(1)} %get-tuple-element.121), channel_id=1, source_target_pairs={{0,4},{2,6},{4,0},{6,2},{1,5},{3,7},{5,1},{7,3},{8,12},{10,14},{12... | collective-permute-start | bytes 1572872 | tf_op jit(solution)/shard_map/ppermute | solution.py:71
  387.2 22.9 %collective-permute-start.20 = (bf16[256,1024]{1,0:T(8,128)(2,1)S(1)}, bf16[256,1024]{1,0:T(8,128)(2,1)S(1)}, u32[]{:S(2)}, u32[]{:S(2)}) collective-permute-start(bf16[256,1024]{1,0:T(8,128)(2,1)S(1)} %get-tuple-element.119), channel_id=1, source_target_pairs={{0,2},{2,0},{4,6},{6,4},{1,3},{3,1},{5,7},{7,5},{8,10},{10,8},{12,... | collective-permute-start | bytes 1572872 | tf_op jit(solution)/shard_map/ppermute | solution.py:71
  410.4 1.2 collective-permute-start.23
  412.1 1.2 collective-permute-start.24
  413.7 15.8 %collective-permute-start.27 = (bf16[256,1024]{1,0:T(8,128)(2,1)S(1)}, bf16[256,1024]{1,0:T(8,128)(2,1)S(1)}, u32[]{:S(2)}, u32[]{:S(2)}) collective-permute-start(bf16[256,1024]{1,0:T(8,128)(2,1)S(1)} %multiply_convert_fusion.8), channel_id=1, source_target_pairs={{0,6},{2,4},{4,2},{6,0},{1,7},{3,5},{5,3},{7,1},{8,14},{10,12},{12... | collective-permute-start | bytes 1572872 | tf_op jit(solution)/shard_map/ppermute | solution.py:71
  415.4 24.5 %collective-permute-start.26 = (bf16[256,1024]{1,0:T(8,128)(2,1)S(1)}, bf16[256,1024]{1,0:T(8,128)(2,1)S(1)}, u32[]{:S(2)}, u32[]{:S(2)}) collective-permute-start(bf16[256,1024]{1,0:T(8,128)(2,1)S(1)} %multiply_convert_fusion.8), channel_id=1, source_target_pairs={{0,4},{2,6},{4,0},{6,2},{1,5},{3,7},{5,1},{7,3},{8,12},{10,14},{12... | collective-permute-start | bytes 1572872 | tf_op jit(solution)/shard_map/ppermute | solution.py:71
  416.7 23.2 %collective-permute-start.25 = (bf16[256,1024]{1,0:T(8,128)(2,1)S(1)}, bf16[256,1024]{1,0:T(8,128)(2,1)S(1)}, u32[]{:S(2)}, u32[]{:S(2)}) collective-permute-start(bf16[256,1024]{1,0:T(8,128)(2,1)S(1)} %multiply_convert_fusion.8), channel_id=1, source_target_pairs={{0,2},{2,0},{4,6},{6,4},{1,3},{3,1},{5,7},{7,5},{8,10},{10,8},{12,... | collective-permute-start | bytes 1572872 | tf_op jit(solution)/shard_map/ppermute | solution.py:71
  417.4 22.8 %collective-permute-start.29 = (bf16[1024,1024]{1,0:T(8,128)(2,1)S(1)}, bf16[1024,1024]{1,0:T(8,128)(2,1)S(1)}, u32[]{:S(2)}, u32[]{:S(2)}) collective-permute-start(bf16[1024,1024]{1,0:T(8,128)(2,1)S(1)} %constant_dynamic-slice_fusion.1), channel_id=1, source_target_pairs={{0,1},{1,0},{2,3},{3,2},{4,5},{5,4},{6,7},{7,6},{8,9},{9,8},{10,11... | collective-permute-start | bytes 6291464 | tf_op jit(solution)/shard_map/ppermute | solution.py:71
  440.1 4.2 collective-permute-start.28
  456.5 7.2 collective-permute-start.30
  478.8 15.8 %collective-permute-start.33 = (bf16[256,1024]{1,0:T(8,128)(2,1)S(1)}, bf16[256,1024]{1,0:T(8,128)(2,1)S(1)}, u32[]{:S(2)}, u32[]{:S(2)}) collective-permute-start(bf16[256,1024]{1,0:T(8,128)(2,1)S(1)} %get-tuple-element.117), channel_id=1, source_target_pairs={{0,6},{2,4},{4,2},{6,0},{1,7},{3,5},{5,3},{7,1},{8,14},{10,12},{12... | collective-permute-start | bytes 1572872 | tf_op jit(solution)/shard_map/ppermute | solution.py:71
  480.6 24.4 %collective-permute-start.32 = (bf16[256,1024]{1,0:T(8,128)(2,1)S(1)}, bf16[256,1024]{1,0:T(8,128)(2,1)S(1)}, u32[]{:S(2)}, u32[]{:S(2)}) collective-permute-start(bf16[256,1024]{1,0:T(8,128)(2,1)S(1)} %get-tuple-element.118), channel_id=1, source_target_pairs={{0,4},{2,6},{4,0},{6,2},{1,5},{3,7},{5,1},{7,3},{8,12},{10,14},{12... | collective-permute-start | bytes 1572872 | tf_op jit(solution)/shard_map/ppermute | solution.py:71
  481.8 23.2 %collective-permute-start.31 = (bf16[256,1024]{1,0:T(8,128)(2,1)S(1)}, bf16[256,1024]{1,0:T(8,128)(2,1)S(1)}, u32[]{:S(2)}, u32[]{:S(2)}) collective-permute-start(bf16[256,1024]{1,0:T(8,128)(2,1)S(1)} %get-tuple-element.116), channel_id=1, source_target_pairs={{0,2},{2,0},{4,6},{6,4},{1,3},{3,1},{5,7},{7,5},{8,10},{10,8},{12,... | collective-permute-start | bytes 1572872 | tf_op jit(solution)/shard_map/ppermute | solution.py:71
  505.7 1.2 collective-permute-start.34
  508.5 15.7 %collective-permute-start.37 = (bf16[256,1024]{1,0:T(8,128)(2,1)S(1)}, bf16[256,1024]{1,0:T(8,128)(2,1)S(1)}, u32[]{:S(2)}, u32[]{:S(2)}) collective-permute-start(bf16[256,1024]{1,0:T(8,128)(2,1)S(1)} %get-tuple-element.131), channel_id=1, source_target_pairs={{0,6},{2,4},{4,2},{6,0},{1,7},{3,5},{5,3},{7,1},{8,14},{10,12},{12... | collective-permute-start | bytes 1572872 | tf_op jit(solution)/shard_map/ppermute | solution.py:71
  510.2 24.5 %collective-permute-start.36 = (bf16[256,1024]{1,0:T(8,128)(2,1)S(1)}, bf16[256,1024]{1,0:T(8,128)(2,1)S(1)}, u32[]{:S(2)}, u32[]{:S(2)}) collective-permute-start(bf16[256,1024]{1,0:T(8,128)(2,1)S(1)} %get-tuple-element.131), channel_id=1, source_target_pairs={{0,4},{2,6},{4,0},{6,2},{1,5},{3,7},{5,1},{7,3},{8,12},{10,14},{12... | collective-permute-start | bytes 1572872 | tf_op jit(solution)/shard_map/ppermute | solution.py:71
  511.4 23.2 %collective-permute-start.35 = (bf16[256,1024]{1,0:T(8,128)(2,1)S(1)}, bf16[256,1024]{1,0:T(8,128)(2,1)S(1)}, u32[]{:S(2)}, u32[]{:S(2)}) collective-permute-start(bf16[256,1024]{1,0:T(8,128)(2,1)S(1)} %get-tuple-element.131), channel_id=1, source_target_pairs={{0,2},{2,0},{4,6},{6,4},{1,3},{3,1},{5,7},{7,5},{8,10},{10,8},{12,... | collective-permute-start | bytes 1572872 | tf_op jit(solution)/shard_map/ppermute | solution.py:71
  536.3 10.1 %collective-permute-start.38 = (bf16[1024,1024]{1,0:T(8,128)(2,1)}, bf16[1024,1024]{1,0:T(8,128)(2,1)}, u32[]{:S(2)}, u32[]{:S(2)}) collective-permute-start(bf16[1024,1024]{1,0:T(8,128)(2,1)} %pad_maximum_fusion.3), channel_id=1, source_target_pairs={{0,1},{1,0},{2,3},{3,2},{4,5},{5,4},{6,7},{7,6},{8,9},{9,8},{10,11... | collective-permute-start | bytes 6291464 | tf_op jit(solution)/shard_map/ppermute | solution.py:71
  537.1 9.2 %collective-permute-start.39 = (bf16[256,1024]{1,0:T(8,128)(2,1)}, bf16[256,1024]{1,0:T(8,128)(2,1)}, u32[]{:S(2)}, u32[]{:S(2)}) collective-permute-start(bf16[256,1024]{1,0:T(8,128)(2,1)} %constant_dynamic-slice_fusion), channel_id=1, source_target_pairs={{0,1},{1,0},{2,3},{3,2},{4,5},{5,4},{6,7},{7,6},{8,9},{9,8},{10,11... | collective-permute-start | bytes 1572872 | tf_op jit(solution)/shard_map/ppermute | solution.py:71
  546.3 113.7 %reduce-scatter.7.cloned.1.call-start = ((), (), s32[]{:S(2)}) async-start(), calls=%async_computation.9 | async-start | bytes 1310720 | tf_op jit(solution)/shard_map/reduce_scatter | solution.py:341
  574.8 3.3 collective-permute-start.40
  578.2 7.1 collective-permute-start.41
  583.1 3.7 collective-permute-start.42
  583.7 4.5 collective-permute-start.43
  590.8 3.8 collective-permute-start.44
  593.4 120.1 %reduce-scatter.5.cloned.1.call-start = ((), (), s32[]{:S(2)}) async-start(), calls=%async_computation.8 | async-start | bytes 3932160 | tf_op jit(solution)/shard_map/reduce_scatter | solution.py:338
  602.6 257.8 %reduce-scatter.9.cloned.1.call-start = ((), (), s32[]{:S(2)}) async-start(), calls=%async_computation.10 | async-start | bytes 10485760 | tf_op jit(solution)/shard_map/reduce_scatter | solution.py:344
  617.9 1.3 collective-permute-start.48
  619.2 4.0 collective-permute-start.49
  623.2 18.3 %collective-permute-start.50 = (f32[4,2048]{1,0:T(4,128)S(1)}, f32[4,2048]{1,0:T(4,128)S(1)}, u32[]{:S(2)}, u32[]{:S(2)}) collective-permute-start(f32[4,2048]{1,0:T(4,128)S(1)} %add.395), channel_id=1, source_target_pairs={{0,4},{2,6},{4,0},{6,2},{1,5},{3,7},{5,1},{7,3},{8,12},{10,14},{12... | collective-permute-start | bytes 98312 | tf_op jit(solution)/shard_map/ppermute | solution.py:71
  641.5 7.5 collective-permute-start.51
  649.0 13.8 %collective-permute-start.52 = (f32[4,2048]{1,0:T(4,128)S(1)}, f32[4,2048]{1,0:T(4,128)S(1)}, u32[]{:S(2)}, u32[]{:S(2)}) collective-permute-start(f32[4,2048]{1,0:T(4,128)S(1)} %add.397), channel_id=1, source_target_pairs={{0,16},{8,24},{16,0},{24,8},{1,17},{9,25},{17,1},{25,9},{2,18},{10... | collective-permute-start | bytes 98312 | tf_op jit(solution)/shard_map/ppermute | solution.py:71
  656.5 16.0 %collective-permute-start.47 = (bf16[256,1024]{1,0:T(8,128)(2,1)}, bf16[256,1024]{1,0:T(8,128)(2,1)S(1)}, u32[]{:S(2)}, u32[]{:S(2)}) collective-permute-start(bf16[256,1024]{1,0:T(8,128)(2,1)} %get-tuple-element.110), channel_id=1, source_target_pairs={{0,6},{2,4},{4,2},{6,0},{1,7},{3,5},{5,3},{7,1},{8,14},{10,12},{12... | collective-permute-start | bytes 1572872 | tf_op jit(solution)/shard_map/ppermute | solution.py:71
  657.9 23.1 %collective-permute-start.46 = (bf16[256,1024]{1,0:T(8,128)(2,1)}, bf16[256,1024]{1,0:T(8,128)(2,1)}, u32[]{:S(2)}, u32[]{:S(2)}) collective-permute-start(bf16[256,1024]{1,0:T(8,128)(2,1)} %get-tuple-element.111), channel_id=1, source_target_pairs={{0,4},{2,6},{4,0},{6,2},{1,5},{3,7},{5,1},{7,3},{8,12},{10,14},{12... | collective-permute-start | bytes 1572872 | tf_op jit(solution)/shard_map/ppermute | solution.py:71
  658.5 55.0 %copy-start.8 = (f32[3,256,512]{1,2,0:T(8,128)S(1)}, f32[3,256,512]{1,2,0:T(8,128)}, u32[]{:S(2)}) copy-start(f32[3,256,512]{1,2,0:T(8,128)} %copy-done.7) | copy-start | bytes 4718596
  658.5 22.5 %collective-permute-start.45 = (bf16[256,1024]{1,0:T(8,128)(2,1)}, bf16[256,1024]{1,0:T(8,128)(2,1)}, u32[]{:S(2)}, u32[]{:S(2)}) collective-permute-start(bf16[256,1024]{1,0:T(8,128)(2,1)} %get-tuple-element.109), channel_id=1, source_target_pairs={{0,2},{2,0},{4,6},{6,4},{1,3},{3,1},{5,7},{7,5},{8,10},{10,8},{12,... | collective-permute-start | bytes 1572872 | tf_op jit(solution)/shard_map/ppermute | solution.py:71
  (81 other events, 736.2 us)
Sparse Core Ops, SparseCore 0:
  10.4 66.1 all-gather.4
  78.7 26.1 all-gather.6
  107.0 148.6 all-gather.8
  297.9 78.4 all-gather.10
  546.4 74.5 reduce-scatter.10
  623.9 28.3 reduce-scatter.6
  654.5 58.9 reduce-scatter.4
  715.9 144.4 reduce-scatter.8

commit v2 on v1

--- a/solution.py
+++ b/solution.py
@@ -1,6 +1,8 @@
 import jax
 import jax.numpy as jnp
 from jax import lax
+from jax.experimental import pallas as pl
+from jax.experimental.pallas import tpu as pltpu
 from jax.sharding import PartitionSpec as P
 
 D = 2048
@@ -105,34 +107,413 @@
     )
 
 
-def scatter_rows(partial_value):
+def scatter_rows(own, low):
+    for k in range(1, lax.axis_size("row")):
+        own = own + swap(low[k - 1], "row", k).astype(jnp.float32)
+    return own
+
+
+VMEM = 48 * 1024 * 1024
+TILE = 256
+NN = (((1,), (0,)), ((), ()))
+NT = (((1,), (1,)), ((), ()))
+TN = (((0,), (0,)), ((), ()))
+
+
+def mm(left, right, dims=NN):
+    return lax.dot_general(left, right, dims, preferred_element_type=jnp.float32)
+
+
+def run(body, grid, ins, outs):
+    place = lax.axis_index("col").astype(jnp.int32).reshape(1)
+    return pl.pallas_call(
+        body,
+        grid_spec=pltpu.PrefetchScalarGridSpec(
+            num_scalar_prefetch=1,
+            grid=grid,
+            in_specs=[pl.BlockSpec(block, where) for _, block, where in ins],
+            out_specs=[pl.BlockSpec(block, where) for _, _, block, where in outs],
+        ),
+        out_shape=[jax.ShapeDtypeStruct(shape, kind) for shape, kind, _, _ in outs],
+        compiler_params=pltpu.CompilerParams(vmem_limit_bytes=VMEM),
+        cost_estimate=pl.CostEstimate(flops=1, bytes_accessed=1, transcendentals=0),
+    )(place, *[array for array, _, _ in ins])
+
+
+def whole(array):
+    zeros = (0,) * array.ndim
+    return (array, array.shape, lambda *_: zeros)
+
+
+def tie_body(value, *refs):
+    pass
+
+
+def tie(value, *earlier):
+    return pl.pallas_call(
+        tie_body,
+        in_specs=[pl.BlockSpec(memory_space=pl.ANY)] * (1 + len(earlier)),
+        out_specs=pl.BlockSpec(memory_space=pl.ANY),
+        out_shape=jax.ShapeDtypeStruct(value.shape, value.dtype),
+        input_output_aliases={0: 0},
+        cost_estimate=pl.CostEstimate(flops=1, bytes_accessed=1, transcendentals=0),
+    )(value, *earlier)
+
+
+def row_outs(extent, columns, tile):
     count = lax.axis_size("row")
-    parts = partial_value.reshape(count, partial_value.shape[0] // count, -1)
-    low = parts.astype(jnp.bfloat16)
-    total = parts[0]
-    for k in range(1, count):
-        total = total + swap(low[k], "row", k).astype(jnp.float32)
-    return total
-
-
-def join_halves(own, axis):
-    half = own.shape[axis]
-    place = lax.axis_index("col") * half
-    shape = list(own.shape)
-    shape[axis] = 2 * half
-    whole = lax.dynamic_update_slice_in_dim(jnp.zeros(shape, own.dtype), own, place, axis)
-    return lax.dynamic_update_slice_in_dim(whole, swap_col(own), half - place, axis)
-
-
-def split_halves(block, axis):
+    rows = extent // count
+    return [
+        ((rows, columns), jnp.float32, (rows, tile), lambda n, c: (0, n)),
+        (
+            (count - 1, rows, columns),
+            jnp.bfloat16,
+            (count - 1, rows, tile),
+            lambda n, c: (0, 0, n),
+        ),
+    ]
+
+
+def put_rows(total, own, low):
+    rows = own.shape[0]
+    own[...] = total[:rows]
+    low[...] = total[rows:].astype(jnp.bfloat16).reshape(low.shape)
+
+
+def project(rows, block):
+    n, _, d, width = block.shape
+    half = width // 2
+    extent = rows.shape[0]
+
+    def body(c, x, mine, theirs, own, far):
+        own[0] = mm(x[...], mine[...].reshape(n * d, half))
+        far[0] = mm(x[...], theirs[...].reshape(n * d, half))
+
+    return run(
+        body,
+        (3,),
+        [
+            whole(rows),
+            (block, (n, 1, d, half), lambda k, c: (0, k, 0, c[0])),
+            (block, (n, 1, d, half), lambda k, c: (0, k, 0, 1 - c[0])),
+        ],
+        [
+            ((3, extent, half), jnp.float32, (1, extent, half), lambda k, c: (k, 0, 0)),
+            ((3, extent, half), jnp.float32, (1, extent, half), lambda k, c: (k, 0, 0)),
+        ],
+    )
+
+
+def mix(own, other, block):
+    n, _, d, width = block.shape
+    extent, half = own.shape
+
+    def body(c, x, y, mine, theirs, out, low):
+        parts = []
+        a = mine[...].reshape(n // 2, 2, d // 2, width)
+        b = theirs[...].reshape(n // 2, 2, d // 2, width)
+        for h in range(2):
+            parts.append(
+                mm(x[...], a[:, h].reshape(half, width)) + mm(y[...], b[:, h].reshape(half, width))
+            )
+        put_rows(jnp.concatenate(parts, 1), out, low)
+
+    return run(
+        body,
+        (1,),
+        [
+            whole(own),
+            whole(other),
+            (block, (n // 2, 1, d, width), lambda n, c: (c[0], 3, 0, 0)),
+            (block, (n // 2, 1, d, width), lambda n, c: (1 - c[0], 3, 0, 0)),
+        ],
+        row_outs(extent, 2 * width, 2 * width),
+    )
+
+
+def mix_back(own, other, block, far):
+    n, _, d, width = block.shape
+    extent = own.shape[0]
+    half = n * d // 4
+
+    def body(c, x, y, mine, theirs, out):
+        a = mine[...].reshape(n // 2, 2, d // 2, width)
+        b = theirs[...].reshape(n // 2, 2, d // 2, width)
+        total = None
+        for h in range(2):
+            cols = slice(h * width, (h + 1) * width)
+            part = mm(x[:, cols], a[:, h].reshape(half, width), NT) + mm(
+                y[:, cols], b[:, h].reshape(half, width), NT
+            )
+            total = part if total is None else total + part
+        out[...] = total.astype(jnp.bfloat16)
+
+    return run(
+        body,
+        (1,),
+        [
+            whole(own),
+            whole(other),
+            (block, (n // 2, 1, d, width), lambda n, c: (c[0], 3, 0, 0)),
+            whole(far),
+        ],
+        [((extent, half), jnp.bfloat16, (extent, half), lambda n, c: (0, 0))],
+    )[0]
+
+
+def widen_send(rows, block, t):
+    n, _, d, width = block.shape
+    part = width // 4
+    extent = rows.shape[0]
+
+    def body(c, x, w, out):
+        out[0] = mm(x[...], w[...].reshape(n * d, part)).astype(jnp.bfloat16)
+
+    return run(
+        body,
+        (2,),
+        [
+            whole(rows),
+            (block, (n, 1, d, part), lambda k, c: (0, k, 0, (1 - c[0]) * 2 + t)),
+        ],
+        [((2, extent, part), jnp.bfloat16, (1, extent, part), lambda k, c: (k, 0, 0))],
+    )[0]
+
+
+def widen(rows, block, arrived, t):
+    n, _, d, width = block.shape
+    part = width // 4
+    extent = rows.shape[0]
+    tiles = part // TILE
+
+    def body(c, x, gate, up, far, kept, out):
+        g = mm(x[...], gate[...].reshape(n * d, TILE)) + far[0].astype(jnp.float32)
+        u = mm(x[...], up[...].reshape(n * d, TILE)) + far[1].astype(jnp.float32)
+        kept[0] = g
+        kept[1] = u
+        out[...] = (g * jax.nn.sigmoid(g) * u).astype(jnp.bfloat16)
+
+    return run(
+        body,
+        (tiles,),
+        [
+            whole(rows),
+            (block, (n, 1, d, TILE), lambda i, c: (0, 0, 0, (c[0] * 2 + t) * tiles + i)),
+            (block, (n, 1, d, TILE), lambda i, c: (0, 1, 0, (c[0] * 2 + t) * tiles + i)),
+            (arrived, (2, extent, TILE), lambda i, c: (0, 0, i)),
+        ],
+        [
+            ((2, extent, part), jnp.float32, (2, extent, TILE), lambda i, c: (0, 0, i)),
+            ((extent, part), jnp.bfloat16, (extent, TILE), lambda i, c: (0, i)),
+        ],
+    )
+
+
+def narrow(own, other, block):
+    pieces = block.reshape(4, block.shape[0] // 4, block.shape[1])
+    _, part, columns = pieces.shape
+    extent = own[0].shape[0]
+
+    def body(c, x0, x1, y0, y1, mine, theirs, out, low):
+        total = mm(x0[...], mine[0]) + mm(x1[...], mine[1])
+        total = total + mm(y0[...], theirs[0]) + mm(y1[...], theirs[1])
+        put_rows(total, out, low)
+
+    return run(
+        body,
+        (columns // TILE,),
+        [whole(x) for x in own + other]
+        + [
+            (pieces, (2, part, TILE), lambda n, c: (c[0], 0, n)),
+            (pieces, (2, part, TILE), lambda n, c: (1 - c[0], 0, n)),
+        ],
+        row_outs(extent, columns, TILE),
+    )
+
+
+def narrow_weight(own, other, grads):
+    extent, part = own[0].shape
+    columns = grads.shape[1]
+
+    def body(c, x0, x1, y0, y1, g, out):
+        for j, x in enumerate((x0, x1, y0, y1)):
+
+            @pl.when(pl.program_id(0) == j)
+            def _(x=x):
+                out[...] = mm(x[...], g[...], TN).astype(jnp.bfloat16)
+
+    def where(i, c):
+        return (jnp.where(i < 2, c[0] * 2 + i, (1 - c[0]) * 2 + i - 2), 0)
+
+    return run(
+        body,
+        (4,),
+        [whole(x) for x in own + other] + [whole(grads)],
+        [((4 * part, columns), jnp.bfloat16, (part, columns), where)],
+    )[0]
+
+
+def narrow_back(own, other, block, far, kept, t):
+    pieces = block.reshape(4, block.shape[0] // 4, block.shape[1])
+    _, part, columns = pieces.shape
+    extent = own.shape[0]
+    tiles = part // TILE
+
+    def body(c, x, y, mine, theirs, saved, out):
+        grad = mm(x[...], mine[0], NT) + mm(y[...], theirs[0], NT)
+        gate = saved[0]
+        sig = jax.nn.sigmoid(gate)
+        out[0] = (grad * saved[1] * sig * (1.0 + gate * (1.0 - sig))).astype(jnp.bfloat16)
+        out[1] = (grad * (gate * sig)).astype(jnp.bfloat16)
+
+    return run(
+        body,
+        (tiles,),
+        [
+            whole(own),
+            whole(other),
+            (pieces, (1, TILE, columns), lambda i, c: (c[0] * 2 + t, i, 0)),
+            (far, (1, TILE, columns), lambda i, c: (t, i, 0)),
+            (kept, (2, extent, TILE), lambda i, c: (0, 0, i)),
+        ],
+        [((2, extent, part), jnp.bfloat16, (2, extent, TILE), lambda i, c: (0, 0, i))],
+    )[0]
+
+
+def widen_back(own, other, block):
+    n, _, d, width = block.shape
+    part = width // 4
+    extent = own[0].shape[1]
+    group = TILE // d
+
+    def body(c, x0, x1, y0, y1, w0, w1, v0, v1, out, low):
+        total = None
+        for x, w in ((x0, w0), (x1, w1), (y0, v0), (y1, v1)):
+            for k in range(2):
+                piece = mm(x[k], w[:, k].reshape(TILE, part), NT)
+                total = piece if total is None else total + piece
+        put_rows(total, out, low)
+
+    shape = (group, 2, d, part)
+    return run(
+        body,
+        (n * d // TILE,),
+        [whole(x) for x in own + other]
+        + [
+            (block, shape, lambda i, c: (i, 0, 0, c[0] * 2)),
+            (block, shape, lambda i, c: (i, 0, 0, c[0] * 2 + 1)),
+            (block, shape, lambda i, c: (i, 0, 0, 2 - c[0] * 2)),
+            (block, shape, lambda i, c: (i, 0, 0, 3 - c[0] * 2)),
+        ],
+        row_outs(extent, n * d, TILE),
+    )
+
+
+def widen_weight(rows, own, other, shape):
+    n, _, d, width = shape
+    extent, features = rows.shape
+    part = width // 4
+    group = TILE // d
+
+    def body(c, x, y0, y1, z0, z1, out):
+        for j, y in enumerate((y0, y1, z0, z1)):
+
+            @pl.when(pl.program_id(1) == j)
+            def _(y=y):
+                for k in range(2):
+                    out[:, k] = (
+                        mm(x[...], y[k], TN).astype(jnp.bfloat16).reshape(group, d, part)
+                    )
+
+    def where(i, j, c):
+        return (i, 0, 0, jnp.where(j < 2, c[0] * 2 + j, (1 - c[0]) * 2 + j - 2))
+
+    return run(
+        body,
+        (features // TILE, 4),
+        [(rows, (extent, TILE), lambda i, j, c: (0, i))] + [whole(y) for y in own + other],
+        [(shape, jnp.bfloat16, (group, 2, d, part), where)],
+    )[0]
+
+
+def project_back(own, other, block):
+    n, _, d, width = block.shape
+    half = width // 2
+    extent = own.shape[1]
+    group = TILE // d
+
+    def body(c, x, y, mine, theirs, out, low):
+        total = None
+        for a, w in ((x, mine), (y, theirs)):
+            for k in range(3):
+                piece = mm(a[k], w[:, k].reshape(TILE, half), NT)
+                total = piece if total is None else total + piece
+        put_rows(total, out, low)
+
+    return run(
+        body,
+        (n * d // TILE,),
+        [
+            whole(own),
+            whole(other),
+            (block, (group, 4, d, half), lambda i, c: (i, 0, 0, c[0])),
+            (block, (group, 4, d, half), lambda i, c: (i, 0, 0, 1 - c[0])),
+        ],
+        row_outs(extent, n * d, TILE),
+    )
+
+
+def entry_mixer_weight(rows, own, other, heads, far_heads, grads, shape):
+    n, _, d, width = shape
+    half = width // 2
+    extent, features = rows.shape
+    group = TILE // d
+    low = jnp.bfloat16
+    fine = TILE // 2
+
+    def body(c, x, y, z, a, b, g, out):
+        for k in range(3):
+            mine = mm(x[...], y[k], TN).astype(low).reshape(group, d, half)
+            theirs = mm(x[...], z[k], TN).astype(low).reshape(group, d, half)
+            for side in range(2):
+
+                @pl.when(c[0] == side)
+                def _():
+                    out[:, k, :, side * half : (side + 1) * half] = mine
+                    out[:, k, :, (1 - side) * half : (2 - side) * half] = theirs
+
+        i = pl.program_id(0)
+        for source, first in ((a, c[0] * 2), (b, (1 - c[0]) * 2)):
+            for j in range(2):
+
+                @pl.when(i == first + j)
+                def _():
+                    piece = mm(source[:, j * fine : (j + 1) * fine], g[...], TN).astype(low)
+                    for h in range(2):
+                        out[:, 3, h * (d // 2) : (h + 1) * (d // 2), :] = piece[
+                            :, h * width : (h + 1) * width
+                        ].reshape(group, d // 2, width)
+
+    return run(
+        body,
+        (features // TILE,),
+        [(rows, (extent, TILE), lambda i, c: (0, i))]
+        + [whole(v) for v in (own, other, heads, far_heads, grads)],
+        [(shape, low, (group, 4, d, width), lambda i, c: (i, 0, 0, 0))],
+    )[0]
+
+
+def take_half(block, axis, which):
     half = block.shape[axis] // 2
-    place = lax.axis_index("col") * half
-    own = lax.dynamic_slice_in_dim(block, place, half, axis)
-    return (own, swap_col(lax.dynamic_slice_in_dim(block, half - place, half, axis)))
-
-
-def dot(equation, left, right):
-    return jnp.einsum(equation, left, right, preferred_element_type=jnp.float32)
+    return lax.dynamic_slice_in_dim(block, which * half, half, axis)
+
+
+def gather_shards(shard):
+    return lax.all_gather(shard, "dp", axis=0, tiled=True)
+
+
+def scatter_shards(values):
+    return lax.psum_scatter(values, "dp", scatter_dimension=0, tiled=True)
 
 
 def on_device(
@@ -155,12 +536,23 @@
     reduce_mean,
     reduce_square,
 ):
-    entry_block, mixer_block, expand_block, reduce_block = (
-        lax.all_gather(entry_weight.astype(jnp.bfloat16), "dp", axis=1, tiled=True),
-        lax.all_gather(mixer_weight.astype(jnp.bfloat16), "dp", axis=0, tiled=True),
-        lax.all_gather(expand_weight.astype(jnp.bfloat16), "dp", axis=1, tiled=True),
-        lax.all_gather(reduce_weight.astype(jnp.bfloat16), "dp", axis=0, tiled=True),
-    )
+    low = jnp.bfloat16
+    shards = lax.axis_size("dp")
+    side = lax.axis_index("col")
+    depth, grid_width = entry_weight.shape[1:]
+    mixer_rows = mixer_weight.shape[0]
+    entry_shard = jnp.concatenate(
+        [
+            entry_weight.astype(low).reshape(-1, grid_width),
+            mixer_weight[:, :grid_width].astype(low),
+            mixer_weight[:, grid_width:].astype(low),
+        ],
+        0,
+    )
+    entry_block = gather_shards(entry_shard).reshape(shards, 4, depth, grid_width)
+    expand_shard = expand_weight.astype(low).reshape(-1, expand_weight.shape[2])
+    expand_block = gather_shards(expand_shard).reshape((shards,) + expand_weight.shape)
+    reduce_block = gather_shards(reduce_weight.astype(low))
     row_size = lax.axis_size("row")
     col_size = lax.axis_size("col")
     local_rows = tokens.shape[0]
@@ -173,7 +565,7 @@
     ).reshape(extent)
     segment, positions = layout_info(seq_lengths[0], indices)
     local_valid = (segment[:local_rows] < seq_lengths.shape[1]).astype(jnp.float32)
-    head_width = entry_block.shape[2] // col_size
+    head_width = grid_width // col_size
     head_start = (row_index * col_size + lax.axis_index("col")) * head_width
     col_start = lax.axis_index("col") * feature_local
     post_gain = lax.dynamic_slice_in_dim(gains[0:2], col_start, feature_local, 1)
@@ -182,11 +574,8 @@
     shrink = HD ** (-0.5)
     inputs = tokens.astype(jnp.float32)
     token_rows = gather_rows(tokens)
-    token_other = swap_col(token_rows)
-    entry_own, entry_far = split_halves(entry_block, 2)
-    projected = dot("td,kdf->ktf", token_rows, entry_own) + dot(
-        "td,kdf->ktf", token_other, entry_far
-    )
+    projected, projected_far = project(token_rows, entry_block)
+    projected = projected + swap_col(projected_far)
     squares = grid_total(jnp.sum(projected[0:2] * projected[0:2], -1))
     query_scale = lax.rsqrt(squares[0] / D + NORM_EPSILON)[:, None]
     key_scale = lax.rsqrt(squares[1] / D + NORM_EPSILON)[:, None]
@@ -227,22 +616,21 @@
         )
         logsums.append(peak + jnp.log(totals))
     attended = jnp.concatenate(outputs, 0).astype(jnp.bfloat16).reshape(extent, head_width)
-    attended_cols = join_halves(attended, 1)
-    branch = scatter_rows(dot("tf,fd->td", attended_cols, mixer_block))
+    attended_other = swap_col(attended)
+    branch = scatter_rows(*mix(attended, attended_other, entry_block))
     branch_scale = lax.rsqrt(feature_total(jnp.sum(branch * branch, -1)) / D + NORM_EPSILON)[
         :, None
     ]
     branch_hat = branch * branch_scale
     hidden = inputs + branch_hat * post_gain[0]
     hidden_rows = gather_rows(hidden.astype(jnp.bfloat16))
-    hidden_other = swap_col(hidden_rows)
-    expand_own, expand_far = split_halves(expand_block, 2)
-    gated = dot("td,kdf->ktf", hidden_rows, expand_own) + dot(
-        "td,kdf->ktf", hidden_other, expand_far
-    )
-    product = (jax.nn.silu(gated[0]) * gated[1]).astype(jnp.bfloat16)
-    product_cols = join_halves(product, 1)
-    second = scatter_rows(dot("tf,fd->td", product_cols, reduce_block))
+    sent = [widen_send(hidden_rows, expand_block, t) for t in range(2)]
+    kept, product = zip(
+        *[widen(hidden_rows, expand_block, swap_col(sent[t]), t) for t in range(2)]
+    )
+    product = list(product)
+    product_other = [swap_col(value) for value in product]
+    second = scatter_rows(*narrow(product, product_other, reduce_block))
     second_scale = lax.rsqrt(feature_total(jnp.sum(second * second, -1)) / D + NORM_EPSILON)[
         :, None
     ]
@@ -256,18 +644,22 @@
         jnp.bfloat16
     )
     second_rows = gather_rows(second_grad)
+    reduce_sum = narrow_weight(product, product_other, second_rows)
+    reduce_grad = scatter_shards(reduce_sum)
     second_other = swap_col(second_rows)
-    reduce_sum = dot("tf,td->fd", product_cols, second_rows)
-    reduce_own, reduce_far = split_halves(reduce_block, 0)
-    product_grad = dot("td,fd->tf", second_rows, reduce_own) + dot(
-        "td,fd->tf", second_other, reduce_far
-    )
-    sigmoid = jax.nn.sigmoid(gated[0])
-    gate_grad = product_grad * gated[1] * sigmoid * (1.0 + gated[0] * (1.0 - sigmoid))
-    up_grad = product_grad * jax.nn.silu(gated[0])
-    gated_grad = join_halves(jnp.stack([gate_grad, up_grad]).astype(jnp.bfloat16), 2)
-    hidden_back = scatter_rows(dot("ktw,kdw->td", gated_grad, expand_block))
-    expand_sum = dot("td,ktw->kdw", hidden_rows, gated_grad)
+    reduce_pieces = reduce_block.reshape(4, -1, reduce_block.shape[1])
+    reduce_far = swap_col(take_half(reduce_pieces, 0, 1 - side))
+    gated_grad = [
+        narrow_back(tie(second_rows, reduce_sum), second_other, reduce_block, reduce_far, kept[t], t)
+        for t in range(2)
+    ]
+    gated_other = [swap_col(value) for value in gated_grad]
+    hidden_back = scatter_rows(*widen_back(gated_grad, gated_other, expand_block))
+    expand_sum = widen_weight(hidden_rows, gated_grad, gated_other, expand_block.shape)
+    expand_grad = scatter_shards(
+        tie(expand_sum, reduce_grad).reshape(-1, expand_block.shape[3])
+    ).reshape(expand_weight.shape)
+    hidden_back = tie(hidden_back, expand_sum)
     hidden_grad = upstream + hidden_back
     gain_first_post = jnp.sum(hidden_grad * branch_hat, 0)
     scaled = hidden_grad * post_gain[0]
@@ -277,12 +669,10 @@
     )
     branch_rows = gather_rows(branch_grad)
     branch_other = swap_col(branch_rows)
-    mixer_sum = dot("tf,td->fd", attended_cols, branch_rows)
-    mixer_own, mixer_far = split_halves(mixer_block, 0)
-    attended_grad = dot("td,fd->tf", branch_rows, mixer_own) + dot(
-        "td,fd->tf", branch_other, mixer_far
-    )
-    attended_low = attended_grad.astype(jnp.bfloat16).reshape(extent, head_count, HD)
+    mixer_far = swap_col(take_half(entry_block[:, 3:], 0, 1 - side))
+    attended_low = mix_back(branch_rows, branch_other, entry_block, mixer_far).reshape(
+        extent, head_count, HD
+    )
     query_parts = []
     key_accum = jnp.zeros((extent, head_count, HD), jnp.float32)
     value_accum = jnp.zeros((extent, head_count, HD), jnp.float32)
@@ -328,26 +718,30 @@
     query_raw = query_scale * (query_scaled - query_hat * head_dots[0][:, None] / D)
     key_raw = key_scale * (key_scaled - key_hat * head_dots[1][:, None] / D)
     value_grad = value_accum.reshape(extent, head_width)
-    projected_grad = join_halves(
-        jnp.stack([query_raw, key_raw, value_grad]).astype(jnp.bfloat16), 2
-    )
-    entry_back = scatter_rows(dot("ktw,kdw->td", projected_grad, entry_block))
-    entry_sum = dot("td,ktw->kdw", token_rows, projected_grad)
+    projected_grad = jnp.stack([query_raw, key_raw, value_grad]).astype(low)
+    projected_other = swap_col(projected_grad)
+    entry_sum = entry_mixer_weight(
+        token_rows,
+        projected_grad,
+        projected_other,
+        attended,
+        attended_other,
+        branch_rows,
+        entry_block.shape,
+    )
+    entry_out = scatter_shards(tie(entry_sum, expand_grad).reshape(-1, grid_width)).astype(
+        jnp.float32
+    )
+    entry_back = scatter_rows(
+        *project_back(tie(projected_grad, entry_sum), projected_other, entry_block)
+    )
     input_grad = hidden_grad + entry_back
-    entry_grad, mixer_grad, expand_grad, reduce_grad = (
-        lax.psum_scatter(
-            entry_sum.astype(jnp.bfloat16), "dp", scatter_dimension=1, tiled=True
-        ).astype(jnp.float32),
-        lax.psum_scatter(
-            mixer_sum.astype(jnp.bfloat16), "dp", scatter_dimension=0, tiled=True
-        ).astype(jnp.float32),
-        lax.psum_scatter(
-            expand_sum.astype(jnp.bfloat16), "dp", scatter_dimension=1, tiled=True
-        ).astype(jnp.float32),
-        lax.psum_scatter(
-            reduce_sum.astype(jnp.bfloat16), "dp", scatter_dimension=0, tiled=True
-        ).astype(jnp.float32),
-    )
+    entry_grad = entry_out[: 3 * depth].reshape(entry_weight.shape)
+    mixer_grad = jnp.concatenate(
+        [entry_out[3 * depth : 3 * depth + mixer_rows], entry_out[3 * depth + mixer_rows :]], 1
+    )
+    expand_grad = expand_grad.astype(jnp.float32)
+    reduce_grad = reduce_grad.astype(jnp.float32)
     gain_local = jnp.zeros((4, D), jnp.float32)
     gain_local = lax.dynamic_update_slice(
         gain_local, jnp.stack([gain_first_post, gain_second_post]), (0, col_start)

time: 901 us -> 725 us (0.80)
  waiting for transfers between devices: 557 us -> 409 us
  Pallas kernels: 0 us -> 105 us
  matrix products: 113 us -> 20.7 us
  local copies, waits for them, and re-layouts: 92.5 us -> 60.4 us
  other arithmetic: 73.6 us -> 62.6 us
    reduce_scatter x4 -> x3, waiting for transfers between devices: 163 us -> 43.6 us  [scatter_shards(): return lax.psum_scatter(values, 'dp', scatter_dimension=0, tiled=True)]
    pallas_call x0 -> x20, Pallas kernels: none -> 105 us  [the longest x15 105 us: run(): pl.pallas_call(body, grid_spec=pltpu.PrefetchScalarGridSpec(num_scalar_pr...]
    dot_general x16 -> x0, matrix products: 95.5 us -> none  [dot(): return jnp.einsum(equation, left, right, preferred_element_type=jnp.float32)]
    all_gather x4 -> x3, waiting for transfers between devices: 204 us -> 153 us  [gather_shards(): return lax.all_gather(shard, 'dp', axis=0, tiled=True)]
    unnamed x194 -> x158, local copies, waits for them, and re-layouts: 60.1 us -> 33.9 us
    ppermute x53 -> x54, waiting for transfers between devices: 191 us -> 213 us  [swap(): lax.ppermute(values, axis, [(i, i ^ distance) for i in range(lax.axis_siz...]
    ppermute x53 -> x54, starting transfers between devices: 43.7 us -> 45.6 us  [swap(): lax.ppermute(values, axis, [(i, i ^ distance) for i in range(lax.axis_siz...]
  transfers between devices with their start and end apart: 61 -> 60, of which waited for: 38 -> 45; matrix products, arithmetic and copies ran while one was open for 22% -> 15% of each run, Pallas kernels for 0% -> 12%
where the time goes in v2:
time: 725 us; the launch traced here: 720 us
  waiting for transfers between devices  409 us (56%)
  Pallas kernels  105 us (14%)
  other arithmetic  62.6 us (9%)
  local copies, waits for them, and re-layouts  60.4 us (8%)
  starting transfers between devices  45.8 us (6%)
  matrix products  20.7 us (3%)
  between operations  15.6 us (2%)
    ppermute x54, waiting for transfers between devices, swap(): lax.ppermute(values, axis, [(i, i ^ distance) for i in range(lax.axis_siz...  213 us
    all_gather x3, waiting for transfers between devices, gather_shards(): return lax.all_gather(shard, 'dp', axis=0, tiled=True)  153 us
    pallas_call x15, Pallas kernels, run(): pl.pallas_call(body, grid_spec=pltpu.PrefetchScalarGridSpec(num_scalar_pr...  105 us
    ppermute x54, starting transfers between devices, swap(): lax.ppermute(values, axis, [(i, i ^ distance) for i in range(lax.axis_siz...  45.6 us
    reduce_scatter x3, waiting for transfers between devices, scatter_shards(): return lax.psum_scatter(values, 'dp', scatter_dimension=0, tiled=True)  43.6 us
    unnamed x158, local copies, waits for them, and re-layouts  33.9 us
    sub x5, other arithmetic, adam_step(): weight - step_rate * (ratio + decay_rate * weight)  21.6 us
  transfers between devices with their start and end apart: 60, of which 45 were waited for; matrix products, arithmetic and copies ran while one was open for 15% of the time, Pallas kernels for 12%

profile of v2, /device:TPU:0, one launch (start us, length us, event | category | flops | bytes accessed | tf_op | source)
XLA Modules:
  0.0 719.7 jit_solution(5983333172451137028)
XLA Ops:
  11.0 3.8 convert_element_type.123
  15.8 2.9 collective-permute-start
  20.3 11.3 %collective-permute-done = bf16[256,1024]{1,0:T(8,128)(2,1)} collective-permute-done((bf16[256,1024]{1,0:T(8,128)(2,1)S(1)}, bf16[256,1024]{1,0:T(8,128)(2,1)}, u32[]{:S(2)}, u32[]{:S(2)}) %collective-permute-start) | collective-permute-done | bytes 524320 | tf_op jit(solution)/shard_map/ppermute | solution.py:73
  32.7 10.8 %collective-permute-done.1 = bf16[256,1024]{1,0:T(8,128)(2,1)} collective-permute-done((bf16[256,1024]{1,0:T(8,128)(2,1)S(1)}, bf16[256,1024]{1,0:T(8,128)(2,1)}, u32[]{:S(2)}, u32[]{:S(2)}) %collective-permute-start.1) | collective-permute-done | bytes 524320 | tf_op jit(solution)/shard_map/ppermute | solution.py:73
  44.6 49.9 %all-gather.4.cloned.1.call-done = bf16[4096,512]{1,0:T(8,128)(2,1)} async-done(((bf16[1024,512]{1,0:T(8,128)(2,1)}), bf16[4096,512]{1,0:T(8,128)(2,1)}) %all-gather.4.cloned.1.call-update) | async-done | bytes 4194320 | tf_op jit(solution)/shard_map/all_gather | solution.py:512
  94.5 6.5 shard_map.345
  105.8 3.1 multiply_cosine_fusion
  110.9 2.3 add.288
  118.2 2.6 fusion.63
  128.3 2.4 collective-permute-done.7
  144.7 2.6 shard_map.346
  151.9 12.4 %collective-permute-done.11 = bf16[256,1024]{1,0:T(8,128)(2,1)S(1)} collective-permute-done((bf16[256,1024]{1,0:T(8,128)(2,1)}, bf16[256,1024]{1,0:T(8,128)(2,1)S(1)}, u32[]{:S(2)}, u32[]{:S(2)}) %collective-permute-start.11) | collective-permute-done | bytes 524320 | tf_op jit(solution)/shard_map/ppermute | solution.py:73
  164.4 9.6 %collective-permute-done.10 = bf16[256,1024]{1,0:T(8,128)(2,1)S(1)} collective-permute-done((bf16[256,1024]{1,0:T(8,128)(2,1)}, bf16[256,1024]{1,0:T(8,128)(2,1)S(1)}, u32[]{:S(2)}, u32[]{:S(2)}) %collective-permute-start.10) | collective-permute-done | bytes 524320 | tf_op jit(solution)/shard_map/ppermute | solution.py:73
  180.8 12.2 %collective-permute-done.15 = bf16[256,1024]{1,0:T(8,128)(2,1)S(1)} collective-permute-done((bf16[256,1024]{1,0:T(8,128)(2,1)S(1)}, bf16[256,1024]{1,0:T(8,128)(2,1)S(1)}, u32[]{:S(2)}, u32[]{:S(2)}) %collective-permute-start.15) | collective-permute-done | bytes 524320 | tf_op jit(solution)/shard_map/ppermute | solution.py:73
  193.0 10.4 %collective-permute-done.14 = bf16[256,1024]{1,0:T(8,128)(2,1)S(1)} collective-permute-done((bf16[256,1024]{1,0:T(8,128)(2,1)S(1)}, bf16[256,1024]{1,0:T(8,128)(2,1)S(1)}, u32[]{:S(2)}, u32[]{:S(2)}) %collective-permute-start.14) | collective-permute-done | bytes 524320 | tf_op jit(solution)/shard_map/ppermute | solution.py:73
  203.7 41.2 %all-gather.6.cloned.1.call-done = bf16[2048,2048]{1,0:T(8,128)(2,1)} async-done(((bf16[512,2048]{1,0:T(8,128)(2,1)}), bf16[2048,2048]{1,0:T(8,128)(2,1)}) %all-gather.6.cloned.1.call-update) | async-done | bytes 8388624 | tf_op jit(solution)/shard_map/all_gather | solution.py:512
  244.9 3.8 shard_map.347
  248.8 3.8 shard_map.349
  253.1 5.2 shard_map.348
  258.4 5.3 shard_map.350
  264.1 61.9 %all-gather.8.cloned.1.call-done = bf16[2048,1024]{1,0:T(8,128)(2,1)} async-done(((bf16[512,1024]{1,0:T(8,128)(2,1)}), bf16[2048,1024]{1,0:T(8,128)(2,1)}) %all-gather.8.cloned.1.call-update) | async-done | bytes 4194320 | tf_op jit(solution)/shard_map/all_gather | solution.py:512
  326.1 8.1 %shard_map.351 = (f32[256,1024]{1,0:T(8,128)S(1)}, bf16[3,256,1024]{2,1,0:T(8,128)(2,1)}) custom-call(s32[1]{0:T(128)} %bitcast.c, bf16[1024,512]{1,0:T(8,128)(2,1)S(1)} %get-tuple-element.40.x0, bf16[1024,512]{1,0:T(8,128)(2,1)} %get-tuple-element.41.x1, bf16[1024,512]{1,0:T(8,128)(2,1)} %collective-permute-done.18.y0, ...), custom_call_target="tpu_custom_call" | custom-call | flops 1 | bytes 1 | tf_op jit(solution)/shard_map/pallas_call | solution.py:129
  335.7 2.5 collective-permute-start.22
  339.3 12.3 %collective-permute-done.22 = bf16[256,1024]{1,0:T(8,128)(2,1)S(1)} collective-permute-done((bf16[256,1024]{1,0:T(8,128)(2,1)S(1)}, bf16[256,1024]{1,0:T(8,128)(2,1)S(1)}, u32[]{:S(2)}, u32[]{:S(2)}) %collective-permute-start.22) | collective-permute-done | bytes 524320 | tf_op jit(solution)/shard_map/ppermute | solution.py:73
  351.5 10.1 %collective-permute-done.21 = bf16[256,1024]{1,0:T(8,128)(2,1)S(1)} collective-permute-done((bf16[256,1024]{1,0:T(8,128)(2,1)S(1)}, bf16[256,1024]{1,0:T(8,128)(2,1)S(1)}, u32[]{:S(2)}, u32[]{:S(2)}) %collective-permute-start.21) | collective-permute-done | bytes 524320 | tf_op jit(solution)/shard_map/ppermute | solution.py:73
  368.8 12.2 %collective-permute-done.27 = bf16[256,1024]{1,0:T(8,128)(2,1)S(1)} collective-permute-done((bf16[256,1024]{1,0:T(8,128)(2,1)S(1)}, bf16[256,1024]{1,0:T(8,128)(2,1)S(1)}, u32[]{:S(2)}, u32[]{:S(2)}) %collective-permute-start.27) | collective-permute-done | bytes 524320 | tf_op jit(solution)/shard_map/ppermute | solution.py:73
  381.0 10.4 %collective-permute-done.26 = bf16[256,1024]{1,0:T(8,128)(2,1)S(1)} collective-permute-done((bf16[256,1024]{1,0:T(8,128)(2,1)S(1)}, bf16[256,1024]{1,0:T(8,128)(2,1)S(1)}, u32[]{:S(2)}, u32[]{:S(2)}) %collective-permute-start.26) | collective-permute-done | bytes 524320 | tf_op jit(solution)/shard_map/ppermute | solution.py:73
  393.0 8.8 %shard_map.352.refs_0_ = bf16[2048,1024]{1,0:T(8,128)(2,1)} custom-call(s32[1]{0:T(128)} %bitcast.c, bf16[1024,512]{1,0:T(8,128)(2,1)S(1)} %get-tuple-element.40.x0, bf16[1024,512]{1,0:T(8,128)(2,1)} %get-tuple-element.41.x1, bf16[1024,512]{1,0:T(8,128)(2,1)} %collective-permute-done.18.y0, bf16[1024,512]{1,0:T(8,128)(2,1)} %collective-permute-done.19.y1, ...), custom_call_target="tpu_custom_call" | custom-call | flops 1 | bytes 1 | tf_op jit(solution)/shard_map/pallas_call | solution.py:129
  401.9 3.1 constant_dynamic-slice_fusion.1
  406.4 3.2 collective-permute-done.29.theirs
  411.2 6.0 shard_map.354.x0.y0
  417.6 6.1 shard_map.355.x1.y1
  424.2 3.8 collective-permute-done.31.y1.z1
  429.4 16.7 %shard_map.357.refs_0_ = bf16[4,2,256,2048]{3,2,1,0:T(8,128)(2,1)} custom-call(s32[1]{0:T(128)} %bitcast.c, bf16[1024,1024]{1,0:T(8,128)(2,1)S(1)} %pad_maximum_fusion.x, bf16[2,1024,512]{2,1,0:T(8,128)(2,1)S(1)} %shard_map.354.x0.y0, bf16[2,1024,512]{2,1,0:T(8,128)(2,1)} %copy-done.6, bf16[2,1024,512]{2,1,0:T(8,128)(2,1)} %copy-done.37, ...), custom_call_target="tpu_custom_call" | custom-call | flops 1 | bytes 1 | tf_op jit(solution)/shard_map/pallas_call | solution.py:129
  446.1 8.4 %copy.137.value = bf16[4,2,256,2048]{3,2,1,0:T(8,128)(2,1)} copy(bf16[4,2,256,2048]{3,2,1,0:T(8,128)(2,1)} %shard_map.357.refs_0_) | data formatting | bytes 16777216
  454.5 22.0 %reduce-scatter.4.cloned.1.call-done.refs_0_ = bf16[512,1024]{1,0:T(8,128)(2,1)} async-done(((bf16[2048,1024]{1,0:T(8,128)(2,1)}), bf16[512,1024]{1,0:T(8,128)(2,1)}) %reduce-scatter.4.cloned.1.call-update) | async-done | bytes 1048592 | tf_op jit(solution)/shard_map/reduce_scatter | solution.py:516
  478.1 13.5 %shard_map.356 = (f32[256,1024]{1,0:T(8,128)S(1)}, bf16[3,256,1024]{2,1,0:T(8,128)(2,1)S(1)}) custom-call(s32[1]{0:T(128)} %bitcast.c, bf16[2,1024,512]{2,1,0:T(8,128)(2,1)S(1)} %copy-done.5, bf16[2,1024,512]{2,1,0:T(8,128)(2,1)} %copy-done.6, bf16[2,1024,512]{2,1,0:T(8,128)(2,1)} %copy-done.37, bf16[2,1024,512]{2,1,0:T(8,128)(2,1)} %copy-done.38, ...), custom_call_target="tpu_custom_call" | custom-call | flops 1 | bytes 1 | tf_op jit(solution)/shard_map/pallas_call | solution.py:129
  491.8 2.4 collective-permute-start.34
  495.3 12.3 %collective-permute-done.34 = bf16[256,1024]{1,0:T(8,128)(2,1)S(1)} collective-permute-done((bf16[256,1024]{1,0:T(8,128)(2,1)S(1)}, bf16[256,1024]{1,0:T(8,128)(2,1)S(1)}, u32[]{:S(2)}, u32[]{:S(2)}) %collective-permute-start.34) | collective-permute-done | bytes 524320 | tf_op jit(solution)/shard_map/ppermute | solution.py:73
  507.6 10.1 %collective-permute-done.33 = bf16[256,1024]{1,0:T(8,128)(2,1)S(1)} collective-permute-done((bf16[256,1024]{1,0:T(8,128)(2,1)S(1)}, bf16[256,1024]{1,0:T(8,128)(2,1)S(1)}, u32[]{:S(2)}, u32[]{:S(2)}) %collective-permute-start.33) | collective-permute-done | bytes 524320 | tf_op jit(solution)/shard_map/ppermute | solution.py:73
  528.6 12.2 %collective-permute-done.38 = bf16[256,1024]{1,0:T(8,128)(2,1)S(1)} collective-permute-done((bf16[256,1024]{1,0:T(8,128)(2,1)S(1)}, bf16[256,1024]{1,0:T(8,128)(2,1)S(1)}, u32[]{:S(2)}, u32[]{:S(2)}) %collective-permute-start.38) | collective-permute-done | bytes 524320 | tf_op jit(solution)/shard_map/ppermute | solution.py:73
  540.8 10.4 %collective-permute-done.37 = bf16[256,1024]{1,0:T(8,128)(2,1)S(1)} collective-permute-done((bf16[256,1024]{1,0:T(8,128)(2,1)S(1)}, bf16[256,1024]{1,0:T(8,128)(2,1)S(1)}, u32[]{:S(2)}, u32[]{:S(2)}) %collective-permute-start.37) | collective-permute-done | bytes 524320 | tf_op jit(solution)/shard_map/ppermute | solution.py:73
  553.7 2.7 collective-permute-done.40.theirs
  556.4 2.3 shard_map.359
  559.8 3.7 multiply_reduce_fusion.1
  578.8 3.0 concatenate.59
  581.8 2.6 multiply_reduce_fusion.3
  584.7 2.8 fusion.6
  589.1 4.2 fusion.21
  603.3 3.4 collective-permute-done.45.z.y
  606.7 10.8 %shard_map.360.refs_0_ = bf16[4,4,256,512]{3,2,1,0:T(8,128)(2,1)} custom-call(s32[1]{0:T(128)} %bitcast.c, bf16[1024,1024]{1,0:T(8,128)(2,1)} %copy-done.7, bf16[3,1024,256]{2,1,0:T(8,128)(2,1)S(1)} %pad_maximum_fusion.3.y.value, bf16[3,1024,256]{2,1,0:T(8,128)(2,1)S(1)} %collective-permute-done.45.z.y, bf16[1024,256]{1,0:T(8,128)(2,1)S(1)} %copy-done.9, ...), custom_call_target="tpu_custom_call" | custom-call | flops 1 | bytes 1 | tf_op jit(solution)/shard_map/pallas_call | solution.py:129
  617.5 4.7 copy.138.value
  626.7 2.4 collective-permute-done.50
  630.7 2.4 collective-permute-done.51
  634.4 6.5 collective-permute-done.52
  641.2 6.1 collective-permute-done.53
  649.5 5.7 shard_map.362
  655.3 2.4 collective-permute-start.48
  658.9 7.2 multiply_subtract_fusion.1
  666.1 3.3 collective-permute-done.48
  669.4 5.5 collective-permute-done.47
  677.5 7.2 %multiply_subtract_fusion = (f32[2,256,2048]{2,1,0:T(8,128)}, f32[2,256,2048]{2,1,0:T(8,128)}, f32[2,256,2048]{2,1,0:T(8,128)}, f32[2,256,2048]{2,1,0:T(8,128)}) fusion(f32[2,256,2048]{2,1,0:T(8,128)S(1)} %copy-done.23, f32[2,256,2048]{2,1,0:T(8,128)S(1)} %copy-done.53, f32[2,256,2048]{2,1,0:T(8,128)S(1)} %copy-done.54, bf16[2,256,2048]{2,1,0:T(8,128)(2,1)S(1)} %bitcast.134), kind=kLoop, calls=%fused_computation.2 | loop fusion | flops 16777216 | bytes 31457280 | tf_op jit(solution)/shard_map/sub | solution.py:69
  684.8 19.9 %reduce-scatter.8.cloned.1.call-done = bf16[1024,512]{1,0:T(8,128)(2,1)} async-done(((bf16[4096,512]{1,0:T(8,128)(2,1)}), bf16[1024,512]{1,0:T(8,128)(2,1)}) %reduce-scatter.8.cloned.1.call-update) | async-done | bytes 1048592 | tf_op jit(solution)/shard_map/reduce_scatter | solution.py:516
  706.1 5.1 multiply_subtract_fusion.2
  (360 shorter events, 131.5 us)
Async XLA Ops:
  7.2 87.3 %all-gather.4.cloned.1.call-start = ((), (), s32[]{:S(2)}) async-start(), calls=%async_computation.3 | async-start | bytes 5242880 | tf_op jit(solution)/shard_map/all_gather | solution.py:512
  10.9 234.0 %all-gather.6.cloned.1.call-start = ((), (), s32[]{:S(2)}) async-start(), calls=%async_computation.4 | async-start | bytes 10485760 | tf_op jit(solution)/shard_map/all_gather | solution.py:512
  14.8 311.2 %all-gather.8.cloned.1.call-start = ((), (), s32[]{:S(2)}) async-start(), calls=%async_computation.5 | async-start | bytes 5242880 | tf_op jit(solution)/shard_map/all_gather | solution.py:512
  15.8 15.8 %collective-permute-start = (bf16[256,1024]{1,0:T(8,128)(2,1)S(1)}, bf16[256,1024]{1,0:T(8,128)(2,1)}, u32[]{:S(2)}, u32[]{:S(2)}) collective-permute-start(bf16[256,1024]{1,0:T(8,128)(2,1)S(1)} %copy-done.46), channel_id=1, source_target_pairs={{0,2},{2,0},{4,6},{6,4},{1,3},{3,1},{5,7},{7,5},{8,10},{10,8},{12,... | collective-permute-start | bytes 1572872 | tf_op jit(solution)/shard_map/ppermute | solution.py:73
  18.8 24.7 %collective-permute-start.1 = (bf16[256,1024]{1,0:T(8,128)(2,1)S(1)}, bf16[256,1024]{1,0:T(8,128)(2,1)}, u32[]{:S(2)}, u32[]{:S(2)}) collective-permute-start(bf16[256,1024]{1,0:T(8,128)(2,1)S(1)} %copy-done.46), channel_id=1, source_target_pairs={{0,4},{2,6},{4,0},{6,2},{1,5},{3,7},{5,1},{7,3},{8,12},{10,14},{12... | collective-permute-start | bytes 1572872 | tf_op jit(solution)/shard_map/ppermute | solution.py:73
  20.3 24.3 %collective-permute-start.2 = (bf16[256,1024]{1,0:T(8,128)(2,1)S(1)}, bf16[256,1024]{1,0:T(8,128)(2,1)S(1)}, u32[]{:S(2)}, u32[]{:S(2)}) collective-permute-start(bf16[256,1024]{1,0:T(8,128)(2,1)S(1)} %copy-done.46), channel_id=1, source_target_pairs={{0,6},{2,4},{4,2},{6,0},{1,7},{3,5},{5,3},{7,1},{8,14},{10,12},{12... | collective-permute-start | bytes 1572872 | tf_op jit(solution)/shard_map/ppermute | solution.py:73
  44.6 56.4 %copy-start.7 = (bf16[1024,1024]{1,0:T(8,128)(2,1)}, bf16[1024,1024]{1,0:T(8,128)(2,1)S(1)}, u32[]{:S(2)}) copy-start(bf16[1024,1024]{1,0:T(8,128)(2,1)S(1)} %constant_dynamic-update-slice_fusion.x) | copy-start | bytes 6291460
  102.7 8.2 %collective-permute-start.3 = (f32[3,1024,256]{2,1,0:T(8,128)}, f32[3,1024,256]{2,1,0:T(8,128)}, u32[]{:S(2)}, u32[]{:S(2)}) collective-permute-start(f32[3,1024,256]{2,1,0:T(8,128)} %get-tuple-element.37), channel_id=1, source_target_pairs={{0,1},{1,0},{2,3},{3,2},{4,5},{5,4},{6,7},{7,6},{8,9},{9,8},{10,11... | collective-permute-start | bytes 9437192 | tf_op jit(solution)/shard_map/ppermute | solution.py:73
  103.8 372.7 %reduce-scatter.4.cloned.1.call-start = ((), (), s32[]{:S(2)}) async-start(), calls=%async_computation.6 | async-start | bytes 5242880 | tf_op jit(solution)/shard_map/reduce_scatter | solution.py:516
  115.2 1.4 collective-permute-start.4
  116.6 10.0 %collective-permute-start.5 = (f32[2,4,256]{2,1,0:T(4,128)S(1)}, f32[2,4,256]{2,1,0:T(4,128)S(1)}, u32[]{:S(2)}, u32[]{:S(2)}) collective-permute-start(f32[2,4,256]{2,1,0:T(4,128)S(1)} %reshape.595), channel_id=1, source_target_pairs={{0,2},{2,0},{4,6},{6,4},{1,3},{3,1},{5,7},{7,5},{8,10},{10,8},{12,... | collective-permute-start | bytes 24584 | tf_op jit(solution)/shard_map/ppermute | solution.py:73
  124.6 3.7 collective-permute-start.6
  126.1 4.5 collective-permute-start.7
  142.7 2.0 collective-permute-start.8
  148.4 28.6 %copy-start.47 = (bf16[256,1024]{1,0:T(8,128)(2,1)S(1)}, bf16[256,1024]{1,0:T(8,128)(2,1)}, u32[]{:S(2)}) copy-start(bf16[256,1024]{1,0:T(8,128)(2,1)} %param.18) | copy-start | bytes 1572868
  148.4 15.9 %collective-permute-start.11 = (bf16[256,1024]{1,0:T(8,128)(2,1)}, bf16[256,1024]{1,0:T(8,128)(2,1)S(1)}, u32[]{:S(2)}, u32[]{:S(2)}) collective-permute-start(bf16[256,1024]{1,0:T(8,128)(2,1)} %get-tuple-element.105), channel_id=1, source_target_pairs={{0,6},{2,4},{4,2},{6,0},{1,7},{3,5},{5,3},{7,1},{8,14},{10,12},{12... | collective-permute-start | bytes 1572872 | tf_op jit(solution)/shard_map/ppermute | solution.py:73
  148.9 25.1 %collective-permute-start.10 = (bf16[256,1024]{1,0:T(8,128)(2,1)}, bf16[256,1024]{1,0:T(8,128)(2,1)S(1)}, u32[]{:S(2)}, u32[]{:S(2)}) collective-permute-start(bf16[256,1024]{1,0:T(8,128)(2,1)} %get-tuple-element.106), channel_id=1, source_target_pairs={{0,4},{2,6},{4,0},{6,2},{1,5},{3,7},{5,1},{7,3},{8,12},{10,14},{12... | collective-permute-start | bytes 1572872 | tf_op jit(solution)/shard_map/ppermute | solution.py:73
  150.4 23.6 %collective-permute-start.9 = (bf16[256,1024]{1,0:T(8,128)(2,1)S(1)}, bf16[256,1024]{1,0:T(8,128)(2,1)}, u32[]{:S(2)}, u32[]{:S(2)}) collective-permute-start(bf16[256,1024]{1,0:T(8,128)(2,1)S(1)} %get-tuple-element.104), channel_id=1, source_target_pairs={{0,2},{2,0},{4,6},{6,4},{1,3},{3,1},{5,7},{7,5},{8,10},{10,8},{12,... | collective-permute-start | bytes 1572872 | tf_op jit(solution)/shard_map/ppermute | solution.py:73
  175.8 27.7 %copy-start.26 = (f32[256,1024]{1,0:T(8,128)}, f32[256,1024]{1,0:T(8,128)S(1)}, u32[]{:S(2)}) copy-start(f32[256,1024]{1,0:T(8,128)S(1)} %get-tuple-element.82) | copy-start | bytes 3145732
  175.8 1.2 collective-permute-start.12
  177.3 15.8 %collective-permute-start.15 = (bf16[256,1024]{1,0:T(8,128)(2,1)S(1)}, bf16[256,1024]{1,0:T(8,128)(2,1)S(1)}, u32[]{:S(2)}, u32[]{:S(2)}) collective-permute-start(bf16[256,1024]{1,0:T(8,128)(2,1)S(1)} %fusion.32), channel_id=1, source_target_pairs={{0,6},{2,4},{4,2},{6,0},{1,7},{3,5},{5,3},{7,1},{8,14},{10,12},{12... | collective-permute-start | bytes 1572872 | tf_op jit(solution)/shard_map/ppermute | solution.py:73
  178.8 24.7 %collective-permute-start.14 = (bf16[256,1024]{1,0:T(8,128)(2,1)S(1)}, bf16[256,1024]{1,0:T(8,128)(2,1)S(1)}, u32[]{:S(2)}, u32[]{:S(2)}) collective-permute-start(bf16[256,1024]{1,0:T(8,128)(2,1)S(1)} %fusion.32), channel_id=1, source_target_pairs={{0,4},{2,6},{4,0},{6,2},{1,5},{3,7},{5,1},{7,3},{8,12},{10,14},{12... | collective-permute-start | bytes 1572872 | tf_op jit(solution)/shard_map/ppermute | solution.py:73
  180.1 23.4 %collective-permute-start.13 = (bf16[256,1024]{1,0:T(8,128)(2,1)S(1)}, bf16[256,1024]{1,0:T(8,128)(2,1)S(1)}, u32[]{:S(2)}, u32[]{:S(2)}) collective-permute-start(bf16[256,1024]{1,0:T(8,128)(2,1)S(1)} %fusion.32), channel_id=1, source_target_pairs={{0,2},{2,0},{4,6},{6,4},{1,3},{3,1},{5,7},{7,5},{8,10},{10,8},{12,... | collective-permute-start | bytes 1572872 | tf_op jit(solution)/shard_map/ppermute | solution.py:73
  248.6 4.4 collective-permute-start.16
  252.5 5.9 collective-permute-start.17
  258.3 67.8 %collective-permute-start.18 = (bf16[1024,512]{1,0:T(8,128)(2,1)S(1)}, bf16[1024,512]{1,0:T(8,128)(2,1)}, u32[]{:S(2)}, u32[]{:S(2)}) collective-permute-start(bf16[1024,512]{1,0:T(8,128)(2,1)S(1)} %get-tuple-element.40.x0), channel_id=1, source_target_pairs={{0,1},{1,0},{2,3},{3,2},{4,5},{5,4},{6,7},{7,6},{8,9},{9,8},{10,11... | collective-permute-start | bytes 3145736 | tf_op jit(solution)/shard_map/ppermute | solution.py:73
  263.7 62.4 %collective-permute-start.19 = (bf16[1024,512]{1,0:T(8,128)(2,1)}, bf16[1024,512]{1,0:T(8,128)(2,1)}, u32[]{:S(2)}, u32[]{:S(2)}) collective-permute-start(bf16[1024,512]{1,0:T(8,128)(2,1)} %get-tuple-element.41.x1), channel_id=1, source_target_pairs={{0,1},{1,0},{2,3},{3,2},{4,5},{5,4},{6,7},{7,6},{8,9},{9,8},{10,11... | collective-permute-start | bytes 3145736 | tf_op jit(solution)/shard_map/ppermute | solution.py:73
  335.7 27.5 %copy-start.28 = (bf16[256,1024]{1,0:T(8,128)(2,1)S(1)}, bf16[256,1024]{1,0:T(8,128)(2,1)}, u32[]{:S(2)}) copy-start(bf16[256,1024]{1,0:T(8,128)(2,1)} %param.19) | copy-start | bytes 1572868
  335.7 15.8 %collective-permute-start.22 = (bf16[256,1024]{1,0:T(8,128)(2,1)S(1)}, bf16[256,1024]{1,0:T(8,128)(2,1)S(1)}, u32[]{:S(2)}, u32[]{:S(2)}) collective-permute-start(bf16[256,1024]{1,0:T(8,128)(2,1)S(1)} %get-tuple-element.102), channel_id=1, source_target_pairs={{0,6},{2,4},{4,2},{6,0},{1,7},{3,5},{5,3},{7,1},{8,14},{10,12},{12... | collective-permute-start | bytes 1572872 | tf_op jit(solution)/shard_map/ppermute | solution.py:73
  338.2 23.4 %collective-permute-start.21 = (bf16[256,1024]{1,0:T(8,128)(2,1)S(1)}, bf16[256,1024]{1,0:T(8,128)(2,1)S(1)}, u32[]{:S(2)}, u32[]{:S(2)}) collective-permute-start(bf16[256,1024]{1,0:T(8,128)(2,1)S(1)} %get-tuple-element.103), channel_id=1, source_target_pairs={{0,4},{2,6},{4,0},{6,2},{1,5},{3,7},{5,1},{7,3},{8,12},{10,14},{12... | collective-permute-start | bytes 1572872 | tf_op jit(solution)/shard_map/ppermute | solution.py:73
  338.7 22.9 %collective-permute-start.20 = (bf16[256,1024]{1,0:T(8,128)(2,1)S(1)}, bf16[256,1024]{1,0:T(8,128)(2,1)S(1)}, u32[]{:S(2)}, u32[]{:S(2)}) collective-permute-start(bf16[256,1024]{1,0:T(8,128)(2,1)S(1)} %get-tuple-element.101), channel_id=1, source_target_pairs={{0,2},{2,0},{4,6},{6,4},{1,3},{3,1},{5,7},{7,5},{8,10},{10,8},{12,... | collective-permute-start | bytes 1572872 | tf_op jit(solution)/shard_map/ppermute | solution.py:73
  362.0 1.2 collective-permute-start.23
  363.7 1.2 collective-permute-start.24
  365.2 15.8 %collective-permute-start.27 = (bf16[256,1024]{1,0:T(8,128)(2,1)S(1)}, bf16[256,1024]{1,0:T(8,128)(2,1)S(1)}, u32[]{:S(2)}, u32[]{:S(2)}) collective-permute-start(bf16[256,1024]{1,0:T(8,128)(2,1)S(1)} %multiply_convert_fusion.5), channel_id=1, source_target_pairs={{0,6},{2,4},{4,2},{6,0},{1,7},{3,5},{5,3},{7,1},{8,14},{10,12},{12... | collective-permute-start | bytes 1572872 | tf_op jit(solution)/shard_map/ppermute | solution.py:73
  367.0 24.5 %collective-permute-start.26 = (bf16[256,1024]{1,0:T(8,128)(2,1)S(1)}, bf16[256,1024]{1,0:T(8,128)(2,1)S(1)}, u32[]{:S(2)}, u32[]{:S(2)}) collective-permute-start(bf16[256,1024]{1,0:T(8,128)(2,1)S(1)} %multiply_convert_fusion.5), channel_id=1, source_target_pairs={{0,4},{2,6},{4,0},{6,2},{1,5},{3,7},{5,1},{7,3},{8,12},{10,14},{12... | collective-permute-start | bytes 1572872 | tf_op jit(solution)/shard_map/ppermute | solution.py:73
  368.3 23.2 %collective-permute-start.25 = (bf16[256,1024]{1,0:T(8,128)(2,1)S(1)}, bf16[256,1024]{1,0:T(8,128)(2,1)S(1)}, u32[]{:S(2)}, u32[]{:S(2)}) collective-permute-start(bf16[256,1024]{1,0:T(8,128)(2,1)S(1)} %multiply_convert_fusion.5), channel_id=1, source_target_pairs={{0,2},{2,0},{4,6},{6,4},{1,3},{3,1},{5,7},{7,5},{8,10},{10,8},{12,... | collective-permute-start | bytes 1572872 | tf_op jit(solution)/shard_map/ppermute | solution.py:73
  401.8 222.1 %reduce-scatter.6.cloned.1.call-start = ((), (), s32[]{:S(2)}) async-start(), calls=%async_computation.7 | async-start | bytes 10485760 | tf_op jit(solution)/shard_map/reduce_scatter | solution.py:516
  401.8 4.6 collective-permute-start.28
  405.0 4.6 collective-permute-start.29
  417.2 7.1 collective-permute-start.30
  423.7 4.3 collective-permute-start.31
  476.5 228.1 %reduce-scatter.8.cloned.1.call-start = ((), (), s32[]{:S(2)}) async-start(), calls=%async_computation.8 | async-start | bytes 5242880 | tf_op jit(solution)/shard_map/reduce_scatter | solution.py:516
  491.8 15.8 %collective-permute-start.34 = (bf16[256,1024]{1,0:T(8,128)(2,1)S(1)}, bf16[256,1024]{1,0:T(8,128)(2,1)S(1)}, u32[]{:S(2)}, u32[]{:S(2)}) collective-permute-start(bf16[256,1024]{1,0:T(8,128)(2,1)S(1)} %get-tuple-element.99), channel_id=1, source_target_pairs={{0,6},{2,4},{4,2},{6,0},{1,7},{3,5},{5,3},{7,1},{8,14},{10,12},{12... | collective-permute-start | bytes 1572872 | tf_op jit(solution)/shard_map/ppermute | solution.py:73
  494.2 23.5 %collective-permute-start.33 = (bf16[256,1024]{1,0:T(8,128)(2,1)S(1)}, bf16[256,1024]{1,0:T(8,128)(2,1)S(1)}, u32[]{:S(2)}, u32[]{:S(2)}) collective-permute-start(bf16[256,1024]{1,0:T(8,128)(2,1)S(1)} %get-tuple-element.100), channel_id=1, source_target_pairs={{0,4},{2,6},{4,0},{6,2},{1,5},{3,7},{5,1},{7,3},{8,12},{10,14},{12... | collective-permute-start | bytes 1572872 | tf_op jit(solution)/shard_map/ppermute | solution.py:73
  494.7 23.0 %collective-permute-start.32 = (bf16[256,1024]{1,0:T(8,128)(2,1)S(1)}, bf16[256,1024]{1,0:T(8,128)(2,1)S(1)}, u32[]{:S(2)}, u32[]{:S(2)}) collective-permute-start(bf16[256,1024]{1,0:T(8,128)(2,1)S(1)} %get-tuple-element.98), channel_id=1, source_target_pairs={{0,2},{2,0},{4,6},{6,4},{1,3},{3,1},{5,7},{7,5},{8,10},{10,8},{12,... | collective-permute-start | bytes 1572872 | tf_op jit(solution)/shard_map/ppermute | solution.py:73
  522.3 1.2 collective-permute-start.35
  525.1 15.7 %collective-permute-start.38 = (bf16[256,1024]{1,0:T(8,128)(2,1)S(1)}, bf16[256,1024]{1,0:T(8,128)(2,1)S(1)}, u32[]{:S(2)}, u32[]{:S(2)}) collective-permute-start(bf16[256,1024]{1,0:T(8,128)(2,1)S(1)} %get-tuple-element.107), channel_id=1, source_target_pairs={{0,6},{2,4},{4,2},{6,0},{1,7},{3,5},{5,3},{7,1},{8,14},{10,12},{12... | collective-permute-start | bytes 1572872 | tf_op jit(solution)/shard_map/ppermute | solution.py:73
  526.8 24.5 %collective-permute-start.37 = (bf16[256,1024]{1,0:T(8,128)(2,1)S(1)}, bf16[256,1024]{1,0:T(8,128)(2,1)S(1)}, u32[]{:S(2)}, u32[]{:S(2)}) collective-permute-start(bf16[256,1024]{1,0:T(8,128)(2,1)S(1)} %get-tuple-element.107), channel_id=1, source_target_pairs={{0,4},{2,6},{4,0},{6,2},{1,5},{3,7},{5,1},{7,3},{8,12},{10,14},{12... | collective-permute-start | bytes 1572872 | tf_op jit(solution)/shard_map/ppermute | solution.py:73
  528.0 23.3 %collective-permute-start.36 = (bf16[256,1024]{1,0:T(8,128)(2,1)S(1)}, bf16[256,1024]{1,0:T(8,128)(2,1)S(1)}, u32[]{:S(2)}, u32[]{:S(2)}) collective-permute-start(bf16[256,1024]{1,0:T(8,128)(2,1)S(1)} %get-tuple-element.107), channel_id=1, source_target_pairs={{0,2},{2,0},{4,6},{6,4},{1,3},{3,1},{5,7},{7,5},{8,10},{10,8},{12,... | collective-permute-start | bytes 1572872 | tf_op jit(solution)/shard_map/ppermute | solution.py:73
  551.5 5.0 collective-permute-start.39
  553.6 2.9 collective-permute-start.40
  584.4 3.2 collective-permute-start.41
  587.6 9.8 %collective-permute-start.42 = (f32[2,4,256]{2,1,0:T(4,128)S(1)}, f32[2,4,256]{2,1,0:T(4,128)S(1)}, u32[]{:S(2)}, u32[]{:S(2)}) collective-permute-start(f32[2,4,256]{2,1,0:T(4,128)S(1)} %reshape.601), channel_id=1, source_target_pairs={{0,2},{2,0},{4,6},{6,4},{1,3},{3,1},{5,7},{7,5},{8,10},{10,8},{12,... | collective-permute-start | bytes 24584 | tf_op jit(solution)/shard_map/ppermute | solution.py:73
  595.4 3.7 collective-permute-start.43
  596.2 4.5 collective-permute-start.44
  603.2 3.5 collective-permute-start.45
  623.9 1.3 collective-permute-start.49
  625.2 4.0 collective-permute-start.50
  629.2 4.0 collective-permute-start.51
  633.2 7.7 %collective-permute-start.52 = (f32[4,2048]{1,0:T(4,128)S(1)}, f32[4,2048]{1,0:T(4,128)S(1)}, u32[]{:S(2)}, u32[]{:S(2)}) collective-permute-start(f32[4,2048]{1,0:T(4,128)S(1)} %add.341), channel_id=1, source_target_pairs={{0,8},{8,0},{16,24},{24,16},{1,9},{9,1},{17,25},{25,17},{2,10},{10... | collective-permute-start | bytes 98312 | tf_op jit(solution)/shard_map/ppermute | solution.py:73
  641.0 6.3 collective-permute-start.53
  655.3 14.1 %collective-permute-start.48 = (bf16[256,1024]{1,0:T(8,128)(2,1)S(1)}, bf16[256,1024]{1,0:T(8,128)(2,1)S(1)}, u32[]{:S(2)}, u32[]{:S(2)}) collective-permute-start(bf16[256,1024]{1,0:T(8,128)(2,1)S(1)} %get-tuple-element.96), channel_id=1, source_target_pairs={{0,6},{2,4},{4,2},{6,0},{1,7},{3,5},{5,3},{7,1},{8,14},{10,12},{12... | collective-permute-start | bytes 1572872 | tf_op jit(solution)/shard_map/ppermute | solution.py:73
  657.7 17.1 %collective-permute-start.47 = (bf16[256,1024]{1,0:T(8,128)(2,1)S(1)}, bf16[256,1024]{1,0:T(8,128)(2,1)S(1)}, u32[]{:S(2)}, u32[]{:S(2)}) collective-permute-start(bf16[256,1024]{1,0:T(8,128)(2,1)S(1)} %get-tuple-element.97), channel_id=1, source_target_pairs={{0,4},{2,6},{4,0},{6,2},{1,5},{3,7},{5,1},{7,3},{8,12},{10,14},{12... | collective-permute-start | bytes 1572872 | tf_op jit(solution)/shard_map/ppermute | solution.py:73
  658.3 16.6 %collective-permute-start.46 = (bf16[256,1024]{1,0:T(8,128)(2,1)S(1)}, bf16[256,1024]{1,0:T(8,128)(2,1)S(1)}, u32[]{:S(2)}, u32[]{:S(2)}) collective-permute-start(bf16[256,1024]{1,0:T(8,128)(2,1)S(1)} %get-tuple-element.95), channel_id=1, source_target_pairs={{0,2},{2,0},{4,6},{6,4},{1,3},{3,1},{5,7},{7,5},{8,10},{10,8},{12,... | collective-permute-start | bytes 1572872 | tf_op jit(solution)/shard_map/ppermute | solution.py:73
  (68 other events, 363.6 us)
Sparse Core Ops, SparseCore 0:
  11.0 83.4 all-gather.3
  96.7 148.1 all-gather.5
  247.0 78.9 all-gather.7
  401.9 74.5 reduce-scatter.3
  478.8 144.9 reduce-scatter.5
  626.1 78.5 reduce-scatter.7

commit v3 on v2

--- a/solution.py
+++ b/solution.py
@@ -102,8 +102,14 @@
 
 
 def gather_rows(block):
+    count = lax.axis_size("row")
+    if count != 4:
+        return jnp.concatenate([block] + [swap(block, "row", k) for k in range(1, count)], 0)
+    half = block.shape[0] // 2
+    first = swap(block, "row", 1)
+    second = swap(block, "row", 2)
     return jnp.concatenate(
-        [block] + [swap(block, "row", k) for k in range(1, lax.axis_size("row"))], 0
+        [block, first, second, swap(first[:half], "row", 2), swap(second[half:], "row", 1)], 0
     )
 
 
@@ -115,6 +121,7 @@
 
 VMEM = 48 * 1024 * 1024
 TILE = 256
+PART = 512
 NN = (((1,), (0,)), ((), ()))
 NT = (((1,), (1,)), ((), ()))
 TN = (((0,), (0,)), ((), ()))
@@ -124,20 +131,25 @@
     return lax.dot_general(left, right, dims, preferred_element_type=jnp.float32)
 
 
-def run(body, grid, ins, outs):
+def run(body, grid, ins, outs, earlier=()):
     place = lax.axis_index("col").astype(jnp.int32).reshape(1)
+
+    def kernel(c, *refs):
+        body(c, *refs[: len(ins)], *refs[len(ins) + len(earlier) :])
+
     return pl.pallas_call(
-        body,
+        kernel,
         grid_spec=pltpu.PrefetchScalarGridSpec(
             num_scalar_prefetch=1,
             grid=grid,
-            in_specs=[pl.BlockSpec(block, where) for _, block, where in ins],
+            in_specs=[pl.BlockSpec(block, where) for _, block, where in ins]
+            + [pl.BlockSpec(memory_space=pl.ANY)] * len(earlier),
             out_specs=[pl.BlockSpec(block, where) for _, _, block, where in outs],
         ),
         out_shape=[jax.ShapeDtypeStruct(shape, kind) for shape, kind, _, _ in outs],
         compiler_params=pltpu.CompilerParams(vmem_limit_bytes=VMEM),
         cost_estimate=pl.CostEstimate(flops=1, bytes_accessed=1, transcendentals=0),
-    )(place, *[array for array, _, _ in ins])
+    )(place, *[array for array, _, _ in ins], *earlier)
 
 
 def whole(array):
@@ -158,6 +170,20 @@
         input_output_aliases={0: 0},
         cost_estimate=pl.CostEstimate(flops=1, bytes_accessed=1, transcendentals=0),
     )(value, *earlier)
+
+
+def ring_gather(shards):
+    count = lax.axis_size("dp")
+    rows = shards[0].shape[0]
+    joined = jnp.zeros((count, len(shards)) + shards[0].shape, shards[0].dtype)
+    pairs = [(i, (i - 1) % count) for i in range(count)]
+    for step in range(count):
+        spot = lax.rem(lax.axis_index("dp") + step, count)
+        if step:
+            shards = [lax.ppermute(shard, "dp", pairs) for shard in shards]
+        for j, shard in enumerate(shards):
+            joined = lax.dynamic_update_slice(joined, shard[None, None], (spot, j, 0, 0))
+    return joined.reshape((count, len(shards) * rows) + joined.shape[3:])
 
 
 def row_outs(extent, columns, tile):
@@ -261,30 +287,35 @@
     )[0]
 
 
+def piece_order(pieces):
+    half = pieces // 2
+    return lambda j, c: jnp.where(j < half, c[0] * half + j, (1 - c[0]) * half + j - half)
+
+
 def widen_send(rows, block, t):
     n, _, d, width = block.shape
-    part = width // 4
+    half = width // PART // 2
     extent = rows.shape[0]
 
     def body(c, x, w, out):
-        out[0] = mm(x[...], w[...].reshape(n * d, part)).astype(jnp.bfloat16)
+        out[0] = mm(x[...], w[...].reshape(n * d, PART)).astype(jnp.bfloat16)
 
     return run(
         body,
         (2,),
         [
             whole(rows),
-            (block, (n, 1, d, part), lambda k, c: (0, k, 0, (1 - c[0]) * 2 + t)),
-        ],
-        [((2, extent, part), jnp.bfloat16, (1, extent, part), lambda k, c: (k, 0, 0))],
+            (block, (n, 1, d, PART), lambda k, c: (0, k, 0, (1 - c[0]) * half + t)),
+        ],
+        [((2, extent, PART), jnp.bfloat16, (1, extent, PART), lambda k, c: (k, 0, 0))],
     )[0]
 
 
 def widen(rows, block, arrived, t):
     n, _, d, width = block.shape
-    part = width // 4
+    half = width // PART // 2
     extent = rows.shape[0]
-    tiles = part // TILE
+    tiles = PART // TILE
 
     def body(c, x, gate, up, far, kept, out):
         g = mm(x[...], gate[...].reshape(n * d, TILE)) + far[0].astype(jnp.float32)
@@ -298,25 +329,29 @@
         (tiles,),
         [
             whole(rows),
-            (block, (n, 1, d, TILE), lambda i, c: (0, 0, 0, (c[0] * 2 + t) * tiles + i)),
-            (block, (n, 1, d, TILE), lambda i, c: (0, 1, 0, (c[0] * 2 + t) * tiles + i)),
+            (block, (n, 1, d, TILE), lambda i, c: (0, 0, 0, (c[0] * half + t) * tiles + i)),
+            (block, (n, 1, d, TILE), lambda i, c: (0, 1, 0, (c[0] * half + t) * tiles + i)),
             (arrived, (2, extent, TILE), lambda i, c: (0, 0, i)),
         ],
         [
-            ((2, extent, part), jnp.float32, (2, extent, TILE), lambda i, c: (0, 0, i)),
-            ((extent, part), jnp.bfloat16, (extent, TILE), lambda i, c: (0, i)),
-        ],
-    )
-
-
-def narrow(own, other, block):
-    pieces = block.reshape(4, block.shape[0] // 4, block.shape[1])
-    _, part, columns = pieces.shape
+            ((2, extent, PART), jnp.float32, (2, extent, TILE), lambda i, c: (0, 0, i)),
+            ((extent, PART), jnp.bfloat16, (extent, TILE), lambda i, c: (0, i)),
+        ],
+    )
+
+
+def narrow(own, other, pieces, earlier=()):
+    count, part, columns = pieces.shape
+    half = count // 2
     extent = own[0].shape[0]
 
-    def body(c, x0, x1, y0, y1, mine, theirs, out, low):
-        total = mm(x0[...], mine[0]) + mm(x1[...], mine[1])
-        total = total + mm(y0[...], theirs[0]) + mm(y1[...], theirs[1])
+    def body(c, *refs):
+        xs = refs[:count]
+        mine, theirs, out, low = refs[count:]
+        total = None
+        for j, x in enumerate(xs):
+            piece = mm(x[...], (mine if j < half else theirs)[j % half])
+            total = piece if total is None else total + piece
         put_rows(total, out, low)
 
     return run(
@@ -324,38 +359,54 @@
         (columns // TILE,),
         [whole(x) for x in own + other]
         + [
-            (pieces, (2, part, TILE), lambda n, c: (c[0], 0, n)),
-            (pieces, (2, part, TILE), lambda n, c: (1 - c[0], 0, n)),
+            (pieces, (half, part, TILE), lambda n, c: (c[0], 0, n)),
+            (pieces, (half, part, TILE), lambda n, c: (1 - c[0], 0, n)),
         ],
         row_outs(extent, columns, TILE),
-    )
-
-
-def narrow_weight(own, other, grads):
-    extent, part = own[0].shape
-    columns = grads.shape[1]
-
-    def body(c, x0, x1, y0, y1, g, out):
-        for j, x in enumerate((x0, x1, y0, y1)):
+        earlier,
+    )
+
+
+def narrow_weight(own, other, grads, earlier=()):
+    groups = len(grads)
+    half = len(own[0])
+    extent, part = own[0][0].shape
+    columns = grads[0].shape[1]
+    order = piece_order(2 * half)
+    flat = [x for j in range(2 * half) for x in ([g[j] for g in own] if j < half else [g[j - half] for g in other])]
+
+    def body(c, *refs):
+        gs = refs[len(flat) : len(flat) + groups]
+        out = refs[-1]
+        for j in range(2 * half):
 
             @pl.when(pl.program_id(0) == j)
-            def _(x=x):
-                out[...] = mm(x[...], g[...], TN).astype(jnp.bfloat16)
-
-    def where(i, c):
-        return (jnp.where(i < 2, c[0] * 2 + i, (1 - c[0]) * 2 + i - 2), 0)
-
-    return run(
-        body,
-        (4,),
-        [whole(x) for x in own + other] + [whole(grads)],
-        [((4 * part, columns), jnp.bfloat16, (part, columns), where)],
+            def _(j=j):
+                total = None
+                for g in range(groups):
+                    piece = mm(refs[j * groups + g][...], gs[g][...], TN)
+                    total = piece if total is None else total + piece
+                out[0] = total.astype(jnp.bfloat16)
+
+    return run(
+        body,
+        (2 * half,),
+        [whole(x) for x in flat] + [whole(g) for g in grads],
+        [
+            (
+                (2 * half, part, columns),
+                jnp.bfloat16,
+                (1, part, columns),
+                lambda i, c: (order(i, c), 0, 0),
+            )
+        ],
+        earlier,
     )[0]
 
 
-def narrow_back(own, other, block, far, kept, t):
-    pieces = block.reshape(4, block.shape[0] // 4, block.shape[1])
-    _, part, columns = pieces.shape
+def narrow_back(own, other, pieces, far, kept, t, earlier=()):
+    count, part, columns = pieces.shape
+    half = count // 2
     extent = own.shape[0]
     tiles = part // TILE
 
@@ -372,71 +423,85 @@
         [
             whole(own),
             whole(other),
-            (pieces, (1, TILE, columns), lambda i, c: (c[0] * 2 + t, i, 0)),
+            (pieces, (1, TILE, columns), lambda i, c: (c[0] * half + t, i, 0)),
             (far, (1, TILE, columns), lambda i, c: (t, i, 0)),
             (kept, (2, extent, TILE), lambda i, c: (0, 0, i)),
         ],
         [((2, extent, part), jnp.bfloat16, (2, extent, TILE), lambda i, c: (0, 0, i))],
+        earlier,
     )[0]
 
 
-def widen_back(own, other, block):
+def widen_back(own, other, block, earlier=()):
     n, _, d, width = block.shape
-    part = width // 4
+    count = width // PART
     extent = own[0].shape[1]
     group = TILE // d
-
-    def body(c, x0, x1, y0, y1, w0, w1, v0, v1, out, low):
+    order = piece_order(count)
+
+    def body(c, *refs):
+        out, low = refs[2 * count :]
         total = None
-        for x, w in ((x0, w0), (x1, w1), (y0, v0), (y1, v1)):
+        for x, w in zip(refs[:count], refs[count : 2 * count]):
             for k in range(2):
-                piece = mm(x[k], w[:, k].reshape(TILE, part), NT)
+                piece = mm(x[k], w[:, k].reshape(TILE, PART), NT)
                 total = piece if total is None else total + piece
         put_rows(total, out, low)
 
-    shape = (group, 2, d, part)
     return run(
         body,
         (n * d // TILE,),
         [whole(x) for x in own + other]
         + [
-            (block, shape, lambda i, c: (i, 0, 0, c[0] * 2)),
-            (block, shape, lambda i, c: (i, 0, 0, c[0] * 2 + 1)),
-            (block, shape, lambda i, c: (i, 0, 0, 2 - c[0] * 2)),
-            (block, shape, lambda i, c: (i, 0, 0, 3 - c[0] * 2)),
+            (block, (group, 2, d, PART), lambda i, c, j=j: (i, 0, 0, order(j, c)))
+            for j in range(count)
         ],
         row_outs(extent, n * d, TILE),
-    )
-
-
-def widen_weight(rows, own, other, shape):
+        earlier,
+    )
+
+
+def widen_weight(rows, own, other, shape, earlier=()):
     n, _, d, width = shape
-    extent, features = rows.shape
-    part = width // 4
+    groups = len(rows)
+    half = len(own[0])
+    extent, features = rows[0].shape
     group = TILE // d
-
-    def body(c, x, y0, y1, z0, z1, out):
-        for j, y in enumerate((y0, y1, z0, z1)):
+    order = piece_order(2 * half)
+    flat = [x for j in range(2 * half) for x in ([g[j] for g in own] if j < half else [g[j - half] for g in other])]
+
+    def body(c, *refs):
+        xs = refs[:groups]
+        ys = refs[groups:-1]
+        out = refs[-1]
+        for j in range(2 * half):
 
             @pl.when(pl.program_id(1) == j)
-            def _(y=y):
+            def _(j=j):
                 for k in range(2):
-                    out[:, k] = (
-                        mm(x[...], y[k], TN).astype(jnp.bfloat16).reshape(group, d, part)
-                    )
-
-    def where(i, j, c):
-        return (i, 0, 0, jnp.where(j < 2, c[0] * 2 + j, (1 - c[0]) * 2 + j - 2))
-
-    return run(
-        body,
-        (features // TILE, 4),
-        [(rows, (extent, TILE), lambda i, j, c: (0, i))] + [whole(y) for y in own + other],
-        [(shape, jnp.bfloat16, (group, 2, d, part), where)],
+                    total = None
+                    for g in range(groups):
+                        piece = mm(xs[g][...], ys[j * groups + g][k], TN)
+                        total = piece if total is None else total + piece
+                    out[:, k] = total.astype(jnp.bfloat16).reshape(group, d, PART)
+
+    return run(
+        body,
+        (features // TILE, 2 * half),
+        [(x, (extent, TILE), lambda i, j, c: (0, i)) for x in rows] + [whole(y) for y in flat],
+        [
+            (
+                shape,
+                jnp.bfloat16,
+                (group, 2, d, PART),
+                lambda i, j, c: (i, 0, 0, order(j, c)),
+            )
+        ],
+        earlier,
     )[0]
 
 
-def project_back(own, other, block):
+def project_back(own, other, block, earlier):
     n, _, d, width = block.shape
     half = width // 2
     extent = own.shape[1]
@@ -460,6 +525,7 @@
             (block, (group, 4, d, half), lambda i, c: (i, 0, 0, 1 - c[0])),
         ],
         row_outs(extent, n * d, TILE),
+        earlier,
     )
 
 
@@ -514,6 +580,65 @@
 
 def scatter_shards(values):
     return lax.psum_scatter(values, "dp", scatter_dimension=0, tiled=True)
+
+
+def adam_values(weight, gradient, moment, square, step_rate):
+    moment_new, square_new, updated = adam_step(
+        weight, gradient, moment, square, step_rate, WEIGHT_DECAY
+    )
+    return (gradient, moment_new, square_new, updated)
+
+
+def adam_call(body, grid, gradients, state, block, where):
+    return run(
+        body,
+        grid,
+        gradients + [(array, block, where) for array in state],
+        [(state[0].shape, jnp.float32, block, where)] * 4,
+    )
+
+
+def adam_rows(gradient, first, blocks, state, step_rate):
+    d = state[0].shape[-2] // (blocks if state[0].ndim == 2 else 1)
+    width = state[0].shape[-1]
+    lead = (1,) * (state[0].ndim - 2)
+
+    def body(c, g, weight, moment, square, *outs):
+        value = g[...].astype(jnp.float32).reshape(weight.shape)
+        for out, result in zip(
+            outs, adam_values(weight[...], value, moment[...], square[...], step_rate)
+        ):
+            out[...] = result
+
+    return adam_call(
+        body,
+        (blocks,),
+        [(gradient, (d, width), lambda k, c: (first + k, 0))],
+        state,
+        lead + (d, width),
+        (lambda k, c: (k, 0, 0)) if lead else (lambda k, c: (k, 0)),
+    )
+
+
+def adam_halves(gradient, first, state, step_rate):
+    rows, width = state[0].shape
+    block = (rows, width // 2)
+
+    def body(c, g, weight, moment, square, *outs):
+        value = g[...].astype(jnp.float32)
+        for out, result in zip(
+            outs, adam_values(weight[...], value, moment[...], square[...], step_rate)
+        ):
+            out[...] = result
+
+    return adam_call(
+        body,
+        (2,),
+        [(gradient, block, lambda k, c: (first + k, 0))],
+        state,
+        block,
+        lambda k, c: (0, k),
+    )
 
 
 def on_device(
@@ -549,10 +674,21 @@
         ],
         0,
     )
-    entry_block = gather_shards(entry_shard).reshape(shards, 4, depth, grid_width)
-    expand_shard = expand_weight.astype(low).reshape(-1, expand_weight.shape[2])
-    expand_block = gather_shards(expand_shard).reshape((shards,) + expand_weight.shape)
-    reduce_block = gather_shards(reduce_weight.astype(low))
+    if shards > 4:
+        entry_block = gather_shards(entry_shard)
+    else:
+        entry_block = ring_gather([entry_shard[: 2 * depth], entry_shard[2 * depth :]])
+    entry_block = entry_block.reshape(shards, 4, depth, grid_width)
+    reduce_low = reduce_weight.astype(low)
+    expand_low = expand_weight.astype(low)
+    expand_block = gather_shards(
+        tie(expand_low, entry_block).reshape(-1, expand_low.shape[2])
+    ).reshape(
+        (shards,) + expand_weight.shape
+    )
+    reduce_pieces = gather_shards(reduce_low).reshape(4, -1, reduce_low.shape[1])
+    halves = range(2)
+
     row_size = lax.axis_size("row")
     col_size = lax.axis_size("col")
     local_rows = tokens.shape[0]
@@ -624,42 +760,49 @@
     branch_hat = branch * branch_scale
     hidden = inputs + branch_hat * post_gain[0]
     hidden_rows = gather_rows(hidden.astype(jnp.bfloat16))
-    sent = [widen_send(hidden_rows, expand_block, t) for t in range(2)]
-    kept, product = zip(
-        *[widen(hidden_rows, expand_block, swap_col(sent[t]), t) for t in range(2)]
-    )
+    sent = [swap_col(widen_send(hidden_rows, expand_block, t)) for t in halves]
+    kept, product = zip(*[widen(hidden_rows, expand_block, sent[t], t) for t in halves])
     product = list(product)
     product_other = [swap_col(value) for value in product]
-    second = scatter_rows(*narrow(product, product_other, reduce_block))
-    second_scale = lax.rsqrt(feature_total(jnp.sum(second * second, -1)) / D + NORM_EPSILON)[
-        :, None
-    ]
+    second = scatter_rows(*narrow(product, product_other, reduce_pieces))
+    upstream = cotangent.astype(jnp.float32) * local_valid[:, None]
+    scaled = upstream * post_gain[1]
+    totals = feature_total(
+        jnp.stack([jnp.sum(second * second, -1), jnp.sum(scaled * second, -1)])
+    )
+    second_scale = lax.rsqrt(totals[0] / D + NORM_EPSILON)[:, None]
     second_hat = second * second_scale
     layer_output = hidden + second_hat * post_gain[1]
-    upstream = cotangent.astype(jnp.float32) * local_valid[:, None]
     gain_second_post = jnp.sum(upstream * second_hat, 0)
-    scaled = upstream * post_gain[1]
-    inner_sum = feature_total(jnp.sum(scaled * second_hat, -1))
-    second_grad = (second_scale * (scaled - second_hat * inner_sum[:, None] / D)).astype(
-        jnp.bfloat16
-    )
+    inner_sum = totals[1][:, None] * second_scale
+    second_grad = (second_scale * (scaled - second_hat * inner_sum / D)).astype(jnp.bfloat16)
     second_rows = gather_rows(second_grad)
-    reduce_sum = narrow_weight(product, product_other, second_rows)
-    reduce_grad = scatter_shards(reduce_sum)
     second_other = swap_col(second_rows)
-    reduce_pieces = reduce_block.reshape(4, -1, reduce_block.shape[1])
+    reduce_sum = narrow_weight([product], [product_other], [second_rows])
     reduce_far = swap_col(take_half(reduce_pieces, 0, 1 - side))
     gated_grad = [
-        narrow_back(tie(second_rows, reduce_sum), second_other, reduce_block, reduce_far, kept[t], t)
-        for t in range(2)
+        narrow_back(
+            second_rows, second_other, reduce_pieces, reduce_far, kept[t], t, [reduce_sum]
+        )
+        for t in halves
     ]
     gated_other = [swap_col(value) for value in gated_grad]
-    hidden_back = scatter_rows(*widen_back(gated_grad, gated_other, expand_block))
-    expand_sum = widen_weight(hidden_rows, gated_grad, gated_other, expand_block.shape)
+    hidden_parts = widen_back(gated_grad, gated_other, expand_block)
+    hidden_back = scatter_rows(*hidden_parts)
+    expand_sum = widen_weight(
+        [hidden_rows], [gated_grad], [gated_other], expand_block.shape, [hidden_parts[1]]
+    )
+    rate = 2.0 * D ** (-0.5)
+    reduce_grad = scatter_shards(reduce_sum.reshape(-1, reduce_low.shape[1]))
     expand_grad = scatter_shards(
-        tie(expand_sum, reduce_grad).reshape(-1, expand_block.shape[3])
-    ).reshape(expand_weight.shape)
-    hidden_back = tie(hidden_back, expand_sum)
+        tie(expand_sum, reduce_grad).reshape(-1, expand_low.shape[2])
+    )
+    reduce_outs = adam_rows(
+        reduce_grad, 0, 2, [reduce_weight, reduce_mean, reduce_square], 2.0 * FF ** (-0.5)
+    )
+    expand_outs = adam_rows(
+        expand_grad, 0, 2, [expand_weight, expand_mean, expand_square], rate
+    )
     hidden_grad = upstream + hidden_back
     gain_first_post = jnp.sum(hidden_grad * branch_hat, 0)
     scaled = hidden_grad * post_gain[0]
@@ -729,19 +872,18 @@
         branch_rows,
         entry_block.shape,
     )
-    entry_out = scatter_shards(tie(entry_sum, expand_grad).reshape(-1, grid_width)).astype(
-        jnp.float32
+    entry_out = scatter_shards(tie(entry_sum, expand_grad).reshape(-1, grid_width))
+    entry_outs = adam_rows(entry_out, 0, 3, [entry_weight, entry_mean, entry_square], rate)
+    mixer_outs = adam_halves(
+        entry_out,
+        3 * depth // mixer_rows,
+        [mixer_weight, mixer_mean, mixer_square],
+        rate,
     )
     entry_back = scatter_rows(
-        *project_back(tie(projected_grad, entry_sum), projected_other, entry_block)
+        *project_back(projected_grad, projected_other, entry_block, [])
     )
     input_grad = hidden_grad + entry_back
-    entry_grad = entry_out[: 3 * depth].reshape(entry_weight.shape)
-    mixer_grad = jnp.concatenate(
-        [entry_out[3 * depth : 3 * depth + mixer_rows], entry_out[3 * depth + mixer_rows :]], 1
-    )
-    expand_grad = expand_grad.astype(jnp.float32)
-    reduce_grad = reduce_grad.astype(jnp.float32)
     gain_local = jnp.zeros((4, D), jnp.float32)
     gain_local = lax.dynamic_update_slice(
         gain_local, jnp.stack([gain_first_post, gain_second_post]), (0, col_start)
@@ -752,18 +894,6 @@
     gain_grad = mesh_total(gain_local)
     gain_momentum, gain_variance, gain_updated = adam_step(
         gains, gain_grad, gain_mean, gain_square, 1.0, 0.0
-    )
-    entry_momentum, entry_variance, entry_updated = adam_step(
-        entry_weight, entry_grad, entry_mean, entry_square, 2.0 * D ** (-0.5), WEIGHT_DECAY
-    )
-    mixer_momentum, mixer_variance, mixer_updated = adam_step(
-        mixer_weight, mixer_grad, mixer_mean, mixer_square, 2.0 * D ** (-0.5), WEIGHT_DECAY
-    )
-    expand_momentum, expand_variance, expand_updated = adam_step(
-        expand_weight, expand_grad, expand_mean, expand_square, 2.0 * D ** (-0.5), WEIGHT_DECAY
-    )
-    reduce_momentum, reduce_variance, reduce_updated = adam_step(
-        reduce_weight, reduce_grad, reduce_mean, reduce_square, 2.0 * FF ** (-0.5), WEIGHT_DECAY
     )
     return (
         layer_output,
@@ -772,22 +902,10 @@
         gain_momentum,
         gain_variance,
         gain_updated,
-        entry_grad,
-        entry_momentum,
-        entry_variance,
-        entry_updated,
-        mixer_grad,
-        mixer_momentum,
-        mixer_variance,
-        mixer_updated,
-        expand_grad,
-        expand_momentum,
-        expand_variance,
-        expand_updated,
-        reduce_grad,
-        reduce_momentum,
-        reduce_variance,
-        reduce_updated,
+        *entry_outs,
+        *mixer_outs,
+        *expand_outs,
+        *reduce_outs,
     )
 
 

time: 725 us -> 709 us (0.978)
  waiting for transfers between devices: 409 us -> 376 us
  starting transfers between devices: 45.8 us -> 73.5 us
  other arithmetic: 62.6 us -> 36.2 us
  Pallas kernels: 105 us -> 127 us
    all_gather x3 -> x2, waiting for transfers between devices: 153 us -> 85.5 us  [gather_shards(): return lax.all_gather(shard, 'dp', axis=0, tiled=True)]
    ppermute x0 -> x6, waiting for transfers between devices: none -> 37.7 us  [ring_gather(): shards = [lax.ppermute(shard, 'dp', pairs) for shard in shards]]
    ppermute x54 -> x57, waiting for transfers between devices: 213 us -> 179 us  [swap(): lax.ppermute(values, axis, [(i, i ^ distance) for i in range(lax.axis_siz...]
    reduce_scatter x3, waiting for transfers between devices: 43.6 us -> 73.4 us  [scatter_shards(): return lax.psum_scatter(values, 'dp', scatter_dimension=0, tiled=True)]
    ppermute x0 -> x6, starting transfers between devices: none -> 22.7 us  [ring_gather(): shards = [lax.ppermute(shard, 'dp', pairs) for shard in shards]]
    pallas_call x15 -> x19, Pallas kernels: 105 us -> 127 us  [run(): pl.pallas_call(kernel, grid_spec=pltpu.PrefetchScalarGridSpec(num_scalar_...]
    sub x5 -> x1, other arithmetic: 21.6 us -> 0.69 us  [adam_step(): weight - step_rate * (ratio + decay_rate * weight)]
    unnamed x158 -> x166, local copies, waits for them, and re-layouts: 33.9 us -> 19.8 us
  transfers between devices with their start and end apart: 60 -> 68, of which waited for: 45 -> 48; matrix products, arithmetic and copies ran while one was open for 15% -> 13% of each run, Pallas kernels for 12% -> 15%
where the time goes in v3:
time: 709 us; the launch traced here: 704 us
  waiting for transfers between devices  376 us (53%)
  Pallas kernels  127 us (18%)
  starting transfers between devices  73.5 us (10%)
  local copies, waits for them, and re-layouts  54.4 us (8%)
  other arithmetic  36.2 us (5%)
  matrix products  21.3 us (3%)
  between operations  15.6 us (2%)
    ppermute x57, waiting for transfers between devices, swap(): lax.ppermute(values, axis, [(i, i ^ distance) for i in range(lax.axis_siz...  179 us
    pallas_call x19, Pallas kernels, run(): pl.pallas_call(kernel, grid_spec=pltpu.PrefetchScalarGridSpec(num_scalar_...  127 us
    all_gather x2, waiting for transfers between devices, gather_shards(): return lax.all_gather(shard, 'dp', axis=0, tiled=True)  85.5 us
    reduce_scatter x3, waiting for transfers between devices, scatter_shards(): return lax.psum_scatter(values, 'dp', scatter_dimension=0, tiled=True)  73.4 us
    ppermute x57, starting transfers between devices, swap(): lax.ppermute(values, axis, [(i, i ^ distance) for i in range(lax.axis_siz...  50.1 us
    ppermute x6, waiting for transfers between devices, ring_gather(): shards = [lax.ppermute(shard, 'dp', pairs) for shard in shards]  37.7 us
    ppermute x6, starting transfers between devices, ring_gather(): shards = [lax.ppermute(shard, 'dp', pairs) for shard in shards]  22.7 us
    unnamed x166, local copies, waits for them, and re-layouts  19.8 us
  transfers between devices with their start and end apart: 68, of which 48 were waited for; matrix products, arithmetic and copies ran while one was open for 13% of the time, Pallas kernels for 15%

profile of v3, /device:TPU:0, one launch (start us, length us, event | category | flops | bytes accessed | tf_op | source)
XLA Modules:
  0.0 703.6 jit_solution(3798983260250418428)
XLA Ops:
  8.9 5.1 collective-permute-start.4
  14.0 2.4 broadcast_in_dim.62
  18.5 7.7 %collective-permute-done.4 = bf16[512,512]{1,0:T(8,128)(2,1)S(1)} collective-permute-done((bf16[512,512]{1,0:T(8,128)(2,1)S(1)}, bf16[512,512]{1,0:T(8,128)(2,1)S(1)}, u32[]{:S(2)}, u32[]{:S(2)}) %collective-permute-start.4) | collective-permute-done | bytes 524320 | tf_op jit(solution)/shard_map/ppermute | solution.py:183
  26.3 4.3 collective-permute-start.6
  30.6 7.0 collective-permute-done.5
  37.5 4.3 collective-permute-start.7
  41.8 3.8 convert_element_type.114.value
  48.8 4.3 collective-permute-start.8
  53.9 6.1 collective-permute-done.7
  60.0 4.3 collective-permute-start.9
  65.9 5.3 collective-permute-done.8
  72.1 9.3 %collective-permute-done.9 = bf16[512,512]{1,0:T(8,128)(2,1)S(1)} collective-permute-done((bf16[512,512]{1,0:T(8,128)(2,1)S(1)}, bf16[512,512]{1,0:T(8,128)(2,1)S(1)}, u32[]{:S(2)}, u32[]{:S(2)}) %collective-permute-start.9) | collective-permute-done | bytes 524320 | tf_op jit(solution)/shard_map/ppermute | solution.py:183
  86.2 9.8 %collective-permute-done = bf16[256,1024]{1,0:T(8,128)(2,1)S(1)} collective-permute-done((bf16[256,1024]{1,0:T(8,128)(2,1)S(1)}, bf16[256,1024]{1,0:T(8,128)(2,1)S(1)}, u32[]{:S(2)}, u32[]{:S(2)}) %collective-permute-start) | collective-permute-done | bytes 524320 | tf_op jit(solution)/shard_map/ppermute | solution.py:73
  103.3 2.4 collective-permute-done.3
  105.7 7.1 %shard_map.345 = (f32[3,1024,256]{2,1,0:T(8,128)S(1)}, f32[3,1024,256]{2,1,0:T(8,128)}) custom-call(s32[1]{0:T(128)} %bitcast.c, bf16[1024,1024]{1,0:T(8,128)(2,1)S(1)} %constant_dynamic-update-slice_fusion.refs_0_, bf16[4,4,256,512]{3,2,1,0:T(8,128)(2,1)} %bitcast.11.refs_1_.refs_2_.refs_3_.refs_0_, ...), custom_call_target="tpu_custom_call" | custom-call | flops 1 | bytes 1 | tf_op jit(solution)/shard_map/pallas_call | solution.py:140
  116.2 3.1 multiply_cosine_fusion
  122.9 3.3 add.265
  154.9 2.6 shard_map.346
  162.2 11.5 %collective-permute-done.16 = bf16[256,1024]{1,0:T(8,128)(2,1)S(1)} collective-permute-done((bf16[256,1024]{1,0:T(8,128)(2,1)}, bf16[256,1024]{1,0:T(8,128)(2,1)S(1)}, u32[]{:S(2)}, u32[]{:S(2)}) %collective-permute-start.16) | collective-permute-done | bytes 524320 | tf_op jit(solution)/shard_map/ppermute | solution.py:73
  173.6 10.9 %collective-permute-done.17 = bf16[256,1024]{1,0:T(8,128)(2,1)S(1)} collective-permute-done((bf16[256,1024]{1,0:T(8,128)(2,1)}, bf16[256,1024]{1,0:T(8,128)(2,1)S(1)}, u32[]{:S(2)}, u32[]{:S(2)}) %collective-permute-start.17) | collective-permute-done | bytes 524320 | tf_op jit(solution)/shard_map/ppermute | solution.py:73
  189.5 12.0 %collective-permute-done.20 = bf16[256,1024]{1,0:T(8,128)(2,1)S(1)} collective-permute-done((bf16[256,1024]{1,0:T(8,128)(2,1)S(1)}, bf16[256,1024]{1,0:T(8,128)(2,1)S(1)}, u32[]{:S(2)}, u32[]{:S(2)}) %collective-permute-start.20) | collective-permute-done | bytes 524320 | tf_op jit(solution)/shard_map/ppermute | solution.py:73
  203.8 5.5 collective-permute-done.22
  210.4 23.5 %all-gather.3.cloned.1.call-done = bf16[2048,2048]{1,0:T(8,128)(2,1)} async-done(((bf16[512,2048]{1,0:T(8,128)(2,1)}), bf16[2048,2048]{1,0:T(8,128)(2,1)}) %all-gather.3.cloned.1.call-update) | async-done | bytes 8388624 | tf_op jit(solution)/shard_map/all_gather | solution.py:578
  233.9 3.8 shard_map.350
  237.8 3.8 shard_map.348
  242.1 5.2 shard_map.351
  247.4 5.3 shard_map.349
  253.1 61.9 %all-gather.5.cloned.1.call-done = bf16[2048,1024]{1,0:T(8,128)(2,1)} async-done(((bf16[512,1024]{1,0:T(8,128)(2,1)}), bf16[2048,1024]{1,0:T(8,128)(2,1)}) %all-gather.5.cloned.1.call-update) | async-done | bytes 4194320 | tf_op jit(solution)/shard_map/all_gather | solution.py:578
  315.1 8.2 %shard_map.352 = (f32[256,1024]{1,0:T(8,128)S(1)}, bf16[3,256,1024]{2,1,0:T(8,128)(2,1)}) custom-call(s32[1]{0:T(128)} %bitcast.c, bf16[1024,512]{1,0:T(8,128)(2,1)} %get-tuple-element.56.refs_0_, bf16[1024,512]{1,0:T(8,128)(2,1)S(1)} %get-tuple-element.57.refs_1_, bf16[1024,512]{1,0:T(8,128)(2,1)} %collective-permute-done.26.refs_2_, ...), custom_call_target="tpu_custom_call" | custom-call | flops 1 | bytes 1 | tf_op jit(solution)/shard_map/pallas_call | solution.py:140
  328.3 11.3 %collective-permute-done.28 = bf16[256,1024]{1,0:T(8,128)(2,1)S(1)} collective-permute-done((bf16[256,1024]{1,0:T(8,128)(2,1)S(1)}, bf16[256,1024]{1,0:T(8,128)(2,1)S(1)}, u32[]{:S(2)}, u32[]{:S(2)}) %collective-permute-start.28) | collective-permute-done | bytes 524320 | tf_op jit(solution)/shard_map/ppermute | solution.py:73
  339.6 11.3 %collective-permute-done.29 = bf16[256,1024]{1,0:T(8,128)(2,1)S(1)} collective-permute-done((bf16[256,1024]{1,0:T(8,128)(2,1)S(1)}, bf16[256,1024]{1,0:T(8,128)(2,1)S(1)}, u32[]{:S(2)}, u32[]{:S(2)}) %collective-permute-start.29) | collective-permute-done | bytes 524320 | tf_op jit(solution)/shard_map/ppermute | solution.py:73
  355.2 12.0 %collective-permute-done.32 = bf16[256,1024]{1,0:T(8,128)(2,1)S(1)} collective-permute-done((bf16[256,1024]{1,0:T(8,128)(2,1)S(1)}, bf16[256,1024]{1,0:T(8,128)(2,1)S(1)}, u32[]{:S(2)}, u32[]{:S(2)}) %collective-permute-start.32) | collective-permute-done | bytes 524320 | tf_op jit(solution)/shard_map/ppermute | solution.py:73
  369.5 5.3 collective-permute-done.34
  377.5 8.8 %shard_map.353.refs_5_ = bf16[4,512,1024]{2,1,0:T(8,128)(2,1)} custom-call(s32[1]{0:T(128)} %bitcast.c, bf16[1024,512]{1,0:T(8,128)(2,1)} %get-tuple-element.56.refs_0_, bf16[1024,512]{1,0:T(8,128)(2,1)S(1)} %get-tuple-element.57.refs_1_, bf16[1024,512]{1,0:T(8,128)(2,1)} %collective-permute-done.26.refs_2_, ...), custom_call_target="tpu_custom_call" | custom-call | flops 1 | bytes 1 | tf_op jit(solution)/shard_map/pallas_call | solution.py:140
  388.8 3.6 collective-permute-done.37.refs_3_
  392.5 3.0 collective-permute-done.36.refs_1_
  396.8 6.1 shard_map.355.refs_1_.refs_2_
  403.1 6.4 shard_map.354.refs_0_.refs_1_
  409.8 4.0 collective-permute-done.38.refs_2_.refs_3_
  415.1 13.5 %shard_map.356 = (f32[256,1024]{1,0:T(8,128)S(1)}, bf16[3,256,1024]{2,1,0:T(8,128)(2,1)S(1)}) custom-call(s32[1]{0:T(128)} %bitcast.c, bf16[2,1024,512]{2,1,0:T(8,128)(2,1)S(1)} %shard_map.354.refs_0_.refs_1_, bf16[2,1024,512]{2,1,0:T(8,128)(2,1)} %copy-done.2, bf16[2,1024,512]{2,1,0:T(8,128)(2,1)} %copy-done.41, bf16[2,1024,512]{2,1,0:T(8,128)(2,1)} %copy-done.38, ...), custom_call_target="tpu_custom_call" | custom-call | flops 1 | bytes 1 | tf_op jit(solution)/shard_map/pallas_call | solution.py:140
  428.7 16.9 %shard_map.360.value = bf16[4,2,256,2048]{3,2,1,0:T(8,128)(2,1)} custom-call(s32[1]{0:T(128)} %bitcast.c, bf16[1024,1024]{1,0:T(8,128)(2,1)S(1)} %constant_dynamic-update-slice_fusion.5.refs_0_, bf16[2,1024,512]{2,1,0:T(8,128)(2,1)S(1)} %shard_map.354.refs_0_.refs_1_, bf16[2,1024,512]{2,1,0:T(8,128)(2,1)} %copy-done.2, bf16[2,1024,512]{2,1,0:T(8,128)(2,1)} %copy-done.41, ...), custom_call_target="tpu_custom_call" | custom-call | flops 1 | bytes 1 | tf_op jit(solution)/shard_map/pallas_call | solution.py:140
  446.7 13.9 %reduce-scatter.4.cloned.1.call-done.refs_0_ = bf16[512,1024]{1,0:T(8,128)(2,1)} async-done(((bf16[2048,1024]{1,0:T(8,128)(2,1)}), bf16[512,1024]{1,0:T(8,128)(2,1)}) %reduce-scatter.4.cloned.1.call-update) | async-done | bytes 1048592 | tf_op jit(solution)/shard_map/reduce_scatter | solution.py:582
  465.7 11.3 %collective-permute-done.40 = bf16[256,1024]{1,0:T(8,128)(2,1)S(1)} collective-permute-done((bf16[256,1024]{1,0:T(8,128)(2,1)S(1)}, bf16[256,1024]{1,0:T(8,128)(2,1)S(1)}, u32[]{:S(2)}, u32[]{:S(2)}) %collective-permute-start.40) | collective-permute-done | bytes 524320 | tf_op jit(solution)/shard_map/ppermute | solution.py:73
  477.0 11.3 %collective-permute-done.41 = bf16[256,1024]{1,0:T(8,128)(2,1)S(1)} collective-permute-done((bf16[256,1024]{1,0:T(8,128)(2,1)S(1)}, bf16[256,1024]{1,0:T(8,128)(2,1)S(1)}, u32[]{:S(2)}, u32[]{:S(2)}) %collective-permute-start.41) | collective-permute-done | bytes 524320 | tf_op jit(solution)/shard_map/ppermute | solution.py:73
  493.9 12.0 %collective-permute-done.44 = bf16[256,1024]{1,0:T(8,128)(2,1)S(1)} collective-permute-done((bf16[256,1024]{1,0:T(8,128)(2,1)S(1)}, bf16[256,1024]{1,0:T(8,128)(2,1)S(1)}, u32[]{:S(2)}, u32[]{:S(2)}) %collective-permute-start.44) | collective-permute-done | bytes 524320 | tf_op jit(solution)/shard_map/ppermute | solution.py:73
  508.2 5.5 collective-permute-done.46
  517.2 2.7 collective-permute-done.49.refs_3_
  523.3 3.7 multiply_reduce_fusion.1
  541.5 3.0 reshape.616
  544.5 2.5 multiply_reduce_fusion.3
  547.4 2.8 fusion.4
  551.5 4.2 fusion.18
  564.9 3.4 collective-permute-done.54.refs_1_.refs_2_
  568.3 11.0 %shard_map.359.value = bf16[4,4,256,512]{3,2,1,0:T(8,128)(2,1)} custom-call(s32[1]{0:T(128)} %bitcast.c, bf16[1024,1024]{1,0:T(8,128)(2,1)} %copy-done.4, bf16[3,1024,256]{2,1,0:T(8,128)(2,1)S(1)} %pad_maximum_fusion.refs_0_.refs_1_, bf16[3,1024,256]{2,1,0:T(8,128)(2,1)S(1)} %collective-permute-done.54.refs_1_.refs_2_, bf16[1024,256]{1,0:T(8,128)(2,1)S(1)} %copy-done.12, ...), custom_call_target="tpu_custom_call" | custom-call | flops 1 | bytes 1 | tf_op jit(solution)/shard_map/pallas_call | solution.py:140
  579.3 28.7 %reduce-scatter.6.cloned.1.call-done.refs_0_ = bf16[512,2048]{1,0:T(8,128)(2,1)} async-done(((bf16[2048,2048]{1,0:T(8,128)(2,1)}), bf16[512,2048]{1,0:T(8,128)(2,1)}) %reduce-scatter.6.cloned.1.call-update) | async-done | bytes 2097168 | tf_op jit(solution)/shard_map/reduce_scatter | solution.py:582
  610.9 2.4 collective-permute-done.59
  614.8 5.9 shard_map.358
  625.9 4.5 collective-permute-done.61
  632.7 4.8 collective-permute-done.62
  638.1 5.4 shard_map.366
  643.5 2.7 collective-permute-done.56
  648.2 10.0 %shard_map.365 = (f32[2,256,2048]{2,1,0:T(8,128)}, f32[2,256,2048]{2,1,0:T(8,128)}, f32[2,256,2048]{2,1,0:T(8,128)}, f32[2,256,2048]{2,1,0:T(8,128)}) custom-call(s32[1]{0:T(128)} %bitcast.c, bf16[512,2048]{1,0:T(8,128)(2,1)S(1)} %copy-done.5, f32[2,256,2048]{2,1,0:T(8,128)} %refs_1_.6, f32[2,256,2048]{2,1,0:T(8,128)} %refs_2_.6, f32[2,256,2048]{2,1,0:T(8,128)} %refs_3_.6), custom_call_target="tpu_custom_call" | custom-call | flops 1 | bytes 1 | tf_op jit(solution)/shard_map/pallas_call | solution.py:140
  658.2 30.8 %reduce-scatter.8.cloned.1.call-done.refs_0_ = bf16[1024,512]{1,0:T(8,128)(2,1)} async-done(((bf16[4096,512]{1,0:T(8,128)(2,1)}), bf16[1024,512]{1,0:T(8,128)(2,1)}) %reduce-scatter.8.cloned.1.call-update) | async-done | bytes 1048592 | tf_op jit(solution)/shard_map/reduce_scatter | solution.py:582
  691.7 3.3 shard_map.363
  (396 shorter events, 156.4 us)
Async XLA Ops:
  7.2 226.7 %all-gather.3.cloned.1.call-start = ((), (), s32[]{:S(2)}) async-start(), calls=%async_computation.3 | async-start | bytes 10485760 | tf_op jit(solution)/shard_map/all_gather | solution.py:578
  8.9 17.4 %collective-permute-start.4 = (bf16[512,512]{1,0:T(8,128)(2,1)S(1)}, bf16[512,512]{1,0:T(8,128)(2,1)S(1)}, u32[]{:S(2)}, u32[]{:S(2)}) collective-permute-start(bf16[512,512]{1,0:T(8,128)(2,1)S(1)} %bitcast.151), channel_id=1, source_target_pairs={{0,24},{8,0},{16,8},{24,16},{1,25},{9,1},{17,9},{25,17},{2,26},{10... | collective-permute-start | bytes 1572872 | tf_op jit(solution)/shard_map/ppermute | solution.py:183
  18.1 19.4 %collective-permute-start.5 = (bf16[512,512]{1,0:T(8,128)(2,1)S(1)}, bf16[512,512]{1,0:T(8,128)(2,1)S(1)}, u32[]{:S(2)}, u32[]{:S(2)}) collective-permute-start(bf16[512,512]{1,0:T(8,128)(2,1)S(1)} %get-tuple-element.107), channel_id=1, source_target_pairs={{0,24},{8,0},{16,8},{24,16},{1,25},{9,1},{17,9},{25,17},{2,26},{10... | collective-permute-start | bytes 1572872 | tf_op jit(solution)/shard_map/ppermute | solution.py:183
  26.3 22.5 %collective-permute-start.6 = (bf16[512,512]{1,0:T(8,128)(2,1)S(1)}, bf16[512,512]{1,0:T(8,128)(2,1)S(1)}, u32[]{:S(2)}, u32[]{:S(2)}) collective-permute-start(bf16[512,512]{1,0:T(8,128)(2,1)S(1)} %collective-permute-done.4), channel_id=1, source_target_pairs={{0,24},{8,0},{16,8},{24,16},{1,25},{9,1},{17,9},{25,17},{2,26},{10... | collective-permute-start | bytes 1572872 | tf_op jit(solution)/shard_map/ppermute | solution.py:183
  37.5 22.5 %collective-permute-start.7 = (bf16[512,512]{1,0:T(8,128)(2,1)S(1)}, bf16[512,512]{1,0:T(8,128)(2,1)S(1)}, u32[]{:S(2)}, u32[]{:S(2)}) collective-permute-start(bf16[512,512]{1,0:T(8,128)(2,1)S(1)} %collective-permute-done.5), channel_id=1, source_target_pairs={{0,24},{8,0},{16,8},{24,16},{1,25},{9,1},{17,9},{25,17},{2,26},{10... | collective-permute-start | bytes 1572872 | tf_op jit(solution)/shard_map/ppermute | solution.py:183
  48.8 22.5 %collective-permute-start.8 = (bf16[512,512]{1,0:T(8,128)(2,1)S(1)}, bf16[512,512]{1,0:T(8,128)(2,1)S(1)}, u32[]{:S(2)}, u32[]{:S(2)}) collective-permute-start(bf16[512,512]{1,0:T(8,128)(2,1)S(1)} %collective-permute-done.6), channel_id=1, source_target_pairs={{0,24},{8,0},{16,8},{24,16},{1,25},{9,1},{17,9},{25,17},{2,26},{10... | collective-permute-start | bytes 1572872 | tf_op jit(solution)/shard_map/ppermute | solution.py:183
  60.0 21.3 %collective-permute-start.9 = (bf16[512,512]{1,0:T(8,128)(2,1)S(1)}, bf16[512,512]{1,0:T(8,128)(2,1)S(1)}, u32[]{:S(2)}, u32[]{:S(2)}) collective-permute-start(bf16[512,512]{1,0:T(8,128)(2,1)S(1)} %collective-permute-done.7), channel_id=1, source_target_pairs={{0,24},{8,0},{16,8},{24,16},{1,25},{9,1},{17,9},{25,17},{2,26},{10... | collective-permute-start | bytes 1572872 | tf_op jit(solution)/shard_map/ppermute | solution.py:183
  82.2 232.9 %all-gather.5.cloned.1.call-start = ((), (), s32[]{:S(2)}) async-start(), calls=%async_computation.4 | async-start | bytes 5242880 | tf_op jit(solution)/shard_map/all_gather | solution.py:578
  83.2 12.8 %collective-permute-start = (bf16[256,1024]{1,0:T(8,128)(2,1)S(1)}, bf16[256,1024]{1,0:T(8,128)(2,1)S(1)}, u32[]{:S(2)}, u32[]{:S(2)}) collective-permute-start(bf16[256,1024]{1,0:T(8,128)(2,1)S(1)} %copy-done.50), channel_id=1, source_target_pairs={{0,2},{2,0},{4,6},{6,4},{1,3},{3,1},{5,7},{7,5},{8,10},{10,8},{12,... | collective-permute-start | bytes 1572872 | tf_op jit(solution)/shard_map/ppermute | solution.py:73
  84.7 13.6 %collective-permute-start.1 = (bf16[256,1024]{1,0:T(8,128)(2,1)S(1)}, bf16[256,1024]{1,0:T(8,128)(2,1)}, u32[]{:S(2)}, u32[]{:S(2)}) collective-permute-start(bf16[256,1024]{1,0:T(8,128)(2,1)S(1)} %copy-done.50), channel_id=1, source_target_pairs={{0,4},{2,6},{4,0},{6,2},{1,5},{3,7},{5,1},{7,3},{8,12},{10,14},{12... | collective-permute-start | bytes 1572872 | tf_op jit(solution)/shard_map/ppermute | solution.py:73
  96.7 6.6 collective-permute-start.2
  99.2 6.4 collective-permute-start.3
  114.5 6.8 collective-permute-start.10
  126.6 1.4 collective-permute-start.11
  128.0 9.5 %collective-permute-start.14 = (f32[2,4,256]{2,1,0:T(4,128)S(1)}, f32[2,4,256]{2,1,0:T(4,128)S(1)}, u32[]{:S(2)}, u32[]{:S(2)}) collective-permute-start(f32[2,4,256]{2,1,0:T(4,128)S(1)} %reshape.611), channel_id=1, source_target_pairs={{0,6},{2,4},{4,2},{6,0},{1,7},{3,5},{5,3},{7,1},{8,14},{10,12},{12... | collective-permute-start | bytes 24584 | tf_op jit(solution)/shard_map/ppermute | solution.py:73
  135.4 3.7 collective-permute-start.13
  137.0 3.7 collective-permute-start.12
  152.9 2.0 collective-permute-start.15
  154.2 306.4 %reduce-scatter.4.cloned.1.call-start = ((), (), s32[]{:S(2)}) async-start(), calls=%async_computation.5 | async-start | bytes 5242880 | tf_op jit(solution)/shard_map/reduce_scatter | solution.py:582
  158.7 15.0 %collective-permute-start.16 = (bf16[256,1024]{1,0:T(8,128)(2,1)}, bf16[256,1024]{1,0:T(8,128)(2,1)S(1)}, u32[]{:S(2)}, u32[]{:S(2)}) collective-permute-start(bf16[256,1024]{1,0:T(8,128)(2,1)} %get-tuple-element.129), channel_id=1, source_target_pairs={{0,2},{2,0},{4,6},{6,4},{1,3},{3,1},{5,7},{7,5},{8,10},{10,8},{12,... | collective-permute-start | bytes 1572872 | tf_op jit(solution)/shard_map/ppermute | solution.py:73
  159.2 25.3 %collective-permute-start.17 = (bf16[256,1024]{1,0:T(8,128)(2,1)}, bf16[256,1024]{1,0:T(8,128)(2,1)S(1)}, u32[]{:S(2)}, u32[]{:S(2)}) collective-permute-start(bf16[256,1024]{1,0:T(8,128)(2,1)} %get-tuple-element.131), channel_id=1, source_target_pairs={{0,4},{2,6},{4,0},{6,2},{1,5},{3,7},{5,1},{7,3},{8,12},{10,14},{12... | collective-permute-start | bytes 1572872 | tf_op jit(solution)/shard_map/ppermute | solution.py:73
  159.8 24.7 %collective-permute-start.18 = (bf16[256,1024]{1,0:T(8,128)(2,1)S(1)}, bf16[256,1024]{1,0:T(8,128)(2,1)}, u32[]{:S(2)}, u32[]{:S(2)}) collective-permute-start(bf16[256,1024]{1,0:T(8,128)(2,1)S(1)} %get-tuple-element.130), channel_id=1, source_target_pairs={{0,6},{2,4},{4,2},{6,0},{1,7},{3,5},{5,3},{7,1},{8,14},{10,12},{12... | collective-permute-start | bytes 1572872 | tf_op jit(solution)/shard_map/ppermute | solution.py:73
  187.4 14.1 %collective-permute-start.20 = (bf16[256,1024]{1,0:T(8,128)(2,1)S(1)}, bf16[256,1024]{1,0:T(8,128)(2,1)S(1)}, u32[]{:S(2)}, u32[]{:S(2)}) collective-permute-start(bf16[256,1024]{1,0:T(8,128)(2,1)S(1)} %get-tuple-element.103), channel_id=1, source_target_pairs={{0,2},{2,0},{4,6},{6,4},{1,3},{3,1},{5,7},{7,5},{8,10},{10,8},{12,... | collective-permute-start | bytes 1572872 | tf_op jit(solution)/shard_map/ppermute | solution.py:73
  188.9 13.9 %collective-permute-start.21 = (bf16[256,1024]{1,0:T(8,128)(2,1)S(1)}, bf16[256,1024]{1,0:T(8,128)(2,1)S(1)}, u32[]{:S(2)}, u32[]{:S(2)}) collective-permute-start(bf16[256,1024]{1,0:T(8,128)(2,1)S(1)} %get-tuple-element.103), channel_id=1, source_target_pairs={{0,4},{2,6},{4,0},{6,2},{1,5},{3,7},{5,1},{7,3},{8,12},{10,14},{12... | collective-permute-start | bytes 1572872 | tf_op jit(solution)/shard_map/ppermute | solution.py:73
  201.5 7.7 %collective-permute-start.22 = (bf16[128,1024]{1,0:T(8,128)(2,1)S(1)}, bf16[128,1024]{1,0:T(8,128)(2,1)S(1)}, u32[]{:S(2)}, u32[]{:S(2)}) collective-permute-start(bf16[128,1024]{1,0:T(8,128)(2,1)S(1)} %slice.386), channel_id=1, source_target_pairs={{0,4},{2,6},{4,0},{6,2},{1,5},{3,7},{5,1},{7,3},{8,12},{10,14},{12... | collective-permute-start | bytes 786440 | tf_op jit(solution)/shard_map/ppermute | solution.py:73
  202.9 7.5 %collective-permute-start.23 = (bf16[128,1024]{1,0:T(8,128)(2,1)S(1)}, bf16[128,1024]{1,0:T(8,128)(2,1)S(1)}, u32[]{:S(2)}, u32[]{:S(2)}) collective-permute-start(bf16[128,1024]{1,0:T(8,128)(2,1)S(1)} %slice.387), channel_id=1, source_target_pairs={{0,2},{2,0},{4,6},{6,4},{1,3},{3,1},{5,7},{7,5},{8,10},{10,8},{12,... | collective-permute-start | bytes 786440 | tf_op jit(solution)/shard_map/ppermute | solution.py:73
  237.7 4.4 collective-permute-start.25
  241.5 5.9 collective-permute-start.24
  247.3 67.8 %collective-permute-start.27 = (bf16[1024,512]{1,0:T(8,128)(2,1)S(1)}, bf16[1024,512]{1,0:T(8,128)(2,1)}, u32[]{:S(2)}, u32[]{:S(2)}) collective-permute-start(bf16[1024,512]{1,0:T(8,128)(2,1)S(1)} %get-tuple-element.57.refs_1_), channel_id=1, source_target_pairs={{0,1},{1,0},{2,3},{3,2},{4,5},{5,4},{6,7},{7,6},{8,9},{9,8},{10,11... | collective-permute-start | bytes 3145736 | tf_op jit(solution)/shard_map/ppermute | solution.py:73
  252.7 62.4 %collective-permute-start.26 = (bf16[1024,512]{1,0:T(8,128)(2,1)}, bf16[1024,512]{1,0:T(8,128)(2,1)}, u32[]{:S(2)}, u32[]{:S(2)}) collective-permute-start(bf16[1024,512]{1,0:T(8,128)(2,1)} %get-tuple-element.56.refs_0_), channel_id=1, source_target_pairs={{0,1},{1,0},{2,3},{3,2},{4,5},{5,4},{6,7},{7,6},{8,9},{9,8},{10,11... | collective-permute-start | bytes 3145736 | tf_op jit(solution)/shard_map/ppermute | solution.py:73
  324.8 14.9 %collective-permute-start.28 = (bf16[256,1024]{1,0:T(8,128)(2,1)S(1)}, bf16[256,1024]{1,0:T(8,128)(2,1)S(1)}, u32[]{:S(2)}, u32[]{:S(2)}) collective-permute-start(bf16[256,1024]{1,0:T(8,128)(2,1)S(1)} %get-tuple-element.126), channel_id=1, source_target_pairs={{0,2},{2,0},{4,6},{6,4},{1,3},{3,1},{5,7},{7,5},{8,10},{10,8},{12,... | collective-permute-start | bytes 1572872 | tf_op jit(solution)/shard_map/ppermute | solution.py:73
  326.3 24.6 %collective-permute-start.29 = (bf16[256,1024]{1,0:T(8,128)(2,1)S(1)}, bf16[256,1024]{1,0:T(8,128)(2,1)S(1)}, u32[]{:S(2)}, u32[]{:S(2)}) collective-permute-start(bf16[256,1024]{1,0:T(8,128)(2,1)S(1)} %get-tuple-element.128), channel_id=1, source_target_pairs={{0,4},{2,6},{4,0},{6,2},{1,5},{3,7},{5,1},{7,3},{8,12},{10,14},{12... | collective-permute-start | bytes 1572872 | tf_op jit(solution)/shard_map/ppermute | solution.py:73
  327.8 23.1 %collective-permute-start.30 = (bf16[256,1024]{1,0:T(8,128)(2,1)S(1)}, bf16[256,1024]{1,0:T(8,128)(2,1)S(1)}, u32[]{:S(2)}, u32[]{:S(2)}) collective-permute-start(bf16[256,1024]{1,0:T(8,128)(2,1)S(1)} %get-tuple-element.127), channel_id=1, source_target_pairs={{0,6},{2,4},{4,2},{6,0},{1,7},{3,5},{5,3},{7,1},{8,14},{10,12},{12... | collective-permute-start | bytes 1572872 | tf_op jit(solution)/shard_map/ppermute | solution.py:73
  353.1 14.1 %collective-permute-start.32 = (bf16[256,1024]{1,0:T(8,128)(2,1)S(1)}, bf16[256,1024]{1,0:T(8,128)(2,1)S(1)}, u32[]{:S(2)}, u32[]{:S(2)}) collective-permute-start(bf16[256,1024]{1,0:T(8,128)(2,1)S(1)} %get-tuple-element.100), channel_id=1, source_target_pairs={{0,2},{2,0},{4,6},{6,4},{1,3},{3,1},{5,7},{7,5},{8,10},{10,8},{12,... | collective-permute-start | bytes 1572872 | tf_op jit(solution)/shard_map/ppermute | solution.py:73
  354.4 14.4 %collective-permute-start.33 = (bf16[256,1024]{1,0:T(8,128)(2,1)S(1)}, bf16[256,1024]{1,0:T(8,128)(2,1)S(1)}, u32[]{:S(2)}, u32[]{:S(2)}) collective-permute-start(bf16[256,1024]{1,0:T(8,128)(2,1)S(1)} %get-tuple-element.100), channel_id=1, source_target_pairs={{0,4},{2,6},{4,0},{6,2},{1,5},{3,7},{5,1},{7,3},{8,12},{10,14},{12... | collective-permute-start | bytes 1572872 | tf_op jit(solution)/shard_map/ppermute | solution.py:73
  367.2 7.6 %collective-permute-start.34 = (bf16[128,1024]{1,0:T(8,128)(2,1)S(1)}, bf16[128,1024]{1,0:T(8,128)(2,1)S(1)}, u32[]{:S(2)}, u32[]{:S(2)}) collective-permute-start(bf16[128,1024]{1,0:T(8,128)(2,1)S(1)} %slice.390), channel_id=1, source_target_pairs={{0,4},{2,6},{4,0},{6,2},{1,5},{3,7},{5,1},{7,3},{8,12},{10,14},{12... | collective-permute-start | bytes 786440 | tf_op jit(solution)/shard_map/ppermute | solution.py:73
  368.8 7.3 %collective-permute-start.35 = (bf16[128,1024]{1,0:T(8,128)(2,1)S(1)}, bf16[128,1024]{1,0:T(8,128)(2,1)S(1)}, u32[]{:S(2)}, u32[]{:S(2)}) collective-permute-start(bf16[128,1024]{1,0:T(8,128)(2,1)S(1)} %slice.391), channel_id=1, source_target_pairs={{0,2},{2,0},{4,6},{6,4},{1,3},{3,1},{5,7},{7,5},{8,10},{10,8},{12,... | collective-permute-start | bytes 786440 | tf_op jit(solution)/shard_map/ppermute | solution.py:73
  386.2 221.7 %reduce-scatter.6.cloned.1.call-start = ((), (), s32[]{:S(2)}) async-start(), calls=%async_computation.6 | async-start | bytes 10485760 | tf_op jit(solution)/shard_map/reduce_scatter | solution.py:582
  388.2 4.2 collective-permute-start.37
  388.5 6.9 collective-permute-start.36
  402.9 6.9 collective-permute-start.39
  409.6 4.2 collective-permute-start.38
  460.6 228.5 %reduce-scatter.8.cloned.1.call-start = ((), (), s32[]{:S(2)}) async-start(), calls=%async_computation.7 | async-start | bytes 5242880 | tf_op jit(solution)/shard_map/reduce_scatter | solution.py:582
  462.1 14.9 %collective-permute-start.40 = (bf16[256,1024]{1,0:T(8,128)(2,1)S(1)}, bf16[256,1024]{1,0:T(8,128)(2,1)S(1)}, u32[]{:S(2)}, u32[]{:S(2)}) collective-permute-start(bf16[256,1024]{1,0:T(8,128)(2,1)S(1)} %get-tuple-element.123), channel_id=1, source_target_pairs={{0,2},{2,0},{4,6},{6,4},{1,3},{3,1},{5,7},{7,5},{8,10},{10,8},{12,... | collective-permute-start | bytes 1572872 | tf_op jit(solution)/shard_map/ppermute | solution.py:73
  463.7 24.7 %collective-permute-start.41 = (bf16[256,1024]{1,0:T(8,128)(2,1)S(1)}, bf16[256,1024]{1,0:T(8,128)(2,1)S(1)}, u32[]{:S(2)}, u32[]{:S(2)}) collective-permute-start(bf16[256,1024]{1,0:T(8,128)(2,1)S(1)} %get-tuple-element.125), channel_id=1, source_target_pairs={{0,4},{2,6},{4,0},{6,2},{1,5},{3,7},{5,1},{7,3},{8,12},{10,14},{12... | collective-permute-start | bytes 1572872 | tf_op jit(solution)/shard_map/ppermute | solution.py:73
  465.1 23.2 %collective-permute-start.42 = (bf16[256,1024]{1,0:T(8,128)(2,1)S(1)}, bf16[256,1024]{1,0:T(8,128)(2,1)S(1)}, u32[]{:S(2)}, u32[]{:S(2)}) collective-permute-start(bf16[256,1024]{1,0:T(8,128)(2,1)S(1)} %get-tuple-element.124), channel_id=1, source_target_pairs={{0,6},{2,4},{4,2},{6,0},{1,7},{3,5},{5,3},{7,1},{8,14},{10,12},{12... | collective-permute-start | bytes 1572872 | tf_op jit(solution)/shard_map/ppermute | solution.py:73
  491.8 14.1 %collective-permute-start.44 = (bf16[256,1024]{1,0:T(8,128)(2,1)S(1)}, bf16[256,1024]{1,0:T(8,128)(2,1)S(1)}, u32[]{:S(2)}, u32[]{:S(2)}) collective-permute-start(bf16[256,1024]{1,0:T(8,128)(2,1)S(1)} %get-tuple-element.97), channel_id=1, source_target_pairs={{0,2},{2,0},{4,6},{6,4},{1,3},{3,1},{5,7},{7,5},{8,10},{10,8},{12,... | collective-permute-start | bytes 1572872 | tf_op jit(solution)/shard_map/ppermute | solution.py:73
  493.0 14.4 %collective-permute-start.45 = (bf16[256,1024]{1,0:T(8,128)(2,1)S(1)}, bf16[256,1024]{1,0:T(8,128)(2,1)S(1)}, u32[]{:S(2)}, u32[]{:S(2)}) collective-permute-start(bf16[256,1024]{1,0:T(8,128)(2,1)S(1)} %get-tuple-element.97), channel_id=1, source_target_pairs={{0,4},{2,6},{4,0},{6,2},{1,5},{3,7},{5,1},{7,3},{8,12},{10,14},{12... | collective-permute-start | bytes 1572872 | tf_op jit(solution)/shard_map/ppermute | solution.py:73
  505.9 7.7 %collective-permute-start.46 = (bf16[128,1024]{1,0:T(8,128)(2,1)S(1)}, bf16[128,1024]{1,0:T(8,128)(2,1)S(1)}, u32[]{:S(2)}, u32[]{:S(2)}) collective-permute-start(bf16[128,1024]{1,0:T(8,128)(2,1)S(1)} %slice.392), channel_id=1, source_target_pairs={{0,4},{2,6},{4,0},{6,2},{1,5},{3,7},{5,1},{7,3},{8,12},{10,14},{12... | collective-permute-start | bytes 786440 | tf_op jit(solution)/shard_map/ppermute | solution.py:73
  507.4 7.5 %collective-permute-start.47 = (bf16[128,1024]{1,0:T(8,128)(2,1)S(1)}, bf16[128,1024]{1,0:T(8,128)(2,1)S(1)}, u32[]{:S(2)}, u32[]{:S(2)}) collective-permute-start(bf16[128,1024]{1,0:T(8,128)(2,1)S(1)} %slice.393), channel_id=1, source_target_pairs={{0,2},{2,0},{4,6},{6,4},{1,3},{3,1},{5,7},{7,5},{8,10},{10,8},{12,... | collective-permute-start | bytes 786440 | tf_op jit(solution)/shard_map/ppermute | solution.py:73
  514.9 5.0 collective-permute-start.48
  517.1 2.9 collective-permute-start.49
  547.1 3.2 collective-permute-start.50
  550.3 9.9 %collective-permute-start.53 = (f32[2,4,256]{2,1,0:T(4,128)S(1)}, f32[2,4,256]{2,1,0:T(4,128)S(1)}, u32[]{:S(2)}, u32[]{:S(2)}) collective-permute-start(f32[2,4,256]{2,1,0:T(4,128)S(1)} %reshape.617), channel_id=1, source_target_pairs={{0,6},{2,4},{4,2},{6,0},{1,7},{3,5},{5,3},{7,1},{8,14},{10,12},{12... | collective-permute-start | bytes 24584 | tf_op jit(solution)/shard_map/ppermute | solution.py:73
  557.7 3.7 collective-permute-start.52
  558.7 3.7 collective-permute-start.51
  564.8 3.5 collective-permute-start.54
  609.3 4.0 collective-permute-start.59
  613.3 11.2 %collective-permute-start.60 = (f32[4,2048]{1,0:T(4,128)S(1)}, f32[4,2048]{1,0:T(4,128)S(1)}, u32[]{:S(2)}, u32[]{:S(2)}) collective-permute-start(f32[4,2048]{1,0:T(4,128)S(1)} %add.316), channel_id=1, source_target_pairs={{0,4},{2,6},{4,0},{6,2},{1,5},{3,7},{5,1},{7,3},{8,12},{10,14},{12... | collective-permute-start | bytes 98312 | tf_op jit(solution)/shard_map/ppermute | solution.py:73
  620.9 22.5 %collective-permute-start.55 = (bf16[256,1024]{1,0:T(8,128)(2,1)S(1)}, bf16[256,1024]{1,0:T(8,128)(2,1)S(1)}, u32[]{:S(2)}, u32[]{:S(2)}) collective-permute-start(bf16[256,1024]{1,0:T(8,128)(2,1)S(1)} %get-tuple-element.120), channel_id=1, source_target_pairs={{0,2},{2,0},{4,6},{6,4},{1,3},{3,1},{5,7},{7,5},{8,10},{10,8},{12,... | collective-permute-start | bytes 1572872 | tf_op jit(solution)/shard_map/ppermute | solution.py:73
  622.6 23.6 %collective-permute-start.56 = (bf16[256,1024]{1,0:T(8,128)(2,1)S(1)}, bf16[256,1024]{1,0:T(8,128)(2,1)S(1)}, u32[]{:S(2)}, u32[]{:S(2)}) collective-permute-start(bf16[256,1024]{1,0:T(8,128)(2,1)S(1)} %get-tuple-element.122), channel_id=1, source_target_pairs={{0,4},{2,6},{4,0},{6,2},{1,5},{3,7},{5,1},{7,3},{8,12},{10,14},{12... | collective-permute-start | bytes 1572872 | tf_op jit(solution)/shard_map/ppermute | solution.py:73
  623.2 23.0 %collective-permute-start.57 = (bf16[256,1024]{1,0:T(8,128)(2,1)S(1)}, bf16[256,1024]{1,0:T(8,128)(2,1)S(1)}, u32[]{:S(2)}, u32[]{:S(2)}) collective-permute-start(bf16[256,1024]{1,0:T(8,128)(2,1)S(1)} %get-tuple-element.121), channel_id=1, source_target_pairs={{0,6},{2,4},{4,2},{6,0},{1,7},{3,5},{5,3},{7,1},{8,14},{10,12},{12... | collective-permute-start | bytes 1572872 | tf_op jit(solution)/shard_map/ppermute | solution.py:73
  624.5 5.9 collective-permute-start.61
  630.4 7.0 collective-permute-start.62
  (76 other events, 593.5 us)
Sparse Core Ops, SparseCore 0:
  82.3 151.5 all-gather.2
  236.0 78.9 all-gather.4
  386.4 74.1 reduce-scatter.3
  462.9 144.9 reduce-scatter.5
  610.2 78.8 reduce-scatter.7

commit v4 on v3

--- a/solution.py
+++ b/solution.py
@@ -92,8 +92,8 @@
     return total.reshape(values.shape)
 
 
-def mesh_total(values):
-    for axis in ("col", "row", "dp"):
+def axes_total(values, axes):
+    for axis in axes:
         distance = 1
         while distance < lax.axis_size(axis):
             values = values + swap(values, axis, distance)
@@ -113,9 +113,9 @@
     )
 
 
-def scatter_rows(own, low):
-    for k in range(1, lax.axis_size("row")):
-        own = own + swap(low[k - 1], "row", k).astype(jnp.float32)
+def scatter_rows(own, *lows):
+    for k, low in enumerate(lows):
+        own = own + swap(low, "row", k + 1).astype(jnp.float32)
     return own
 
 
@@ -186,24 +186,41 @@
     return joined.reshape((count, len(shards) * rows) + joined.shape[3:])
 
 
+def ring_scatter(values, wait=None):
+    count = lax.axis_size("dp")
+    pairs = [(i, (i - 1) % count) for i in range(count)]
+
+    def term(value, step):
+        spot = lax.rem(lax.axis_index("dp") + step, count)
+        return lax.dynamic_index_in_dim(value, spot, 0, keepdims=False)
+
+    totals = [term(value, 1) for value in values]
+    for step in range(1, count):
+        arrived = [lax.ppermute(total, "dp", pairs) for total in totals]
+        if step == 2 and wait is not None:
+            arrived[0] = tie(arrived[0], wait)
+        totals = [
+            (term(value, step + 1).astype(jnp.float32) + part.astype(jnp.float32)).astype(
+                value.dtype
+            )
+            for value, part in zip(values, arrived)
+        ]
+    return totals
+
+
 def row_outs(extent, columns, tile):
     count = lax.axis_size("row")
     rows = extent // count
     return [
-        ((rows, columns), jnp.float32, (rows, tile), lambda n, c: (0, n)),
-        (
-            (count - 1, rows, columns),
-            jnp.bfloat16,
-            (count - 1, rows, tile),
-            lambda n, c: (0, 0, n),
-        ),
+        ((rows, columns), kind, (rows, tile), lambda n, c: (0, n))
+        for kind in [jnp.float32] + [jnp.bfloat16] * (count - 1)
     ]
 
 
-def put_rows(total, own, low):
-    rows = own.shape[0]
-    own[...] = total[:rows]
-    low[...] = total[rows:].astype(jnp.bfloat16).reshape(low.shape)
+def put_rows(total, outs):
+    rows = outs[0].shape[0]
+    for k, out in enumerate(outs):
+        out[...] = total[k * rows : (k + 1) * rows].astype(out.dtype)
 
 
 def project(rows, block):
@@ -234,7 +251,7 @@
     n, _, d, width = block.shape
     extent, half = own.shape
 
-    def body(c, x, y, mine, theirs, out, low):
+    def body(c, x, y, mine, theirs, *outs):
         parts = []
         a = mine[...].reshape(n // 2, 2, d // 2, width)
         b = theirs[...].reshape(n // 2, 2, d // 2, width)
@@ -242,7 +259,7 @@
             parts.append(
                 mm(x[...], a[:, h].reshape(half, width)) + mm(y[...], b[:, h].reshape(half, width))
             )
-        put_rows(jnp.concatenate(parts, 1), out, low)
+        put_rows(jnp.concatenate(parts, 1), outs)
 
     return run(
         body,
@@ -347,12 +364,12 @@
 
     def body(c, *refs):
         xs = refs[:count]
-        mine, theirs, out, low = refs[count:]
+        mine, theirs, *outs = refs[count:]
         total = None
         for j, x in enumerate(xs):
             piece = mm(x[...], (mine if j < half else theirs)[j % half])
             total = piece if total is None else total + piece
-        put_rows(total, out, low)
+        put_rows(total, outs)
 
     return run(
         body,
@@ -440,13 +457,13 @@
     order = piece_order(count)
 
     def body(c, *refs):
-        out, low = refs[2 * count :]
+        outs = refs[2 * count :]
         total = None
         for x, w in zip(refs[:count], refs[count : 2 * count]):
             for k in range(2):
                 piece = mm(x[k], w[:, k].reshape(TILE, PART), NT)
                 total = piece if total is None else total + piece
-        put_rows(total, out, low)
+        put_rows(total, outs)
 
     return run(
         body,
@@ -507,13 +524,13 @@
     extent = own.shape[1]
     group = TILE // d
 
-    def body(c, x, y, mine, theirs, out, low):
+    def body(c, x, y, mine, theirs, *outs):
         total = None
         for a, w in ((x, mine), (y, theirs)):
             for k in range(3):
                 piece = mm(a[k], w[:, k].reshape(TILE, half), NT)
                 total = piece if total is None else total + piece
-        put_rows(total, out, low)
+        put_rows(total, outs)
 
     return run(
         body,
@@ -537,16 +554,17 @@
     low = jnp.bfloat16
     fine = TILE // 2
 
-    def body(c, x, y, z, a, b, g, out):
+    def body(c, x, y, z, a, b, g, first, second):
         for k in range(3):
+            out = (first, second)[k // 2]
             mine = mm(x[...], y[k], TN).astype(low).reshape(group, d, half)
             theirs = mm(x[...], z[k], TN).astype(low).reshape(group, d, half)
             for side in range(2):
 
                 @pl.when(c[0] == side)
                 def _():
-                    out[:, k, :, side * half : (side + 1) * half] = mine
-                    out[:, k, :, (1 - side) * half : (2 - side) * half] = theirs
+                    out[:, k % 2, :, side * half : (side + 1) * half] = mine
+                    out[:, k % 2, :, (1 - side) * half : (2 - side) * half] = theirs
 
         i = pl.program_id(0)
         for source, first in ((a, c[0] * 2), (b, (1 - c[0]) * 2)):
@@ -556,7 +574,7 @@
                 def _():
                     piece = mm(source[:, j * fine : (j + 1) * fine], g[...], TN).astype(low)
                     for h in range(2):
-                        out[:, 3, h * (d // 2) : (h + 1) * (d // 2), :] = piece[
+                        second[:, 1, h * (d // 2) : (h + 1) * (d // 2), :] = piece[
                             :, h * width : (h + 1) * width
                         ].reshape(group, d // 2, width)
 
@@ -565,8 +583,8 @@
         (features // TILE,),
         [(rows, (extent, TILE), lambda i, c: (0, i))]
         + [whole(v) for v in (own, other, heads, far_heads, grads)],
-        [(shape, low, (group, 4, d, width), lambda i, c: (i, 0, 0, 0))],
-    )[0]
+        [((n, 2, d, width), low, (group, 2, d, width), lambda i, c: (i, 0, 0, 0))] * 2,
+    )
 
 
 def take_half(block, axis, which):
@@ -589,16 +607,17 @@
     return (gradient, moment_new, square_new, updated)
 
 
-def adam_call(body, grid, gradients, state, block, where):
+def adam_call(body, grid, gradients, state, block, where, earlier=()):
     return run(
         body,
         grid,
         gradients + [(array, block, where) for array in state],
         [(state[0].shape, jnp.float32, block, where)] * 4,
-    )
-
-
-def adam_rows(gradient, first, blocks, state, step_rate):
+        earlier,
+    )
+
+
+def adam_rows(gradient, first, blocks, state, step_rate, earlier=()):
     d = state[0].shape[-2] // (blocks if state[0].ndim == 2 else 1)
     width = state[0].shape[-1]
     lead = (1,) * (state[0].ndim - 2)
@@ -617,6 +636,7 @@
         state,
         lead + (d, width),
         (lambda k, c: (k, 0, 0)) if lead else (lambda k, c: (k, 0)),
+        earlier,
     )
 
 
@@ -683,9 +703,8 @@
     expand_low = expand_weight.astype(low)
     expand_block = gather_shards(
         tie(expand_low, entry_block).reshape(-1, expand_low.shape[2])
-    ).reshape(
-        (shards,) + expand_weight.shape
-    )
+    )
+    expand_block = expand_block.reshape((shards,) + expand_weight.shape)
     reduce_pieces = gather_shards(reduce_low).reshape(4, -1, reduce_low.shape[1])
     halves = range(2)
 
@@ -800,9 +819,6 @@
     reduce_outs = adam_rows(
         reduce_grad, 0, 2, [reduce_weight, reduce_mean, reduce_square], 2.0 * FF ** (-0.5)
     )
-    expand_outs = adam_rows(
-        expand_grad, 0, 2, [expand_weight, expand_mean, expand_square], rate
-    )
     hidden_grad = upstream + hidden_back
     gain_first_post = jnp.sum(hidden_grad * branch_hat, 0)
     scaled = hidden_grad * post_gain[0]
@@ -863,6 +879,14 @@
     value_grad = value_accum.reshape(extent, head_width)
     projected_grad = jnp.stack([query_raw, key_raw, value_grad]).astype(low)
     projected_other = swap_col(projected_grad)
+    gain_local = jnp.zeros((4, D), jnp.float32)
+    gain_local = lax.dynamic_update_slice(
+        gain_local, jnp.stack([gain_first_post, gain_second_post]), (0, col_start)
+    )
+    gain_local = lax.dynamic_update_slice(
+        gain_local, jnp.stack([gain_query, gain_key]), (2, head_start)
+    )
+    gain_local = axes_total(gain_local, ("dp",))
     entry_sum = entry_mixer_weight(
         token_rows,
         projected_grad,
@@ -872,7 +896,16 @@
         branch_rows,
         entry_block.shape,
     )
-    entry_out = scatter_shards(tie(entry_sum, expand_grad).reshape(-1, grid_width))
+    expand_outs = adam_rows(
+        expand_grad, 0, 2, [expand_weight, expand_mean, expand_square], rate
+    )
+    if shards > 4:
+        joined = jnp.concatenate(entry_sum, 1)
+        entry_out = scatter_shards(tie(joined, expand_grad).reshape(-1, grid_width))
+    else:
+        entry_out = jnp.concatenate(
+            ring_scatter([tie(value, gain_local) for value in entry_sum], expand_outs[0]), 0
+        ).reshape(-1, grid_width)
     entry_outs = adam_rows(entry_out, 0, 3, [entry_weight, entry_mean, entry_square], rate)
     mixer_outs = adam_halves(
         entry_out,
@@ -884,14 +917,7 @@
         *project_back(projected_grad, projected_other, entry_block, [])
     )
     input_grad = hidden_grad + entry_back
-    gain_local = jnp.zeros((4, D), jnp.float32)
-    gain_local = lax.dynamic_update_slice(
-        gain_local, jnp.stack([gain_first_post, gain_second_post]), (0, col_start)
-    )
-    gain_local = lax.dynamic_update_slice(
-        gain_local, jnp.stack([gain_query, gain_key]), (2, head_start)
-    )
-    gain_grad = mesh_total(gain_local)
+    gain_grad = axes_total(gain_local, ("col", "row"))
     gain_momentum, gain_variance, gain_updated = adam_step(
         gains, gain_grad, gain_mean, gain_square, 1.0, 0.0
     )

time: 709 us -> 694 us (0.979)
  waiting for transfers between devices: 376 us -> 338 us
  other arithmetic: 36.2 us -> 46.1 us
  starting transfers between devices: 73.5 us -> 82.8 us
    reduce_scatter x3 -> x2, waiting for transfers between devices: 73.4 us -> 12.9 us  [scatter_shards(): return lax.psum_scatter(values, 'dp', scatter_dimension=0, tiled=True)]
    ppermute x0 -> x6, waiting for transfers between devices: none -> 24.1 us  [ring_scatter(): arrived = [lax.ppermute(total, 'dp', pairs) for total in totals]]
    ppermute x0 -> x6, starting transfers between devices: none -> 12.2 us  [ring_scatter(): arrived = [lax.ppermute(total, 'dp', pairs) for total in totals]]
    unnamed x166 -> x176, local copies, waits for them, and re-layouts: 19.8 us -> 24.1 us
  transfers between devices with their start and end apart: 68 -> 73, of which waited for: 48 -> 48; matrix products, arithmetic and copies ran while one was open for 13% -> 14% of each run, Pallas kernels for 15% -> 15%
where the time goes in v4:
time: 694 us; the launch traced here: 688 us
  waiting for transfers between devices  338 us (49%)
  Pallas kernels  126 us (18%)
  starting transfers between devices  82.8 us (12%)
  local copies, waits for them, and re-layouts  59.1 us (9%)
  other arithmetic  46.1 us (7%)
  matrix products  20.7 us (3%)
  between operations  15.4 us (2%)
    ppermute x57, waiting for transfers between devices, swap(): lax.ppermute(values, axis, [(i, i ^ distance) for i in range(lax.axis_siz...  178 us
    pallas_call x19, Pallas kernels, run(): pl.pallas_call(kernel, grid_spec=pltpu.PrefetchScalarGridSpec(num_scalar_...  126 us
    all_gather x2, waiting for transfers between devices, gather_shards(): return lax.all_gather(shard, 'dp', axis=0, tiled=True)  85.1 us
    ppermute x57, starting transfers between devices, swap(): lax.ppermute(values, axis, [(i, i ^ distance) for i in range(lax.axis_siz...  47.8 us
    ppermute x6, waiting for transfers between devices, ring_gather(): shards = [lax.ppermute(shard, 'dp', pairs) for shard in shards]  37.7 us
    unnamed x176, local copies, waits for them, and re-layouts  24.1 us
    ppermute x6, waiting for transfers between devices, ring_scatter(): arrived = [lax.ppermute(total, 'dp', pairs) for total in totals]  24.1 us
    ppermute x6, starting transfers between devices, ring_gather(): shards = [lax.ppermute(shard, 'dp', pairs) for shard in shards]  22.7 us
  transfers between devices with their start and end apart: 73, of which 48 were waited for; matrix products, arithmetic and copies ran while one was open for 14% of the time, Pallas kernels for 15%

profile of v4, /device:TPU:0, one launch (start us, length us, event | category | flops | bytes accessed | tf_op | source)
XLA Modules:
  0.0 688.1 jit_solution(2657949992592820908)
XLA Ops:
  8.9 5.1 collective-permute-start.4
  18.5 7.7 %collective-permute-done.4 = bf16[512,512]{1,0:T(8,128)(2,1)S(1)} collective-permute-done((bf16[512,512]{1,0:T(8,128)(2,1)S(1)}, bf16[512,512]{1,0:T(8,128)(2,1)S(1)}, u32[]{:S(2)}, u32[]{:S(2)}) %collective-permute-start.4) | collective-permute-done | bytes 524320 | tf_op jit(solution)/shard_map/ppermute | solution.py:183
  26.3 4.3 collective-permute-start.6
  30.6 7.0 %collective-permute-done.5 = bf16[512,512]{1,0:T(8,128)(2,1)S(1)} collective-permute-done((bf16[512,512]{1,0:T(8,128)(2,1)S(1)}, bf16[512,512]{1,0:T(8,128)(2,1)S(1)}, u32[]{:S(2)}, u32[]{:S(2)}) %collective-permute-start.5) | collective-permute-done | bytes 524320 | tf_op jit(solution)/shard_map/ppermute | solution.py:183
  37.5 4.3 collective-permute-start.7
  41.8 3.8 convert_element_type.186.value
  48.8 4.3 collective-permute-start.8
  53.9 6.1 collective-permute-done.7
  60.0 4.3 collective-permute-start.9
  65.9 5.3 collective-permute-done.8
  72.1 9.3 %collective-permute-done.9 = bf16[512,512]{1,0:T(8,128)(2,1)S(1)} collective-permute-done((bf16[512,512]{1,0:T(8,128)(2,1)S(1)}, bf16[512,512]{1,0:T(8,128)(2,1)S(1)}, u32[]{:S(2)}, u32[]{:S(2)}) %collective-permute-start.9) | collective-permute-done | bytes 524320 | tf_op jit(solution)/shard_map/ppermute | solution.py:183
  86.2 9.8 %collective-permute-done = bf16[256,1024]{1,0:T(8,128)(2,1)S(1)} collective-permute-done((bf16[256,1024]{1,0:T(8,128)(2,1)S(1)}, bf16[256,1024]{1,0:T(8,128)(2,1)S(1)}, u32[]{:S(2)}, u32[]{:S(2)}) %collective-permute-start) | collective-permute-done | bytes 524320 | tf_op jit(solution)/shard_map/ppermute | solution.py:73
  105.7 7.1 %shard_map.345 = (f32[3,1024,256]{2,1,0:T(8,128)S(1)}, f32[3,1024,256]{2,1,0:T(8,128)}) custom-call(s32[1]{0:T(128)} %bitcast.c, bf16[1024,1024]{1,0:T(8,128)(2,1)S(1)} %constant_dynamic-update-slice_fusion.refs_0_, bf16[4,4,256,512]{3,2,1,0:T(8,128)(2,1)} %bitcast.11.refs_1_.refs_2_.refs_3_.refs_0_, ...), custom_call_target="tpu_custom_call" | custom-call | flops 1 | bytes 1 | tf_op jit(solution)/shard_map/pallas_call | solution.py:140
  117.5 3.1 multiply_cosine_fusion
  162.2 11.4 %collective-permute-done.16 = bf16[256,1024]{1,0:T(8,128)(2,1)} collective-permute-done((bf16[256,1024]{1,0:T(8,128)(2,1)S(1)}, bf16[256,1024]{1,0:T(8,128)(2,1)}, u32[]{:S(2)}, u32[]{:S(2)}) %collective-permute-start.16) | collective-permute-done | bytes 524320 | tf_op jit(solution)/shard_map/ppermute | solution.py:73
  173.6 10.7 %collective-permute-done.17 = bf16[256,1024]{1,0:T(8,128)(2,1)} collective-permute-done((bf16[256,1024]{1,0:T(8,128)(2,1)S(1)}, bf16[256,1024]{1,0:T(8,128)(2,1)}, u32[]{:S(2)}, u32[]{:S(2)}) %collective-permute-start.17) | collective-permute-done | bytes 524320 | tf_op jit(solution)/shard_map/ppermute | solution.py:73
  190.0 12.0 %collective-permute-done.20 = bf16[256,1024]{1,0:T(8,128)(2,1)S(1)} collective-permute-done((bf16[256,1024]{1,0:T(8,128)(2,1)S(1)}, bf16[256,1024]{1,0:T(8,128)(2,1)S(1)}, u32[]{:S(2)}, u32[]{:S(2)}) %collective-permute-start.20) | collective-permute-done | bytes 524320 | tf_op jit(solution)/shard_map/ppermute | solution.py:73
  204.2 5.5 collective-permute-done.22
  210.7 23.1 %all-gather.3.cloned.1.call-done = bf16[2048,2048]{1,0:T(8,128)(2,1)} async-done(((bf16[512,2048]{1,0:T(8,128)(2,1)}), bf16[2048,2048]{1,0:T(8,128)(2,1)}) %all-gather.3.cloned.1.call-update) | async-done | bytes 8388624 | tf_op jit(solution)/shard_map/all_gather | solution.py:596
  233.9 3.8 shard_map.350
  237.8 3.8 shard_map.348
  242.1 5.2 shard_map.351
  247.4 5.3 shard_map.349
  253.1 61.9 %all-gather.5.cloned.1.call-done = bf16[2048,1024]{1,0:T(8,128)(2,1)} async-done(((bf16[512,1024]{1,0:T(8,128)(2,1)}), bf16[2048,1024]{1,0:T(8,128)(2,1)}) %all-gather.5.cloned.1.call-update) | async-done | bytes 4194320 | tf_op jit(solution)/shard_map/all_gather | solution.py:596
  315.1 7.6 %shard_map.352 = (f32[256,1024]{1,0:T(8,128)S(1)}, bf16[256,1024]{1,0:T(8,128)(2,1)S(1)}, bf16[256,1024]{1,0:T(8,128)(2,1)S(1)}, bf16[256,1024]{1,0:T(8,128)(2,1)S(1)}) custom-call(s32[1]{0:T(128)} %bitcast.c, bf16[1024,512]{1,0:T(8,128)(2,1)} %get-tuple-element.68.refs_0_, bf16[1024,512]{1,0:T(8,128)(2,1)S(1)} %get-tuple-element.69.refs_1_, ...), custom_call_target="tpu_custom_call" | custom-call | flops 1 | bytes 1 | tf_op jit(solution)/shard_map/pallas_call | solution.py:140
  326.3 11.3 %collective-permute-done.28 = bf16[256,1024]{1,0:T(8,128)(2,1)S(1)} collective-permute-done((bf16[256,1024]{1,0:T(8,128)(2,1)S(1)}, bf16[256,1024]{1,0:T(8,128)(2,1)S(1)}, u32[]{:S(2)}, u32[]{:S(2)}) %collective-permute-start.28) | collective-permute-done | bytes 524320 | tf_op jit(solution)/shard_map/ppermute | solution.py:73
  337.6 11.3 %collective-permute-done.29 = bf16[256,1024]{1,0:T(8,128)(2,1)S(1)} collective-permute-done((bf16[256,1024]{1,0:T(8,128)(2,1)S(1)}, bf16[256,1024]{1,0:T(8,128)(2,1)S(1)}, u32[]{:S(2)}, u32[]{:S(2)}) %collective-permute-start.29) | collective-permute-done | bytes 524320 | tf_op jit(solution)/shard_map/ppermute | solution.py:73
  353.2 12.0 %collective-permute-done.32 = bf16[256,1024]{1,0:T(8,128)(2,1)S(1)} collective-permute-done((bf16[256,1024]{1,0:T(8,128)(2,1)S(1)}, bf16[256,1024]{1,0:T(8,128)(2,1)S(1)}, u32[]{:S(2)}, u32[]{:S(2)}) %collective-permute-start.32) | collective-permute-done | bytes 524320 | tf_op jit(solution)/shard_map/ppermute | solution.py:73
  367.5 5.3 collective-permute-done.34
  375.4 8.8 %shard_map.353.refs_5_ = bf16[4,512,1024]{2,1,0:T(8,128)(2,1)} custom-call(s32[1]{0:T(128)} %bitcast.c, bf16[1024,512]{1,0:T(8,128)(2,1)} %get-tuple-element.68.refs_0_, bf16[1024,512]{1,0:T(8,128)(2,1)S(1)} %get-tuple-element.69.refs_1_, bf16[1024,512]{1,0:T(8,128)(2,1)} %collective-permute-done.26.refs_2_, ...), custom_call_target="tpu_custom_call" | custom-call | flops 1 | bytes 1 | tf_op jit(solution)/shard_map/pallas_call | solution.py:140
  386.8 3.6 collective-permute-done.37.refs_3_
  390.4 3.0 collective-permute-done.36.refs_1_
  394.7 6.0 shard_map.355.refs_1_.refs_2_
  401.0 6.4 shard_map.354.refs_0_.refs_1_
  407.6 4.0 collective-permute-done.38.refs_2_.refs_3_
  413.0 13.5 %shard_map.356 = (f32[256,1024]{1,0:T(8,128)S(1)}, bf16[256,1024]{1,0:T(8,128)(2,1)S(1)}, bf16[256,1024]{1,0:T(8,128)(2,1)S(1)}, bf16[256,1024]{1,0:T(8,128)(2,1)S(1)}) custom-call(s32[1]{0:T(128)} %bitcast.c, bf16[2,1024,512]{2,1,0:T(8,128)(2,1)S(1)} %shard_map.354.refs_0_.refs_1_, bf16[2,1024,512]{2,1,0:T(8,128)(2,1)} %copy-done.2, ...), custom_call_target="tpu_custom_call" | custom-call | flops 1 | bytes 1 | tf_op jit(solution)/shard_map/pallas_call | solution.py:140
  428.1 16.8 %shard_map.361.value = bf16[4,2,256,2048]{3,2,1,0:T(8,128)(2,1)} custom-call(s32[1]{0:T(128)} %bitcast.c, bf16[1024,1024]{1,0:T(8,128)(2,1)S(1)} %constant_dynamic-update-slice_fusion.5.refs_0_, bf16[2,1024,512]{2,1,0:T(8,128)(2,1)S(1)} %shard_map.354.refs_0_.refs_1_, bf16[2,1024,512]{2,1,0:T(8,128)(2,1)} %copy-done.2, bf16[2,1024,512]{2,1,0:T(8,128)(2,1)} %copy-done.52, ...), custom_call_target="tpu_custom_call" | custom-call | flops 1 | bytes 1 | tf_op jit(solution)/shard_map/pallas_call | solution.py:140
  445.7 12.9 %reduce-scatter.3.cloned.1.call-done.refs_0_ = bf16[512,1024]{1,0:T(8,128)(2,1)} async-done(((bf16[2048,1024]{1,0:T(8,128)(2,1)}), bf16[512,1024]{1,0:T(8,128)(2,1)}) %reduce-scatter.3.cloned.1.call-update) | async-done | bytes 1048592 | tf_op jit(solution)/shard_map/reduce_scatter | solution.py:600
  463.1 11.3 %collective-permute-done.40 = bf16[256,1024]{1,0:T(8,128)(2,1)S(1)} collective-permute-done((bf16[256,1024]{1,0:T(8,128)(2,1)S(1)}, bf16[256,1024]{1,0:T(8,128)(2,1)S(1)}, u32[]{:S(2)}, u32[]{:S(2)}) %collective-permute-start.40) | collective-permute-done | bytes 524320 | tf_op jit(solution)/shard_map/ppermute | solution.py:73
  474.4 11.3 %collective-permute-done.41 = bf16[256,1024]{1,0:T(8,128)(2,1)S(1)} collective-permute-done((bf16[256,1024]{1,0:T(8,128)(2,1)S(1)}, bf16[256,1024]{1,0:T(8,128)(2,1)S(1)}, u32[]{:S(2)}, u32[]{:S(2)}) %collective-permute-start.41) | collective-permute-done | bytes 524320 | tf_op jit(solution)/shard_map/ppermute | solution.py:73
  485.7 3.7 multiply_reduce_fusion.5
  492.9 12.0 %collective-permute-done.44 = bf16[256,1024]{1,0:T(8,128)(2,1)S(1)} collective-permute-done((bf16[256,1024]{1,0:T(8,128)(2,1)S(1)}, bf16[256,1024]{1,0:T(8,128)(2,1)S(1)}, u32[]{:S(2)}, u32[]{:S(2)}) %collective-permute-start.44) | collective-permute-done | bytes 524320 | tf_op jit(solution)/shard_map/ppermute | solution.py:73
  507.2 5.5 collective-permute-done.46
  516.3 2.8 collective-permute-done.49.refs_3_
  522.4 3.7 multiply_reduce_fusion.1
  540.5 3.0 reshape.628
  546.4 2.8 fusion.4
  550.9 4.2 fusion.18
  565.7 6.0 collective-permute-done.58
  572.5 6.5 collective-permute-done.59
  579.7 10.9 %shard_map.359 = (bf16[4,2,256,512]{3,2,1,0:T(8,128)(2,1)}, bf16[4,2,256,512]{3,2,1,0:T(8,128)(2,1)}) custom-call(s32[1]{0:T(128)} %bitcast.c, bf16[1024,1024]{1,0:T(8,128)(2,1)} %copy-done.4, bf16[3,1024,256]{2,1,0:T(8,128)(2,1)S(1)} %pad_maximum_fusion.refs_0_.refs_1_, bf16[3,1024,256]{2,1,0:T(8,128)(2,1)S(1)} %collective-permute-done.54.refs_1_.refs_2_, ...), custom_call_target="tpu_custom_call" | custom-call | flops 1 | bytes 1 | tf_op jit(solution)/shard_map/pallas_call | solution.py:140
  592.4 3.0 collective-permute-start.66
  599.8 2.7 collective-permute-done.61
  604.0 6.6 shard_map.358
  613.4 3.8 collective-permute-done.66
  619.4 8.8 %collective-permute-done.63 = bf16[2,256,512]{2,1,0:T(8,128)(2,1)} collective-permute-done((bf16[2,256,512]{2,1,0:T(8,128)(2,1)}, bf16[2,256,512]{2,1,0:T(8,128)(2,1)}, u32[]{:S(2)}, u32[]{:S(2)}) %collective-permute-start.63) | collective-permute-done | bytes 524320 | tf_op jit(solution)/shard_map/ppermute | solution.py:199
  628.2 3.0 collective-permute-start.67
  635.1 5.2 shard_map.368
  640.4 3.2 collective-permute-done.67
  644.5 4.3 collective-permute-start.68
  650.4 9.4 %shard_map.363 = (f32[2,256,2048]{2,1,0:T(8,128)}, f32[2,256,2048]{2,1,0:T(8,128)}, f32[2,256,2048]{2,1,0:T(8,128)}, f32[2,256,2048]{2,1,0:T(8,128)}) custom-call(s32[1]{0:T(128)} %bitcast.c, bf16[512,2048]{1,0:T(8,128)(2,1)S(1)} %copy-done.18, f32[2,256,2048]{2,1,0:T(8,128)} %refs_1_.4, f32[2,256,2048]{2,1,0:T(8,128)} %refs_2_.4, f32[2,256,2048]{2,1,0:T(8,128)} %refs_3_.4), custom_call_target="tpu_custom_call" | custom-call | flops 1 | bytes 1 | tf_op jit(solution)/shard_map/pallas_call | solution.py:140
  663.6 2.7 add_add_fusion
  667.8 8.3 %collective-permute-done.65 = bf16[2,256,512]{2,1,0:T(8,128)(2,1)S(1)} collective-permute-done((bf16[2,256,512]{2,1,0:T(8,128)(2,1)S(1)}, bf16[2,256,512]{2,1,0:T(8,128)(2,1)S(1)}, u32[]{:S(2)}, u32[]{:S(2)}) %collective-permute-start.65) | collective-permute-done | bytes 524320 | tf_op jit(solution)/shard_map/ppermute | solution.py:199
  676.4 3.3 shard_map.366
  (422 shorter events, 178.2 us)
Async XLA Ops:
  7.2 226.7 %all-gather.3.cloned.1.call-start = ((), (), s32[]{:S(2)}) async-start(), calls=%async_computation.2 | async-start | bytes 10485760 | tf_op jit(solution)/shard_map/all_gather | solution.py:596
  8.9 17.4 %collective-permute-start.4 = (bf16[512,512]{1,0:T(8,128)(2,1)S(1)}, bf16[512,512]{1,0:T(8,128)(2,1)S(1)}, u32[]{:S(2)}, u32[]{:S(2)}) collective-permute-start(bf16[512,512]{1,0:T(8,128)(2,1)S(1)} %bitcast.150), channel_id=1, source_target_pairs={{0,24},{8,0},{16,8},{24,16},{1,25},{9,1},{17,9},{25,17},{2,26},{10... | collective-permute-start | bytes 1572872 | tf_op jit(solution)/shard_map/ppermute | solution.py:183
  18.1 19.4 %collective-permute-start.5 = (bf16[512,512]{1,0:T(8,128)(2,1)S(1)}, bf16[512,512]{1,0:T(8,128)(2,1)S(1)}, u32[]{:S(2)}, u32[]{:S(2)}) collective-permute-start(bf16[512,512]{1,0:T(8,128)(2,1)S(1)} %get-tuple-element.127), channel_id=1, source_target_pairs={{0,24},{8,0},{16,8},{24,16},{1,25},{9,1},{17,9},{25,17},{2,26},{10... | collective-permute-start | bytes 1572872 | tf_op jit(solution)/shard_map/ppermute | solution.py:183
  26.3 22.5 %collective-permute-start.6 = (bf16[512,512]{1,0:T(8,128)(2,1)S(1)}, bf16[512,512]{1,0:T(8,128)(2,1)S(1)}, u32[]{:S(2)}, u32[]{:S(2)}) collective-permute-start(bf16[512,512]{1,0:T(8,128)(2,1)S(1)} %collective-permute-done.4), channel_id=1, source_target_pairs={{0,24},{8,0},{16,8},{24,16},{1,25},{9,1},{17,9},{25,17},{2,26},{10... | collective-permute-start | bytes 1572872 | tf_op jit(solution)/shard_map/ppermute | solution.py:183
  37.5 22.5 %collective-permute-start.7 = (bf16[512,512]{1,0:T(8,128)(2,1)S(1)}, bf16[512,512]{1,0:T(8,128)(2,1)S(1)}, u32[]{:S(2)}, u32[]{:S(2)}) collective-permute-start(bf16[512,512]{1,0:T(8,128)(2,1)S(1)} %collective-permute-done.5), channel_id=1, source_target_pairs={{0,24},{8,0},{16,8},{24,16},{1,25},{9,1},{17,9},{25,17},{2,26},{10... | collective-permute-start | bytes 1572872 | tf_op jit(solution)/shard_map/ppermute | solution.py:183
  48.8 22.5 %collective-permute-start.8 = (bf16[512,512]{1,0:T(8,128)(2,1)S(1)}, bf16[512,512]{1,0:T(8,128)(2,1)S(1)}, u32[]{:S(2)}, u32[]{:S(2)}) collective-permute-start(bf16[512,512]{1,0:T(8,128)(2,1)S(1)} %collective-permute-done.6), channel_id=1, source_target_pairs={{0,24},{8,0},{16,8},{24,16},{1,25},{9,1},{17,9},{25,17},{2,26},{10... | collective-permute-start | bytes 1572872 | tf_op jit(solution)/shard_map/ppermute | solution.py:183
  60.0 21.3 %collective-permute-start.9 = (bf16[512,512]{1,0:T(8,128)(2,1)S(1)}, bf16[512,512]{1,0:T(8,128)(2,1)S(1)}, u32[]{:S(2)}, u32[]{:S(2)}) collective-permute-start(bf16[512,512]{1,0:T(8,128)(2,1)S(1)} %collective-permute-done.7), channel_id=1, source_target_pairs={{0,24},{8,0},{16,8},{24,16},{1,25},{9,1},{17,9},{25,17},{2,26},{10... | collective-permute-start | bytes 1572872 | tf_op jit(solution)/shard_map/ppermute | solution.py:183
  82.2 232.9 %all-gather.5.cloned.1.call-start = ((), (), s32[]{:S(2)}) async-start(), calls=%async_computation.3 | async-start | bytes 5242880 | tf_op jit(solution)/shard_map/all_gather | solution.py:596
  83.2 12.8 %collective-permute-start = (bf16[256,1024]{1,0:T(8,128)(2,1)S(1)}, bf16[256,1024]{1,0:T(8,128)(2,1)S(1)}, u32[]{:S(2)}, u32[]{:S(2)}) collective-permute-start(bf16[256,1024]{1,0:T(8,128)(2,1)S(1)} %copy-done.57), channel_id=1, source_target_pairs={{0,2},{2,0},{4,6},{6,4},{1,3},{3,1},{5,7},{7,5},{8,10},{10,8},{12,... | collective-permute-start | bytes 1572872 | tf_op jit(solution)/shard_map/ppermute | solution.py:73
  84.7 13.6 %collective-permute-start.1 = (bf16[256,1024]{1,0:T(8,128)(2,1)S(1)}, bf16[256,1024]{1,0:T(8,128)(2,1)}, u32[]{:S(2)}, u32[]{:S(2)}) collective-permute-start(bf16[256,1024]{1,0:T(8,128)(2,1)S(1)} %copy-done.57), channel_id=1, source_target_pairs={{0,4},{2,6},{4,0},{6,2},{1,5},{3,7},{5,1},{7,3},{8,12},{10,14},{12... | collective-permute-start | bytes 1572872 | tf_op jit(solution)/shard_map/ppermute | solution.py:73
  96.7 6.6 collective-permute-start.2
  99.2 6.4 collective-permute-start.3
  114.5 8.0 %collective-permute-start.10 = (f32[3,1024,256]{2,1,0:T(8,128)}, f32[3,1024,256]{2,1,0:T(8,128)}, u32[]{:S(2)}, u32[]{:S(2)}) collective-permute-start(f32[3,1024,256]{2,1,0:T(8,128)} %get-tuple-element.63), channel_id=1, source_target_pairs={{0,1},{1,0},{2,3},{3,2},{4,5},{5,4},{6,7},{7,6},{8,9},{9,8},{10,11... | collective-permute-start | bytes 9437192 | tf_op jit(solution)/shard_map/ppermute | solution.py:73
  115.7 342.9 %reduce-scatter.3.cloned.1.call-start = ((), (), s32[]{:S(2)}) async-start(), calls=%async_computation.4 | async-start | bytes 5242880 | tf_op jit(solution)/shard_map/reduce_scatter | solution.py:600
  128.3 10.0 %collective-permute-start.14 = (f32[2,4,256]{2,1,0:T(4,128)S(1)}, f32[2,4,256]{2,1,0:T(4,128)S(1)}, u32[]{:S(2)}, u32[]{:S(2)}) collective-permute-start(f32[2,4,256]{2,1,0:T(4,128)S(1)} %reshape.623), channel_id=1, source_target_pairs={{0,6},{2,4},{4,2},{6,0},{1,7},{3,5},{5,3},{7,1},{8,14},{10,12},{12... | collective-permute-start | bytes 24584 | tf_op jit(solution)/shard_map/ppermute | solution.py:73
  136.2 3.7 collective-permute-start.13
  137.8 3.7 collective-permute-start.12
  158.7 14.9 %collective-permute-start.16 = (bf16[256,1024]{1,0:T(8,128)(2,1)S(1)}, bf16[256,1024]{1,0:T(8,128)(2,1)}, u32[]{:S(2)}, u32[]{:S(2)}) collective-permute-start(bf16[256,1024]{1,0:T(8,128)(2,1)S(1)} %get-tuple-element.65), channel_id=1, source_target_pairs={{0,2},{2,0},{4,6},{6,4},{1,3},{3,1},{5,7},{7,5},{8,10},{10,8},{12,... | collective-permute-start | bytes 1572872 | tf_op jit(solution)/shard_map/ppermute | solution.py:73
  159.2 25.0 %collective-permute-start.17 = (bf16[256,1024]{1,0:T(8,128)(2,1)S(1)}, bf16[256,1024]{1,0:T(8,128)(2,1)}, u32[]{:S(2)}, u32[]{:S(2)}) collective-permute-start(bf16[256,1024]{1,0:T(8,128)(2,1)S(1)} %get-tuple-element.66), channel_id=1, source_target_pairs={{0,4},{2,6},{4,0},{6,2},{1,5},{3,7},{5,1},{7,3},{8,12},{10,14},{12... | collective-permute-start | bytes 1572872 | tf_op jit(solution)/shard_map/ppermute | solution.py:73
  159.8 24.5 %collective-permute-start.18 = (bf16[256,1024]{1,0:T(8,128)(2,1)S(1)}, bf16[256,1024]{1,0:T(8,128)(2,1)}, u32[]{:S(2)}, u32[]{:S(2)}) collective-permute-start(bf16[256,1024]{1,0:T(8,128)(2,1)S(1)} %get-tuple-element.67), channel_id=1, source_target_pairs={{0,6},{2,4},{4,2},{6,0},{1,7},{3,5},{5,3},{7,1},{8,14},{10,12},{12... | collective-permute-start | bytes 1572872 | tf_op jit(solution)/shard_map/ppermute | solution.py:73
  187.9 14.1 %collective-permute-start.20 = (bf16[256,1024]{1,0:T(8,128)(2,1)S(1)}, bf16[256,1024]{1,0:T(8,128)(2,1)S(1)}, u32[]{:S(2)}, u32[]{:S(2)}) collective-permute-start(bf16[256,1024]{1,0:T(8,128)(2,1)S(1)} %get-tuple-element.123), channel_id=1, source_target_pairs={{0,2},{2,0},{4,6},{6,4},{1,3},{3,1},{5,7},{7,5},{8,10},{10,8},{12,... | collective-permute-start | bytes 1572872 | tf_op jit(solution)/shard_map/ppermute | solution.py:73
  189.4 13.8 %collective-permute-start.21 = (bf16[256,1024]{1,0:T(8,128)(2,1)S(1)}, bf16[256,1024]{1,0:T(8,128)(2,1)S(1)}, u32[]{:S(2)}, u32[]{:S(2)}) collective-permute-start(bf16[256,1024]{1,0:T(8,128)(2,1)S(1)} %get-tuple-element.123), channel_id=1, source_target_pairs={{0,4},{2,6},{4,0},{6,2},{1,5},{3,7},{5,1},{7,3},{8,12},{10,14},{12... | collective-permute-start | bytes 1572872 | tf_op jit(solution)/shard_map/ppermute | solution.py:73
  202.0 7.7 %collective-permute-start.22 = (bf16[128,1024]{1,0:T(8,128)(2,1)S(1)}, bf16[128,1024]{1,0:T(8,128)(2,1)S(1)}, u32[]{:S(2)}, u32[]{:S(2)}) collective-permute-start(bf16[128,1024]{1,0:T(8,128)(2,1)S(1)} %slice.338), channel_id=1, source_target_pairs={{0,4},{2,6},{4,0},{6,2},{1,5},{3,7},{5,1},{7,3},{8,12},{10,14},{12... | collective-permute-start | bytes 786440 | tf_op jit(solution)/shard_map/ppermute | solution.py:73
  203.3 7.5 %collective-permute-start.23 = (bf16[128,1024]{1,0:T(8,128)(2,1)S(1)}, bf16[128,1024]{1,0:T(8,128)(2,1)S(1)}, u32[]{:S(2)}, u32[]{:S(2)}) collective-permute-start(bf16[128,1024]{1,0:T(8,128)(2,1)S(1)} %slice.339), channel_id=1, source_target_pairs={{0,2},{2,0},{4,6},{6,4},{1,3},{3,1},{5,7},{7,5},{8,10},{10,8},{12,... | collective-permute-start | bytes 786440 | tf_op jit(solution)/shard_map/ppermute | solution.py:73
  237.7 4.4 collective-permute-start.25
  241.5 5.9 collective-permute-start.24
  247.3 67.8 %collective-permute-start.27 = (bf16[1024,512]{1,0:T(8,128)(2,1)S(1)}, bf16[1024,512]{1,0:T(8,128)(2,1)}, u32[]{:S(2)}, u32[]{:S(2)}) collective-permute-start(bf16[1024,512]{1,0:T(8,128)(2,1)S(1)} %get-tuple-element.69.refs_1_), channel_id=1, source_target_pairs={{0,1},{1,0},{2,3},{3,2},{4,5},{5,4},{6,7},{7,6},{8,9},{9,8},{10,11... | collective-permute-start | bytes 3145736 | tf_op jit(solution)/shard_map/ppermute | solution.py:73
  252.7 62.4 %collective-permute-start.26 = (bf16[1024,512]{1,0:T(8,128)(2,1)}, bf16[1024,512]{1,0:T(8,128)(2,1)}, u32[]{:S(2)}, u32[]{:S(2)}) collective-permute-start(bf16[1024,512]{1,0:T(8,128)(2,1)} %get-tuple-element.68.refs_0_), channel_id=1, source_target_pairs={{0,1},{1,0},{2,3},{3,2},{4,5},{5,4},{6,7},{7,6},{8,9},{9,8},{10,11... | collective-permute-start | bytes 3145736 | tf_op jit(solution)/shard_map/ppermute | solution.py:73
  322.7 14.9 %collective-permute-start.28 = (bf16[256,1024]{1,0:T(8,128)(2,1)S(1)}, bf16[256,1024]{1,0:T(8,128)(2,1)S(1)}, u32[]{:S(2)}, u32[]{:S(2)}) collective-permute-start(bf16[256,1024]{1,0:T(8,128)(2,1)S(1)} %get-tuple-element.71), channel_id=1, source_target_pairs={{0,2},{2,0},{4,6},{6,4},{1,3},{3,1},{5,7},{7,5},{8,10},{10,8},{12,... | collective-permute-start | bytes 1572872 | tf_op jit(solution)/shard_map/ppermute | solution.py:73
  324.3 24.6 %collective-permute-start.29 = (bf16[256,1024]{1,0:T(8,128)(2,1)S(1)}, bf16[256,1024]{1,0:T(8,128)(2,1)S(1)}, u32[]{:S(2)}, u32[]{:S(2)}) collective-permute-start(bf16[256,1024]{1,0:T(8,128)(2,1)S(1)} %get-tuple-element.72), channel_id=1, source_target_pairs={{0,4},{2,6},{4,0},{6,2},{1,5},{3,7},{5,1},{7,3},{8,12},{10,14},{12... | collective-permute-start | bytes 1572872 | tf_op jit(solution)/shard_map/ppermute | solution.py:73
  325.8 23.1 %collective-permute-start.30 = (bf16[256,1024]{1,0:T(8,128)(2,1)S(1)}, bf16[256,1024]{1,0:T(8,128)(2,1)S(1)}, u32[]{:S(2)}, u32[]{:S(2)}) collective-permute-start(bf16[256,1024]{1,0:T(8,128)(2,1)S(1)} %get-tuple-element.73), channel_id=1, source_target_pairs={{0,6},{2,4},{4,2},{6,0},{1,7},{3,5},{5,3},{7,1},{8,14},{10,12},{12... | collective-permute-start | bytes 1572872 | tf_op jit(solution)/shard_map/ppermute | solution.py:73
  351.1 14.1 %collective-permute-start.32 = (bf16[256,1024]{1,0:T(8,128)(2,1)S(1)}, bf16[256,1024]{1,0:T(8,128)(2,1)S(1)}, u32[]{:S(2)}, u32[]{:S(2)}) collective-permute-start(bf16[256,1024]{1,0:T(8,128)(2,1)S(1)} %get-tuple-element.120), channel_id=1, source_target_pairs={{0,2},{2,0},{4,6},{6,4},{1,3},{3,1},{5,7},{7,5},{8,10},{10,8},{12,... | collective-permute-start | bytes 1572872 | tf_op jit(solution)/shard_map/ppermute | solution.py:73
  352.3 14.4 %collective-permute-start.33 = (bf16[256,1024]{1,0:T(8,128)(2,1)S(1)}, bf16[256,1024]{1,0:T(8,128)(2,1)S(1)}, u32[]{:S(2)}, u32[]{:S(2)}) collective-permute-start(bf16[256,1024]{1,0:T(8,128)(2,1)S(1)} %get-tuple-element.120), channel_id=1, source_target_pairs={{0,4},{2,6},{4,0},{6,2},{1,5},{3,7},{5,1},{7,3},{8,12},{10,14},{12... | collective-permute-start | bytes 1572872 | tf_op jit(solution)/shard_map/ppermute | solution.py:73
  365.2 7.6 %collective-permute-start.34 = (bf16[128,1024]{1,0:T(8,128)(2,1)S(1)}, bf16[128,1024]{1,0:T(8,128)(2,1)S(1)}, u32[]{:S(2)}, u32[]{:S(2)}) collective-permute-start(bf16[128,1024]{1,0:T(8,128)(2,1)S(1)} %slice.342), channel_id=1, source_target_pairs={{0,4},{2,6},{4,0},{6,2},{1,5},{3,7},{5,1},{7,3},{8,12},{10,14},{12... | collective-permute-start | bytes 786440 | tf_op jit(solution)/shard_map/ppermute | solution.py:73
  366.7 7.3 %collective-permute-start.35 = (bf16[128,1024]{1,0:T(8,128)(2,1)S(1)}, bf16[128,1024]{1,0:T(8,128)(2,1)S(1)}, u32[]{:S(2)}, u32[]{:S(2)}) collective-permute-start(bf16[128,1024]{1,0:T(8,128)(2,1)S(1)} %slice.343), channel_id=1, source_target_pairs={{0,2},{2,0},{4,6},{6,4},{1,3},{3,1},{5,7},{7,5},{8,10},{10,8},{12,... | collective-permute-start | bytes 786440 | tf_op jit(solution)/shard_map/ppermute | solution.py:73
  384.2 264.5 %reduce-scatter.5.cloned.1.call-start = ((), (), s32[]{:S(2)}) async-start(), calls=%async_computation.5 | async-start | bytes 10485760 | tf_op jit(solution)/shard_map/reduce_scatter | solution.py:600
  386.2 4.2 collective-permute-start.37
  386.5 6.9 %collective-permute-start.36 = (bf16[1024,1024]{1,0:T(8,128)(2,1)S(1)}, bf16[1024,1024]{1,0:T(8,128)(2,1)S(1)}, u32[]{:S(2)}, u32[]{:S(2)}) collective-permute-start(bf16[1024,1024]{1,0:T(8,128)(2,1)S(1)} %copy-done.1), channel_id=1, source_target_pairs={{0,1},{1,0},{2,3},{3,2},{4,5},{5,4},{6,7},{7,6},{8,9},{9,8},{10,11... | collective-permute-start | bytes 6291464 | tf_op jit(solution)/shard_map/ppermute | solution.py:73
  400.8 6.8 collective-permute-start.39
  407.4 4.2 collective-permute-start.38
  459.6 14.8 %collective-permute-start.40 = (bf16[256,1024]{1,0:T(8,128)(2,1)S(1)}, bf16[256,1024]{1,0:T(8,128)(2,1)S(1)}, u32[]{:S(2)}, u32[]{:S(2)}) collective-permute-start(bf16[256,1024]{1,0:T(8,128)(2,1)S(1)} %copy-done.24), channel_id=1, source_target_pairs={{0,2},{2,0},{4,6},{6,4},{1,3},{3,1},{5,7},{7,5},{8,10},{10,8},{12,... | collective-permute-start | bytes 1572872 | tf_op jit(solution)/shard_map/ppermute | solution.py:73
  461.1 24.7 %collective-permute-start.41 = (bf16[256,1024]{1,0:T(8,128)(2,1)S(1)}, bf16[256,1024]{1,0:T(8,128)(2,1)S(1)}, u32[]{:S(2)}, u32[]{:S(2)}) collective-permute-start(bf16[256,1024]{1,0:T(8,128)(2,1)S(1)} %copy-done.30), channel_id=1, source_target_pairs={{0,4},{2,6},{4,0},{6,2},{1,5},{3,7},{5,1},{7,3},{8,12},{10,14},{12... | collective-permute-start | bytes 1572872 | tf_op jit(solution)/shard_map/ppermute | solution.py:73
  462.6 23.2 %collective-permute-start.42 = (bf16[256,1024]{1,0:T(8,128)(2,1)S(1)}, bf16[256,1024]{1,0:T(8,128)(2,1)S(1)}, u32[]{:S(2)}, u32[]{:S(2)}) collective-permute-start(bf16[256,1024]{1,0:T(8,128)(2,1)S(1)} %copy-done.28), channel_id=1, source_target_pairs={{0,6},{2,4},{4,2},{6,0},{1,7},{3,5},{5,3},{7,1},{8,14},{10,12},{12... | collective-permute-start | bytes 1572872 | tf_op jit(solution)/shard_map/ppermute | solution.py:73
  490.8 14.1 %collective-permute-start.44 = (bf16[256,1024]{1,0:T(8,128)(2,1)S(1)}, bf16[256,1024]{1,0:T(8,128)(2,1)S(1)}, u32[]{:S(2)}, u32[]{:S(2)}) collective-permute-start(bf16[256,1024]{1,0:T(8,128)(2,1)S(1)} %get-tuple-element.117), channel_id=1, source_target_pairs={{0,2},{2,0},{4,6},{6,4},{1,3},{3,1},{5,7},{7,5},{8,10},{10,8},{12,... | collective-permute-start | bytes 1572872 | tf_op jit(solution)/shard_map/ppermute | solution.py:73
  492.1 14.4 %collective-permute-start.45 = (bf16[256,1024]{1,0:T(8,128)(2,1)S(1)}, bf16[256,1024]{1,0:T(8,128)(2,1)S(1)}, u32[]{:S(2)}, u32[]{:S(2)}) collective-permute-start(bf16[256,1024]{1,0:T(8,128)(2,1)S(1)} %get-tuple-element.117), channel_id=1, source_target_pairs={{0,4},{2,6},{4,0},{6,2},{1,5},{3,7},{5,1},{7,3},{8,12},{10,14},{12... | collective-permute-start | bytes 1572872 | tf_op jit(solution)/shard_map/ppermute | solution.py:73
  504.9 7.7 %collective-permute-start.46 = (bf16[128,1024]{1,0:T(8,128)(2,1)S(1)}, bf16[128,1024]{1,0:T(8,128)(2,1)S(1)}, u32[]{:S(2)}, u32[]{:S(2)}) collective-permute-start(bf16[128,1024]{1,0:T(8,128)(2,1)S(1)} %slice.344), channel_id=1, source_target_pairs={{0,4},{2,6},{4,0},{6,2},{1,5},{3,7},{5,1},{7,3},{8,12},{10,14},{12... | collective-permute-start | bytes 786440 | tf_op jit(solution)/shard_map/ppermute | solution.py:73
  506.5 7.5 %collective-permute-start.47 = (bf16[128,1024]{1,0:T(8,128)(2,1)S(1)}, bf16[128,1024]{1,0:T(8,128)(2,1)S(1)}, u32[]{:S(2)}, u32[]{:S(2)}) collective-permute-start(bf16[128,1024]{1,0:T(8,128)(2,1)S(1)} %slice.345), channel_id=1, source_target_pairs={{0,2},{2,0},{4,6},{6,4},{1,3},{3,1},{5,7},{7,5},{8,10},{10,8},{12,... | collective-permute-start | bytes 786440 | tf_op jit(solution)/shard_map/ppermute | solution.py:73
  514.0 5.0 collective-permute-start.48
  549.3 9.8 %collective-permute-start.53 = (f32[2,4,256]{2,1,0:T(4,128)S(1)}, f32[2,4,256]{2,1,0:T(4,128)S(1)}, u32[]{:S(2)}, u32[]{:S(2)}) collective-permute-start(f32[2,4,256]{2,1,0:T(4,128)S(1)} %reshape.629), channel_id=1, source_target_pairs={{0,6},{2,4},{4,2},{6,0},{1,7},{3,5},{5,3},{7,1},{8,14},{10,12},{12... | collective-permute-start | bytes 24584 | tf_op jit(solution)/shard_map/ppermute | solution.py:73
  557.1 3.7 collective-permute-start.52
  563.9 15.7 %collective-permute-start.54 = (bf16[3,1024,256]{2,1,0:T(8,128)(2,1)S(1)}, bf16[3,1024,256]{2,1,0:T(8,128)(2,1)S(1)}, u32[]{:S(2)}, u32[]{:S(2)}) collective-permute-start(bf16[3,1024,256]{2,1,0:T(8,128)(2,1)S(1)} %pad_maximum_fusion.refs_0_.refs_1_), channel_id=1, source_target_pairs={{0,1},{1,0},{2,3},{3,2},{4,5},{5,4},{6,7},{7,6},{8,9},{9,8},{10,11... | collective-permute-start | bytes 4718600 | tf_op jit(solution)/shard_map/ppermute | solution.py:73
  564.1 7.6 %collective-permute-start.58 = (f32[4,2048]{1,0:T(4,128)S(1)}, f32[4,2048]{1,0:T(4,128)S(1)}, u32[]{:S(2)}, u32[]{:S(2)}) collective-permute-start(f32[4,2048]{1,0:T(4,128)S(1)} %maximum_dynamic-update-slice_fusion.1), channel_id=1, source_target_pairs={{0,8},{8,0},{16,24},{24,16},{1,9},{9,1},{17,25},{25,17},{2,10},{10... | collective-permute-start | bytes 98312 | tf_op jit(solution)/shard_map/ppermute | solution.py:73
  571.7 7.3 %collective-permute-start.59 = (f32[4,2048]{1,0:T(4,128)S(1)}, f32[4,2048]{1,0:T(4,128)S(1)}, u32[]{:S(2)}, u32[]{:S(2)}) collective-permute-start(f32[4,2048]{1,0:T(4,128)S(1)} %add.352), channel_id=1, source_target_pairs={{0,16},{8,24},{16,0},{24,8},{1,17},{9,25},{17,1},{25,9},{2,18},{10... | collective-permute-start | bytes 98312 | tf_op jit(solution)/shard_map/ppermute | solution.py:73
  592.4 24.8 %collective-permute-start.66 = (bf16[2,256,512]{2,1,0:T(8,128)(2,1)}, bf16[2,256,512]{2,1,0:T(8,128)(2,1)}, u32[]{:S(2)}, u32[]{:S(2)}) collective-permute-start(bf16[2,256,512]{2,1,0:T(8,128)(2,1)} %dynamic-slice_bitcast_fusion), channel_id=1, source_target_pairs={{0,24},{8,0},{16,8},{24,16},{1,25},{9,1},{17,9},{25,17},{2,26},{10... | collective-permute-start | bytes 1572872 | tf_op jit(solution)/shard_map/ppermute | solution.py:199
  597.3 30.9 %collective-permute-start.63 = (bf16[2,256,512]{2,1,0:T(8,128)(2,1)}, bf16[2,256,512]{2,1,0:T(8,128)(2,1)}, u32[]{:S(2)}, u32[]{:S(2)}) collective-permute-start(bf16[2,256,512]{2,1,0:T(8,128)(2,1)} %dynamic-slice_bitcast_fusion.1), channel_id=1, source_target_pairs={{0,24},{8,0},{16,8},{24,16},{1,25},{9,1},{17,9},{25,17},{2,26},{10... | collective-permute-start | bytes 1572872 | tf_op jit(solution)/shard_map/ppermute | solution.py:199
  598.5 4.0 collective-permute-start.61
  602.5 30.0 %collective-permute-start.62 = (f32[4,2048]{1,0:T(4,128)S(1)}, f32[4,2048]{1,0:T(4,128)S(1)}, u32[]{:S(2)}, u32[]{:S(2)}) collective-permute-start(f32[4,2048]{1,0:T(4,128)S(1)} %add.355), channel_id=1, source_target_pairs={{0,4},{2,6},{4,0},{6,2},{1,5},{3,7},{5,1},{7,3},{8,12},{10,14},{12... | collective-permute-start | bytes 98312 | tf_op jit(solution)/shard_map/ppermute | solution.py:73
  611.6 51.9 %collective-permute-start.55 = (bf16[256,1024]{1,0:T(8,128)(2,1)}, bf16[256,1024]{1,0:T(8,128)(2,1)}, u32[]{:S(2)}, u32[]{:S(2)}) collective-permute-start(bf16[256,1024]{1,0:T(8,128)(2,1)} %get-tuple-element.81), channel_id=1, source_target_pairs={{0,2},{2,0},{4,6},{6,4},{1,3},{3,1},{5,7},{7,5},{8,10},{10,8},{12,... | collective-permute-start | bytes 1572872 | tf_op jit(solution)/shard_map/ppermute | solution.py:73
  611.6 51.9 %collective-permute-start.56 = (bf16[256,1024]{1,0:T(8,128)(2,1)}, bf16[256,1024]{1,0:T(8,128)(2,1)}, u32[]{:S(2)}, u32[]{:S(2)}) collective-permute-start(bf16[256,1024]{1,0:T(8,128)(2,1)} %get-tuple-element.82), channel_id=1, source_target_pairs={{0,4},{2,6},{4,0},{6,2},{1,5},{3,7},{5,1},{7,3},{8,12},{10,14},{12... | collective-permute-start | bytes 1572872 | tf_op jit(solution)/shard_map/ppermute | solution.py:73
  617.2 46.3 %collective-permute-start.57 = (bf16[256,1024]{1,0:T(8,128)(2,1)}, bf16[256,1024]{1,0:T(8,128)(2,1)}, u32[]{:S(2)}, u32[]{:S(2)}) collective-permute-start(bf16[256,1024]{1,0:T(8,128)(2,1)} %get-tuple-element.83), channel_id=1, source_target_pairs={{0,6},{2,4},{4,2},{6,0},{1,7},{3,5},{5,3},{7,1},{8,14},{10,12},{12... | collective-permute-start | bytes 1572872 | tf_op jit(solution)/shard_map/ppermute | solution.py:73
  628.2 15.3 %collective-permute-start.67 = (bf16[2,256,512]{2,1,0:T(8,128)(2,1)S(1)}, bf16[2,256,512]{2,1,0:T(8,128)(2,1)S(1)}, u32[]{:S(2)}, u32[]{:S(2)}) collective-permute-start(bf16[2,256,512]{2,1,0:T(8,128)(2,1)S(1)} %fusion.25), channel_id=1, source_target_pairs={{0,24},{8,0},{16,8},{24,16},{1,25},{9,1},{17,9},{25,17},{2,26},{10... | collective-permute-start | bytes 1572872 | tf_op jit(solution)/shard_map/ppermute | solution.py:199
  632.6 27.2 %collective-permute-start.64 = (bf16[2,256,512]{2,1,0:T(8,128)(2,1)S(1)}, bf16[2,256,512]{2,1,0:T(8,128)(2,1)S(1)}, u32[]{:S(2)}, u32[]{:S(2)}) collective-permute-start(bf16[2,256,512]{2,1,0:T(8,128)(2,1)S(1)} %fusion.28), channel_id=1, source_target_pairs={{0,24},{8,0},{16,8},{24,16},{1,25},{9,1},{17,9},{25,17},{2,26},{10... | collective-permute-start | bytes 1572872 | tf_op jit(solution)/shard_map/ppermute | solution.py:199
  644.5 21.8 %collective-permute-start.68 = (bf16[2,256,512]{2,1,0:T(8,128)(2,1)}, bf16[2,256,512]{2,1,0:T(8,128)(2,1)}, u32[]{:S(2)}, u32[]{:S(2)}) collective-permute-start(bf16[2,256,512]{2,1,0:T(8,128)(2,1)} %fusion.26), channel_id=1, source_target_pairs={{0,24},{8,0},{16,8},{24,16},{1,25},{9,1},{17,9},{25,17},{2,26},{10... | collective-permute-start | bytes 1572872 | tf_op jit(solution)/shard_map/ppermute | solution.py:199
  663.4 12.7 %collective-permute-start.65 = (bf16[2,256,512]{2,1,0:T(8,128)(2,1)S(1)}, bf16[2,256,512]{2,1,0:T(8,128)(2,1)S(1)}, u32[]{:S(2)}, u32[]{:S(2)}) collective-permute-start(bf16[2,256,512]{2,1,0:T(8,128)(2,1)S(1)} %fusion.29), channel_id=1, source_target_pairs={{0,24},{8,0},{16,8},{24,16},{1,25},{9,1},{17,9},{25,17},{2,26},{10... | collective-permute-start | bytes 1572872 | tf_op jit(solution)/shard_map/ppermute | solution.py:199
  (86 other events, 563.1 us)
Sparse Core Ops, SparseCore 0:
  82.3 151.5 all-gather.2
  236.0 78.9 all-gather.4
  384.3 74.1 reduce-scatter.2
  460.9 155.2 reduce-scatter.4

commit v5 on v4

--- a/solution.py
+++ b/solution.py
@@ -421,14 +421,15 @@
     )[0]
 
 
-def narrow_back(own, other, pieces, far, kept, t, earlier=()):
-    count, part, columns = pieces.shape
+def narrow_back(own, other, parts, far, kept, t, earlier=()):
+    count, part, cut = parts[0].shape
     half = count // 2
     extent = own.shape[0]
     tiles = part // TILE
 
-    def body(c, x, y, mine, theirs, saved, out):
-        grad = mm(x[...], mine[0], NT) + mm(y[...], theirs[0], NT)
+    def body(c, x, y, a_mine, b_mine, a_theirs, b_theirs, saved, out):
+        grad = mm(x[:, :cut], a_mine[0], NT) + mm(x[:, cut:], b_mine[0], NT)
+        grad = grad + mm(y[:, :cut], a_theirs[0], NT) + mm(y[:, cut:], b_theirs[0], NT)
         gate = saved[0]
         sig = jax.nn.sigmoid(gate)
         out[0] = (grad * saved[1] * sig * (1.0 + gate * (1.0 - sig))).astype(jnp.bfloat16)
@@ -437,13 +438,13 @@
     return run(
         body,
         (tiles,),
-        [
-            whole(own),
-            whole(other),
-            (pieces, (1, TILE, columns), lambda i, c: (c[0] * half + t, i, 0)),
-            (far, (1, TILE, columns), lambda i, c: (t, i, 0)),
-            (kept, (2, extent, TILE), lambda i, c: (0, 0, i)),
-        ],
+        [whole(own), whole(other)]
+        + [
+            (block, (1, TILE, block.shape[2]), lambda i, c: (c[0] * half + t, i, 0))
+            for block in parts
+        ]
+        + [(block, (1, TILE, block.shape[2]), lambda i, c: (t, i, 0)) for block in far]
+        + [(kept, (2, extent, TILE), lambda i, c: (0, 0, i))],
         [((2, extent, part), jnp.bfloat16, (2, extent, TILE), lambda i, c: (0, 0, i))],
         earlier,
     )[0]
@@ -705,7 +706,8 @@
         tie(expand_low, entry_block).reshape(-1, expand_low.shape[2])
     )
     expand_block = expand_block.reshape((shards,) + expand_weight.shape)
-    reduce_pieces = gather_shards(reduce_low).reshape(4, -1, reduce_low.shape[1])
+    cut = reduce_low.shape[1] * 3 // 4
+    reduce_first = gather_shards(reduce_low[:, :cut])
     halves = range(2)
 
     row_size = lax.axis_size("row")
@@ -783,7 +785,16 @@
     kept, product = zip(*[widen(hidden_rows, expand_block, sent[t], t) for t in halves])
     product = list(product)
     product_other = [swap_col(value) for value in product]
-    second = scatter_rows(*narrow(product, product_other, reduce_pieces))
+    reduce_second = gather_shards(tie(reduce_low[:, cut:], reduce_first, *product_other))
+    reduce_parts = [
+        block.reshape(4, -1, block.shape[1]) for block in (reduce_first, reduce_second)
+    ]
+    main_own, *main_low = narrow(product, product_other, reduce_parts[0])
+    main_arrived = [swap(value, "row", k + 1) for k, value in enumerate(main_low)]
+    rest = narrow(product, product_other, reduce_parts[1], main_arrived)
+    for value in main_arrived:
+        main_own = main_own + value.astype(jnp.float32)
+    second = jnp.concatenate([main_own, scatter_rows(*rest)], 1)
     upstream = cotangent.astype(jnp.float32) * local_valid[:, None]
     scaled = upstream * post_gain[1]
     totals = feature_total(
@@ -796,12 +807,12 @@
     inner_sum = totals[1][:, None] * second_scale
     second_grad = (second_scale * (scaled - second_hat * inner_sum / D)).astype(jnp.bfloat16)
     second_rows = gather_rows(second_grad)
+    reduce_sum = narrow_weight([product], [product_other], [second_rows])
     second_other = swap_col(second_rows)
-    reduce_sum = narrow_weight([product], [product_other], [second_rows])
-    reduce_far = swap_col(take_half(reduce_pieces, 0, 1 - side))
+    reduce_far = [swap_col(take_half(part, 0, 1 - side)) for part in reduce_parts]
     gated_grad = [
         narrow_back(
-            second_rows, second_other, reduce_pieces, reduce_far, kept[t], t, [reduce_sum]
+            second_rows, second_other, reduce_parts, reduce_far, kept[t], t, [reduce_sum]
         )
         for t in halves
     ]

time: 694 us -> 688 us (level)
  waiting for transfers between devices: 338 us -> 317 us
  local copies, waits for them, and re-layouts: 59.1 us -> 66.3 us
    all_gather x2 -> x3, waiting for transfers between devices: 85.1 us -> 68.1 us  [gather_shards(): return lax.all_gather(shard, 'dp', axis=0, tiled=True)]
    ppermute x57 -> x61, waiting for transfers between devices: 178 us -> 171 us  [swap(): lax.ppermute(values, axis, [(i, i ^ distance) for i in range(lax.axis_siz...]
    unnamed x176 -> x230, local copies, waits for them, and re-layouts: 24.1 us -> 29.4 us
    ppermute x57 -> x61, starting transfers between devices: 47.8 us -> 51.9 us  [swap(): lax.ppermute(values, axis, [(i, i ^ distance) for i in range(lax.axis_siz...]
    pallas_call x19 -> x20, Pallas kernels: 126 us -> 129 us  [run(): pl.pallas_call(kernel, grid_spec=pltpu.PrefetchScalarGridSpec(num_scalar_...]
  transfers between devices with their start and end apart: 73 -> 78, of which waited for: 48 -> 52; matrix products, arithmetic and copies ran while one was open for 14% -> 15% of each run, Pallas kernels for 15% -> 16%
where the time goes in v5:
time: 688 us; the launch traced here: 682 us
  waiting for transfers between devices  317 us (46%)
  Pallas kernels  129 us (19%)
  starting transfers between devices  86.9 us (13%)
  local copies, waits for them, and re-layouts  66.3 us (10%)
  other arithmetic  46.4 us (7%)
  matrix products  20.5 us (3%)
  between operations  15.8 us (2%)
    ppermute x61, waiting for transfers between devices, swap(): lax.ppermute(values, axis, [(i, i ^ distance) for i in range(lax.axis_siz...  171 us
    pallas_call x20, Pallas kernels, run(): pl.pallas_call(kernel, grid_spec=pltpu.PrefetchScalarGridSpec(num_scalar_...  129 us
    all_gather x3, waiting for transfers between devices, gather_shards(): return lax.all_gather(shard, 'dp', axis=0, tiled=True)  68.1 us
    ppermute x61, starting transfers between devices, swap(): lax.ppermute(values, axis, [(i, i ^ distance) for i in range(lax.axis_siz...  51.9 us
    ppermute x6, waiting for transfers between devices, ring_gather(): shards = [lax.ppermute(shard, 'dp', pairs) for shard in shards]  37.7 us
    unnamed x230, local copies, waits for them, and re-layouts  29.4 us
    ppermute x6, waiting for transfers between devices, ring_scatter(): arrived = [lax.ppermute(total, 'dp', pairs) for total in totals]  23.9 us
    ppermute x6, starting transfers between devices, ring_gather(): shards = [lax.ppermute(shard, 'dp', pairs) for shard in shards]  22.7 us
  transfers between devices with their start and end apart: 78, of which 52 were waited for; matrix products, arithmetic and copies ran while one was open for 15% of the time, Pallas kernels for 16%

profile of v5, /device:TPU:0, one launch (start us, length us, event | category | flops | bytes accessed | tf_op | source)
XLA Modules:
  0.0 682.5 jit_solution(9401038063967917812)
XLA Ops:
  8.9 5.1 collective-permute-start.4
  18.5 7.7 %collective-permute-done.4 = bf16[512,512]{1,0:T(8,128)(2,1)S(1)} collective-permute-done((bf16[512,512]{1,0:T(8,128)(2,1)S(1)}, bf16[512,512]{1,0:T(8,128)(2,1)S(1)}, u32[]{:S(2)}, u32[]{:S(2)}) %collective-permute-start.4) | collective-permute-done | bytes 524320 | tf_op jit(solution)/shard_map/ppermute | solution.py:183
  26.3 4.3 collective-permute-start.6
  30.6 7.0 %collective-permute-done.5 = bf16[512,512]{1,0:T(8,128)(2,1)S(1)} collective-permute-done((bf16[512,512]{1,0:T(8,128)(2,1)S(1)}, bf16[512,512]{1,0:T(8,128)(2,1)S(1)}, u32[]{:S(2)}, u32[]{:S(2)}) %collective-permute-start.5) | collective-permute-done | bytes 524320 | tf_op jit(solution)/shard_map/ppermute | solution.py:183
  37.5 4.3 collective-permute-start.7
  41.8 3.8 convert_element_type.195.value
  48.8 4.3 collective-permute-start.8
  53.9 6.1 collective-permute-done.7
  60.0 4.3 collective-permute-start.9
  65.9 5.3 collective-permute-done.8
  72.1 9.3 %collective-permute-done.9 = bf16[512,512]{1,0:T(8,128)(2,1)S(1)} collective-permute-done((bf16[512,512]{1,0:T(8,128)(2,1)S(1)}, bf16[512,512]{1,0:T(8,128)(2,1)S(1)}, u32[]{:S(2)}, u32[]{:S(2)}) %collective-permute-start.9) | collective-permute-done | bytes 524320 | tf_op jit(solution)/shard_map/ppermute | solution.py:183
  86.2 9.8 %collective-permute-done = bf16[256,1024]{1,0:T(8,128)(2,1)S(1)} collective-permute-done((bf16[256,1024]{1,0:T(8,128)(2,1)S(1)}, bf16[256,1024]{1,0:T(8,128)(2,1)S(1)}, u32[]{:S(2)}, u32[]{:S(2)}) %collective-permute-start) | collective-permute-done | bytes 524320 | tf_op jit(solution)/shard_map/ppermute | solution.py:73
  105.7 7.1 %shard_map.345 = (f32[3,1024,256]{2,1,0:T(8,128)S(1)}, f32[3,1024,256]{2,1,0:T(8,128)}) custom-call(s32[1]{0:T(128)} %bitcast.c, bf16[1024,1024]{1,0:T(8,128)(2,1)S(1)} %constant_dynamic-update-slice_fusion.refs_0_, bf16[4,4,256,512]{3,2,1,0:T(8,128)(2,1)} %bitcast.11.refs_1_.refs_2_.refs_3_.refs_0_, ...), custom_call_target="tpu_custom_call" | custom-call | flops 1 | bytes 1 | tf_op jit(solution)/shard_map/pallas_call | solution.py:140
  116.2 3.1 multiply_cosine_fusion
  122.9 3.3 add.312
  162.9 9.0 %collective-permute-done.16 = bf16[256,1024]{1,0:T(8,128)(2,1)} collective-permute-done((bf16[256,1024]{1,0:T(8,128)(2,1)S(1)}, bf16[256,1024]{1,0:T(8,128)(2,1)}, u32[]{:S(2)}, u32[]{:S(2)}) %collective-permute-start.16) | collective-permute-done | bytes 524320 | tf_op jit(solution)/shard_map/ppermute | solution.py:73
  171.9 10.7 %collective-permute-done.17 = bf16[256,1024]{1,0:T(8,128)(2,1)} collective-permute-done((bf16[256,1024]{1,0:T(8,128)(2,1)S(1)}, bf16[256,1024]{1,0:T(8,128)(2,1)}, u32[]{:S(2)}, u32[]{:S(2)}) %collective-permute-start.17) | collective-permute-done | bytes 524320 | tf_op jit(solution)/shard_map/ppermute | solution.py:73
  187.9 12.0 %collective-permute-done.20 = bf16[256,1024]{1,0:T(8,128)(2,1)S(1)} collective-permute-done((bf16[256,1024]{1,0:T(8,128)(2,1)S(1)}, bf16[256,1024]{1,0:T(8,128)(2,1)S(1)}, u32[]{:S(2)}, u32[]{:S(2)}) %collective-permute-start.20) | collective-permute-done | bytes 524320 | tf_op jit(solution)/shard_map/ppermute | solution.py:73
  202.2 5.4 collective-permute-done.22
  208.6 25.3 %all-gather.4.cloned.1.call-done = bf16[2048,2048]{1,0:T(8,128)(2,1)} async-done(((bf16[512,2048]{1,0:T(8,128)(2,1)}), bf16[2048,2048]{1,0:T(8,128)(2,1)}) %all-gather.4.cloned.1.call-update) | async-done | bytes 8388624 | tf_op jit(solution)/shard_map/all_gather | solution.py:597
  233.9 3.8 shard_map.350
  237.8 3.8 shard_map.348
  242.1 5.3 shard_map.351
  247.5 5.3 shard_map.349
  254.9 42.9 %all-gather.6.cloned.1.call-done.refs_0_ = bf16[2048,768]{1,0:T(8,128)(2,1)} async-done(((bf16[512,768]{1,0:T(8,128)(2,1)}), bf16[2048,768]{1,0:T(8,128)(2,1)}) %all-gather.6.cloned.1.call-update) | async-done | bytes 3145744 | tf_op jit(solution)/shard_map/all_gather | solution.py:597
  300.1 6.2 shard_map.352
  311.3 8.0 %collective-permute-done.28.refs_6_ = bf16[256,768]{1,0:T(8,128)(2,1)S(1)} collective-permute-done((bf16[256,768]{1,0:T(8,128)(2,1)S(1)}, bf16[256,768]{1,0:T(8,128)(2,1)S(1)}, u32[]{:S(2)}, u32[]{:S(2)}) %collective-permute-start.28) | collective-permute-done | bytes 393248 | tf_op jit(solution)/shard_map/ppermute | solution.py:73
  319.2 8.4 %collective-permute-done.29.refs_7_ = bf16[256,768]{1,0:T(8,128)(2,1)S(1)} collective-permute-done((bf16[256,768]{1,0:T(8,128)(2,1)S(1)}, bf16[256,768]{1,0:T(8,128)(2,1)S(1)}, u32[]{:S(2)}, u32[]{:S(2)}) %collective-permute-start.29) | collective-permute-done | bytes 393248 | tf_op jit(solution)/shard_map/ppermute | solution.py:73
  331.1 3.5 shard_map.354
  346.9 11.8 %collective-permute-done.35 = bf16[256,1024]{1,0:T(8,128)(2,1)S(1)} collective-permute-done((bf16[256,1024]{1,0:T(8,128)(2,1)S(1)}, bf16[256,1024]{1,0:T(8,128)(2,1)S(1)}, u32[]{:S(2)}, u32[]{:S(2)}) %collective-permute-start.35) | collective-permute-done | bytes 524320 | tf_op jit(solution)/shard_map/ppermute | solution.py:73
  361.2 5.2 collective-permute-done.37
  368.6 8.8 %shard_map.355.refs_7_ = bf16[4,512,1024]{2,1,0:T(8,128)(2,1)} custom-call(s32[1]{0:T(128)} %bitcast.c, bf16[1024,512]{1,0:T(8,128)(2,1)} %get-tuple-element.72.refs_0_, bf16[1024,512]{1,0:T(8,128)(2,1)} %get-tuple-element.73.refs_1_, bf16[1024,512]{1,0:T(8,128)(2,1)} %collective-permute-done.26.refs_2_.refs_1_, bf16[1024,512]{1,0:T(8,128)(2,1)S(1)} %copy-done.4, ...), custom_call_target="tpu_custom_call" | custom-call | flops 1 | bytes 1 | tf_op jit(solution)/shard_map/pallas_call | solution.py:140
  379.8 4.1 collective-permute-done.40.refs_4_
  384.7 6.5 shard_map.357.refs_1_.refs_2_
  391.4 6.6 shard_map.356.refs_0_.refs_1_
  398.2 4.1 collective-permute-done.42.refs_2_.refs_3_
  403.6 13.5 %shard_map.358 = (f32[256,1024]{1,0:T(8,128)S(1)}, bf16[256,1024]{1,0:T(8,128)(2,1)S(1)}, bf16[256,1024]{1,0:T(8,128)(2,1)S(1)}, bf16[256,1024]{1,0:T(8,128)(2,1)S(1)}) custom-call(s32[1]{0:T(128)} %bitcast.c, bf16[2,1024,512]{2,1,0:T(8,128)(2,1)S(1)} %shard_map.356.refs_0_.refs_1_, bf16[2,1024,512]{2,1,0:T(8,128)(2,1)} %copy-done.1, ...), custom_call_target="tpu_custom_call" | custom-call | flops 1 | bytes 1 | tf_op jit(solution)/shard_map/pallas_call | solution.py:140
  418.7 16.9 %shard_map.363.value = bf16[4,2,256,2048]{3,2,1,0:T(8,128)(2,1)} custom-call(s32[1]{0:T(128)} %bitcast.c, bf16[1024,1024]{1,0:T(8,128)(2,1)S(1)} %constant_dynamic-update-slice_fusion.5.refs_0_, bf16[2,1024,512]{2,1,0:T(8,128)(2,1)S(1)} %shard_map.356.refs_0_.refs_1_, bf16[2,1024,512]{2,1,0:T(8,128)(2,1)} %copy-done.1, bf16[2,1024,512]{2,1,0:T(8,128)(2,1)} %copy-done.58, ...), custom_call_target="tpu_custom_call" | custom-call | flops 1 | bytes 1 | tf_op jit(solution)/shard_map/pallas_call | solution.py:140
  436.5 16.5 %reduce-scatter.3.cloned.1.call-done.refs_0_ = bf16[512,1024]{1,0:T(8,128)(2,1)} async-done(((bf16[2048,1024]{1,0:T(8,128)(2,1)}), bf16[512,1024]{1,0:T(8,128)(2,1)}) %reduce-scatter.3.cloned.1.call-update) | async-done | bytes 1048592 | tf_op jit(solution)/shard_map/reduce_scatter | solution.py:601
  457.5 11.3 %collective-permute-done.44 = bf16[256,1024]{1,0:T(8,128)(2,1)S(1)} collective-permute-done((bf16[256,1024]{1,0:T(8,128)(2,1)S(1)}, bf16[256,1024]{1,0:T(8,128)(2,1)S(1)}, u32[]{:S(2)}, u32[]{:S(2)}) %collective-permute-start.44) | collective-permute-done | bytes 524320 | tf_op jit(solution)/shard_map/ppermute | solution.py:73
  468.8 11.3 %collective-permute-done.45 = bf16[256,1024]{1,0:T(8,128)(2,1)S(1)} collective-permute-done((bf16[256,1024]{1,0:T(8,128)(2,1)S(1)}, bf16[256,1024]{1,0:T(8,128)(2,1)S(1)}, u32[]{:S(2)}, u32[]{:S(2)}) %collective-permute-start.45) | collective-permute-done | bytes 524320 | tf_op jit(solution)/shard_map/ppermute | solution.py:73
  480.1 3.6 multiply_reduce_fusion.5
  487.2 12.0 %collective-permute-done.48 = bf16[256,1024]{1,0:T(8,128)(2,1)S(1)} collective-permute-done((bf16[256,1024]{1,0:T(8,128)(2,1)S(1)}, bf16[256,1024]{1,0:T(8,128)(2,1)S(1)}, u32[]{:S(2)}, u32[]{:S(2)}) %collective-permute-start.48) | collective-permute-done | bytes 524320 | tf_op jit(solution)/shard_map/ppermute | solution.py:73
  501.6 5.4 collective-permute-done.50
  510.6 2.7 collective-permute-done.53.refs_3_
  516.7 3.7 multiply_reduce_fusion.1
  534.8 3.0 reshape.633
  540.8 2.8 fusion.4
  545.2 4.2 fusion.18
  560.0 6.0 collective-permute-done.62
  566.9 6.5 collective-permute-done.63
  574.0 11.0 %shard_map.361 = (bf16[4,2,256,512]{3,2,1,0:T(8,128)(2,1)}, bf16[4,2,256,512]{3,2,1,0:T(8,128)(2,1)}) custom-call(s32[1]{0:T(128)} %bitcast.c, bf16[1024,1024]{1,0:T(8,128)(2,1)} %copy-done.6, bf16[3,1024,256]{2,1,0:T(8,128)(2,1)S(1)} %pad_maximum_fusion.refs_0_.refs_1_, bf16[3,1024,256]{2,1,0:T(8,128)(2,1)S(1)} %collective-permute-done.58.refs_1_.refs_2_, ...), custom_call_target="tpu_custom_call" | custom-call | flops 1 | bytes 1 | tf_op jit(solution)/shard_map/pallas_call | solution.py:140
  586.8 3.0 collective-permute-start.70
  598.4 6.7 shard_map.360
  607.9 3.7 collective-permute-done.70
  613.9 8.7 %collective-permute-done.67 = bf16[2,256,512]{2,1,0:T(8,128)(2,1)} collective-permute-done((bf16[2,256,512]{2,1,0:T(8,128)(2,1)}, bf16[2,256,512]{2,1,0:T(8,128)(2,1)}, u32[]{:S(2)}, u32[]{:S(2)}) %collective-permute-start.67) | collective-permute-done | bytes 524320 | tf_op jit(solution)/shard_map/ppermute | solution.py:199
  622.6 3.0 collective-permute-start.71
  629.5 5.2 shard_map.370
  634.7 3.2 collective-permute-done.71
  638.8 4.3 collective-permute-start.72
  644.7 9.4 %shard_map.365 = (f32[2,256,2048]{2,1,0:T(8,128)}, f32[2,256,2048]{2,1,0:T(8,128)}, f32[2,256,2048]{2,1,0:T(8,128)}, f32[2,256,2048]{2,1,0:T(8,128)}) custom-call(s32[1]{0:T(128)} %bitcast.c, bf16[512,2048]{1,0:T(8,128)(2,1)S(1)} %copy-done.19, f32[2,256,2048]{2,1,0:T(8,128)} %refs_1_.4, f32[2,256,2048]{2,1,0:T(8,128)} %refs_2_.4, f32[2,256,2048]{2,1,0:T(8,128)} %refs_3_.4), custom_call_target="tpu_custom_call" | custom-call | flops 1 | bytes 1 | tf_op jit(solution)/shard_map/pallas_call | solution.py:140
  658.0 2.7 add_add_fusion
  662.2 8.3 %collective-permute-done.69 = bf16[2,256,512]{2,1,0:T(8,128)(2,1)S(1)} collective-permute-done((bf16[2,256,512]{2,1,0:T(8,128)(2,1)S(1)}, bf16[2,256,512]{2,1,0:T(8,128)(2,1)S(1)}, u32[]{:S(2)}, u32[]{:S(2)}) %collective-permute-start.69) | collective-permute-done | bytes 524320 | tf_op jit(solution)/shard_map/ppermute | solution.py:199
  670.8 3.3 shard_map.368
  (494 shorter events, 193.6 us)
Async XLA Ops:
  7.2 226.7 %all-gather.4.cloned.1.call-start = ((), (), s32[]{:S(2)}) async-start(), calls=%async_computation.2 | async-start | bytes 10485760 | tf_op jit(solution)/shard_map/all_gather | solution.py:597
  8.9 17.4 %collective-permute-start.4 = (bf16[512,512]{1,0:T(8,128)(2,1)S(1)}, bf16[512,512]{1,0:T(8,128)(2,1)S(1)}, u32[]{:S(2)}, u32[]{:S(2)}) collective-permute-start(bf16[512,512]{1,0:T(8,128)(2,1)S(1)} %bitcast.156), channel_id=1, source_target_pairs={{0,24},{8,0},{16,8},{24,16},{1,25},{9,1},{17,9},{25,17},{2,26},{10... | collective-permute-start | bytes 1572872 | tf_op jit(solution)/shard_map/ppermute | solution.py:183
  18.1 19.4 %collective-permute-start.5 = (bf16[512,512]{1,0:T(8,128)(2,1)S(1)}, bf16[512,512]{1,0:T(8,128)(2,1)S(1)}, u32[]{:S(2)}, u32[]{:S(2)}) collective-permute-start(bf16[512,512]{1,0:T(8,128)(2,1)S(1)} %get-tuple-element.134), channel_id=1, source_target_pairs={{0,24},{8,0},{16,8},{24,16},{1,25},{9,1},{17,9},{25,17},{2,26},{10... | collective-permute-start | bytes 1572872 | tf_op jit(solution)/shard_map/ppermute | solution.py:183
  26.3 22.5 %collective-permute-start.6 = (bf16[512,512]{1,0:T(8,128)(2,1)S(1)}, bf16[512,512]{1,0:T(8,128)(2,1)S(1)}, u32[]{:S(2)}, u32[]{:S(2)}) collective-permute-start(bf16[512,512]{1,0:T(8,128)(2,1)S(1)} %collective-permute-done.4), channel_id=1, source_target_pairs={{0,24},{8,0},{16,8},{24,16},{1,25},{9,1},{17,9},{25,17},{2,26},{10... | collective-permute-start | bytes 1572872 | tf_op jit(solution)/shard_map/ppermute | solution.py:183
  37.5 22.5 %collective-permute-start.7 = (bf16[512,512]{1,0:T(8,128)(2,1)S(1)}, bf16[512,512]{1,0:T(8,128)(2,1)S(1)}, u32[]{:S(2)}, u32[]{:S(2)}) collective-permute-start(bf16[512,512]{1,0:T(8,128)(2,1)S(1)} %collective-permute-done.5), channel_id=1, source_target_pairs={{0,24},{8,0},{16,8},{24,16},{1,25},{9,1},{17,9},{25,17},{2,26},{10... | collective-permute-start | bytes 1572872 | tf_op jit(solution)/shard_map/ppermute | solution.py:183
  48.8 22.5 %collective-permute-start.8 = (bf16[512,512]{1,0:T(8,128)(2,1)S(1)}, bf16[512,512]{1,0:T(8,128)(2,1)S(1)}, u32[]{:S(2)}, u32[]{:S(2)}) collective-permute-start(bf16[512,512]{1,0:T(8,128)(2,1)S(1)} %collective-permute-done.6), channel_id=1, source_target_pairs={{0,24},{8,0},{16,8},{24,16},{1,25},{9,1},{17,9},{25,17},{2,26},{10... | collective-permute-start | bytes 1572872 | tf_op jit(solution)/shard_map/ppermute | solution.py:183
  60.0 21.3 %collective-permute-start.9 = (bf16[512,512]{1,0:T(8,128)(2,1)S(1)}, bf16[512,512]{1,0:T(8,128)(2,1)S(1)}, u32[]{:S(2)}, u32[]{:S(2)}) collective-permute-start(bf16[512,512]{1,0:T(8,128)(2,1)S(1)} %collective-permute-done.7), channel_id=1, source_target_pairs={{0,24},{8,0},{16,8},{24,16},{1,25},{9,1},{17,9},{25,17},{2,26},{10... | collective-permute-start | bytes 1572872 | tf_op jit(solution)/shard_map/ppermute | solution.py:183
  82.2 215.6 %all-gather.6.cloned.1.call-start = ((), (), s32[]{:S(2)}) async-start(), calls=%async_computation.3 | async-start | bytes 3932160 | tf_op jit(solution)/shard_map/all_gather | solution.py:597
  83.2 12.8 %collective-permute-start = (bf16[256,1024]{1,0:T(8,128)(2,1)S(1)}, bf16[256,1024]{1,0:T(8,128)(2,1)S(1)}, u32[]{:S(2)}, u32[]{:S(2)}) collective-permute-start(bf16[256,1024]{1,0:T(8,128)(2,1)S(1)} %copy-done.63), channel_id=1, source_target_pairs={{0,2},{2,0},{4,6},{6,4},{1,3},{3,1},{5,7},{7,5},{8,10},{10,8},{12,... | collective-permute-start | bytes 1572872 | tf_op jit(solution)/shard_map/ppermute | solution.py:73
  84.7 13.6 %collective-permute-start.1 = (bf16[256,1024]{1,0:T(8,128)(2,1)S(1)}, bf16[256,1024]{1,0:T(8,128)(2,1)}, u32[]{:S(2)}, u32[]{:S(2)}) collective-permute-start(bf16[256,1024]{1,0:T(8,128)(2,1)S(1)} %copy-done.63), channel_id=1, source_target_pairs={{0,4},{2,6},{4,0},{6,2},{1,5},{3,7},{5,1},{7,3},{8,12},{10,14},{12... | collective-permute-start | bytes 1572872 | tf_op jit(solution)/shard_map/ppermute | solution.py:73
  96.7 6.6 collective-permute-start.2
  99.2 6.4 collective-permute-start.3
  114.5 6.7 collective-permute-start.10
  128.0 9.5 %collective-permute-start.14 = (f32[2,4,256]{2,1,0:T(4,128)S(1)}, f32[2,4,256]{2,1,0:T(4,128)S(1)}, u32[]{:S(2)}, u32[]{:S(2)}) collective-permute-start(f32[2,4,256]{2,1,0:T(4,128)S(1)} %reshape.627), channel_id=1, source_target_pairs={{0,6},{2,4},{4,2},{6,0},{1,7},{3,5},{5,3},{7,1},{8,14},{10,12},{12... | collective-permute-start | bytes 24584 | tf_op jit(solution)/shard_map/ppermute | solution.py:73
  156.9 14.9 %collective-permute-start.16 = (bf16[256,1024]{1,0:T(8,128)(2,1)S(1)}, bf16[256,1024]{1,0:T(8,128)(2,1)}, u32[]{:S(2)}, u32[]{:S(2)}) collective-permute-start(bf16[256,1024]{1,0:T(8,128)(2,1)S(1)} %get-tuple-element.69), channel_id=1, source_target_pairs={{0,2},{2,0},{4,6},{6,4},{1,3},{3,1},{5,7},{7,5},{8,10},{10,8},{12,... | collective-permute-start | bytes 1572872 | tf_op jit(solution)/shard_map/ppermute | solution.py:73
  157.5 25.0 %collective-permute-start.17 = (bf16[256,1024]{1,0:T(8,128)(2,1)S(1)}, bf16[256,1024]{1,0:T(8,128)(2,1)}, u32[]{:S(2)}, u32[]{:S(2)}) collective-permute-start(bf16[256,1024]{1,0:T(8,128)(2,1)S(1)} %get-tuple-element.70), channel_id=1, source_target_pairs={{0,4},{2,6},{4,0},{6,2},{1,5},{3,7},{5,1},{7,3},{8,12},{10,14},{12... | collective-permute-start | bytes 1572872 | tf_op jit(solution)/shard_map/ppermute | solution.py:73
  158.1 24.4 %collective-permute-start.18 = (bf16[256,1024]{1,0:T(8,128)(2,1)S(1)}, bf16[256,1024]{1,0:T(8,128)(2,1)}, u32[]{:S(2)}, u32[]{:S(2)}) collective-permute-start(bf16[256,1024]{1,0:T(8,128)(2,1)S(1)} %get-tuple-element.71), channel_id=1, source_target_pairs={{0,6},{2,4},{4,2},{6,0},{1,7},{3,5},{5,3},{7,1},{8,14},{10,12},{12... | collective-permute-start | bytes 1572872 | tf_op jit(solution)/shard_map/ppermute | solution.py:73
  162.8 166.3 %all-gather.8.cloned.1.call-start = ((), (), s32[]{:S(2)}) async-start(), calls=%async_computation.4 | async-start | bytes 1310720 | tf_op jit(solution)/shard_map/all_gather | solution.py:597
  185.8 14.1 %collective-permute-start.20 = (bf16[256,1024]{1,0:T(8,128)(2,1)S(1)}, bf16[256,1024]{1,0:T(8,128)(2,1)S(1)}, u32[]{:S(2)}, u32[]{:S(2)}) collective-permute-start(bf16[256,1024]{1,0:T(8,128)(2,1)S(1)} %get-tuple-element.130), channel_id=1, source_target_pairs={{0,2},{2,0},{4,6},{6,4},{1,3},{3,1},{5,7},{7,5},{8,10},{10,8},{12,... | collective-permute-start | bytes 1572872 | tf_op jit(solution)/shard_map/ppermute | solution.py:73
  187.3 13.8 %collective-permute-start.21 = (bf16[256,1024]{1,0:T(8,128)(2,1)S(1)}, bf16[256,1024]{1,0:T(8,128)(2,1)S(1)}, u32[]{:S(2)}, u32[]{:S(2)}) collective-permute-start(bf16[256,1024]{1,0:T(8,128)(2,1)S(1)} %get-tuple-element.130), channel_id=1, source_target_pairs={{0,4},{2,6},{4,0},{6,2},{1,5},{3,7},{5,1},{7,3},{8,12},{10,14},{12... | collective-permute-start | bytes 1572872 | tf_op jit(solution)/shard_map/ppermute | solution.py:73
  199.9 7.7 %collective-permute-start.22 = (bf16[128,1024]{1,0:T(8,128)(2,1)S(1)}, bf16[128,1024]{1,0:T(8,128)(2,1)S(1)}, u32[]{:S(2)}, u32[]{:S(2)}) collective-permute-start(bf16[128,1024]{1,0:T(8,128)(2,1)S(1)} %slice.346), channel_id=1, source_target_pairs={{0,4},{2,6},{4,0},{6,2},{1,5},{3,7},{5,1},{7,3},{8,12},{10,14},{12... | collective-permute-start | bytes 786440 | tf_op jit(solution)/shard_map/ppermute | solution.py:73
  201.1 7.5 %collective-permute-start.23 = (bf16[128,1024]{1,0:T(8,128)(2,1)S(1)}, bf16[128,1024]{1,0:T(8,128)(2,1)S(1)}, u32[]{:S(2)}, u32[]{:S(2)}) collective-permute-start(bf16[128,1024]{1,0:T(8,128)(2,1)S(1)} %slice.347), channel_id=1, source_target_pairs={{0,2},{2,0},{4,6},{6,4},{1,3},{3,1},{5,7},{7,5},{8,10},{10,8},{12,... | collective-permute-start | bytes 786440 | tf_op jit(solution)/shard_map/ppermute | solution.py:73
  237.7 4.4 collective-permute-start.25
  241.5 6.0 collective-permute-start.24
  247.4 50.4 %collective-permute-start.27 = (bf16[1024,512]{1,0:T(8,128)(2,1)}, bf16[1024,512]{1,0:T(8,128)(2,1)S(1)}, u32[]{:S(2)}, u32[]{:S(2)}) collective-permute-start(bf16[1024,512]{1,0:T(8,128)(2,1)} %get-tuple-element.73.refs_1_), channel_id=1, source_target_pairs={{0,1},{1,0},{2,3},{3,2},{4,5},{5,4},{6,7},{7,6},{8,9},{9,8},{10,11... | collective-permute-start | bytes 3145736 | tf_op jit(solution)/shard_map/ppermute | solution.py:73
  252.8 45.0 %collective-permute-start.26 = (bf16[1024,512]{1,0:T(8,128)(2,1)}, bf16[1024,512]{1,0:T(8,128)(2,1)}, u32[]{:S(2)}, u32[]{:S(2)}) collective-permute-start(bf16[1024,512]{1,0:T(8,128)(2,1)} %get-tuple-element.72.refs_0_), channel_id=1, source_target_pairs={{0,1},{1,0},{2,3},{3,2},{4,5},{5,4},{6,7},{7,6},{8,9},{9,8},{10,11... | collective-permute-start | bytes 3145736 | tf_op jit(solution)/shard_map/ppermute | solution.py:73
  298.8 154.1 %reduce-scatter.3.cloned.1.call-start = ((), (), s32[]{:S(2)}) async-start(), calls=%async_computation.5 | async-start | bytes 5242880 | tf_op jit(solution)/shard_map/reduce_scatter | solution.py:601
  307.2 12.0 %collective-permute-start.28 = (bf16[256,768]{1,0:T(8,128)(2,1)S(1)}, bf16[256,768]{1,0:T(8,128)(2,1)S(1)}, u32[]{:S(2)}, u32[]{:S(2)}) collective-permute-start(bf16[256,768]{1,0:T(8,128)(2,1)S(1)} %get-tuple-element.75), channel_id=1, source_target_pairs={{0,2},{2,0},{4,6},{6,4},{1,3},{3,1},{5,7},{7,5},{8,10},{10,8},{12,... | collective-permute-start | bytes 1179656 | tf_op jit(solution)/shard_map/ppermute | solution.py:73
  308.7 19.0 %collective-permute-start.29 = (bf16[256,768]{1,0:T(8,128)(2,1)S(1)}, bf16[256,768]{1,0:T(8,128)(2,1)S(1)}, u32[]{:S(2)}, u32[]{:S(2)}) collective-permute-start(bf16[256,768]{1,0:T(8,128)(2,1)S(1)} %get-tuple-element.76), channel_id=1, source_target_pairs={{0,4},{2,6},{4,0},{6,2},{1,5},{3,7},{5,1},{7,3},{8,12},{10,14},{12... | collective-permute-start | bytes 1179656 | tf_op jit(solution)/shard_map/ppermute | solution.py:73
  310.2 18.2 %collective-permute-start.30 = (bf16[256,768]{1,0:T(8,128)(2,1)S(1)}, bf16[256,768]{1,0:T(8,128)(2,1)S(1)}, u32[]{:S(2)}, u32[]{:S(2)}) collective-permute-start(bf16[256,768]{1,0:T(8,128)(2,1)S(1)} %get-tuple-element.77), channel_id=1, source_target_pairs={{0,6},{2,4},{4,2},{6,0},{1,7},{3,5},{5,3},{7,1},{8,14},{10,12},{12... | collective-permute-start | bytes 1179656 | tf_op jit(solution)/shard_map/ppermute | solution.py:73
  334.6 5.8 collective-permute-start.31
  335.1 6.1 collective-permute-start.32
  336.7 5.9 collective-permute-start.33
  344.7 14.1 %collective-permute-start.35 = (bf16[256,1024]{1,0:T(8,128)(2,1)S(1)}, bf16[256,1024]{1,0:T(8,128)(2,1)S(1)}, u32[]{:S(2)}, u32[]{:S(2)}) collective-permute-start(bf16[256,1024]{1,0:T(8,128)(2,1)S(1)} %get-tuple-element.128), channel_id=1, source_target_pairs={{0,2},{2,0},{4,6},{6,4},{1,3},{3,1},{5,7},{7,5},{8,10},{10,8},{12,... | collective-permute-start | bytes 1572872 | tf_op jit(solution)/shard_map/ppermute | solution.py:73
  346.2 13.7 %collective-permute-start.36 = (bf16[256,1024]{1,0:T(8,128)(2,1)S(1)}, bf16[256,1024]{1,0:T(8,128)(2,1)S(1)}, u32[]{:S(2)}, u32[]{:S(2)}) collective-permute-start(bf16[256,1024]{1,0:T(8,128)(2,1)S(1)} %get-tuple-element.128), channel_id=1, source_target_pairs={{0,4},{2,6},{4,0},{6,2},{1,5},{3,7},{5,1},{7,3},{8,12},{10,14},{12... | collective-permute-start | bytes 1572872 | tf_op jit(solution)/shard_map/ppermute | solution.py:73
  358.8 7.6 %collective-permute-start.37 = (bf16[128,1024]{1,0:T(8,128)(2,1)S(1)}, bf16[128,1024]{1,0:T(8,128)(2,1)S(1)}, u32[]{:S(2)}, u32[]{:S(2)}) collective-permute-start(bf16[128,1024]{1,0:T(8,128)(2,1)S(1)} %slice.352), channel_id=1, source_target_pairs={{0,4},{2,6},{4,0},{6,2},{1,5},{3,7},{5,1},{7,3},{8,12},{10,14},{12... | collective-permute-start | bytes 786440 | tf_op jit(solution)/shard_map/ppermute | solution.py:73
  360.0 7.3 %collective-permute-start.38 = (bf16[128,1024]{1,0:T(8,128)(2,1)S(1)}, bf16[128,1024]{1,0:T(8,128)(2,1)S(1)}, u32[]{:S(2)}, u32[]{:S(2)}) collective-permute-start(bf16[128,1024]{1,0:T(8,128)(2,1)S(1)} %slice.353), channel_id=1, source_target_pairs={{0,2},{2,0},{4,6},{6,4},{1,3},{3,1},{5,7},{7,5},{8,10},{10,8},{12,... | collective-permute-start | bytes 786440 | tf_op jit(solution)/shard_map/ppermute | solution.py:73
  377.4 265.7 %reduce-scatter.5.cloned.1.call-start = ((), (), s32[]{:S(2)}) async-start(), calls=%async_computation.6 | async-start | bytes 10485760 | tf_op jit(solution)/shard_map/reduce_scatter | solution.py:601
  377.5 7.2 %collective-permute-start.39 = (bf16[1024,1024]{1,0:T(8,128)(2,1)}, bf16[1024,1024]{1,0:T(8,128)(2,1)}, u32[]{:S(2)}, u32[]{:S(2)}) collective-permute-start(bf16[1024,1024]{1,0:T(8,128)(2,1)} %copy-done.45), channel_id=1, source_target_pairs={{0,1},{1,0},{2,3},{3,2},{4,5},{5,4},{6,7},{7,6},{8,9},{9,8},{10,11... | collective-permute-start | bytes 6291464 | tf_op jit(solution)/shard_map/ppermute | solution.py:73
  379.1 4.8 collective-permute-start.40
  379.7 5.0 collective-permute-start.41
  391.2 7.0 %collective-permute-start.43 = (bf16[2,1024,512]{2,1,0:T(8,128)(2,1)S(1)}, bf16[2,1024,512]{2,1,0:T(8,128)(2,1)S(1)}, u32[]{:S(2)}, u32[]{:S(2)}) collective-permute-start(bf16[2,1024,512]{2,1,0:T(8,128)(2,1)S(1)} %shard_map.357.refs_1_.refs_2_), channel_id=1, source_target_pairs={{0,1},{1,0},{2,3},{3,2},{4,5},{5,4},{6,7},{7,6},{8,9},{9,8},{10,11... | collective-permute-start | bytes 6291464 | tf_op jit(solution)/shard_map/ppermute | solution.py:73
  454.0 14.8 %collective-permute-start.44 = (bf16[256,1024]{1,0:T(8,128)(2,1)S(1)}, bf16[256,1024]{1,0:T(8,128)(2,1)S(1)}, u32[]{:S(2)}, u32[]{:S(2)}) collective-permute-start(bf16[256,1024]{1,0:T(8,128)(2,1)S(1)} %copy-done.31), channel_id=1, source_target_pairs={{0,2},{2,0},{4,6},{6,4},{1,3},{3,1},{5,7},{7,5},{8,10},{10,8},{12,... | collective-permute-start | bytes 1572872 | tf_op jit(solution)/shard_map/ppermute | solution.py:73
  455.4 24.7 %collective-permute-start.45 = (bf16[256,1024]{1,0:T(8,128)(2,1)S(1)}, bf16[256,1024]{1,0:T(8,128)(2,1)S(1)}, u32[]{:S(2)}, u32[]{:S(2)}) collective-permute-start(bf16[256,1024]{1,0:T(8,128)(2,1)S(1)} %copy-done.37), channel_id=1, source_target_pairs={{0,4},{2,6},{4,0},{6,2},{1,5},{3,7},{5,1},{7,3},{8,12},{10,14},{12... | collective-permute-start | bytes 1572872 | tf_op jit(solution)/shard_map/ppermute | solution.py:73
  456.9 23.2 %collective-permute-start.46 = (bf16[256,1024]{1,0:T(8,128)(2,1)S(1)}, bf16[256,1024]{1,0:T(8,128)(2,1)S(1)}, u32[]{:S(2)}, u32[]{:S(2)}) collective-permute-start(bf16[256,1024]{1,0:T(8,128)(2,1)S(1)} %copy-done.35), channel_id=1, source_target_pairs={{0,6},{2,4},{4,2},{6,0},{1,7},{3,5},{5,3},{7,1},{8,14},{10,12},{12... | collective-permute-start | bytes 1572872 | tf_op jit(solution)/shard_map/ppermute | solution.py:73
  485.1 14.1 %collective-permute-start.48 = (bf16[256,1024]{1,0:T(8,128)(2,1)S(1)}, bf16[256,1024]{1,0:T(8,128)(2,1)S(1)}, u32[]{:S(2)}, u32[]{:S(2)}) collective-permute-start(bf16[256,1024]{1,0:T(8,128)(2,1)S(1)} %get-tuple-element.125), channel_id=1, source_target_pairs={{0,2},{2,0},{4,6},{6,4},{1,3},{3,1},{5,7},{7,5},{8,10},{10,8},{12,... | collective-permute-start | bytes 1572872 | tf_op jit(solution)/shard_map/ppermute | solution.py:73
  486.4 14.4 %collective-permute-start.49 = (bf16[256,1024]{1,0:T(8,128)(2,1)S(1)}, bf16[256,1024]{1,0:T(8,128)(2,1)S(1)}, u32[]{:S(2)}, u32[]{:S(2)}) collective-permute-start(bf16[256,1024]{1,0:T(8,128)(2,1)S(1)} %get-tuple-element.125), channel_id=1, source_target_pairs={{0,4},{2,6},{4,0},{6,2},{1,5},{3,7},{5,1},{7,3},{8,12},{10,14},{12... | collective-permute-start | bytes 1572872 | tf_op jit(solution)/shard_map/ppermute | solution.py:73
  499.2 7.7 %collective-permute-start.50 = (bf16[128,1024]{1,0:T(8,128)(2,1)S(1)}, bf16[128,1024]{1,0:T(8,128)(2,1)S(1)}, u32[]{:S(2)}, u32[]{:S(2)}) collective-permute-start(bf16[128,1024]{1,0:T(8,128)(2,1)S(1)} %slice.354), channel_id=1, source_target_pairs={{0,4},{2,6},{4,0},{6,2},{1,5},{3,7},{5,1},{7,3},{8,12},{10,14},{12... | collective-permute-start | bytes 786440 | tf_op jit(solution)/shard_map/ppermute | solution.py:73
  500.8 7.5 %collective-permute-start.51 = (bf16[128,1024]{1,0:T(8,128)(2,1)S(1)}, bf16[128,1024]{1,0:T(8,128)(2,1)S(1)}, u32[]{:S(2)}, u32[]{:S(2)}) collective-permute-start(bf16[128,1024]{1,0:T(8,128)(2,1)S(1)} %slice.355), channel_id=1, source_target_pairs={{0,2},{2,0},{4,6},{6,4},{1,3},{3,1},{5,7},{7,5},{8,10},{10,8},{12,... | collective-permute-start | bytes 786440 | tf_op jit(solution)/shard_map/ppermute | solution.py:73
  508.3 5.0 collective-permute-start.52
  543.6 9.8 %collective-permute-start.57 = (f32[2,4,256]{2,1,0:T(4,128)S(1)}, f32[2,4,256]{2,1,0:T(4,128)S(1)}, u32[]{:S(2)}, u32[]{:S(2)}) collective-permute-start(f32[2,4,256]{2,1,0:T(4,128)S(1)} %reshape.634), channel_id=1, source_target_pairs={{0,6},{2,4},{4,2},{6,0},{1,7},{3,5},{5,3},{7,1},{8,14},{10,12},{12... | collective-permute-start | bytes 24584 | tf_op jit(solution)/shard_map/ppermute | solution.py:73
  558.3 15.7 %collective-permute-start.58 = (bf16[3,1024,256]{2,1,0:T(8,128)(2,1)S(1)}, bf16[3,1024,256]{2,1,0:T(8,128)(2,1)S(1)}, u32[]{:S(2)}, u32[]{:S(2)}) collective-permute-start(bf16[3,1024,256]{2,1,0:T(8,128)(2,1)S(1)} %pad_maximum_fusion.refs_0_.refs_1_), channel_id=1, source_target_pairs={{0,1},{1,0},{2,3},{3,2},{4,5},{5,4},{6,7},{7,6},{8,9},{9,8},{10,11... | collective-permute-start | bytes 4718600 | tf_op jit(solution)/shard_map/ppermute | solution.py:73
  558.5 7.6 %collective-permute-start.62 = (f32[4,2048]{1,0:T(4,128)S(1)}, f32[4,2048]{1,0:T(4,128)S(1)}, u32[]{:S(2)}, u32[]{:S(2)}) collective-permute-start(f32[4,2048]{1,0:T(4,128)S(1)} %maximum_dynamic-update-slice_fusion.1), channel_id=1, source_target_pairs={{0,8},{8,0},{16,24},{24,16},{1,9},{9,1},{17,25},{25,17},{2,10},{10... | collective-permute-start | bytes 98312 | tf_op jit(solution)/shard_map/ppermute | solution.py:73
  566.1 7.3 %collective-permute-start.63 = (f32[4,2048]{1,0:T(4,128)S(1)}, f32[4,2048]{1,0:T(4,128)S(1)}, u32[]{:S(2)}, u32[]{:S(2)}) collective-permute-start(f32[4,2048]{1,0:T(4,128)S(1)} %add.365), channel_id=1, source_target_pairs={{0,16},{8,24},{16,0},{24,8},{1,17},{9,25},{17,1},{25,9},{2,18},{10... | collective-permute-start | bytes 98312 | tf_op jit(solution)/shard_map/ppermute | solution.py:73
  586.8 24.7 %collective-permute-start.70 = (bf16[2,256,512]{2,1,0:T(8,128)(2,1)}, bf16[2,256,512]{2,1,0:T(8,128)(2,1)}, u32[]{:S(2)}, u32[]{:S(2)}) collective-permute-start(bf16[2,256,512]{2,1,0:T(8,128)(2,1)} %dynamic-slice_bitcast_fusion), channel_id=1, source_target_pairs={{0,24},{8,0},{16,8},{24,16},{1,25},{9,1},{17,9},{25,17},{2,26},{10... | collective-permute-start | bytes 1572872 | tf_op jit(solution)/shard_map/ppermute | solution.py:199
  591.7 30.8 %collective-permute-start.67 = (bf16[2,256,512]{2,1,0:T(8,128)(2,1)}, bf16[2,256,512]{2,1,0:T(8,128)(2,1)}, u32[]{:S(2)}, u32[]{:S(2)}) collective-permute-start(bf16[2,256,512]{2,1,0:T(8,128)(2,1)} %dynamic-slice_bitcast_fusion.1), channel_id=1, source_target_pairs={{0,24},{8,0},{16,8},{24,16},{1,25},{9,1},{17,9},{25,17},{2,26},{10... | collective-permute-start | bytes 1572872 | tf_op jit(solution)/shard_map/ppermute | solution.py:199
  596.9 30.0 %collective-permute-start.66 = (f32[4,2048]{1,0:T(4,128)S(1)}, f32[4,2048]{1,0:T(4,128)S(1)}, u32[]{:S(2)}, u32[]{:S(2)}) collective-permute-start(f32[4,2048]{1,0:T(4,128)S(1)} %add.368), channel_id=1, source_target_pairs={{0,4},{2,6},{4,0},{6,2},{1,5},{3,7},{5,1},{7,3},{8,12},{10,14},{12... | collective-permute-start | bytes 98312 | tf_op jit(solution)/shard_map/ppermute | solution.py:73
  606.0 51.8 %collective-permute-start.59 = (bf16[256,1024]{1,0:T(8,128)(2,1)}, bf16[256,1024]{1,0:T(8,128)(2,1)}, u32[]{:S(2)}, u32[]{:S(2)}) collective-permute-start(bf16[256,1024]{1,0:T(8,128)(2,1)} %get-tuple-element.89), channel_id=1, source_target_pairs={{0,2},{2,0},{4,6},{6,4},{1,3},{3,1},{5,7},{7,5},{8,10},{10,8},{12,... | collective-permute-start | bytes 1572872 | tf_op jit(solution)/shard_map/ppermute | solution.py:73
  606.0 51.8 %collective-permute-start.60 = (bf16[256,1024]{1,0:T(8,128)(2,1)}, bf16[256,1024]{1,0:T(8,128)(2,1)}, u32[]{:S(2)}, u32[]{:S(2)}) collective-permute-start(bf16[256,1024]{1,0:T(8,128)(2,1)} %get-tuple-element.90), channel_id=1, source_target_pairs={{0,4},{2,6},{4,0},{6,2},{1,5},{3,7},{5,1},{7,3},{8,12},{10,14},{12... | collective-permute-start | bytes 1572872 | tf_op jit(solution)/shard_map/ppermute | solution.py:73
  611.6 46.3 %collective-permute-start.61 = (bf16[256,1024]{1,0:T(8,128)(2,1)}, bf16[256,1024]{1,0:T(8,128)(2,1)}, u32[]{:S(2)}, u32[]{:S(2)}) collective-permute-start(bf16[256,1024]{1,0:T(8,128)(2,1)} %get-tuple-element.91), channel_id=1, source_target_pairs={{0,6},{2,4},{4,2},{6,0},{1,7},{3,5},{5,3},{7,1},{8,14},{10,12},{12... | collective-permute-start | bytes 1572872 | tf_op jit(solution)/shard_map/ppermute | solution.py:73
  622.6 15.3 %collective-permute-start.71 = (bf16[2,256,512]{2,1,0:T(8,128)(2,1)S(1)}, bf16[2,256,512]{2,1,0:T(8,128)(2,1)S(1)}, u32[]{:S(2)}, u32[]{:S(2)}) collective-permute-start(bf16[2,256,512]{2,1,0:T(8,128)(2,1)S(1)} %fusion.25), channel_id=1, source_target_pairs={{0,24},{8,0},{16,8},{24,16},{1,25},{9,1},{17,9},{25,17},{2,26},{10... | collective-permute-start | bytes 1572872 | tf_op jit(solution)/shard_map/ppermute | solution.py:199
  626.9 27.2 %collective-permute-start.68 = (bf16[2,256,512]{2,1,0:T(8,128)(2,1)S(1)}, bf16[2,256,512]{2,1,0:T(8,128)(2,1)S(1)}, u32[]{:S(2)}, u32[]{:S(2)}) collective-permute-start(bf16[2,256,512]{2,1,0:T(8,128)(2,1)S(1)} %fusion.28), channel_id=1, source_target_pairs={{0,24},{8,0},{16,8},{24,16},{1,25},{9,1},{17,9},{25,17},{2,26},{10... | collective-permute-start | bytes 1572872 | tf_op jit(solution)/shard_map/ppermute | solution.py:199
  638.8 21.8 %collective-permute-start.72 = (bf16[2,256,512]{2,1,0:T(8,128)(2,1)}, bf16[2,256,512]{2,1,0:T(8,128)(2,1)}, u32[]{:S(2)}, u32[]{:S(2)}) collective-permute-start(bf16[2,256,512]{2,1,0:T(8,128)(2,1)} %fusion.26), channel_id=1, source_target_pairs={{0,24},{8,0},{16,8},{24,16},{1,25},{9,1},{17,9},{25,17},{2,26},{10... | collective-permute-start | bytes 1572872 | tf_op jit(solution)/shard_map/ppermute | solution.py:199
  657.8 12.7 %collective-permute-start.69 = (bf16[2,256,512]{2,1,0:T(8,128)(2,1)S(1)}, bf16[2,256,512]{2,1,0:T(8,128)(2,1)S(1)}, u32[]{:S(2)}, u32[]{:S(2)}) collective-permute-start(bf16[2,256,512]{2,1,0:T(8,128)(2,1)S(1)} %fusion.29), channel_id=1, source_target_pairs={{0,24},{8,0},{16,8},{24,16},{1,25},{9,1},{17,9},{25,17},{2,26},{10... | collective-permute-start | bytes 1572872 | tf_op jit(solution)/shard_map/ppermute | solution.py:199
  (118 other events, 746.9 us)
Sparse Core Ops, SparseCore 0:
  82.3 151.5 all-gather.3
  236.0 61.7 all-gather.5
  299.9 26.5 all-gather.7
  377.5 75.3 reduce-scatter.2
  455.2 155.2 reduce-scatter.4

commit v6 on v5

--- a/solution.py
+++ b/solution.py
@@ -791,7 +791,7 @@
     ]
     main_own, *main_low = narrow(product, product_other, reduce_parts[0])
     main_arrived = [swap(value, "row", k + 1) for k, value in enumerate(main_low)]
-    rest = narrow(product, product_other, reduce_parts[1], main_arrived)
+    rest = narrow(product, product_other, reduce_parts[1], main_arrived[:2])
     for value in main_arrived:
         main_own = main_own + value.astype(jnp.float32)
     second = jnp.concatenate([main_own, scatter_rows(*rest)], 1)

time: 688 us -> 687 us (level)
    unnamed x230 -> x226, local copies, waits for them, and re-layouts: 29.4 us -> 27.6 us
  transfers between devices with their start and end apart: 78 -> 78, of which waited for: 52 -> 52; matrix products, arithmetic and copies ran while one was open for 15% -> 15% of each run, Pallas kernels for 16% -> 17%
where the time goes in v6:
time: 687 us; the launch traced here: 681 us
  waiting for transfers between devices  317 us (46%)
  Pallas kernels  130 us (19%)
  starting transfers between devices  86.3 us (13%)
  local copies, waits for them, and re-layouts  64.5 us (9%)
  other arithmetic  47.4 us (7%)
  matrix products  20.5 us (3%)
  between operations  15.8 us (2%)
    ppermute x61, waiting for transfers between devices, swap(): lax.ppermute(values, axis, [(i, i ^ distance) for i in range(lax.axis_siz...  171 us
    pallas_call x20, Pallas kernels, run(): pl.pallas_call(kernel, grid_spec=pltpu.PrefetchScalarGridSpec(num_scalar_...  130 us
    all_gather x3, waiting for transfers between devices, gather_shards(): return lax.all_gather(shard, 'dp', axis=0, tiled=True)  68.2 us
    ppermute x61, starting transfers between devices, swap(): lax.ppermute(values, axis, [(i, i ^ distance) for i in range(lax.axis_siz...  51.3 us
    ppermute x6, waiting for transfers between devices, ring_gather(): shards = [lax.ppermute(shard, 'dp', pairs) for shard in shards]  37.7 us
    unnamed x226, local copies, waits for them, and re-layouts  27.6 us
    ppermute x6, waiting for transfers between devices, ring_scatter(): arrived = [lax.ppermute(total, 'dp', pairs) for total in totals]  23.7 us
    ppermute x6, starting transfers between devices, ring_gather(): shards = [lax.ppermute(shard, 'dp', pairs) for shard in shards]  22.7 us
  transfers between devices with their start and end apart: 78, of which 52 were waited for; matrix products, arithmetic and copies ran while one was open for 15% of the time, Pallas kernels for 17%

profile of v6, /device:TPU:0, one launch (start us, length us, event | category | flops | bytes accessed | tf_op | source)
XLA Modules:
  0.0 681.3 jit_solution(14704895640255790104)
XLA Ops:
  8.9 5.1 collective-permute-start.4
  18.5 7.7 %collective-permute-done.4 = bf16[512,512]{1,0:T(8,128)(2,1)S(1)} collective-permute-done((bf16[512,512]{1,0:T(8,128)(2,1)S(1)}, bf16[512,512]{1,0:T(8,128)(2,1)S(1)}, u32[]{:S(2)}, u32[]{:S(2)}) %collective-permute-start.4) | collective-permute-done | bytes 524320 | tf_op jit(solution)/shard_map/ppermute | solution.py:183
  26.3 4.3 collective-permute-start.6
  30.6 7.0 %collective-permute-done.5 = bf16[512,512]{1,0:T(8,128)(2,1)S(1)} collective-permute-done((bf16[512,512]{1,0:T(8,128)(2,1)S(1)}, bf16[512,512]{1,0:T(8,128)(2,1)S(1)}, u32[]{:S(2)}, u32[]{:S(2)}) %collective-permute-start.5) | collective-permute-done | bytes 524320 | tf_op jit(solution)/shard_map/ppermute | solution.py:183
  37.5 4.3 collective-permute-start.7
  41.8 3.8 convert_element_type.195.value
  48.8 4.3 collective-permute-start.8
  53.9 6.1 collective-permute-done.7
  60.0 4.3 collective-permute-start.9
  65.9 5.3 collective-permute-done.8
  72.1 9.3 %collective-permute-done.9 = bf16[512,512]{1,0:T(8,128)(2,1)S(1)} collective-permute-done((bf16[512,512]{1,0:T(8,128)(2,1)S(1)}, bf16[512,512]{1,0:T(8,128)(2,1)S(1)}, u32[]{:S(2)}, u32[]{:S(2)}) %collective-permute-start.9) | collective-permute-done | bytes 524320 | tf_op jit(solution)/shard_map/ppermute | solution.py:183
  86.2 9.8 %collective-permute-done = bf16[256,1024]{1,0:T(8,128)(2,1)S(1)} collective-permute-done((bf16[256,1024]{1,0:T(8,128)(2,1)S(1)}, bf16[256,1024]{1,0:T(8,128)(2,1)S(1)}, u32[]{:S(2)}, u32[]{:S(2)}) %collective-permute-start) | collective-permute-done | bytes 524320 | tf_op jit(solution)/shard_map/ppermute | solution.py:73
  105.7 7.1 %shard_map.345 = (f32[3,1024,256]{2,1,0:T(8,128)S(1)}, f32[3,1024,256]{2,1,0:T(8,128)}) custom-call(s32[1]{0:T(128)} %bitcast.c, bf16[1024,1024]{1,0:T(8,128)(2,1)S(1)} %constant_dynamic-update-slice_fusion.refs_0_, bf16[4,4,256,512]{3,2,1,0:T(8,128)(2,1)} %bitcast.11.refs_1_.refs_2_.refs_3_.refs_0_, ...), custom_call_target="tpu_custom_call" | custom-call | flops 1 | bytes 1 | tf_op jit(solution)/shard_map/pallas_call | solution.py:140
  116.2 3.1 multiply_cosine_fusion
  122.9 3.3 add.312
  162.8 9.0 %collective-permute-done.16 = bf16[256,1024]{1,0:T(8,128)(2,1)} collective-permute-done((bf16[256,1024]{1,0:T(8,128)(2,1)S(1)}, bf16[256,1024]{1,0:T(8,128)(2,1)}, u32[]{:S(2)}, u32[]{:S(2)}) %collective-permute-start.16) | collective-permute-done | bytes 524320 | tf_op jit(solution)/shard_map/ppermute | solution.py:73
  171.8 10.7 %collective-permute-done.17 = bf16[256,1024]{1,0:T(8,128)(2,1)} collective-permute-done((bf16[256,1024]{1,0:T(8,128)(2,1)S(1)}, bf16[256,1024]{1,0:T(8,128)(2,1)}, u32[]{:S(2)}, u32[]{:S(2)}) %collective-permute-start.17) | collective-permute-done | bytes 524320 | tf_op jit(solution)/shard_map/ppermute | solution.py:73
  187.8 12.0 %collective-permute-done.20 = bf16[256,1024]{1,0:T(8,128)(2,1)S(1)} collective-permute-done((bf16[256,1024]{1,0:T(8,128)(2,1)S(1)}, bf16[256,1024]{1,0:T(8,128)(2,1)S(1)}, u32[]{:S(2)}, u32[]{:S(2)}) %collective-permute-start.20) | collective-permute-done | bytes 524320 | tf_op jit(solution)/shard_map/ppermute | solution.py:73
  202.1 5.4 collective-permute-done.22
  208.6 25.3 %all-gather.4.cloned.1.call-done = bf16[2048,2048]{1,0:T(8,128)(2,1)} async-done(((bf16[512,2048]{1,0:T(8,128)(2,1)}), bf16[2048,2048]{1,0:T(8,128)(2,1)}) %all-gather.4.cloned.1.call-update) | async-done | bytes 8388624 | tf_op jit(solution)/shard_map/all_gather | solution.py:597
  233.9 3.8 shard_map.350
  237.8 3.8 shard_map.348
  242.1 5.3 shard_map.351
  247.5 5.3 shard_map.349
  254.9 42.9 %all-gather.6.cloned.1.call-done.refs_0_ = bf16[2048,768]{1,0:T(8,128)(2,1)} async-done(((bf16[512,768]{1,0:T(8,128)(2,1)}), bf16[2048,768]{1,0:T(8,128)(2,1)}) %all-gather.6.cloned.1.call-update) | async-done | bytes 3145744 | tf_op jit(solution)/shard_map/all_gather | solution.py:597
  300.1 6.9 %shard_map.352 = (f32[256,768]{1,0:T(8,128)S(1)}, bf16[256,768]{1,0:T(8,128)(2,1)S(1)}, bf16[256,768]{1,0:T(8,128)(2,1)S(1)}, bf16[256,768]{1,0:T(8,128)(2,1)}) custom-call(s32[1]{0:T(128)} %bitcast.c, bf16[1024,512]{1,0:T(8,128)(2,1)} %get-tuple-element.72.refs_0_, bf16[1024,512]{1,0:T(8,128)(2,1)} %get-tuple-element.73.refs_1_, ...), custom_call_target="tpu_custom_call" | custom-call | flops 1 | bytes 1 | tf_op jit(solution)/shard_map/pallas_call | solution.py:140
  311.9 8.0 %collective-permute-done.28.refs_6_ = bf16[256,768]{1,0:T(8,128)(2,1)S(1)} collective-permute-done((bf16[256,768]{1,0:T(8,128)(2,1)S(1)}, bf16[256,768]{1,0:T(8,128)(2,1)S(1)}, u32[]{:S(2)}, u32[]{:S(2)}) %collective-permute-start.28) | collective-permute-done | bytes 393248 | tf_op jit(solution)/shard_map/ppermute | solution.py:73
  319.8 8.4 %collective-permute-done.29.refs_7_ = bf16[256,768]{1,0:T(8,128)(2,1)S(1)} collective-permute-done((bf16[256,768]{1,0:T(8,128)(2,1)S(1)}, bf16[256,768]{1,0:T(8,128)(2,1)S(1)}, u32[]{:S(2)}, u32[]{:S(2)}) %collective-permute-start.29) | collective-permute-done | bytes 393248 | tf_op jit(solution)/shard_map/ppermute | solution.py:73
  330.0 3.5 shard_map.354
  345.6 12.0 %collective-permute-done.35 = bf16[256,1024]{1,0:T(8,128)(2,1)S(1)} collective-permute-done((bf16[256,1024]{1,0:T(8,128)(2,1)S(1)}, bf16[256,1024]{1,0:T(8,128)(2,1)S(1)}, u32[]{:S(2)}, u32[]{:S(2)}) %collective-permute-start.35) | collective-permute-done | bytes 524320 | tf_op jit(solution)/shard_map/ppermute | solution.py:73
  359.9 5.4 collective-permute-done.37
  367.5 8.8 %shard_map.355.refs_7_ = bf16[4,512,1024]{2,1,0:T(8,128)(2,1)} custom-call(s32[1]{0:T(128)} %bitcast.c, bf16[1024,512]{1,0:T(8,128)(2,1)} %get-tuple-element.72.refs_0_, bf16[1024,512]{1,0:T(8,128)(2,1)} %get-tuple-element.73.refs_1_, bf16[1024,512]{1,0:T(8,128)(2,1)} %collective-permute-done.26.refs_2_.refs_1_, bf16[1024,512]{1,0:T(8,128)(2,1)S(1)} %copy-done.4, ...), custom_call_target="tpu_custom_call" | custom-call | flops 1 | bytes 1 | tf_op jit(solution)/shard_map/pallas_call | solution.py:140
  378.7 4.1 collective-permute-done.40.refs_4_
  383.5 6.5 shard_map.357.refs_1_.refs_2_
  390.2 6.6 shard_map.356.refs_0_.refs_1_
  397.0 4.1 collective-permute-done.42.refs_2_.refs_3_
  402.4 13.5 %shard_map.358 = (f32[256,1024]{1,0:T(8,128)S(1)}, bf16[256,1024]{1,0:T(8,128)(2,1)S(1)}, bf16[256,1024]{1,0:T(8,128)(2,1)S(1)}, bf16[256,1024]{1,0:T(8,128)(2,1)S(1)}) custom-call(s32[1]{0:T(128)} %bitcast.c, bf16[2,1024,512]{2,1,0:T(8,128)(2,1)S(1)} %shard_map.356.refs_0_.refs_1_, bf16[2,1024,512]{2,1,0:T(8,128)(2,1)} %copy-done.1, ...), custom_call_target="tpu_custom_call" | custom-call | flops 1 | bytes 1 | tf_op jit(solution)/shard_map/pallas_call | solution.py:140
  417.6 16.9 %shard_map.363.value = bf16[4,2,256,2048]{3,2,1,0:T(8,128)(2,1)} custom-call(s32[1]{0:T(128)} %bitcast.c, bf16[1024,1024]{1,0:T(8,128)(2,1)S(1)} %constant_dynamic-update-slice_fusion.5.refs_0_, bf16[2,1024,512]{2,1,0:T(8,128)(2,1)S(1)} %shard_map.356.refs_0_.refs_1_, bf16[2,1024,512]{2,1,0:T(8,128)(2,1)} %copy-done.1, bf16[2,1024,512]{2,1,0:T(8,128)(2,1)} %copy-done.56, ...), custom_call_target="tpu_custom_call" | custom-call | flops 1 | bytes 1 | tf_op jit(solution)/shard_map/pallas_call | solution.py:140
  435.3 16.5 %reduce-scatter.3.cloned.1.call-done.refs_0_ = bf16[512,1024]{1,0:T(8,128)(2,1)} async-done(((bf16[2048,1024]{1,0:T(8,128)(2,1)}), bf16[512,1024]{1,0:T(8,128)(2,1)}) %reduce-scatter.3.cloned.1.call-update) | async-done | bytes 1048592 | tf_op jit(solution)/shard_map/reduce_scatter | solution.py:601
  456.3 11.3 %collective-permute-done.44 = bf16[256,1024]{1,0:T(8,128)(2,1)S(1)} collective-permute-done((bf16[256,1024]{1,0:T(8,128)(2,1)S(1)}, bf16[256,1024]{1,0:T(8,128)(2,1)S(1)}, u32[]{:S(2)}, u32[]{:S(2)}) %collective-permute-start.44) | collective-permute-done | bytes 524320 | tf_op jit(solution)/shard_map/ppermute | solution.py:73
  467.6 11.3 %collective-permute-done.45 = bf16[256,1024]{1,0:T(8,128)(2,1)S(1)} collective-permute-done((bf16[256,1024]{1,0:T(8,128)(2,1)S(1)}, bf16[256,1024]{1,0:T(8,128)(2,1)S(1)}, u32[]{:S(2)}, u32[]{:S(2)}) %collective-permute-start.45) | collective-permute-done | bytes 524320 | tf_op jit(solution)/shard_map/ppermute | solution.py:73
  479.0 3.6 multiply_reduce_fusion.5
  486.1 12.0 %collective-permute-done.48 = bf16[256,1024]{1,0:T(8,128)(2,1)S(1)} collective-permute-done((bf16[256,1024]{1,0:T(8,128)(2,1)S(1)}, bf16[256,1024]{1,0:T(8,128)(2,1)S(1)}, u32[]{:S(2)}, u32[]{:S(2)}) %collective-permute-start.48) | collective-permute-done | bytes 524320 | tf_op jit(solution)/shard_map/ppermute | solution.py:73
  500.4 5.4 collective-permute-done.50
  509.4 2.7 collective-permute-done.53.refs_3_
  515.5 3.7 multiply_reduce_fusion.1
  533.7 3.0 reshape.633
  539.6 2.8 fusion.4
  544.1 4.2 fusion.18
  558.9 6.0 collective-permute-done.62
  565.8 6.5 collective-permute-done.63
  572.9 11.0 %shard_map.361 = (bf16[4,2,256,512]{3,2,1,0:T(8,128)(2,1)}, bf16[4,2,256,512]{3,2,1,0:T(8,128)(2,1)}) custom-call(s32[1]{0:T(128)} %bitcast.c, bf16[1024,1024]{1,0:T(8,128)(2,1)} %copy-done.6, bf16[3,1024,256]{2,1,0:T(8,128)(2,1)S(1)} %pad_maximum_fusion.refs_0_.refs_1_, bf16[3,1024,256]{2,1,0:T(8,128)(2,1)S(1)} %collective-permute-done.58.refs_1_.refs_2_, ...), custom_call_target="tpu_custom_call" | custom-call | flops 1 | bytes 1 | tf_op jit(solution)/shard_map/pallas_call | solution.py:140
  585.7 3.0 collective-permute-start.70
  597.2 6.7 shard_map.360
  606.9 3.6 collective-permute-done.70
  612.7 8.7 %collective-permute-done.67 = bf16[2,256,512]{2,1,0:T(8,128)(2,1)} collective-permute-done((bf16[2,256,512]{2,1,0:T(8,128)(2,1)}, bf16[2,256,512]{2,1,0:T(8,128)(2,1)}, u32[]{:S(2)}, u32[]{:S(2)}) %collective-permute-start.67) | collective-permute-done | bytes 524320 | tf_op jit(solution)/shard_map/ppermute | solution.py:199
  621.4 3.0 collective-permute-start.71
  628.3 5.2 shard_map.370
  633.6 3.2 collective-permute-done.71
  637.7 4.3 collective-permute-start.72
  643.6 9.4 %shard_map.365 = (f32[2,256,2048]{2,1,0:T(8,128)}, f32[2,256,2048]{2,1,0:T(8,128)}, f32[2,256,2048]{2,1,0:T(8,128)}, f32[2,256,2048]{2,1,0:T(8,128)}) custom-call(s32[1]{0:T(128)} %bitcast.c, bf16[512,2048]{1,0:T(8,128)(2,1)S(1)} %copy-done.19, f32[2,256,2048]{2,1,0:T(8,128)} %refs_1_.4, f32[2,256,2048]{2,1,0:T(8,128)} %refs_2_.4, f32[2,256,2048]{2,1,0:T(8,128)} %refs_3_.4), custom_call_target="tpu_custom_call" | custom-call | flops 1 | bytes 1 | tf_op jit(solution)/shard_map/pallas_call | solution.py:140
  656.8 2.7 add_add_fusion
  661.0 8.3 %collective-permute-done.69 = bf16[2,256,512]{2,1,0:T(8,128)(2,1)S(1)} collective-permute-done((bf16[2,256,512]{2,1,0:T(8,128)(2,1)S(1)}, bf16[2,256,512]{2,1,0:T(8,128)(2,1)S(1)}, u32[]{:S(2)}, u32[]{:S(2)}) %collective-permute-start.69) | collective-permute-done | bytes 524320 | tf_op jit(solution)/shard_map/ppermute | solution.py:199
  669.7 3.3 shard_map.368
  (490 shorter events, 191.7 us)
Async XLA Ops:
  7.2 226.7 %all-gather.4.cloned.1.call-start = ((), (), s32[]{:S(2)}) async-start(), calls=%async_computation.2 | async-start | bytes 10485760 | tf_op jit(solution)/shard_map/all_gather | solution.py:597
  8.9 17.4 %collective-permute-start.4 = (bf16[512,512]{1,0:T(8,128)(2,1)S(1)}, bf16[512,512]{1,0:T(8,128)(2,1)S(1)}, u32[]{:S(2)}, u32[]{:S(2)}) collective-permute-start(bf16[512,512]{1,0:T(8,128)(2,1)S(1)} %bitcast.156), channel_id=1, source_target_pairs={{0,24},{8,0},{16,8},{24,16},{1,25},{9,1},{17,9},{25,17},{2,26},{10... | collective-permute-start | bytes 1572872 | tf_op jit(solution)/shard_map/ppermute | solution.py:183
  18.1 19.4 %collective-permute-start.5 = (bf16[512,512]{1,0:T(8,128)(2,1)S(1)}, bf16[512,512]{1,0:T(8,128)(2,1)S(1)}, u32[]{:S(2)}, u32[]{:S(2)}) collective-permute-start(bf16[512,512]{1,0:T(8,128)(2,1)S(1)} %get-tuple-element.134), channel_id=1, source_target_pairs={{0,24},{8,0},{16,8},{24,16},{1,25},{9,1},{17,9},{25,17},{2,26},{10... | collective-permute-start | bytes 1572872 | tf_op jit(solution)/shard_map/ppermute | solution.py:183
  26.3 22.5 %collective-permute-start.6 = (bf16[512,512]{1,0:T(8,128)(2,1)S(1)}, bf16[512,512]{1,0:T(8,128)(2,1)S(1)}, u32[]{:S(2)}, u32[]{:S(2)}) collective-permute-start(bf16[512,512]{1,0:T(8,128)(2,1)S(1)} %collective-permute-done.4), channel_id=1, source_target_pairs={{0,24},{8,0},{16,8},{24,16},{1,25},{9,1},{17,9},{25,17},{2,26},{10... | collective-permute-start | bytes 1572872 | tf_op jit(solution)/shard_map/ppermute | solution.py:183
  37.5 22.5 %collective-permute-start.7 = (bf16[512,512]{1,0:T(8,128)(2,1)S(1)}, bf16[512,512]{1,0:T(8,128)(2,1)S(1)}, u32[]{:S(2)}, u32[]{:S(2)}) collective-permute-start(bf16[512,512]{1,0:T(8,128)(2,1)S(1)} %collective-permute-done.5), channel_id=1, source_target_pairs={{0,24},{8,0},{16,8},{24,16},{1,25},{9,1},{17,9},{25,17},{2,26},{10... | collective-permute-start | bytes 1572872 | tf_op jit(solution)/shard_map/ppermute | solution.py:183
  48.8 22.5 %collective-permute-start.8 = (bf16[512,512]{1,0:T(8,128)(2,1)S(1)}, bf16[512,512]{1,0:T(8,128)(2,1)S(1)}, u32[]{:S(2)}, u32[]{:S(2)}) collective-permute-start(bf16[512,512]{1,0:T(8,128)(2,1)S(1)} %collective-permute-done.6), channel_id=1, source_target_pairs={{0,24},{8,0},{16,8},{24,16},{1,25},{9,1},{17,9},{25,17},{2,26},{10... | collective-permute-start | bytes 1572872 | tf_op jit(solution)/shard_map/ppermute | solution.py:183
  60.0 21.3 %collective-permute-start.9 = (bf16[512,512]{1,0:T(8,128)(2,1)S(1)}, bf16[512,512]{1,0:T(8,128)(2,1)S(1)}, u32[]{:S(2)}, u32[]{:S(2)}) collective-permute-start(bf16[512,512]{1,0:T(8,128)(2,1)S(1)} %collective-permute-done.7), channel_id=1, source_target_pairs={{0,24},{8,0},{16,8},{24,16},{1,25},{9,1},{17,9},{25,17},{2,26},{10... | collective-permute-start | bytes 1572872 | tf_op jit(solution)/shard_map/ppermute | solution.py:183
  82.2 215.6 %all-gather.6.cloned.1.call-start = ((), (), s32[]{:S(2)}) async-start(), calls=%async_computation.3 | async-start | bytes 3932160 | tf_op jit(solution)/shard_map/all_gather | solution.py:597
  83.2 12.8 %collective-permute-start = (bf16[256,1024]{1,0:T(8,128)(2,1)S(1)}, bf16[256,1024]{1,0:T(8,128)(2,1)S(1)}, u32[]{:S(2)}, u32[]{:S(2)}) collective-permute-start(bf16[256,1024]{1,0:T(8,128)(2,1)S(1)} %copy-done.61), channel_id=1, source_target_pairs={{0,2},{2,0},{4,6},{6,4},{1,3},{3,1},{5,7},{7,5},{8,10},{10,8},{12,... | collective-permute-start | bytes 1572872 | tf_op jit(solution)/shard_map/ppermute | solution.py:73
  84.7 13.6 %collective-permute-start.1 = (bf16[256,1024]{1,0:T(8,128)(2,1)S(1)}, bf16[256,1024]{1,0:T(8,128)(2,1)}, u32[]{:S(2)}, u32[]{:S(2)}) collective-permute-start(bf16[256,1024]{1,0:T(8,128)(2,1)S(1)} %copy-done.61), channel_id=1, source_target_pairs={{0,4},{2,6},{4,0},{6,2},{1,5},{3,7},{5,1},{7,3},{8,12},{10,14},{12... | collective-permute-start | bytes 1572872 | tf_op jit(solution)/shard_map/ppermute | solution.py:73
  96.7 6.6 collective-permute-start.2
  99.2 6.4 collective-permute-start.3
  114.5 6.7 collective-permute-start.10
  128.0 9.5 %collective-permute-start.14 = (f32[2,4,256]{2,1,0:T(4,128)S(1)}, f32[2,4,256]{2,1,0:T(4,128)S(1)}, u32[]{:S(2)}, u32[]{:S(2)}) collective-permute-start(f32[2,4,256]{2,1,0:T(4,128)S(1)} %reshape.627), channel_id=1, source_target_pairs={{0,6},{2,4},{4,2},{6,0},{1,7},{3,5},{5,3},{7,1},{8,14},{10,12},{12... | collective-permute-start | bytes 24584 | tf_op jit(solution)/shard_map/ppermute | solution.py:73
  156.9 14.9 %collective-permute-start.16 = (bf16[256,1024]{1,0:T(8,128)(2,1)S(1)}, bf16[256,1024]{1,0:T(8,128)(2,1)}, u32[]{:S(2)}, u32[]{:S(2)}) collective-permute-start(bf16[256,1024]{1,0:T(8,128)(2,1)S(1)} %get-tuple-element.69), channel_id=1, source_target_pairs={{0,2},{2,0},{4,6},{6,4},{1,3},{3,1},{5,7},{7,5},{8,10},{10,8},{12,... | collective-permute-start | bytes 1572872 | tf_op jit(solution)/shard_map/ppermute | solution.py:73
  157.5 25.0 %collective-permute-start.17 = (bf16[256,1024]{1,0:T(8,128)(2,1)S(1)}, bf16[256,1024]{1,0:T(8,128)(2,1)}, u32[]{:S(2)}, u32[]{:S(2)}) collective-permute-start(bf16[256,1024]{1,0:T(8,128)(2,1)S(1)} %get-tuple-element.70), channel_id=1, source_target_pairs={{0,4},{2,6},{4,0},{6,2},{1,5},{3,7},{5,1},{7,3},{8,12},{10,14},{12... | collective-permute-start | bytes 1572872 | tf_op jit(solution)/shard_map/ppermute | solution.py:73
  158.1 24.4 %collective-permute-start.18 = (bf16[256,1024]{1,0:T(8,128)(2,1)S(1)}, bf16[256,1024]{1,0:T(8,128)(2,1)}, u32[]{:S(2)}, u32[]{:S(2)}) collective-permute-start(bf16[256,1024]{1,0:T(8,128)(2,1)S(1)} %get-tuple-element.71), channel_id=1, source_target_pairs={{0,6},{2,4},{4,2},{6,0},{1,7},{3,5},{5,3},{7,1},{8,14},{10,12},{12... | collective-permute-start | bytes 1572872 | tf_op jit(solution)/shard_map/ppermute | solution.py:73
  162.8 166.2 %all-gather.8.cloned.1.call-start = ((), (), s32[]{:S(2)}) async-start(), calls=%async_computation.4 | async-start | bytes 1310720 | tf_op jit(solution)/shard_map/all_gather | solution.py:597
  185.7 14.1 %collective-permute-start.20 = (bf16[256,1024]{1,0:T(8,128)(2,1)S(1)}, bf16[256,1024]{1,0:T(8,128)(2,1)S(1)}, u32[]{:S(2)}, u32[]{:S(2)}) collective-permute-start(bf16[256,1024]{1,0:T(8,128)(2,1)S(1)} %get-tuple-element.130), channel_id=1, source_target_pairs={{0,2},{2,0},{4,6},{6,4},{1,3},{3,1},{5,7},{7,5},{8,10},{10,8},{12,... | collective-permute-start | bytes 1572872 | tf_op jit(solution)/shard_map/ppermute | solution.py:73
  187.3 13.8 %collective-permute-start.21 = (bf16[256,1024]{1,0:T(8,128)(2,1)S(1)}, bf16[256,1024]{1,0:T(8,128)(2,1)S(1)}, u32[]{:S(2)}, u32[]{:S(2)}) collective-permute-start(bf16[256,1024]{1,0:T(8,128)(2,1)S(1)} %get-tuple-element.130), channel_id=1, source_target_pairs={{0,4},{2,6},{4,0},{6,2},{1,5},{3,7},{5,1},{7,3},{8,12},{10,14},{12... | collective-permute-start | bytes 1572872 | tf_op jit(solution)/shard_map/ppermute | solution.py:73
  199.8 7.7 %collective-permute-start.22 = (bf16[128,1024]{1,0:T(8,128)(2,1)S(1)}, bf16[128,1024]{1,0:T(8,128)(2,1)S(1)}, u32[]{:S(2)}, u32[]{:S(2)}) collective-permute-start(bf16[128,1024]{1,0:T(8,128)(2,1)S(1)} %slice.346), channel_id=1, source_target_pairs={{0,4},{2,6},{4,0},{6,2},{1,5},{3,7},{5,1},{7,3},{8,12},{10,14},{12... | collective-permute-start | bytes 786440 | tf_op jit(solution)/shard_map/ppermute | solution.py:73
  201.1 7.5 %collective-permute-start.23 = (bf16[128,1024]{1,0:T(8,128)(2,1)S(1)}, bf16[128,1024]{1,0:T(8,128)(2,1)S(1)}, u32[]{:S(2)}, u32[]{:S(2)}) collective-permute-start(bf16[128,1024]{1,0:T(8,128)(2,1)S(1)} %slice.347), channel_id=1, source_target_pairs={{0,2},{2,0},{4,6},{6,4},{1,3},{3,1},{5,7},{7,5},{8,10},{10,8},{12,... | collective-permute-start | bytes 786440 | tf_op jit(solution)/shard_map/ppermute | solution.py:73
  237.7 4.4 collective-permute-start.25
  241.5 6.0 collective-permute-start.24
  247.4 50.4 %collective-permute-start.27 = (bf16[1024,512]{1,0:T(8,128)(2,1)}, bf16[1024,512]{1,0:T(8,128)(2,1)S(1)}, u32[]{:S(2)}, u32[]{:S(2)}) collective-permute-start(bf16[1024,512]{1,0:T(8,128)(2,1)} %get-tuple-element.73.refs_1_), channel_id=1, source_target_pairs={{0,1},{1,0},{2,3},{3,2},{4,5},{5,4},{6,7},{7,6},{8,9},{9,8},{10,11... | collective-permute-start | bytes 3145736 | tf_op jit(solution)/shard_map/ppermute | solution.py:73
  252.8 45.0 %collective-permute-start.26 = (bf16[1024,512]{1,0:T(8,128)(2,1)}, bf16[1024,512]{1,0:T(8,128)(2,1)}, u32[]{:S(2)}, u32[]{:S(2)}) collective-permute-start(bf16[1024,512]{1,0:T(8,128)(2,1)} %get-tuple-element.72.refs_0_), channel_id=1, source_target_pairs={{0,1},{1,0},{2,3},{3,2},{4,5},{5,4},{6,7},{7,6},{8,9},{9,8},{10,11... | collective-permute-start | bytes 3145736 | tf_op jit(solution)/shard_map/ppermute | solution.py:73
  298.8 153.0 %reduce-scatter.3.cloned.1.call-start = ((), (), s32[]{:S(2)}) async-start(), calls=%async_computation.5 | async-start | bytes 5242880 | tf_op jit(solution)/shard_map/reduce_scatter | solution.py:601
  307.8 12.0 %collective-permute-start.28 = (bf16[256,768]{1,0:T(8,128)(2,1)S(1)}, bf16[256,768]{1,0:T(8,128)(2,1)S(1)}, u32[]{:S(2)}, u32[]{:S(2)}) collective-permute-start(bf16[256,768]{1,0:T(8,128)(2,1)S(1)} %get-tuple-element.75), channel_id=1, source_target_pairs={{0,2},{2,0},{4,6},{6,4},{1,3},{3,1},{5,7},{7,5},{8,10},{10,8},{12,... | collective-permute-start | bytes 1179656 | tf_op jit(solution)/shard_map/ppermute | solution.py:73
  309.3 19.0 %collective-permute-start.29 = (bf16[256,768]{1,0:T(8,128)(2,1)S(1)}, bf16[256,768]{1,0:T(8,128)(2,1)S(1)}, u32[]{:S(2)}, u32[]{:S(2)}) collective-permute-start(bf16[256,768]{1,0:T(8,128)(2,1)S(1)} %get-tuple-element.76), channel_id=1, source_target_pairs={{0,4},{2,6},{4,0},{6,2},{1,5},{3,7},{5,1},{7,3},{8,12},{10,14},{12... | collective-permute-start | bytes 1179656 | tf_op jit(solution)/shard_map/ppermute | solution.py:73
  310.8 26.3 %collective-permute-start.30 = (bf16[256,768]{1,0:T(8,128)(2,1)}, bf16[256,768]{1,0:T(8,128)(2,1)}, u32[]{:S(2)}, u32[]{:S(2)}) collective-permute-start(bf16[256,768]{1,0:T(8,128)(2,1)} %get-tuple-element.77), channel_id=1, source_target_pairs={{0,6},{2,4},{4,2},{6,0},{1,7},{3,5},{5,3},{7,1},{8,14},{10,12},{12... | collective-permute-start | bytes 1179656 | tf_op jit(solution)/shard_map/ppermute | solution.py:73
  333.5 5.2 collective-permute-start.31
  333.6 5.9 collective-permute-start.32
  335.6 5.9 collective-permute-start.33
  343.5 14.1 %collective-permute-start.35 = (bf16[256,1024]{1,0:T(8,128)(2,1)S(1)}, bf16[256,1024]{1,0:T(8,128)(2,1)S(1)}, u32[]{:S(2)}, u32[]{:S(2)}) collective-permute-start(bf16[256,1024]{1,0:T(8,128)(2,1)S(1)} %get-tuple-element.128), channel_id=1, source_target_pairs={{0,2},{2,0},{4,6},{6,4},{1,3},{3,1},{5,7},{7,5},{8,10},{10,8},{12,... | collective-permute-start | bytes 1572872 | tf_op jit(solution)/shard_map/ppermute | solution.py:73
  345.1 13.7 %collective-permute-start.36 = (bf16[256,1024]{1,0:T(8,128)(2,1)S(1)}, bf16[256,1024]{1,0:T(8,128)(2,1)S(1)}, u32[]{:S(2)}, u32[]{:S(2)}) collective-permute-start(bf16[256,1024]{1,0:T(8,128)(2,1)S(1)} %get-tuple-element.128), channel_id=1, source_target_pairs={{0,4},{2,6},{4,0},{6,2},{1,5},{3,7},{5,1},{7,3},{8,12},{10,14},{12... | collective-permute-start | bytes 1572872 | tf_op jit(solution)/shard_map/ppermute | solution.py:73
  357.6 7.6 %collective-permute-start.37 = (bf16[128,1024]{1,0:T(8,128)(2,1)S(1)}, bf16[128,1024]{1,0:T(8,128)(2,1)S(1)}, u32[]{:S(2)}, u32[]{:S(2)}) collective-permute-start(bf16[128,1024]{1,0:T(8,128)(2,1)S(1)} %slice.352), channel_id=1, source_target_pairs={{0,4},{2,6},{4,0},{6,2},{1,5},{3,7},{5,1},{7,3},{8,12},{10,14},{12... | collective-permute-start | bytes 786440 | tf_op jit(solution)/shard_map/ppermute | solution.py:73
  358.8 7.3 %collective-permute-start.38 = (bf16[128,1024]{1,0:T(8,128)(2,1)S(1)}, bf16[128,1024]{1,0:T(8,128)(2,1)S(1)}, u32[]{:S(2)}, u32[]{:S(2)}) collective-permute-start(bf16[128,1024]{1,0:T(8,128)(2,1)S(1)} %slice.353), channel_id=1, source_target_pairs={{0,2},{2,0},{4,6},{6,4},{1,3},{3,1},{5,7},{7,5},{8,10},{10,8},{12,... | collective-permute-start | bytes 786440 | tf_op jit(solution)/shard_map/ppermute | solution.py:73
  376.3 265.7 %reduce-scatter.5.cloned.1.call-start = ((), (), s32[]{:S(2)}) async-start(), calls=%async_computation.6 | async-start | bytes 10485760 | tf_op jit(solution)/shard_map/reduce_scatter | solution.py:601
  376.3 7.2 %collective-permute-start.39 = (bf16[1024,1024]{1,0:T(8,128)(2,1)}, bf16[1024,1024]{1,0:T(8,128)(2,1)}, u32[]{:S(2)}, u32[]{:S(2)}) collective-permute-start(bf16[1024,1024]{1,0:T(8,128)(2,1)} %copy-done.43), channel_id=1, source_target_pairs={{0,1},{1,0},{2,3},{3,2},{4,5},{5,4},{6,7},{7,6},{8,9},{9,8},{10,11... | collective-permute-start | bytes 6291464 | tf_op jit(solution)/shard_map/ppermute | solution.py:73
  378.0 4.8 collective-permute-start.40
  378.5 5.0 collective-permute-start.41
  390.0 7.0 %collective-permute-start.43 = (bf16[2,1024,512]{2,1,0:T(8,128)(2,1)S(1)}, bf16[2,1024,512]{2,1,0:T(8,128)(2,1)S(1)}, u32[]{:S(2)}, u32[]{:S(2)}) collective-permute-start(bf16[2,1024,512]{2,1,0:T(8,128)(2,1)S(1)} %shard_map.357.refs_1_.refs_2_), channel_id=1, source_target_pairs={{0,1},{1,0},{2,3},{3,2},{4,5},{5,4},{6,7},{7,6},{8,9},{9,8},{10,11... | collective-permute-start | bytes 6291464 | tf_op jit(solution)/shard_map/ppermute | solution.py:73
  452.8 14.8 %collective-permute-start.44 = (bf16[256,1024]{1,0:T(8,128)(2,1)S(1)}, bf16[256,1024]{1,0:T(8,128)(2,1)S(1)}, u32[]{:S(2)}, u32[]{:S(2)}) collective-permute-start(bf16[256,1024]{1,0:T(8,128)(2,1)S(1)} %copy-done.29), channel_id=1, source_target_pairs={{0,2},{2,0},{4,6},{6,4},{1,3},{3,1},{5,7},{7,5},{8,10},{10,8},{12,... | collective-permute-start | bytes 1572872 | tf_op jit(solution)/shard_map/ppermute | solution.py:73
  454.3 24.7 %collective-permute-start.45 = (bf16[256,1024]{1,0:T(8,128)(2,1)S(1)}, bf16[256,1024]{1,0:T(8,128)(2,1)S(1)}, u32[]{:S(2)}, u32[]{:S(2)}) collective-permute-start(bf16[256,1024]{1,0:T(8,128)(2,1)S(1)} %copy-done.35), channel_id=1, source_target_pairs={{0,4},{2,6},{4,0},{6,2},{1,5},{3,7},{5,1},{7,3},{8,12},{10,14},{12... | collective-permute-start | bytes 1572872 | tf_op jit(solution)/shard_map/ppermute | solution.py:73
  455.8 23.2 %collective-permute-start.46 = (bf16[256,1024]{1,0:T(8,128)(2,1)S(1)}, bf16[256,1024]{1,0:T(8,128)(2,1)S(1)}, u32[]{:S(2)}, u32[]{:S(2)}) collective-permute-start(bf16[256,1024]{1,0:T(8,128)(2,1)S(1)} %copy-done.33), channel_id=1, source_target_pairs={{0,6},{2,4},{4,2},{6,0},{1,7},{3,5},{5,3},{7,1},{8,14},{10,12},{12... | collective-permute-start | bytes 1572872 | tf_op jit(solution)/shard_map/ppermute | solution.py:73
  484.0 14.1 %collective-permute-start.48 = (bf16[256,1024]{1,0:T(8,128)(2,1)S(1)}, bf16[256,1024]{1,0:T(8,128)(2,1)S(1)}, u32[]{:S(2)}, u32[]{:S(2)}) collective-permute-start(bf16[256,1024]{1,0:T(8,128)(2,1)S(1)} %get-tuple-element.125), channel_id=1, source_target_pairs={{0,2},{2,0},{4,6},{6,4},{1,3},{3,1},{5,7},{7,5},{8,10},{10,8},{12,... | collective-permute-start | bytes 1572872 | tf_op jit(solution)/shard_map/ppermute | solution.py:73
  485.2 14.4 %collective-permute-start.49 = (bf16[256,1024]{1,0:T(8,128)(2,1)S(1)}, bf16[256,1024]{1,0:T(8,128)(2,1)S(1)}, u32[]{:S(2)}, u32[]{:S(2)}) collective-permute-start(bf16[256,1024]{1,0:T(8,128)(2,1)S(1)} %get-tuple-element.125), channel_id=1, source_target_pairs={{0,4},{2,6},{4,0},{6,2},{1,5},{3,7},{5,1},{7,3},{8,12},{10,14},{12... | collective-permute-start | bytes 1572872 | tf_op jit(solution)/shard_map/ppermute | solution.py:73
  498.1 7.7 %collective-permute-start.50 = (bf16[128,1024]{1,0:T(8,128)(2,1)S(1)}, bf16[128,1024]{1,0:T(8,128)(2,1)S(1)}, u32[]{:S(2)}, u32[]{:S(2)}) collective-permute-start(bf16[128,1024]{1,0:T(8,128)(2,1)S(1)} %slice.354), channel_id=1, source_target_pairs={{0,4},{2,6},{4,0},{6,2},{1,5},{3,7},{5,1},{7,3},{8,12},{10,14},{12... | collective-permute-start | bytes 786440 | tf_op jit(solution)/shard_map/ppermute | solution.py:73
  499.6 7.5 %collective-permute-start.51 = (bf16[128,1024]{1,0:T(8,128)(2,1)S(1)}, bf16[128,1024]{1,0:T(8,128)(2,1)S(1)}, u32[]{:S(2)}, u32[]{:S(2)}) collective-permute-start(bf16[128,1024]{1,0:T(8,128)(2,1)S(1)} %slice.355), channel_id=1, source_target_pairs={{0,2},{2,0},{4,6},{6,4},{1,3},{3,1},{5,7},{7,5},{8,10},{10,8},{12,... | collective-permute-start | bytes 786440 | tf_op jit(solution)/shard_map/ppermute | solution.py:73
  507.1 5.0 collective-permute-start.52
  542.5 9.8 %collective-permute-start.57 = (f32[2,4,256]{2,1,0:T(4,128)S(1)}, f32[2,4,256]{2,1,0:T(4,128)S(1)}, u32[]{:S(2)}, u32[]{:S(2)}) collective-permute-start(f32[2,4,256]{2,1,0:T(4,128)S(1)} %reshape.634), channel_id=1, source_target_pairs={{0,6},{2,4},{4,2},{6,0},{1,7},{3,5},{5,3},{7,1},{8,14},{10,12},{12... | collective-permute-start | bytes 24584 | tf_op jit(solution)/shard_map/ppermute | solution.py:73
  557.2 15.7 %collective-permute-start.58 = (bf16[3,1024,256]{2,1,0:T(8,128)(2,1)S(1)}, bf16[3,1024,256]{2,1,0:T(8,128)(2,1)S(1)}, u32[]{:S(2)}, u32[]{:S(2)}) collective-permute-start(bf16[3,1024,256]{2,1,0:T(8,128)(2,1)S(1)} %pad_maximum_fusion.refs_0_.refs_1_), channel_id=1, source_target_pairs={{0,1},{1,0},{2,3},{3,2},{4,5},{5,4},{6,7},{7,6},{8,9},{9,8},{10,11... | collective-permute-start | bytes 4718600 | tf_op jit(solution)/shard_map/ppermute | solution.py:73
  557.3 7.6 %collective-permute-start.62 = (f32[4,2048]{1,0:T(4,128)S(1)}, f32[4,2048]{1,0:T(4,128)S(1)}, u32[]{:S(2)}, u32[]{:S(2)}) collective-permute-start(f32[4,2048]{1,0:T(4,128)S(1)} %maximum_dynamic-update-slice_fusion.1), channel_id=1, source_target_pairs={{0,8},{8,0},{16,24},{24,16},{1,9},{9,1},{17,25},{25,17},{2,10},{10... | collective-permute-start | bytes 98312 | tf_op jit(solution)/shard_map/ppermute | solution.py:73
  564.9 7.3 %collective-permute-start.63 = (f32[4,2048]{1,0:T(4,128)S(1)}, f32[4,2048]{1,0:T(4,128)S(1)}, u32[]{:S(2)}, u32[]{:S(2)}) collective-permute-start(f32[4,2048]{1,0:T(4,128)S(1)} %add.365), channel_id=1, source_target_pairs={{0,16},{8,24},{16,0},{24,8},{1,17},{9,25},{17,1},{25,9},{2,18},{10... | collective-permute-start | bytes 98312 | tf_op jit(solution)/shard_map/ppermute | solution.py:73
  585.7 24.7 %collective-permute-start.70 = (bf16[2,256,512]{2,1,0:T(8,128)(2,1)}, bf16[2,256,512]{2,1,0:T(8,128)(2,1)}, u32[]{:S(2)}, u32[]{:S(2)}) collective-permute-start(bf16[2,256,512]{2,1,0:T(8,128)(2,1)} %dynamic-slice_bitcast_fusion), channel_id=1, source_target_pairs={{0,24},{8,0},{16,8},{24,16},{1,25},{9,1},{17,9},{25,17},{2,26},{10... | collective-permute-start | bytes 1572872 | tf_op jit(solution)/shard_map/ppermute | solution.py:199
  590.6 30.8 %collective-permute-start.67 = (bf16[2,256,512]{2,1,0:T(8,128)(2,1)}, bf16[2,256,512]{2,1,0:T(8,128)(2,1)}, u32[]{:S(2)}, u32[]{:S(2)}) collective-permute-start(bf16[2,256,512]{2,1,0:T(8,128)(2,1)} %dynamic-slice_bitcast_fusion.1), channel_id=1, source_target_pairs={{0,24},{8,0},{16,8},{24,16},{1,25},{9,1},{17,9},{25,17},{2,26},{10... | collective-permute-start | bytes 1572872 | tf_op jit(solution)/shard_map/ppermute | solution.py:199
  595.8 30.0 %collective-permute-start.66 = (f32[4,2048]{1,0:T(4,128)S(1)}, f32[4,2048]{1,0:T(4,128)S(1)}, u32[]{:S(2)}, u32[]{:S(2)}) collective-permute-start(f32[4,2048]{1,0:T(4,128)S(1)} %add.368), channel_id=1, source_target_pairs={{0,4},{2,6},{4,0},{6,2},{1,5},{3,7},{5,1},{7,3},{8,12},{10,14},{12... | collective-permute-start | bytes 98312 | tf_op jit(solution)/shard_map/ppermute | solution.py:73
  604.9 51.8 %collective-permute-start.59 = (bf16[256,1024]{1,0:T(8,128)(2,1)}, bf16[256,1024]{1,0:T(8,128)(2,1)}, u32[]{:S(2)}, u32[]{:S(2)}) collective-permute-start(bf16[256,1024]{1,0:T(8,128)(2,1)} %get-tuple-element.89), channel_id=1, source_target_pairs={{0,2},{2,0},{4,6},{6,4},{1,3},{3,1},{5,7},{7,5},{8,10},{10,8},{12,... | collective-permute-start | bytes 1572872 | tf_op jit(solution)/shard_map/ppermute | solution.py:73
  604.9 51.8 %collective-permute-start.60 = (bf16[256,1024]{1,0:T(8,128)(2,1)}, bf16[256,1024]{1,0:T(8,128)(2,1)}, u32[]{:S(2)}, u32[]{:S(2)}) collective-permute-start(bf16[256,1024]{1,0:T(8,128)(2,1)} %get-tuple-element.90), channel_id=1, source_target_pairs={{0,4},{2,6},{4,0},{6,2},{1,5},{3,7},{5,1},{7,3},{8,12},{10,14},{12... | collective-permute-start | bytes 1572872 | tf_op jit(solution)/shard_map/ppermute | solution.py:73
  610.4 46.3 %collective-permute-start.61 = (bf16[256,1024]{1,0:T(8,128)(2,1)}, bf16[256,1024]{1,0:T(8,128)(2,1)}, u32[]{:S(2)}, u32[]{:S(2)}) collective-permute-start(bf16[256,1024]{1,0:T(8,128)(2,1)} %get-tuple-element.91), channel_id=1, source_target_pairs={{0,6},{2,4},{4,2},{6,0},{1,7},{3,5},{5,3},{7,1},{8,14},{10,12},{12... | collective-permute-start | bytes 1572872 | tf_op jit(solution)/shard_map/ppermute | solution.py:73
  621.4 15.3 %collective-permute-start.71 = (bf16[2,256,512]{2,1,0:T(8,128)(2,1)S(1)}, bf16[2,256,512]{2,1,0:T(8,128)(2,1)S(1)}, u32[]{:S(2)}, u32[]{:S(2)}) collective-permute-start(bf16[2,256,512]{2,1,0:T(8,128)(2,1)S(1)} %fusion.25), channel_id=1, source_target_pairs={{0,24},{8,0},{16,8},{24,16},{1,25},{9,1},{17,9},{25,17},{2,26},{10... | collective-permute-start | bytes 1572872 | tf_op jit(solution)/shard_map/ppermute | solution.py:199
  625.8 27.2 %collective-permute-start.68 = (bf16[2,256,512]{2,1,0:T(8,128)(2,1)S(1)}, bf16[2,256,512]{2,1,0:T(8,128)(2,1)S(1)}, u32[]{:S(2)}, u32[]{:S(2)}) collective-permute-start(bf16[2,256,512]{2,1,0:T(8,128)(2,1)S(1)} %fusion.28), channel_id=1, source_target_pairs={{0,24},{8,0},{16,8},{24,16},{1,25},{9,1},{17,9},{25,17},{2,26},{10... | collective-permute-start | bytes 1572872 | tf_op jit(solution)/shard_map/ppermute | solution.py:199
  637.7 21.8 %collective-permute-start.72 = (bf16[2,256,512]{2,1,0:T(8,128)(2,1)}, bf16[2,256,512]{2,1,0:T(8,128)(2,1)}, u32[]{:S(2)}, u32[]{:S(2)}) collective-permute-start(bf16[2,256,512]{2,1,0:T(8,128)(2,1)} %fusion.26), channel_id=1, source_target_pairs={{0,24},{8,0},{16,8},{24,16},{1,25},{9,1},{17,9},{25,17},{2,26},{10... | collective-permute-start | bytes 1572872 | tf_op jit(solution)/shard_map/ppermute | solution.py:199
  656.6 12.7 %collective-permute-start.69 = (bf16[2,256,512]{2,1,0:T(8,128)(2,1)S(1)}, bf16[2,256,512]{2,1,0:T(8,128)(2,1)S(1)}, u32[]{:S(2)}, u32[]{:S(2)}) collective-permute-start(bf16[2,256,512]{2,1,0:T(8,128)(2,1)S(1)} %fusion.29), channel_id=1, source_target_pairs={{0,24},{8,0},{16,8},{24,16},{1,25},{9,1},{17,9},{25,17},{2,26},{10... | collective-permute-start | bytes 1572872 | tf_op jit(solution)/shard_map/ppermute | solution.py:199
  (116 other events, 743.8 us)
Sparse Core Ops, SparseCore 0:
  82.3 151.5 all-gather.3
  236.0 61.7 all-gather.5
  299.9 26.5 all-gather.7
  376.4 75.3 reduce-scatter.2
  454.1 155.2 reduce-scatter.4
